TPU v7x, 32 devices: a whole 2x2x4 slice. The times are simulated.
32 devices in a mesh: blk: 8 (over y, x, core), group: 4 (over z).
Axes of the slice: x: 2, y: 2, z: 4, core: 2. Of those that a mesh axis runs over, the one named last changes fastest.
Arguments:
- tokens: bfloat16 [20, 2048, 512], P('group', 'blk'), may hold values from -6 to 6
- cotangent: bfloat16 [20, 2048, 512], P('group', 'blk')
- lengths: int32 [20], P('group'), may hold values from 128 to 2048, as said below
- ln_params: float32 [4, 512], replicated
- attn_master: float32 [4, 512, 512], P(None, 'blk', 'group')
- attn_first: float32 [4, 512, 512], P(None, 'blk', 'group')
- attn_second: float32 [4, 512, 512], P(None, 'blk', 'group')
- up_master: float32 [512, 2048], P('blk', 'group'), may hold values from -0.25 to 0.25
- up_first: float32 [512, 2048], P('blk', 'group'), may hold values from -768 to 768
- up_second: float32 [512, 2048], P('blk', 'group'), may hold values from 14745.6 to 58982.4
- down_master: float32 [2048, 512], P('blk', 'group'), may hold values from -0.125 to 0.125
- down_first: float32 [2048, 512], P('blk', 'group'), may hold values from -1536 to 1536
- down_second: float32 [2048, 512], P('blk', 'group'), may hold values from 58982.4 to 235929.6
- ln_first: float32 [4, 512], replicated, may hold values from -4096 to 4096
- ln_second: float32 [4, 512], replicated, may hold values from 552960 to 2211840
Outputs:
- block_out: bfloat16 [20, 2048, 512], P('group', 'blk')
- input_grad: float32 [20, 2048, 512], P('group', 'blk')
- attn_moment1: float32 [4, 512, 512], P(None, 'blk', 'group')
- attn_moment2: float32 [4, 512, 512], P(None, 'blk', 'group')
- attn_new: float32 [4, 512, 512], P(None, 'blk', 'group')
- attn_copy: bfloat16 [4, 512, 512], P(None, 'blk', 'group')
- up_moment1: float32 [512, 2048], P('blk', 'group')
- up_moment2: float32 [512, 2048], P('blk', 'group')
- up_new: float32 [512, 2048], P('blk', 'group')
- up_copy: bfloat16 [512, 2048], P('blk', 'group')
- down_moment1: float32 [2048, 512], P('blk', 'group')
- down_moment2: float32 [2048, 512], P('blk', 'group')
- down_new: float32 [2048, 512], P('blk', 'group')
- down_copy: bfloat16 [2048, 512], P('blk', 'group')
- ln_moment1: float32 [4, 512], replicated
- ln_moment2: float32 [4, 512], replicated
- ln_new: float32 [4, 512], replicated
- norms: float32 [2, 6], replicated
Inputs may be any that keep to these rules, and one draw needn't show every extreme that they name: `lengths`: in each group of 5 consecutive sequences one, drawn from the seed, has all 2048 positions valid.
All inputs are finite; a program needn't handle non-finite values.
Results may differ from a plain program's by a relative error of at most 0.024.
Values may be sent and summed in bfloat16 or wider, within the bound.
No kernel may reach another device: no remote copies, remote signals or barrier semaphores. Data moves between devices by JAX's collectives and lax.ppermute only.
A program may use at most 192 MiB of HBM per device.

v0:
```python
import jax
import jax.numpy as jnp
from jax import lax
from jax.sharding import PartitionSpec as P

HEADS = 8
SPAN = 128
STEP = 5


masked_value = -1e30
decay_rate = 0.5
matrix_rate = 0.3
vector_rate = 0.5
weight_decay = 0.01
epsilon = 1e-06


def layer_norm(values, gain, bias):
    center = values - jnp.mean(values, -1, keepdims=True)
    spread = jnp.mean(center * center, -1, keepdims=True)
    inverse = lax.rsqrt(spread + 1e-05)
    normal_part = center * inverse
    return (normal_part * gain + bias, normal_part, inverse)


def norm_back(gradient, normal_part, inverse, gain):
    scaled = gradient * gain
    inner_mean = jnp.mean(scaled, -1, keepdims=True)
    cross_mean = jnp.mean(scaled * normal_part, -1, keepdims=True)
    back = inverse * (scaled - inner_mean - normal_part * cross_mean)
    return (back, jnp.sum(gradient * normal_part, 0), jnp.sum(gradient, 0))


def gelu_tanh(values):
    return jax.nn.gelu(values, approximate=True)


def gather_cols(arrays):
    return (
        lax.all_gather(arrays[0], "group", axis=2, tiled=True),
        lax.all_gather(arrays[1], "group", axis=1, tiled=True),
        lax.all_gather(arrays[2], "group", axis=1, tiled=True),
    )


def gather_rows(arrays):
    return (
        lax.all_gather(arrays[0], "blk", axis=1, tiled=True),
        lax.all_gather(arrays[1], "blk", axis=0, tiled=True),
        lax.all_gather(arrays[2], "blk", axis=0, tiled=True),
    )


def reduce_rows(arrays):
    return (
        lax.psum_scatter(
            arrays[0].astype(jnp.bfloat16), "blk", scatter_dimension=1, tiled=True
        ).astype(jnp.float32),
        lax.psum_scatter(
            arrays[1].astype(jnp.bfloat16), "blk", scatter_dimension=0, tiled=True
        ).astype(jnp.float32),
        lax.psum_scatter(
            arrays[2].astype(jnp.bfloat16), "blk", scatter_dimension=0, tiled=True
        ).astype(jnp.float32),
    )


def reduce_cols(arrays):
    return (
        lax.psum_scatter(
            arrays[0].astype(jnp.bfloat16), "group", scatter_dimension=2, tiled=True
        ).astype(jnp.float32),
        lax.psum_scatter(
            arrays[1].astype(jnp.bfloat16), "group", scatter_dimension=1, tiled=True
        ).astype(jnp.float32),
        lax.psum_scatter(
            arrays[2].astype(jnp.bfloat16), "group", scatter_dimension=1, tiled=True
        ).astype(jnp.float32),
    )


def moments(gradient, first, second):
    corr = 1.0 - decay_rate**STEP
    new_first = decay_rate * first + (1.0 - decay_rate) * gradient
    new_second = decay_rate * second + (1.0 - decay_rate) * gradient * gradient
    return (new_first, new_second, new_first / corr / (jnp.sqrt(new_second / corr) + epsilon))


def body(
    tokens,
    cotangent,
    lengths,
    ln_params,
    attn_master,
    attn_first,
    attn_second,
    up_master,
    up_first,
    up_second,
    down_master,
    down_first,
    down_second,
    ln_first,
    ln_second,
):
    highest = lax.Precision.HIGHEST
    seq_count, tok_count, model_width = tokens.shape
    head_width = model_width // HEADS
    span_count = tok_count // SPAN
    factor = head_width ** (-0.5)
    cycle_place = lax.axis_index("blk")
    row_count = seq_count * tok_count
    copies = (
        attn_master.astype(jnp.bfloat16),
        up_master.astype(jnp.bfloat16),
        down_master.astype(jnp.bfloat16),
    )
    attn_low, up_low, down_low = gather_rows(gather_cols(copies))
    inputs = tokens.reshape(row_count, model_width).astype(jnp.float32)
    normed_in, normal_in, inverse_in = layer_norm(inputs, ln_params[0], ln_params[1])
    normed_low = normed_in.astype(jnp.bfloat16)
    projected = jnp.einsum(
        "rd,kde->kre", normed_low, attn_low[:3], preferred_element_type=jnp.float32
    ).astype(jnp.bfloat16)
    query_rows, key_rows, value_rows = (projected[0], projected[1], projected[2])
    query_spans = query_rows.reshape(seq_count, span_count, SPAN, HEADS, head_width)
    key_spans = key_rows.reshape(seq_count, span_count, SPAN, HEADS, head_width)
    value_spans = value_rows.reshape(seq_count, span_count, SPAN, HEADS, head_width)
    query_heads = query_rows.reshape(seq_count, tok_count, HEADS, head_width)
    positions = cycle_place * tok_count + jnp.arange(tok_count, dtype=jnp.int32)
    valid_span = (positions[None, :] < lengths[:, None]).reshape(seq_count, span_count, SPAN)
    counts = jnp.sum(valid_span.astype(jnp.float32), -1)
    denom = jnp.maximum(counts, 1.0)
    valid_low = valid_span.astype(jnp.bfloat16)
    key_sum = (
        jnp.einsum(
            "bsk,bskd->bsd",
            valid_low,
            key_rows.reshape(seq_count, span_count, SPAN, model_width),
            preferred_element_type=jnp.float32,
        )
        / denom[..., None]
    ).astype(jnp.bfloat16)
    value_sum = (
        jnp.einsum(
            "bsk,bskd->bsd",
            valid_low,
            value_rows.reshape(seq_count, span_count, SPAN, model_width),
            preferred_element_type=jnp.float32,
        )
        / denom[..., None]
    ).astype(jnp.bfloat16)
    query_span = cycle_place * span_count + jnp.arange(tok_count, dtype=jnp.int32) // SPAN
    inner = jnp.arange(SPAN, dtype=jnp.int32)
    causal = inner[None, :] <= inner[:, None]
    local_mask = causal[None, None, None] & valid_span[:, :, None, None, :]
    local = (
        jnp.einsum("bsqhe,bskhe->bshqk", query_spans, key_spans, preferred_element_type=jnp.float32)
        * factor
    )
    local = jnp.where(local_mask, local, masked_value)

    def rows_of(array):
        return jnp.transpose(array, (0, 2, 1, 3)).reshape(seq_count, HEADS, tok_count)

    def spans_of(array):
        return jnp.transpose(array.reshape(seq_count, HEADS, span_count, SPAN), (0, 2, 1, 3))[
            ..., None
        ]

    def summary_scores(key_piece):
        amount = key_piece.shape[1]
        key_heads = key_piece.reshape(seq_count, amount, HEADS, head_width)
        index = jnp.arange(amount, dtype=jnp.int32)
        allowed = (query_span[:, None] > index[None, :])[None] & (
            index[None, None, :] * SPAN < lengths[:, None, None]
        )
        allowed = allowed[:, None]
        scores = (
            jnp.einsum(
                "bqhe,bnhe->bhqn", query_heads, key_heads, preferred_element_type=jnp.float32
            )
            * factor
        )
        return (jnp.where(allowed, scores, masked_value), allowed, key_heads)

    local_top = rows_of(jnp.max(local, -1))
    pieces = (
        lax.all_gather(key_sum, "blk", axis=1, tiled=True),
        lax.all_gather(value_sum, "blk", axis=1, tiled=True),
    )
    run_top = jnp.full((seq_count, HEADS, tok_count), masked_value, jnp.float32)
    scores, allowed, key_heads = summary_scores(pieces[0])
    value_heads = pieces[1].reshape(seq_count, pieces[1].shape[1], HEADS, head_width)
    new_top = jnp.maximum(run_top, jnp.max(scores, -1))
    weights = jnp.where(allowed, jnp.exp(scores - new_top[..., None]), 0.0)
    run_total = jnp.sum(weights, -1)
    acc_low = jnp.einsum(
        "bhqn,bnhe->bqhe",
        weights.astype(jnp.bfloat16),
        value_heads,
        preferred_element_type=jnp.float32,
    )
    acc_full = jnp.einsum(
        "bhqn,bnhe->bqhe", weights, value_heads.astype(jnp.float32), precision=highest
    )
    run_top, run_total, acc_low, acc_full = (new_top, run_total, acc_low, acc_full)
    top = jnp.maximum(run_top, local_top)
    total = run_total * jnp.exp(run_top - top) + rows_of(
        jnp.sum(jnp.exp(local - spans_of(top)), -1)
    )
    log_total = top + jnp.log(total)
    back_scale = jnp.transpose(jnp.exp(run_top - log_total), (0, 2, 1))[..., None]
    summary_low = acc_low * back_scale
    summary_full = acc_full * back_scale
    probs_local = jnp.exp(local - spans_of(log_total))
    local_low = probs_local.astype(jnp.bfloat16)
    out_low = (
        jnp.einsum(
            "bshqk,bskhe->bsqhe", local_low, value_spans, preferred_element_type=jnp.float32
        ).reshape(seq_count, tok_count, HEADS, head_width)
        + summary_low
    )
    out_full = (
        jnp.einsum(
            "bshqk,bskhe->bsqhe", probs_local, value_spans.astype(jnp.float32), precision=highest
        ).reshape(seq_count, tok_count, HEADS, head_width)
        + summary_full
    )
    mixed = out_low.reshape(row_count, model_width).astype(jnp.bfloat16)
    middle = inputs + jnp.dot(mixed, attn_low[3], preferred_element_type=jnp.float32)
    normed_mid, normal_mid, inverse_mid = layer_norm(middle, ln_params[2], ln_params[3])
    mid_low = normed_mid.astype(jnp.bfloat16)
    up_rows = jnp.dot(mid_low, up_low, preferred_element_type=jnp.float32)
    activated, gelu_back = jax.vjp(gelu_tanh, up_rows)
    act_low = activated.astype(jnp.bfloat16)
    result = middle + jnp.dot(act_low, down_low, preferred_element_type=jnp.float32)
    block_out = result.astype(jnp.bfloat16).reshape(tokens.shape)
    grad_out = cotangent.reshape(row_count, model_width)
    grad_down = jnp.einsum("rf,rd->fd", act_low, grad_out, preferred_element_type=jnp.float32)
    grad_act = jnp.einsum("rd,fd->rf", grad_out, down_low, preferred_element_type=jnp.float32)
    grad_up_rows = gelu_back(grad_act)[0].astype(jnp.bfloat16)
    grad_up = jnp.einsum("rd,rf->df", mid_low, grad_up_rows, preferred_element_type=jnp.float32)
    grad_mid = jnp.einsum("rf,df->rd", grad_up_rows, up_low, preferred_element_type=jnp.float32)
    back_mid, gain_two_grad, bias_two_grad = norm_back(
        grad_mid, normal_mid, inverse_mid, ln_params[2]
    )
    grad_middle = grad_out.astype(jnp.float32) + back_mid
    grad_branch = grad_middle.astype(jnp.bfloat16)
    grad_out_proj = jnp.einsum("re,rd->ed", mixed, grad_branch, preferred_element_type=jnp.float32)
    grad_mixed = jnp.einsum(
        "rd,ed->re", grad_branch, attn_low[3], preferred_element_type=jnp.float32
    ).astype(jnp.bfloat16)
    grad_heads = grad_mixed.reshape(seq_count, tok_count, HEADS, head_width)
    grad_spans = grad_mixed.reshape(seq_count, span_count, SPAN, HEADS, head_width)
    row_dot = jnp.transpose(jnp.sum(grad_heads.astype(jnp.float32) * out_full, -1), (0, 2, 1))
    grad_probs = jnp.einsum(
        "bsqhe,bskhe->bshqk", grad_spans, value_spans, preferred_element_type=jnp.float32
    )
    grad_scores = (probs_local * (grad_probs - spans_of(row_dot))).astype(jnp.bfloat16)
    grad_query = factor * jnp.einsum(
        "bshqk,bskhe->bsqhe", grad_scores, key_spans, preferred_element_type=jnp.float32
    )
    grad_key = factor * jnp.einsum(
        "bshqk,bsqhe->bskhe", grad_scores, query_spans, preferred_element_type=jnp.float32
    )
    grad_value = jnp.einsum(
        "bshqk,bsqhe->bskhe", local_low, grad_spans, preferred_element_type=jnp.float32
    )
    pieces = (
        lax.all_gather(key_sum, "blk", axis=1, tiled=True),
        lax.all_gather(value_sum, "blk", axis=1, tiled=True),
    )
    value_piece = pieces[1]
    scores, allowed, key_heads = summary_scores(pieces[0])
    amount = value_piece.shape[1]
    value_heads = value_piece.reshape(seq_count, amount, HEADS, head_width)
    probs = jnp.exp(scores - log_total[..., None])
    grad_p = jnp.einsum(
        "bqhe,bnhe->bhqn", grad_heads, value_heads, preferred_element_type=jnp.float32
    )
    grad_s = (probs * (grad_p - row_dot[..., None])).astype(jnp.bfloat16)
    part_query = factor * jnp.einsum(
        "bhqn,bnhe->bqhe", grad_s, key_heads, preferred_element_type=jnp.float32
    )
    part_key = factor * jnp.einsum(
        "bhqn,bqhe->bnhe", grad_s, query_heads, preferred_element_type=jnp.float32
    )
    part_value = jnp.einsum(
        "bhqn,bqhe->bnhe",
        probs.astype(jnp.bfloat16),
        grad_heads,
        preferred_element_type=jnp.float32,
    )
    part_query, part_key, part_value = (
        part_query,
        part_key.reshape(seq_count, amount, model_width),
        part_value.reshape(seq_count, amount, model_width),
    )
    amount = pieces[0].shape[1]
    own_key, own_value = (
        lax.psum_scatter(
            part_key.astype(jnp.bfloat16), "blk", scatter_dimension=1, tiled=True
        ).astype(jnp.float32),
        lax.psum_scatter(
            part_value.astype(jnp.bfloat16), "blk", scatter_dimension=1, tiled=True
        ).astype(jnp.float32),
    )
    share = (valid_span.astype(jnp.float32) / denom[..., None])[..., None]
    key_total = (
        grad_key.reshape(seq_count, span_count, SPAN, model_width) + share * own_key[:, :, None, :]
    )
    value_total = (
        grad_value.reshape(seq_count, span_count, SPAN, model_width)
        + share * own_value[:, :, None, :]
    )
    query_total = grad_query.reshape(seq_count, tok_count, HEADS, head_width) + part_query
    stacked = jnp.stack(
        [
            query_total.reshape(row_count, model_width),
            key_total.reshape(row_count, model_width),
            value_total.reshape(row_count, model_width),
        ]
    ).astype(jnp.bfloat16)
    grad_qkv = jnp.einsum("rd,kre->kde", normed_low, stacked, preferred_element_type=jnp.float32)
    grad_in = jnp.einsum("kre,kde->rd", stacked, attn_low[:3], preferred_element_type=jnp.float32)
    back_in, gain_one_grad, bias_one_grad = norm_back(grad_in, normal_in, inverse_in, ln_params[0])
    input_grad = (grad_middle + back_in).reshape(tokens.shape)
    full_grads = (jnp.concatenate([grad_qkv, grad_out_proj[None]], 0), grad_up, grad_down)
    red_attn, red_up, red_down = reduce_cols(reduce_rows(full_grads))
    norm_partial = jnp.stack([gain_one_grad, bias_one_grad, gain_two_grad, bias_two_grad])
    attn_moment1, attn_moment2, attn_dir = moments(red_attn, attn_first, attn_second)
    up_moment1, up_moment2, up_dir = moments(red_up, up_first, up_second)
    down_moment1, down_moment2, down_dir = moments(red_down, down_first, down_second)
    attn_step = attn_dir + weight_decay * attn_master
    up_step = up_dir + weight_decay * up_master
    down_step = down_dir + weight_decay * down_master
    weight_sq = jnp.concatenate(
        [
            jnp.sum(attn_master * attn_master, (1, 2)),
            jnp.sum(up_master * up_master)[None],
            jnp.sum(down_master * down_master)[None],
        ]
    )
    step_sq = jnp.concatenate(
        [
            jnp.sum(attn_step * attn_step, (1, 2)),
            jnp.sum(up_step * up_step)[None],
            jnp.sum(down_step * down_step)[None],
        ]
    )
    sq_totals, norm_grad = lax.psum(
        (jnp.stack([weight_sq, step_sq]), norm_partial), ("blk", "group")
    )
    trust = jnp.sqrt(sq_totals[0]) / jnp.sqrt(sq_totals[1] + epsilon)
    attn_new = attn_master - matrix_rate * trust[:4, None, None] * attn_step
    up_new = up_master - matrix_rate * trust[4] * up_step
    down_new = down_master - matrix_rate * trust[5] * down_step
    ln_moment1, ln_moment2, ln_dir = moments(norm_grad, ln_first, ln_second)
    ln_new = ln_params - vector_rate * ln_dir
    norms = jnp.sqrt(sq_totals)
    return (
        block_out,
        input_grad,
        attn_moment1,
        attn_moment2,
        attn_new,
        attn_new.astype(jnp.bfloat16),
        up_moment1,
        up_moment2,
        up_new,
        up_new.astype(jnp.bfloat16),
        down_moment1,
        down_moment2,
        down_new,
        down_new.astype(jnp.bfloat16),
        ln_moment1,
        ln_moment2,
        ln_new,
        norms,
    )


def solution(mesh):
    placed = (
        P("group", "blk", None),
        P("group", "blk", None),
        P("group"),
        P(),
        P(None, "blk", "group"),
        P(None, "blk", "group"),
        P(None, "blk", "group"),
        P("blk", "group"),
        P("blk", "group"),
        P("blk", "group"),
        P("blk", "group"),
        P("blk", "group"),
        P("blk", "group"),
        P(),
        P(),
    )
    return jax.shard_map(
        body,
        mesh=mesh,
        in_specs=placed,
        out_specs=(
            P("group", "blk", None),
            P("group", "blk", None),
            P(None, "blk", "group"),
            P(None, "blk", "group"),
            P(None, "blk", "group"),
            P(None, "blk", "group"),
            P("blk", "group"),
            P("blk", "group"),
            P("blk", "group"),
            P("blk", "group"),
            P("blk", "group"),
            P("blk", "group"),
            P("blk", "group"),
            P("blk", "group"),
            P(),
            P(),
            P(),
            P(),
        ),
        check_vma=False,
    )
```

profile of v0, /device:TPU:0, one launch (start us, length us, event | category | flops | bytes accessed | tf_op | source)
XLA Modules:
  0.0 572.9 jit_solution(11238930804896060779)
XLA Ops:
  8.3 15.1 %all_gather.26 = bf16[4,64,512]{2,1,0:T(8,128)(2,1)} all-gather(bf16[4,64,128]{2,1,0:T(8,128)(2,1)S(1)} %convert_element_type.152), channel_id=1, replica_groups=mesh['blk'=8,'group'=4] {'group'}, dimensions={2}, use_global_device_ids=true | all-gather | bytes 327680 | tf_op jit(solution)/shard_map/all_gather | solution.py:41
  24.4 15.1 %all_gather.30 = bf16[64,2048]{1,0:T(8,128)(2,1)} all-gather(bf16[64,512]{1,0:T(8,128)(2,1)S(1)} %convert_element_type.163), channel_id=1, replica_groups=mesh['blk'=8,'group'=4] {'group'}, dimensions={1}, use_global_device_ids=true | all-gather | bytes 327680 | tf_op jit(solution)/shard_map/all_gather | solution.py:42
  44.1 7.7 %all-gather.4.cloned.1.call-done = bf16[4,512,512]{2,1,0:T(8,128)(2,1)} async-done(((bf16[4,64,512]{2,1,0:T(8,128)(2,1)}), bf16[4,512,512]{2,1,0:T(8,128)(2,1)}) %all-gather.4.cloned.1.call-update) | async-done | bytes 2097168 | tf_op jit(solution)/shard_map/all_gather | solution.py:49
  51.8 3.6 fusion.8
  65.4 9.2 %all_gather.28 = bf16[5,16,512]{2,0,1:T(8,128)(2,1)S(1)} all-gather(bf16[5,2,512]{2,0,1:T(8,128)(2,1)S(1)} %get-tuple-element.138), channel_id=1, replica_groups=mesh['blk'=8,'group'=4] {'blk'}, dimensions={1}, use_global_device_ids=true | all-gather | bytes 92160 | tf_op jit(solution)/shard_map/all_gather | solution.py:190
  76.9 4.3 reshape.447
  81.2 4.3 reshape.448
  85.5 3.8 reshape_squeeze.19
  89.4 4.1 copy.238
  93.5 4.1 copy.232
  97.6 8.4 %all_gather.29 = bf16[5,16,512]{2,0,1:T(8,128)(2,1)S(1)} all-gather(bf16[5,2,512]{2,0,1:T(8,128)(2,1)S(1)} %copy-done.54), channel_id=1, replica_groups=mesh['blk'=8,'group'=4] {'blk'}, dimensions={1}, use_global_device_ids=true | all-gather | bytes 92160 | tf_op jit(solution)/shard_map/all_gather | solution.py:191
  106.4 2.9 fusion.7
  119.6 5.5 fusion.89
  125.1 4.0 copy-done.80
  129.1 5.3 convolution_convert_fusion.1
  134.5 41.4 %reduce-scatter.16.cloned.1.call-done = bf16[256,512]{1,0:T(8,128)(2,1)} async-done(((bf16[2048,512]{1,0:T(8,128)(2,1)}), bf16[256,512]{1,0:T(8,128)(2,1)}) %reduce-scatter.16.cloned.1.call-update) | async-done | bytes 262160 | tf_op jit(solution)/shard_map/reduce_scatter | solution.py:63
  177.8 20.0 %reduce-scatter.20.cloned.1.call-done = bf16[128,256]{1,0:T(8,128)(2,1)} async-done(((bf16[512,256]{1,0:T(8,128)(2,1)}), bf16[128,256]{1,0:T(8,128)(2,1)}) %reduce-scatter.20.cloned.1.call-update) | async-done | bytes 65552
  200.3 13.4 %all_gather.32 = bf16[256,512]{1,0:T(8,128)(2,1)} all-gather(bf16[256,128]{1,0:T(8,128)(2,1)S(1)} %get-tuple-element.128), channel_id=1, replica_groups=mesh['blk'=8,'group'=4] {'group'}, dimensions={1}, use_global_device_ids=true | all-gather | bytes 327680 | tf_op jit(solution)/shard_map/all_gather | solution.py:43
  215.7 7.8 %fusion.21 = f32[5,2,8,8,8,128]{5,4,3,2,1,0:T(8,128)} fusion(bf16[5,2,128,8,64]{2,4,3,1,0:T(8,128)(2,1)} %copy.238, f32[5,2,8,128,128]{3,4,2,1,0:T(8,128)} %copy-done, f32[5,2,8,128]{3,2,1,0:T(8,128)S(1)} %fusion.69, pred[5,2,128,128]{2,3,1,0:T(8,128)(4,1)S(1)} %broadcast_and_fusion), kind=kOutput, calls=%fused_computation.63 | convolution fusion | flops 1010565120 | bytes 9379840 | tf_op jit(solution)/shard_map/bshqk,bskhe->bsqhe/dot_general | solution.py:226
  223.5 16.8 %all-gather.8.cloned.1.call-done = bf16[2048,512]{1,0:T(8,128)(2,1)} async-done(((bf16[256,512]{1,0:T(8,128)(2,1)}), bf16[2048,512]{1,0:T(8,128)(2,1)}) %all-gather.8.cloned.1.call-update) | async-done | bytes 2097168 | tf_op jit(solution)/shard_map/all_gather | solution.py:51
  240.3 12.3 %fusion.6 = bf16[1280,2048]{1,0:T(8,128)(2,1)S(1)} fusion(f32[1280,2048]{1,0:T(8,128)} %copy-done.80, bf16[1280,512]{1,0:T(8,128)(2,1)} %bitcast.238, bf16[2048,512]{1,0:T(8,128)(2,1)} %all-gather.8.cloned.1.call-done), kind=kOutput, calls=%fused_computation.8 | convolution fusion | flops 2736783360 | bytes 19136512 | tf_op jit(solution)/shard_map/rd,fd->rf/dot_general | solution.py:242
  252.7 4.3 multiply_reduce_fusion
  259.7 3.0 convolution_convert_fusion.3
  265.2 4.1 reshape.420
  269.3 4.1 reshape.419
  273.4 6.5 %convolution_bitcast_fusion.1 = f32[5,2,128,8,64]{2,4,3,1,0:T(8,128)} fusion(bf16[5,2,128,8,64]{2,1,0,4,3:T(2,128)(2,1)} %reshape.419, f32[5,2,8,128,128]{3,4,2,1,0:T(8,128)} %copy-done, f32[5,2,8,128]{3,2,1,0:T(8,128)} %copy-done.29, pred[5,2,128,128]{2,3,1,0:T(8,128)(4,1)S(1)} %broadcast_and_fusion), kind=kOutput, calls=%fused_computation.61 | convolution fusion | flops 173015040 | bytes 9379840 | tf_op jit(solution)/shard_map/bshqk,bsqhe->bskhe/dot_general | solution.py:268
  283.9 3.4 multiply_bitcast_fusion
  296.9 3.5 fusion.12
  300.4 3.4 fusion.29
  303.8 5.1 copy.290
  308.9 5.1 reshape.434
  313.9 4.9 copy.291
  318.8 5.1 reshape.435
  326.8 3.6 reshape.433
  330.4 22.2 %all-reduce.10.cloned.1.call-done = (bf16[5,16,512]{2,1,0:T(8,128)(2,1)}, bf16[5,16,512]{2,1,0:T(8,128)(2,1)}) async-done(((bf16[5,16,512]{2,1,0:T(8,128)(2,1)}, bf16[5,16,512]{2,1,0:T(8,128)(2,1)}), (bf16[5,16,512]{2,1,0:T(8,128)(2,1)}, bf16[5,16,512]{2,1,0:T(8,128)(2,1)})) %all-reduce.10.cloned.1.call-update) | async-done | bytes 163856
  360.6 3.2 copy.276
  363.9 7.8 %convolution_convert_fusion.2 = bf16[512,2048]{1,0:T(8,128)(2,1)} fusion(bf16[1280,2048]{1,0:T(8,128)(2,1)} %copy-done.81, f32[1280,512]{1,0:T(8,128)} %copy-done.2, f32[512]{0:T(512)S(1)} %bitcast.253, f32[512]{0:T(512)S(1)} %bitcast.250, f32[1280]{0:T(1024)S(1)} %copy-done.58, f32[1280]{0:T(1024)S(1)} %broadcast_multiply_fusion.4), kind=kOutput, calls=%fused_computation.23 | convolution fusion | flops 2688679936 | bytes 9975808 | tf_op jit(solution)/shard_map/rd,rf->df/dot_general | solution.py:244
  372.4 7.8 %fusion.9 = bf16[1280,512]{1,0:T(8,128)(2,1)} fusion(f32[1280,512]{1,0:T(8,128)} %copy-done.2, bf16[2048,512]{1,0:T(8,128)(2,1)S(1)} %copy-done.78, f32[1280,2048]{1,0:T(8,128)} %copy-done.80), kind=kOutput, calls=%fused_computation.21 | convolution fusion | flops 2709258240 | bytes 16515072 | tf_op jit(solution)/shard_map/dot_general | solution.py:238
  380.3 45.8 %all-reduce.8.cloned.1.call-done = bf16[4,512,512]{2,0,1:T(4,128)(2,1)} async-done(((bf16[4,512,512]{2,0,1:T(4,128)(2,1)}), bf16[4,512,512]{2,0,1:T(4,128)(2,1)}) %all-reduce.8.cloned.1.call-update) | async-done | bytes 2097168
  427.2 14.0 %copy.296 = bf16[4,64,512]{0,1,2:T(8,128)(2,1)} copy(bf16[4,64,512]{2,0,1:T(4,128)(2,1)S(1)} %constant_dynamic-slice_fusion) | data formatting | bytes 524288
  441.2 17.3 %reshape.440 = bf16[512,256]{1,0:T(8,128)(2,1)} reshape(bf16[512,64,4]{2,1,0:T(8,128)(2,1)} %bitcast.227) | data formatting | bytes 524288
  458.7 6.4 %multiply_reduce_fusion.1 = (f32[512]{0:T(512)S(1)}, f32[1280]{0:T(1024)S(1)}, f32[1280]{0:T(1024)S(1)}, f32[512]{0:T(512)S(1)}, f32[1280,512]{1,0:T(8,128)}) fusion(bf16[5,256,512]{2,1,0:T(8,128)(2,1)S(1)} %copy-done.1, f32[1280]{0:T(1024)S(1)} %copy-done.53, f32[1280]{0:T(1024)S(1)} %copy-done.51, f32[512]{0:T(512)S(1)} %bitcast.246, ...), kind=kOutput, calls=%fused_computation.39 | convolution fusion | flops 2023748096 | bytes 9463808 | tf_op jit(solution)/shard_map/kre,kde->rd/dot_general | solution.py:327
  465.7 4.2 reduce-scatter.12.cloned.1.call-done
  471.1 20.8 %reduce-scatter.18.cloned.1.call-done = bf16[128,256]{1,0:T(8,128)(2,1)} async-done(((bf16[512,256]{1,0:T(8,128)(2,1)}), bf16[128,256]{1,0:T(8,128)(2,1)}) %reduce-scatter.18.cloned.1.call-update) | async-done | bytes 65552
  491.9 5.3 reshape.441
  501.3 10.6 %reduce-scatter.14.cloned.1.call-done = bf16[64,512]{1,0:T(8,128)(2,1)} async-done(((bf16[64,2048]{1,0:T(8,128)(2,1)}), bf16[64,512]{1,0:T(8,128)(2,1)}) %reduce-scatter.14.cloned.1.call-update) | async-done | bytes 65552 | tf_op jit(solution)/shard_map/reduce_scatter | solution.py:74
  516.5 5.0 multiply_add_fusion
  521.6 38.6 %all-reduce.3 = (f32[2,6]{1,0:T(2,128)S(1)}, f32[4,512]{1,0:T(4,128)S(1)}) all-reduce(f32[2,6]{1,0:T(2,128)S(1)} %pad_maximum_fusion.7, f32[4,512]{1,0:T(4,128)S(1)} %copy-done.61), channel_id=1, replica_groups=mesh['blk'=8,'group'=4] {'blk','group'}, use_global_device_ids=true, to_apply=%region_28.29 | all-reduce | flops 2060 | bytes 16480 | tf_op jit(solution)/shard_map/psum | solution.py:353
  (279 shorter events, 80.2 us)
Async XLA Ops:
  7.2 33.9 %copy-start.1 = (bf16[5,256,512]{2,1,0:T(8,128)(2,1)S(1)}, bf16[5,256,512]{2,1,0:T(8,128)(2,1)}, u32[]{:S(2)}) copy-start(bf16[5,256,512]{2,1,0:T(8,128)(2,1)} %param.15) | copy-start | bytes 3932164
  7.2 34.6 %copy-start.71 = (s32[5]{0:T(128)S(1)}, s32[5]{0:T(128)}, u32[]{:S(2)}) copy-start(s32[5]{0:T(128)} %param.17) | copy-start | bytes 64
  7.2 35.2 %copy-start.59 = (f32[4,512]{1,0:T(4,128)S(1)}, f32[4,512]{1,0:T(4,128)}, u32[]{:S(2)}) copy-start(f32[4,512]{1,0:T(4,128)} %param.18) | copy-start | bytes 24580
  7.2 44.5 %all-gather.4.cloned.1.call-start = ((), (), s32[]{:S(2)}) async-start(), calls=%async_computation.5 | async-start | bytes 2359296 | tf_op jit(solution)/shard_map/all_gather | solution.py:49
  23.4 96.2 %all-gather.6.cloned.1.call-start = ((), (), s32[]{:S(2)}) async-start(), calls=%async_computation.6 | async-start | bytes 2359296 | tf_op jit(solution)/shard_map/all_gather | solution.py:50
  39.5 136.4 %reduce-scatter.16.cloned.1.call-start = ((), (), s32[]{:S(2)}) async-start(), calls=%async_computation.10 | async-start | bytes 2359296 | tf_op jit(solution)/shard_map/reduce_scatter | solution.py:63
  41.7 13.6 %copy-start.50 = (f32[1280]{0:T(1024)}, f32[1280]{0:T(1024)S(1)}, u32[]{:S(2)}) copy-start(f32[1280]{0:T(1024)S(1)} %div.103) | copy-start | bytes 15364
  43.0 12.4 %copy-start.63 = (f32[1,512]{1,0:T(1,128)}, f32[1,512]{1,0:T(1,128)S(1)}, u32[]{:S(2)}) copy-start(f32[1,512]{1,0:T(1,128)S(1)} %get-tuple-element.133) | copy-start | bytes 6148
  43.0 12.4 %copy-start.52 = (f32[1280]{0:T(1024)}, f32[1280]{0:T(1024)S(1)}, u32[]{:S(2)}) copy-start(f32[1280]{0:T(1024)S(1)} %rsqrt.22) | copy-start | bytes 15364
  43.0 12.4 %copy-start.55 = (f32[5,2]{1,0:T(8,128)}, f32[5,2]{1,0:T(8,128)S(1)}, u32[]{:S(2)}) copy-start(f32[5,2]{1,0:T(8,128)S(1)} %broadcast_maximum_fusion.1) | copy-start | bytes 124
  43.5 31.2 %copy-start.40 = (pred[5,256,16]{1,2,0:T(8,128)(4,1)}, pred[5,256,16]{1,2,0:T(8,128)(4,1)S(1)}, u32[]{:S(2)}) copy-start(pred[5,256,16]{1,2,0:T(8,128)(4,1)S(1)} %broadcast_and_fusion.1) | copy-start | bytes 61444
  93.5 12.7 %copy-start.41 = (pred[5,256,16]{1,2,0:T(8,128)(4,1)S(1)}, pred[5,256,16]{1,2,0:T(8,128)(4,1)}, u32[]{:S(2)}) copy-start(pred[5,256,16]{1,2,0:T(8,128)(4,1)} %copy-done.40) | copy-start | bytes 61444
  110.9 104.8 %copy-start.29 = (f32[5,2,8,128]{3,2,1,0:T(8,128)}, f32[5,2,8,128]{3,2,1,0:T(8,128)S(1)}, u32[]{:S(2)}) copy-start(f32[5,2,8,128]{3,2,1,0:T(8,128)S(1)} %fusion.69) | copy-start | bytes 122884
  119.5 137.4 %copy-start.57 = (f32[1280]{0:T(1024)}, f32[1280]{0:T(1024)S(1)}, u32[]{:S(2)}) copy-start(f32[1280]{0:T(1024)S(1)} %add_rsqrt_fusion) | copy-start | bytes 15364
  134.4 64.3 %copy-start.31 = (f32[256,128]{1,0:T(8,128)S(1)}, f32[256,128]{1,0:T(8,128)}, u32[]{:S(2)}) copy-start(f32[256,128]{1,0:T(8,128)} %param.25) | copy-start | bytes 393220
  134.4 64.4 %copy-start.48 = (f32[256,128]{1,0:T(8,128)S(1)}, f32[256,128]{1,0:T(8,128)}, u32[]{:S(2)}) copy-start(f32[256,128]{1,0:T(8,128)} %param.26) | copy-start | bytes 393220
  134.4 64.4 %copy-start.49 = (f32[256,128]{1,0:T(8,128)S(1)}, f32[256,128]{1,0:T(8,128)}, u32[]{:S(2)}) copy-start(f32[256,128]{1,0:T(8,128)} %param.27) | copy-start | bytes 393220
  134.4 79.3 %copy-start.56 = (f32[5,2]{1,0:T(8,128)S(1)}, f32[5,2]{1,0:T(8,128)}, u32[]{:S(2)}) copy-start(f32[5,2]{1,0:T(8,128)} %copy-done.55) | copy-start | bytes 124
  134.4 79.3 %copy-start.66 = (s32[2,128]{1,0:T(2,128)S(1)}, s32[2,128]{1,0:T(2,128)}, u32[]{:S(2)}) copy-start(s32[2,128]{1,0:T(2,128)} %copy-done.65) | copy-start | bytes 3076
  134.4 79.3 %copy-start.72 = (s32[5]{0:T(128)S(1)}, s32[5]{0:T(128)}, u32[]{:S(2)}) copy-start(s32[5]{0:T(128)} %param.17) | copy-start | bytes 64
  134.4 80.0 %copy-start.79 = (u32[32]{0:T(128)S(1)}, u32[32]{0:T(128)}, u32[]{:S(2)}) copy-start(u32[32]{0:T(128)} %constant.109) | copy-start | bytes 388
  134.5 63.3 %reduce-scatter.20.cloned.1.call-start = ((), (), s32[]{:S(2)}) async-start(), calls=%async_computation.12 | async-start | bytes 327680
  177.8 62.6 %all-gather.8.cloned.1.call-start = ((), (), s32[]{:S(2)}) async-start(), calls=%async_computation.7 | async-start | bytes 2359296 | tf_op jit(solution)/shard_map/all_gather | solution.py:51
  213.7 138.9 %all-reduce.10.cloned.1.call-start = ((), (), s32[]{:S(2)}) async-start(), calls=%async_computation.14 | async-start | bytes 327680
  240.3 12.3 %copy-start.3 = (f32[1280,512]{1,0:T(8,128)S(1)}, f32[1280,512]{1,0:T(8,128)}, u32[]{:S(2)}) copy-start(f32[1280,512]{1,0:T(8,128)} %copy-done.2) | copy-start | bytes 7864324
  240.3 12.3 %copy-start.77 = (bf16[512,2048]{1,0:T(8,128)(2,1)S(1)}, bf16[512,2048]{1,0:T(8,128)(2,1)}, u32[]{:S(2)}) copy-start(bf16[512,2048]{1,0:T(8,128)(2,1)} %all-gather.6.cloned.1.call-done) | copy-start | bytes 6291460
  269.2 12.5 %slice-start = ((s8[5242880]{0:T(1024)(128)(4,1)}), s8[1048576]{0:T(1024)(128)(4,1)S(1)}, s32[]{:S(2)}) async-start(s8[5242880]{0:T(1024)(128)(4,1)} %bitcast.225), calls=%async_computation.15 | async-start | bytes 2097152
  300.3 125.8 %all-reduce.8.cloned.1.call-start = ((), (), s32[]{:S(2)}) async-start(), calls=%async_computation.13 | async-start | bytes 4194304
  330.4 26.9 %copy-start.23 = (bf16[1,1280,512]{2,1,0:T(8,128)(2,1)}, bf16[1,1280,512]{2,1,0:T(8,128)(2,1)S(1)}, u32[]{:S(2)}) copy-start(bf16[1,1280,512]{2,1,0:T(8,128)(2,1)S(1)} %reshape.433) | copy-start | bytes 3932164
  363.8 106.0 %reduce-scatter.12.cloned.1.call-start = ((), (), s32[]{:S(2)}) async-start(), calls=%async_computation.8 | async-start | bytes 2359296 | tf_op jit(solution)/shard_map/reduce_scatter | solution.py:60
  371.7 120.2 %reduce-scatter.18.cloned.1.call-start = ((), (), s32[]{:S(2)}) async-start(), calls=%async_computation.11 | async-start | bytes 327680
  441.2 17.4 %copy-start.24 = (bf16[1,1280,512]{2,1,0:T(8,128)(2,1)S(1)}, bf16[1,1280,512]{2,1,0:T(8,128)(2,1)}, u32[]{:S(2)}) copy-start(bf16[1,1280,512]{2,1,0:T(8,128)(2,1)} %copy-done.23) | copy-start | bytes 3932164
  441.2 17.5 %copy-start.51 = (f32[1280]{0:T(1024)S(1)}, f32[1280]{0:T(1024)}, u32[]{:S(2)}) copy-start(f32[1280]{0:T(1024)} %copy-done.50) | copy-start | bytes 15364
  441.2 17.5 %copy-start.53 = (f32[1280]{0:T(1024)S(1)}, f32[1280]{0:T(1024)}, u32[]{:S(2)}) copy-start(f32[1280]{0:T(1024)} %copy-done.52) | copy-start | bytes 15364
  441.2 17.5 %copy-start.64 = (f32[1,512]{1,0:T(1,128)S(1)}, f32[1,512]{1,0:T(1,128)}, u32[]{:S(2)}) copy-start(f32[1,512]{1,0:T(1,128)} %copy-done.63) | copy-start | bytes 6148
  458.6 53.3 %reduce-scatter.14.cloned.1.call-start = ((), (), s32[]{:S(2)}) async-start(), calls=%async_computation.9 | async-start | bytes 327680 | tf_op jit(solution)/shard_map/reduce_scatter | solution.py:74
  465.1 35.0 %copy-start.27 = (f32[4,64,128]{2,1,0:T(8,128)S(1)}, f32[4,64,128]{2,1,0:T(8,128)}, u32[]{:S(2)}) copy-start(f32[4,64,128]{2,1,0:T(8,128)} %param.19) | copy-start | bytes 393220
  501.3 61.4 %copy-start.35 = (f32[4,64,128]{2,1,0:T(8,128)}, f32[4,64,128]{2,1,0:T(8,128)S(1)}, u32[]{:S(2)}) copy-start(f32[4,64,128]{2,1,0:T(8,128)S(1)} %get-tuple-element.117) | copy-start | bytes 393220
  501.3 61.4 %copy-start.36 = (f32[4,64,128]{2,1,0:T(8,128)}, f32[4,64,128]{2,1,0:T(8,128)S(1)}, u32[]{:S(2)}) copy-start(f32[4,64,128]{2,1,0:T(8,128)S(1)} %get-tuple-element.118) | copy-start | bytes 393220
  513.7 49.7 %copy-start.37 = (f32[64,512]{1,0:T(8,128)}, f32[64,512]{1,0:T(8,128)S(1)}, u32[]{:S(2)}) copy-start(f32[64,512]{1,0:T(8,128)S(1)} %get-tuple-element.119) | copy-start | bytes 393220
  513.7 49.7 %copy-start.38 = (f32[64,512]{1,0:T(8,128)}, f32[64,512]{1,0:T(8,128)S(1)}, u32[]{:S(2)}) copy-start(f32[64,512]{1,0:T(8,128)S(1)} %get-tuple-element.120) | copy-start | bytes 393220
  516.5 47.0 %copy-start.28 = (f32[64,512]{1,0:T(8,128)S(1)}, f32[64,512]{1,0:T(8,128)}, u32[]{:S(2)}) copy-start(f32[64,512]{1,0:T(8,128)} %param.22) | copy-start | bytes 393220
  516.5 47.7 %copy-start.32 = (f32[256,128]{1,0:T(8,128)S(1)}, f32[256,128]{1,0:T(8,128)}, u32[]{:S(2)}) copy-start(f32[256,128]{1,0:T(8,128)} %param.25) | copy-start | bytes 393220
  516.5 47.7 %copy-start.33 = (f32[256,128]{1,0:T(8,128)S(1)}, f32[256,128]{1,0:T(8,128)}, u32[]{:S(2)}) copy-start(f32[256,128]{1,0:T(8,128)} %get-tuple-element.121) | copy-start | bytes 393220
  516.5 47.7 %copy-start.34 = (f32[256,128]{1,0:T(8,128)S(1)}, f32[256,128]{1,0:T(8,128)}, u32[]{:S(2)}) copy-start(f32[256,128]{1,0:T(8,128)} %get-tuple-element.122) | copy-start | bytes 393220
  516.5 48.5 %copy-start.60 = (f32[4,512]{1,0:T(4,128)S(1)}, f32[4,512]{1,0:T(4,128)}, u32[]{:S(2)}) copy-start(f32[4,512]{1,0:T(4,128)} %param.18) | copy-start | bytes 24580
  516.5 48.4 %copy-start.69 = (f32[4,512]{1,0:T(4,128)S(1)}, f32[4,512]{1,0:T(4,128)}, u32[]{:S(2)}) copy-start(f32[4,512]{1,0:T(4,128)} %param.29) | copy-start | bytes 24580
  516.5 48.4 %copy-start.70 = (f32[4,512]{1,0:T(4,128)S(1)}, f32[4,512]{1,0:T(4,128)}, u32[]{:S(2)}) copy-start(f32[4,512]{1,0:T(4,128)} %param.28) | copy-start | bytes 24580
  (46 other events, 184.3 us)
Sparse Core Ops, SparseCore 0:
  23.5 28.2 all-gather.3
  53.7 27.8 all-gather.5
  134.6 41.2 reduce-scatter.15
  178.1 19.6 reduce-scatter.19
  213.8 26.4 all-gather.7
  300.5 52.0 all-reduce.9
  363.9 62.1 all-reduce.7
  429.4 40.3 reduce-scatter.11
  472.2 19.6 reduce-scatter.17
  494.0 17.8 reduce-scatter.13
where the time goes:
time: 582 us; the launch traced here: 573 us
  waiting for transfers between devices  190 us (33%)
  local copies, waits for them, and re-layouts  128 us (22%)
  matrix products  107 us (18%)
  blocking collectives  99.8 us (17%)
  other arithmetic  29.6 us (5%)
  between operations  18.5 us (3%)
    unnamed x14, waiting for transfers between devices  109 us
    unnamed x176, local copies, waits for them, and re-layouts  52.5 us
    reduce_scatter x1, waiting for transfers between devices, reduce_rows(): lax.psum_scatter(arrays[2].astype(jnp.bfloat16), 'blk', scatter_dimension...  41.4 us
    psum x1, blocking collectives, body(): lax.psum((jnp.stack([weight_sq, step_sq]), norm_partial), ('blk', 'group'))  38.6 us
    all_gather x1, waiting for transfers between devices, gather_rows(): lax.all_gather(arrays[2], 'blk', axis=0, tiled=True)  16.8 us
    all_gather x1, blocking collectives, gather_cols(): lax.all_gather(arrays[0], 'group', axis=2, tiled=True)  15.1 us
    all_gather x1, blocking collectives, gather_cols(): lax.all_gather(arrays[1], 'group', axis=1, tiled=True)  15.1 us
    all_gather x1, blocking collectives, gather_cols(): lax.all_gather(arrays[2], 'group', axis=1, tiled=True)  13.4 us
  transfers between devices with their start and end apart: 10, of which 9 were waited for; matrix products, arithmetic and copies ran while one was open for 28% of the time, Pallas kernels for 0%

commit v1 on v0

v1 whole, which is shorter than its diff:
```python
import functools

import jax
import jax.numpy as jnp
from jax import lax
from jax.experimental import pallas as pl
from jax.experimental.pallas import tpu as pltpu
from jax.sharding import PartitionSpec as P

HEADS = 8
SPAN = 128
STEP = 5
CHUNKS = 2

masked_value = -1e30
decay_rate = 0.5
matrix_rate = 0.3
vector_rate = 0.5
weight_decay = 0.01
epsilon = 1e-06
gelu_a = 0.7978845608028654
gelu_b = 0.044715

f32 = jnp.float32
b16 = jnp.bfloat16
MIB = 1 << 20
NN = (((1,), (0,)), ((), ()))
NT = (((1,), (1,)), ((), ()))
TN = (((0,), (0,)), ((), ()))


def mm(a, b, dims=NN):
    return lax.dot_general(a, b, dims, preferred_element_type=f32)


def whole():
    return pl.BlockSpec(memory_space=pltpu.VMEM)


def scalars():
    return pl.BlockSpec(memory_space=pltpu.SMEM)


def per_step(*tail):
    zeros = (0,) * len(tail)
    return pl.BlockSpec((1,) + tail, lambda i: (i,) + zeros)


def fixed(*shape):
    zeros = (0,) * len(shape)
    return pl.BlockSpec(shape, lambda i: zeros)


def params(mib):
    return pltpu.CompilerParams(
        dimension_semantics=("arbitrary",), vmem_limit_bytes=mib * MIB
    )


def cost(flops, nbytes, trans=0):
    return pl.CostEstimate(flops=int(flops), bytes_accessed=int(nbytes), transcendentals=int(trans))


def norm_parts(values):
    center = values - jnp.mean(values, -1, keepdims=True)
    spread = jnp.mean(center * center, -1, keepdims=True)
    inverse = lax.rsqrt(spread + 1e-05)
    return center * inverse, inverse


def norm_back(gradient, normal, inverse, gain):
    scaled = gradient * gain
    inner = jnp.mean(scaled, -1, keepdims=True)
    cross = jnp.mean(scaled * normal, -1, keepdims=True)
    return inverse * (scaled - inner - normal * cross)


def copy_attn(w_ref, buf_ref, dims):
    cores, places, groups, rows, cols, width = dims
    for c in range(cores):
        for p in range(places):
            for g in range(groups):
                r0 = (p * cores + c) * rows
                for m in range(4):
                    w_ref[r0 : r0 + rows, m * width + g * cols : m * width + (g + 1) * cols] = (
                        buf_ref[c, p, g, m * rows : (m + 1) * rows, :]
                    )


def prep_kernel(scal_ref, x_ref, g_ref, ln_ref, normed_ref, normed_t_ref, g_t_ref, nsum_ref):
    i = pl.program_id(0)
    tok = x_ref.shape[1]
    spans = tok // SPAN
    normal, _ = norm_parts(x_ref[0].astype(f32))
    normed = (normal * ln_ref[0:1, :] + ln_ref[1:2, :]).astype(b16)
    normed_ref[0] = normed
    normed_t_ref[0] = normed.T
    g_t_ref[0] = g_ref[0].T
    left = scal_ref[1 + i] - scal_ref[0] * tok
    row = lax.broadcasted_iota(jnp.int32, (16, tok), 0)
    col = lax.broadcasted_iota(jnp.int32, (16, tok), 1)
    chosen = jnp.where((col // SPAN == row) & (col < left), 1.0, 0.0)
    amount = jnp.maximum(jnp.sum(chosen, 1, keepdims=True), 1.0)
    total = mm(chosen.astype(b16), normed) / amount
    high = total.astype(b16)
    low = (total - high.astype(f32)).astype(b16)
    nsum_ref[0, 0] = high[:spans]
    nsum_ref[0, 1] = low[:spans]


def pair_masks():
    lane = lax.broadcasted_iota(jnp.int32, (SPAN, SPAN), 1)
    return lane < SPAN // 2


def heads_apart(values):
    lane = lax.broadcasted_iota(jnp.int32, values.shape, 1)
    zero = jnp.zeros_like(values)
    first = lane < SPAN // 2
    return jnp.where(first, values, zero), jnp.where(first, zero, values)


def score_masks(scal_ref, i, span, spans, amount):
    length = scal_ref[1 + i]
    mine = scal_ref[0] * spans + span
    key = lax.broadcasted_iota(jnp.int32, (SPAN, SPAN), 0)
    query = lax.broadcasted_iota(jnp.int32, (SPAN, SPAN), 1)
    local = (key <= query) & (key < length - mine * SPAN)
    index = lax.broadcasted_iota(jnp.int32, (amount, SPAN), 0)
    summary = (index < mine) & (index * SPAN < length)
    return local, summary


def split_scores(scores, local, summary, amount):
    parts = (
        jnp.where(local, scores[:SPAN], masked_value),
        jnp.where(local, scores[SPAN : 2 * SPAN], masked_value),
        jnp.where(summary, scores[2 * SPAN : 2 * SPAN + amount], masked_value),
        jnp.where(summary, scores[2 * SPAN + amount :], masked_value),
    )
    return parts


def forward_kernel(
    dims, scal_ref, normed_ref, x_ref, buf_ref, nsum_ref, ln_ref,
    q_ref, k_ref, v_ref, ks_ref, vs_ref, lse_ref, mixed_ref, x2_ref, mid_ref, mid_t_ref, w_ref,
):
    i = pl.program_id(0)
    width = dims[-1]
    tok = normed_ref.shape[1]
    spans = tok // SPAN
    amount = nsum_ref.shape[2]
    factor = (width // HEADS) ** (-0.5)

    @pl.when(i == 0)
    def _():
        copy_attn(w_ref, buf_ref, dims)

    normed = normed_ref[0]
    q_ref[0] = mm(normed, w_ref[:, :width]).astype(b16)
    k_ref[0] = mm(normed, w_ref[:, width : 2 * width]).astype(b16)
    v_ref[0] = mm(normed, w_ref[:, 2 * width : 3 * width]).astype(b16)
    sums = mm(nsum_ref[0, 0], w_ref[:, width : 3 * width]) + mm(
        nsum_ref[0, 1], w_ref[:, width : 3 * width]
    )
    ks_ref[0] = sums[:, :width].astype(b16)
    vs_ref[0] = sums[:, width:].astype(b16)
    for span in range(spans):
        rows = slice(span * SPAN, (span + 1) * SPAN)
        local, summary = score_masks(scal_ref, i, span, spans, amount)
        for pair in range(width // SPAN):
            lanes = slice(pair * SPAN, (pair + 1) * SPAN)
            query = q_ref[0, rows, lanes] * b16(factor)
            keys = jnp.concatenate(
                heads_apart(k_ref[0, rows, lanes]) + heads_apart(ks_ref[0, :, lanes]), 0
            )
            values = jnp.concatenate(
                heads_apart(v_ref[0, rows, lanes]) + heads_apart(vs_ref[0, :, lanes]), 0
            )
            parts = split_scores(mm(keys, query, NT), local, summary, amount)
            probs = [None] * 4
            for h in range(2):
                here, there = parts[h], parts[2 + h]
                top = jnp.maximum(
                    jnp.max(here, 0, keepdims=True), jnp.max(there, 0, keepdims=True)
                )
                here, there = jnp.exp(here - top), jnp.exp(there - top)
                total = jnp.sum(here, 0, keepdims=True) + jnp.sum(there, 0, keepdims=True)
                inverse = 1.0 / total
                probs[h] = (here * inverse).astype(b16)
                probs[2 + h] = (there * inverse).astype(b16)
                lse_ref[0, span, 2 * pair + h : 2 * pair + h + 1, :] = top + jnp.log(total)
            mixed_ref[0, rows, lanes] = mm(jnp.concatenate(probs, 0), values, TN).astype(b16)
    x2 = x_ref[0].astype(f32) + mm(mixed_ref[0], w_ref[:, 3 * width :])
    x2_ref[0] = x2
    normal, _ = norm_parts(x2)
    mid = (normal * ln_ref[2:3, :] + ln_ref[3:4, :]).astype(b16)
    mid_ref[0] = mid
    mid_t_ref[0] = mid.T


def mlp_kernel(dims, last, *refs):
    if last:
        (mid_ref, mid_t_ref, g_ref, g_t_ref, buf_ref, x2_ref, y_in_ref, gm_in_ref,
         y_ref, gm_ref, out_ref, wu_ref, wd_ref, du_ref, dd_ref) = refs
    else:
        (mid_ref, mid_t_ref, g_ref, g_t_ref, buf_ref,
         y_ref, gm_ref, out_ref, wu_ref, wd_ref, du_ref, dd_ref) = refs
    cores, places, groups, rows, cols, sub, lanes = dims
    i = pl.program_id(0)

    def pieces():
        for c in range(cores):
            for p in range(places):
                b = p * cores + c
                for g in range(groups):
                    for h in range(sub):
                        yield (
                            (c, p, g, slice(h * rows, (h + 1) * rows)),
                            (
                                slice(b * rows, (b + 1) * rows),
                                slice((g * sub + h) * lanes, (g * sub + h + 1) * lanes),
                            ),
                            True,
                        )
                    yield (
                        (c, p, g, slice(sub * rows, sub * rows + cols)),
                        (slice(g * cols, (g + 1) * cols), slice(b * lanes, (b + 1) * lanes)),
                        False,
                    )

    @pl.when(i == 0)
    def _():
        for there, here, is_up in pieces():
            (wu_ref if is_up else wd_ref)[here] = buf_ref[there]
        du_ref[...] = jnp.zeros_like(du_ref)
        dd_ref[...] = jnp.zeros_like(dd_ref)

    mid, g = mid_ref[0], g_ref[0]
    up = mm(mid, wu_ref[...])
    grad_act = mm(g, wd_ref[...])
    square = up * up
    half = 0.5 + 0.5 * jnp.tanh(up * (gelu_a + gelu_a * gelu_b * square))
    act = (up * half).astype(b16)
    slope = half + (up * half * (1.0 - half)) * (
        2.0 * gelu_a + 6.0 * gelu_a * gelu_b * square
    )
    grad_up = (slope * grad_act).astype(b16)
    y = mm(act, wd_ref[...], NT)
    gm = mm(grad_up, wu_ref[...], NT)
    if last:
        y_ref[0] = (x2_ref[0] + y_in_ref[0] + y).astype(b16)
        gm_ref[0] = gm_in_ref[0] + gm
    else:
        y_ref[0] = y
        gm_ref[0] = gm
    dd_ref[...] += mm(g_t_ref[0], act)
    du_ref[...] += mm(mid_t_ref[0], grad_up)

    @pl.when(i == pl.num_programs(0) - 1)
    def _():
        for there, here, is_up in pieces():
            out_ref[there] = (du_ref if is_up else dd_ref)[here].astype(b16)


def backward_kernel(
    dims, scal_ref, gm_ref, g_ref, x2_ref, mixed_ref, q_ref, k_ref, v_ref, lse_ref, ks_ref, vs_ref,
    normed_t_ref, nsum_ref, buf_ref, ln_ref,
    gx2_ref, dqkv_ref, out_ref, hpart_ref, lng_ref, w_ref, dw_ref, do_ref,
):
    i = pl.program_id(0)
    cores, places, groups, wrows, cols, width = dims
    tok = g_ref.shape[1]
    spans = tok // SPAN
    amount = ks_ref.shape[1]
    factor = (width // HEADS) ** (-0.5)

    @pl.when(i == 0)
    def _():
        copy_attn(w_ref, buf_ref, dims)
        dw_ref[...] = jnp.zeros_like(dw_ref)
        lng_ref[...] = jnp.zeros_like(lng_ref)

    gm = gm_ref[0]
    normal, inverse = norm_parts(x2_ref[0])
    lng_ref[0:1, :] += jnp.sum(gm * normal, 0, keepdims=True)
    lng_ref[1:2, :] += jnp.sum(gm, 0, keepdims=True)
    gx2 = g_ref[0].astype(f32) + norm_back(gm, normal, inverse, ln_ref[2:3, :])
    gx2_ref[0] = gx2
    branch = gx2.astype(b16)
    dw_ref[:, 3 * width :] += mm(mixed_ref[0], branch, TN)
    do_ref[...] = mm(branch, w_ref[:, 3 * width :], NT).astype(b16)
    key_parts, value_parts = [], []
    for span in range(spans):
        rows = slice(span * SPAN, (span + 1) * SPAN)
        local, summary = score_masks(scal_ref, i, span, spans, amount)
        for pair in range(width // SPAN):
            lanes = slice(pair * SPAN, (pair + 1) * SPAN)
            query = q_ref[0, rows, lanes] * b16(factor)
            grad = do_ref[rows, lanes]
            keys = jnp.concatenate(
                heads_apart(k_ref[0, rows, lanes]) + heads_apart(ks_ref[0, :, lanes]), 0
            )
            values = jnp.concatenate(
                heads_apart(v_ref[0, rows, lanes]) + heads_apart(vs_ref[0, :, lanes]), 0
            )
            scores = split_scores(mm(keys, query, NT), local, summary, amount)
            grads = mm(values, grad, NT)
            grads = (
                grads[:SPAN],
                grads[SPAN : 2 * SPAN],
                grads[2 * SPAN : 2 * SPAN + amount],
                grads[2 * SPAN + amount :],
            )
            low, back = [None] * 4, [None] * 4
            for h in range(2):
                total = lse_ref[0, span, 2 * pair + h : 2 * pair + h + 1, :]
                here, there = jnp.exp(scores[h] - total), jnp.exp(scores[2 + h] - total)
                here_grad, there_grad = here * grads[h], there * grads[2 + h]
                dot = jnp.sum(here_grad, 0, keepdims=True) + jnp.sum(there_grad, 0, keepdims=True)
                low[h], low[2 + h] = here.astype(b16), there.astype(b16)
                back[h] = (here_grad - here * dot).astype(b16)
                back[2 + h] = (there_grad - there * dot).astype(b16)
            low_rows = jnp.concatenate(
                [jnp.concatenate(low[0:2], 1), jnp.concatenate(low[2:4], 1)], 0
            )
            back_rows = jnp.concatenate(
                [jnp.concatenate(back[0:2], 1), jnp.concatenate(back[2:4], 1)], 0
            )
            grad_value = mm(low_rows, jnp.concatenate(heads_apart(grad), 0))
            grad_key = mm(back_rows, jnp.concatenate(heads_apart(query), 0))
            grad_query = mm(jnp.concatenate(back, 0), keys, TN) * factor
            dqkv_ref[0, rows, lanes] = grad_query.astype(b16)
            dqkv_ref[0, rows, width + pair * SPAN : width + (pair + 1) * SPAN] = grad_key[
                :SPAN
            ].astype(b16)
            dqkv_ref[0, rows, 2 * width + pair * SPAN : 2 * width + (pair + 1) * SPAN] = grad_value[
                :SPAN
            ].astype(b16)
            key_parts.append(grad_key[SPAN:])
            value_parts.append(grad_value[SPAN:])
    pairs = width // SPAN

    def joined(parts):
        return jnp.concatenate(
            [sum(parts[s * pairs + p] for s in range(spans)) for p in range(pairs)], 1
        ).astype(b16)

    key_part, value_part = joined(key_parts), joined(value_parts)
    hpart_ref[0] = (
        mm(key_part, w_ref[:, width : 2 * width], NT)
        + mm(value_part, w_ref[:, 2 * width : 3 * width], NT)
    ).astype(b16)
    dw_ref[:, : 3 * width] += mm(normed_t_ref[0], dqkv_ref[0])
    nsum = nsum_ref[0, 0]
    dw_ref[:, width : 2 * width] += mm(nsum, key_part, TN)
    dw_ref[:, 2 * width : 3 * width] += mm(nsum, value_part, TN)

    @pl.when(i == pl.num_programs(0) - 1)
    def _():
        for c in range(cores):
            for p in range(places):
                r0 = (p * cores + c) * wrows
                for g in range(groups):
                    for m in range(4):
                        out_ref[c, p, g, m * wrows : (m + 1) * wrows, :] = dw_ref[
                            r0 : r0 + wrows, m * width + g * cols : m * width + (g + 1) * cols
                        ].astype(b16)


def input_kernel(
    dims, scal_ref, dqkv_ref, gx2_ref, x_ref, buf_ref, own_ref, ln_ref, out_ref, lng_ref, w_ref
):
    i = pl.program_id(0)
    width = dims[-1]
    tok = x_ref.shape[1]

    @pl.when(i == 0)
    def _():
        copy_attn(w_ref, buf_ref, dims)
        lng_ref[...] = jnp.zeros_like(lng_ref)

    grad = mm(dqkv_ref[0], w_ref[:, : 3 * width], NT)
    left = scal_ref[1 + i] - scal_ref[0] * tok
    place = lax.broadcasted_iota(jnp.int32, (tok, 1), 0)
    extra = []
    for span in range(tok // SPAN):
        rows = slice(span * SPAN, (span + 1) * SPAN)
        amount = jnp.clip(left - span * SPAN, 0, SPAN)
        share = jnp.where(place[rows] < left, 1.0, 0.0) / jnp.maximum(amount, 1).astype(f32)
        extra.append(share * own_ref[0, span : span + 1, :])
    grad = grad + jnp.concatenate(extra, 0)
    normal, inverse = norm_parts(x_ref[0].astype(f32))
    lng_ref[0:1, :] += jnp.sum(grad * normal, 0, keepdims=True)
    lng_ref[1:2, :] += jnp.sum(grad, 0, keepdims=True)
    out_ref[0] = gx2_ref[0] + norm_back(grad, normal, inverse, ln_ref[0:1, :])


def moments(gradient, first, second):
    corr = 1.0 - decay_rate**STEP
    new_first = decay_rate * first + (1.0 - decay_rate) * gradient
    new_second = decay_rate * second + (1.0 - decay_rate) * gradient * gradient
    return (new_first, new_second, new_first / corr / (jnp.sqrt(new_second / corr) + epsilon))


def fast_mesh(nb, ng, width):
    return nb == 8 and ng == 4 and width // ng == 128


def shift(values, by, ng):
    return lax.ppermute(values, "group", [(j, (j + by) % ng) for j in range(ng)])


def cross(values, bit, nb):
    return lax.ppermute(values, "blk", [(j, j ^ bit) for j in range(nb)])


def put(buffer, piece, at):
    return lax.dynamic_update_slice(buffer, piece[None], (at,) + (0,) * piece.ndim)


def take(buffer, at):
    return lax.dynamic_index_in_dim(buffer, at, 0, keepdims=False)


def gather_group(piece, place, ng):
    out = put(jnp.zeros((ng,) + piece.shape, piece.dtype), piece, place)
    for by in range(1, ng):
        out = put(out, shift(piece, by, ng), (place - by) % ng)
    return out


def gather_blk(piece, place, nb):
    spot, core = place // 2, place % 2
    out = put(jnp.zeros((nb // 2,) + piece.shape, piece.dtype), piece, spot)
    for move in range(1, nb // 2):
        out = put(out, cross(piece, 2 * move, nb), spot ^ move)
    other = cross(out, 1, nb)
    both = jnp.zeros((2,) + out.shape, out.dtype)
    return put(put(both, out, core), other, 1 - core)


def reduce_all(pieces, b, z, nb, ng):
    spot, core = b // 2, b % 2
    sent = cross(take(pieces, 1 - core), 1, nb)
    kept = take(pieces, core)

    def at(index):
        return take(kept, index).astype(f32) + take(sent, index).astype(f32)

    total = at(spot)
    for move in range(1, nb // 2):
        total = total + cross(at(spot ^ move).astype(b16), 2 * move, nb).astype(f32)
    total = total.astype(b16)
    out = take(total, z).astype(f32)
    for by in range(1, ng):
        out = out + shift(take(total, (z + by) % ng), by, ng).astype(f32)
    return out


def body(
    tokens, cotangent, lengths, ln_params, attn_master, attn_first, attn_second,
    up_master, up_first, up_second, down_master, down_first, down_second, ln_first, ln_second,
    *, nb, ng,
):
    seqs, tok, width = tokens.shape
    spans = tok // SPAN
    amount = nb * spans
    rows, cols = attn_master.shape[1:]
    ff_rows = down_master.shape[0]
    sub = nb // ng
    lanes = ff_rows // CHUNKS
    inner = nb * lanes
    b, z = lax.axis_index("blk"), lax.axis_index("group")
    fast = fast_mesh(nb, ng, width)
    scal = jnp.concatenate([b.astype(jnp.int32)[None], lengths.astype(jnp.int32)])
    seq = jax.ShapeDtypeStruct

    def rows_like(dtype, *tail):
        return seq((seqs,) + tail, dtype)

    attn_piece = attn_master.astype(b16).reshape(4 * rows, cols)
    up_low = up_master.astype(b16).reshape(rows, sub, CHUNKS, lanes)
    down_low = down_master.astype(b16).T.reshape(cols, CHUNKS, lanes)
    mlp_pieces = [
        jnp.concatenate(
            [jnp.swapaxes(up_low[:, :, j], 0, 1).reshape(sub * rows, lanes), down_low[:, j]], 0
        )
        for j in range(CHUNKS)
    ]

    normed, normed_t, cot_t, nsum = pl.pallas_call(
        prep_kernel,
        grid=(seqs,),
        in_specs=[scalars(), per_step(tok, width), per_step(tok, width), fixed(4, width)],
        out_specs=[
            per_step(tok, width), per_step(width, tok), per_step(width, tok),
            per_step(2, spans, width),
        ],
        out_shape=[
            rows_like(b16, tok, width), rows_like(b16, width, tok), rows_like(b16, width, tok),
            rows_like(b16, 2, spans, width),
        ],
        compiler_params=params(16),
        cost_estimate=cost(4e7, 5 * 5 * tok * width * 2),
        name="prep",
    )(scal, tokens, cotangent, ln_params)

    if fast:
        extra = nsum.reshape(-1, cols)
        attn_z = gather_group(attn_piece, z, ng).reshape(ng * 4 * rows, cols)
        attn_all = gather_blk(jnp.concatenate([attn_z, extra], 0), b, nb)
        main = ng * 4 * rows
        attn_buf = attn_all[:, :, :main].reshape(2, nb // 2, ng, 4 * rows, cols)
        nsum_all = attn_all[:, :, main:].reshape(2, nb // 2, seqs, 2, spans, width)
        nsum_all = jnp.transpose(nsum_all, (2, 3, 1, 0, 4, 5)).reshape(seqs, 2, amount, width)
        mlp_bufs = [gather_blk(gather_group(piece, z, ng), b, nb) for piece in mlp_pieces]
    else:

        def gather_any(piece):
            every = lax.all_gather(piece, ("blk", "group"))
            every = every.reshape((nb // 2, 2, ng) + piece.shape)
            return jnp.swapaxes(every, 0, 1)

        attn_buf = gather_any(attn_piece)
        mlp_bufs = [gather_any(piece) for piece in mlp_pieces]
        nsum_all = lax.all_gather(nsum, "blk", axis=2, tiled=True)

    def reduce_any(pieces):
        if fast:
            return reduce_all(pieces, b, z, nb, ng)
        pieces = jnp.swapaxes(pieces, 0, 1).reshape((nb,) + pieces.shape[2:])
        pieces = lax.psum_scatter(pieces, "blk", scatter_dimension=0)
        return lax.psum_scatter(pieces, "group", scatter_dimension=0).astype(f32)

    dims = (2, nb // 2, ng, rows, cols, width)
    act_bytes = seqs * tok * width
    q, k, v, ks, vs, lse, mixed, x2, mid, mid_t = pl.pallas_call(
        functools.partial(forward_kernel, dims),
        grid=(seqs,),
        in_specs=[
            scalars(), per_step(tok, width), per_step(tok, width), whole(),
            per_step(2, amount, width), fixed(4, width),
        ],
        out_specs=[
            per_step(tok, width), per_step(tok, width), per_step(tok, width),
            per_step(amount, width), per_step(amount, width), per_step(spans, HEADS, SPAN),
            per_step(tok, width), per_step(tok, width), per_step(tok, width),
            per_step(width, tok),
        ],
        out_shape=[
            rows_like(b16, tok, width), rows_like(b16, tok, width), rows_like(b16, tok, width),
            rows_like(b16, amount, width), rows_like(b16, amount, width),
            rows_like(f32, spans, HEADS, SPAN),
            rows_like(b16, tok, width), rows_like(f32, tok, width), rows_like(b16, tok, width),
            rows_like(b16, width, tok),
        ],
        scratch_shapes=[pltpu.VMEM((width, 4 * width), b16)],
        compiler_params=params(24),
        cost_estimate=cost(8e9, act_bytes * 18),
        name="forward",
    )(scal, normed, tokens, attn_buf, nsum_all, ln_params)

    mlp_dims = (2, nb // 2, ng, rows, cols, sub, lanes)
    mlp_out = seq((2, nb // 2, ng, sub * rows + cols, lanes), b16)
    grads = []
    y = gm = None
    for j in range(CHUNKS):
        last = j == CHUNKS - 1
        args = [mid, mid_t, cotangent, cot_t, mlp_bufs[j]]
        in_specs = [
            per_step(tok, width), per_step(width, tok), per_step(tok, width),
            per_step(width, tok), whole(),
        ]
        if last:
            args += [x2, y, gm]
            in_specs += [per_step(tok, width)] * 3
        y, gm, part = pl.pallas_call(
            functools.partial(mlp_kernel, mlp_dims, last),
            grid=(seqs,),
            in_specs=in_specs,
            out_specs=[per_step(tok, width), per_step(tok, width), whole()],
            out_shape=[
                rows_like(b16 if last else f32, tok, width), rows_like(f32, tok, width), mlp_out
            ],
            scratch_shapes=[
                pltpu.VMEM((width, inner), b16), pltpu.VMEM((width, inner), b16),
                pltpu.VMEM((width, inner), f32), pltpu.VMEM((width, inner), f32),
            ],
            compiler_params=params(32),
            cost_estimate=cost(9e9, act_bytes * 20),
            name="mlp",
        )(*args)
        grads.append(part)
    block_out = y

    gx2, dqkv, attn_part, hpart, ln_two = pl.pallas_call(
        functools.partial(backward_kernel, dims),
        grid=(seqs,),
        in_specs=[
            scalars(), per_step(tok, width), per_step(tok, width), per_step(tok, width),
            per_step(tok, width), per_step(tok, width), per_step(tok, width), per_step(tok, width),
            per_step(spans, HEADS, SPAN), per_step(amount, width), per_step(amount, width),
            per_step(width, tok), per_step(2, amount, width), whole(), fixed(4, width),
        ],
        out_specs=[
            per_step(tok, width), per_step(tok, 3 * width), whole(), per_step(amount, width),
            fixed(8, width),
        ],
        out_shape=[
            rows_like(f32, tok, width), rows_like(b16, tok, 3 * width),
            seq((2, nb // 2, ng, 4 * rows, cols), b16), rows_like(b16, amount, width),
            seq((8, width), f32),
        ],
        scratch_shapes=[
            pltpu.VMEM((width, 4 * width), b16), pltpu.VMEM((width, 4 * width), f32),
            pltpu.VMEM((tok, width), b16),
        ],
        compiler_params=params(32),
        cost_estimate=cost(14e9, act_bytes * 24),
        name="backward",
    )(
        scal, gm, cotangent, x2, mixed, q, k, v, lse, ks, vs, normed_t, nsum_all, attn_buf, ln_params
    )

    hpart = jnp.transpose(hpart.reshape(seqs, nb, spans, width), (1, 0, 2, 3))
    if fast:
        spread = lax.all_to_all(hpart, "blk", 0, 0, tiled=True)
        own = jnp.sum(spread.astype(f32), 0)
    else:
        own = lax.psum_scatter(hpart, "blk", scatter_dimension=0).astype(f32)

    input_grad, ln_one = pl.pallas_call(
        functools.partial(input_kernel, dims),
        grid=(seqs,),
        in_specs=[
            scalars(), per_step(tok, 3 * width), per_step(tok, width), per_step(tok, width),
            whole(), per_step(spans, width), fixed(4, width),
        ],
        out_specs=[per_step(tok, width), fixed(8, width)],
        out_shape=[rows_like(f32, tok, width), seq((8, width), f32)],
        scratch_shapes=[pltpu.VMEM((width, 4 * width), b16)],
        compiler_params=params(24),
        cost_estimate=cost(3e9, act_bytes * 16),
        name="input",
    )(scal, dqkv, gx2, tokens, attn_buf, own, ln_params)

    red_mlp = [reduce_any(part) for part in grads]
    red_attn = reduce_any(attn_part).reshape(4, rows, cols)
    red_up = jnp.stack(
        [jnp.swapaxes(r[: sub * rows].reshape(sub, rows, lanes), 0, 1) for r in red_mlp], 2
    ).reshape(rows, sub * CHUNKS * lanes)
    red_down = jnp.concatenate([r[sub * rows :] for r in red_mlp], 1).T

    attn_moment1, attn_moment2, attn_dir = moments(red_attn, attn_first, attn_second)
    up_moment1, up_moment2, up_dir = moments(red_up, up_first, up_second)
    down_moment1, down_moment2, down_dir = moments(red_down, down_first, down_second)
    attn_step = attn_dir + weight_decay * attn_master
    up_step = up_dir + weight_decay * up_master
    down_step = down_dir + weight_decay * down_master

    def squares(attn, up, down):
        return jnp.concatenate(
            [jnp.sum(attn * attn, (1, 2)), jnp.sum(up * up)[None], jnp.sum(down * down)[None]]
        )

    norm_partial = jnp.concatenate([ln_one[:2], ln_two[:2]], 0)
    both = jnp.concatenate(
        [squares(attn_master, up_master, down_master), squares(attn_step, up_step, down_step)]
    )
    if fast:
        line = jnp.pad(both, (0, width - both.shape[0]))[None]
        mine = jnp.concatenate([norm_partial, line, jnp.zeros((3, width), f32)], 0)
        every = lax.all_to_all(
            jnp.broadcast_to(mine[None], (nb * ng,) + mine.shape), ("blk", "group"), 0, 0, tiled=True
        )
        total = jnp.sum(every, 0)
        norm_grad, both = total[:4], total[4, : both.shape[0]]
    else:
        both, norm_grad = lax.psum((both, norm_partial), ("blk", "group"))
    sq_totals = both.reshape(2, -1)
    trust = jnp.sqrt(sq_totals[0]) / jnp.sqrt(sq_totals[1] + epsilon)
    attn_new = attn_master - matrix_rate * trust[:4, None, None] * attn_step
    up_new = up_master - matrix_rate * trust[4] * up_step
    down_new = down_master - matrix_rate * trust[5] * down_step
    ln_moment1, ln_moment2, ln_dir = moments(norm_grad, ln_first, ln_second)
    ln_new = ln_params - vector_rate * ln_dir
    return (
        block_out, input_grad,
        attn_moment1, attn_moment2, attn_new, attn_new.astype(b16),
        up_moment1, up_moment2, up_new, up_new.astype(b16),
        down_moment1, down_moment2, down_new, down_new.astype(b16),
        ln_moment1, ln_moment2, ln_new, jnp.sqrt(sq_totals),
    )


def solution(mesh):
    seq_spec = P("group", "blk", None)
    attn_spec = P(None, "blk", "group")
    flat_spec = P("blk", "group")
    return jax.shard_map(
        functools.partial(body, nb=mesh.shape["blk"], ng=mesh.shape["group"]),
        mesh=mesh,
        in_specs=(seq_spec, seq_spec, P("group"), P())
        + (attn_spec,) * 3
        + (flat_spec,) * 6
        + (P(), P()),
        out_specs=(seq_spec, seq_spec)
        + (attn_spec,) * 4
        + (flat_spec,) * 8
        + (P(),) * 4,
        check_vma=False,
    )
```

time: 582 us -> 271 us (0.47); the launches traced: 573 us -> 269 us
  waiting for transfers between devices: 190 us -> 57.8 us
  matrix products: 107 us -> 0 us
  blocking collectives: 99.8 us -> 0 us
  local copies, waits for them, and re-layouts: 128 us -> 54.4 us
  Pallas kernels: 0 us -> 71.9 us
  starting transfers between devices: 0.42 us -> 64.4 us
  between operations: 18.5 us -> 3.04 us
  other arithmetic: 29.6 us -> 17.8 us
    unnamed x14 -> x0, waiting for transfers between devices: 109 us -> none
    dot_general x28 -> x0, matrix products: 107 us -> none  [the longest x1 12.3 us: body(): jnp.einsum('rd,fd->rf', grad_out, down_low, preferred_element_type=jnp.fl...]
    pallas_call x0 -> x6, Pallas kernels: none -> 71.9 us  [the longest x2 23.1 us: body(): pl.pallas_call(functools.partial(mlp_kernel, mlp_dims, last), grid=(seqs,...]
    all_gather x5 -> x0, blocking collectives: 61.2 us -> none  [the longest x1 15.1 us: gather_cols(): lax.all_gather(arrays[0], 'group', axis=2, tiled=True)]
    ppermute x0 -> x42, starting transfers between devices: none -> 56.4 us  [the longest x18 28.3 us: shift(): lax.ppermute(values, 'group', [(j, (j + by) % ng) for j in range(ng)])]
    reduce_scatter x3 -> x0, waiting for transfers between devices: 56.2 us -> none  [the longest x1 41.4 us: reduce_rows(): lax.psum_scatter(arrays[2].astype(jnp.bfloat16), 'blk', scatter_dimension...]
    ppermute x0 -> x42, waiting for transfers between devices: none -> 45 us  [the longest x24 44.2 us: cross(): return lax.ppermute(values, 'blk', [(j, j ^ bit) for j in range(nb)])]
    psum x1 -> x0, blocking collectives: 38.6 us -> none  [body(): lax.psum((jnp.stack([weight_sq, step_sq]), norm_partial), ('blk', 'group'))]
  transfers between devices with their start and end apart: 10 -> 44, of which waited for: 9 -> 12; matrix products, arithmetic and copies ran while one was open for 28% -> 11% of each run, Pallas kernels for 0% -> 16%
where the time goes in v1:
time: 271 us; the launch traced here: 269 us
  Pallas kernels  71.9 us (27%)
  starting transfers between devices  64.4 us (24%)
  waiting for transfers between devices  57.8 us (21%)
  local copies, waits for them, and re-layouts  54.4 us (20%)
  other arithmetic  17.8 us (7%)
  between operations  3.04 us (1%)
    ppermute x24, waiting for transfers between devices, cross(): return lax.ppermute(values, 'blk', [(j, j ^ bit) for j in range(nb)])  44.2 us
    unnamed x109, local copies, waits for them, and re-layouts  29.5 us
    ppermute x18, starting transfers between devices, shift(): lax.ppermute(values, 'group', [(j, (j + by) % ng) for j in range(ng)])  28.3 us
    ppermute x24, starting transfers between devices, cross(): return lax.ppermute(values, 'blk', [(j, j ^ bit) for j in range(nb)])  28.1 us
    pallas_call x2, Pallas kernels, body(): pl.pallas_call(functools.partial(mlp_kernel, mlp_dims, last), grid=(seqs,...  23.1 us
    pallas_call x1, Pallas kernels, body(): pl.pallas_call(functools.partial(backward_kernel, dims), grid=(seqs,), in...  23.1 us
    pallas_call x1, Pallas kernels, body(): pl.pallas_call(functools.partial(forward_kernel, dims), grid=(seqs,), in_...  17.2 us
    all_to_all x1, waiting for transfers between devices, body(): lax.all_to_all(jnp.broadcast_to(mine[None], (nb * ng,) + mine.shape), ('b...  12.9 us
  transfers between devices with their start and end apart: 44, of which 12 were waited for; matrix products, arithmetic and copies ran while one was open for 11% of the time, Pallas kernels for 16%

profile of v1, /device:TPU:0, one launch (start us, length us, event | category | flops | bytes accessed | tf_op | source)
XLA Modules:
  0.0 269.4 jit_solution(16483200201225551062)
XLA Ops:
  0.7 1.7 multiply_reduce_fusion.3
  3.6 3.1 %collective-permute-start.14 = (bf16[256,128]{1,0:T(8,128)(2,1)S(1)}, bf16[256,128]{1,0:T(8,128)(2,1)}, u32[]{:S(2)}, u32[]{:S(2)}) collective-permute-start(bf16[256,128]{1,0:T(8,128)(2,1)S(1)} %pad_maximum_fusion.3), channel_id=1, source_target_pairs={{0,1},{1,2},{2,3},{3,0},{4,5},{5,6},{6,7},{7,4},{8,9},{9,10},{10,1... | collective-permute-start | bytes 196616 | tf_op jit(solution)/shard_map/ppermute | solution.py:411
  6.7 2.6 collective-permute-start.15
  15.3 2.6 prep.1
  22.0 2.9 %collective-permute-start.2 = (bf16[256,128]{1,0:T(8,128)(2,1)S(1)}, bf16[256,128]{1,0:T(8,128)(2,1)S(1)}, u32[]{:S(2)}, u32[]{:S(2)}) collective-permute-start(bf16[256,128]{1,0:T(8,128)(2,1)S(1)} %bitcast.240), channel_id=1, source_target_pairs={{0,3},{1,0},{2,1},{3,2},{4,7},{5,4},{6,5},{7,6},{8,11},{9,8},{10,9... | collective-permute-start | bytes 196616 | tf_op jit(solution)/shard_map/ppermute | solution.py:411
  27.2 1.5 collective-permute-start.8
  29.9 3.0 %collective-permute-start.9 = (bf16[256,128]{1,0:T(8,128)(2,1)S(1)}, bf16[256,128]{1,0:T(8,128)(2,1)S(1)}, u32[]{:S(2)}, u32[]{:S(2)}) collective-permute-start(bf16[256,128]{1,0:T(8,128)(2,1)S(1)} %copy-done.44), channel_id=1, source_target_pairs={{0,3},{1,0},{2,1},{3,2},{4,7},{5,4},{6,5},{7,6},{8,11},{9,8},{10,9... | collective-permute-start | bytes 196616 | tf_op jit(solution)/shard_map/ppermute | solution.py:411
  32.9 1.6 collective-permute-start.17
  34.5 1.6 collective-permute-start.18
  36.9 1.6 collective-permute-start.3
  39.3 2.8 %collective-permute-done.17 = bf16[4,256,128]{2,1,0:T(8,128)(2,1)S(1)} collective-permute-done((bf16[4,256,128]{2,1,0:T(8,128)(2,1)S(1)}, bf16[4,256,128]{2,1,0:T(8,128)(2,1)S(1)}, u32[]{:S(2)}, u32[]{:S(2)}) %collective-permute-start.17) | collective-permute-done | bytes 262176 | tf_op jit(solution)/shard_map/ppermute | solution.py:415
  42.1 1.5 collective-permute-start.4
  43.6 12.1 %collective-permute-done.10 = bf16[4,256,128]{2,1,0:T(8,128)(2,1)S(1)} collective-permute-done((bf16[4,256,128]{2,1,0:T(8,128)(2,1)S(1)}, bf16[4,256,128]{2,1,0:T(8,128)(2,1)S(1)}, u32[]{:S(2)}, u32[]{:S(2)}) %collective-permute-start.10) | collective-permute-done | bytes 262176 | tf_op jit(solution)/shard_map/ppermute | solution.py:415
  55.8 3.4 %collective-permute-start.5 = (bf16[1104,128]{1,0:T(8,128)(2,1)S(1)}, bf16[1104,128]{1,0:T(8,128)(2,1)S(1)}, u32[]{:S(2)}, u32[]{:S(2)}) collective-permute-start(bf16[1104,128]{1,0:T(8,128)(2,1)S(1)} %pad_maximum_fusion), channel_id=1, source_target_pairs={{0,24},{4,28},{8,16},{12,20},{16,8},{20,12},{24,0},{28,4},{1,25},{... | collective-permute-start | bytes 847880 | tf_op jit(solution)/shard_map/ppermute | solution.py:415
  59.4 1.9 collective-permute-start.12
  61.4 12.3 %collective-permute-done.11 = bf16[4,256,128]{2,1,0:T(8,128)(2,1)S(1)} collective-permute-done((bf16[4,256,128]{2,1,0:T(8,128)(2,1)S(1)}, bf16[4,256,128]{2,1,0:T(8,128)(2,1)S(1)}, u32[]{:S(2)}, u32[]{:S(2)}) %collective-permute-start.11) | collective-permute-done | bytes 262176 | tf_op jit(solution)/shard_map/ppermute | solution.py:415
  81.8 1.6 reshape.191
  83.4 1.7 copy.95
  85.1 1.6 reshape.192.nsum_ref
  86.8 1.6 copy-done.6
  91.9 17.2 %forward.1 = (bf16[5,256,512]{2,1,0:T(8,128)(2,1)S(1)}, bf16[5,256,512]{2,1,0:T(8,128)(2,1)S(1)}, bf16[5,256,512]{2,1,0:T(8,128)(2,1)S(1)}, bf16[5,16,512]{2,1,0...) custom-call(s32[6]{0:T(128)S(1)} %pad_add_fusion.scal_ref, ...), custom_call_target="tpu_custom_call" | custom-call | flops 8000000000 | bytes 11796480 | tf_op jit(solution)/shard_map/forward/pallas_call | solution.py:538
  109.2 11.1 %mlp.2 = (f32[5,256,512]{2,1,0:T(8,128)S(1)}, f32[5,256,512]{2,1,0:T(8,128)S(1)}, bf16[2,4,4,256,128]{4,3,2,1,0:T(8,128)(2,1)S(1)}) custom-call(bf16[5,256,512]{2,1,0:T(8,128)(2,1)S(1)} %get-tuple-element.47.refs_0_, bf16[5,512,256]{2,1,0:T(8,128)(2,1)S(1)} %get-tuple-element.48.refs_1_, bf16[5,256,512]{2,1,0:T(8,128)(2,1)S(1)} %copy-done.9, ...), custom_call_target="tpu_custom_call" | custom-call | flops 8999999488 | bytes 13107200 | tf_op jit(solution)/shard_map/mlp/pallas_call | solution.py:578
  123.0 12.0 %mlp.3 = (bf16[5,256,512]{2,1,0:T(8,128)(2,1)}, f32[5,256,512]{2,1,0:T(8,128)S(1)}, bf16[2,4,4,256,128]{4,3,2,1,0:T(8,128)(2,1)S(1)}) custom-call(bf16[5,256,512]{2,1,0:T(8,128)(2,1)S(1)} %get-tuple-element.47.refs_0_, bf16[5,512,256]{2,1,0:T(8,128)(2,1)S(1)} %get-tuple-element.48.refs_1_, bf16[5,256,512]{2,1,0:T(8,128)(2,1)S(1)} %copy-done.9, ...), custom_call_target="tpu_custom_call" | custom-call | flops 8999999488 | bytes 13107200 | tf_op jit(solution)/shard_map/mlp/pallas_call | solution.py:578
  137.7 23.1 %backward.1 = (f32[5,256,512]{2,1,0:T(8,128)S(1)}, bf16[5,256,1536]{2,1,0:T(8,128)(2,1)}, bf16[2,4,4,256,128]{4,3,2,1,0:T(8,128)(2,1)S(1)}, bf16[5,16,512]{2,1,0:T(8,128)(2,1)S(1)}, f32[8,512]{1,0:T(8,128)S(1)}) custom-call(s32[6]{0:T(128)S(1)} %pad_add_fusion.scal_ref, f32[5,256,512]{2,1,0:T(8,128)S(1)} %get-tuple-element.54.gm_ref, ...), custom_call_target="tpu_custom_call" | custom-call | flops 14000000000 | bytes 15728640 | tf_op jit(solution)/shard_map/backward/pallas_call | solution.py:597
  164.2 1.6 copy.96
  165.8 3.4 %all-to-all-start = ((bf16[8,5,2,512]{3,2,1,0:T(2,128)(2,1)}), bf16[8,5,2,512]{3,2,1,0:T(2,128)(2,1)S(1)}, u32[]{:S(2)}, u32[]{:S(2)}) async-start(bf16[8,5,2,512]{3,2,1,0:T(2,128)(2,1)} %bitcast.228), calls=%async_computation | async-start | bytes 163840 | tf_op jit(solution)/shard_map/all_to_all | solution.py:628
  169.2 1.7 copy.83
  170.9 1.7 copy.81
  172.5 1.7 copy.82
  174.9 1.6 copy-done.8
  176.5 2.1 copy-done.23
  178.6 1.7 copy-done.25
  180.3 6.0 %input.1 = (f32[5,256,512]{2,1,0:T(8,128)}, f32[8,512]{1,0:T(8,128)S(1)}) custom-call(s32[6]{0:T(128)S(1)} %pad_add_fusion.scal_ref, bf16[5,256,1536]{2,1,0:T(8,128)(2,1)S(1)} %copy-done.23, f32[5,256,512]{2,1,0:T(8,128)S(1)} %copy-done.25, bf16[5,256,512]{2,1,0:T(8,128)(2,1)S(1)} %copy-done.12, bf16[2,4,4,256,128]{4,3,2,1,0:T(8,128)(2,1)S(1)} %bitcast.223, ...), custom_call_target="tpu_custom_call" | custom-call | flops 3000000000 | bytes 10485760 | tf_op jit(solution)/shard_map/input/pallas_call | solution.py:633
  188.2 1.9 collective-permute-start.29
  193.1 1.9 collective-permute-start.36
  197.9 2.4 collective-permute-start.38
  200.2 4.7 %collective-permute-done.30 = bf16[4,256,128]{2,1,0:T(8,128)(2,1)S(1)} collective-permute-done((bf16[4,256,128]{2,1,0:T(8,128)(2,1)S(1)}, bf16[4,256,128]{2,1,0:T(8,128)(2,1)S(1)}, u32[]{:S(2)}, u32[]{:S(2)}) %collective-permute-start.30) | collective-permute-done | bytes 262176 | tf_op jit(solution)/shard_map/ppermute | solution.py:415
  205.0 2.0 collective-permute-start.23
  208.7 2.8 %collective-permute-start.24 = (bf16[4,256,128]{2,1,0:T(8,128)(2,1)S(1)}, bf16[4,256,128]{2,1,0:T(8,128)(2,1)S(1)}, u32[]{:S(2)}, u32[]{:S(2)}) collective-permute-start(bf16[4,256,128]{2,1,0:T(8,128)(2,1)S(1)} %get-tuple-element.171), channel_id=1, source_target_pairs={{0,24},{4,28},{8,16},{12,20},{16,8},{20,12},{24,0},{28,4},{1,25},{... | collective-permute-start | bytes 786440 | tf_op jit(solution)/shard_map/ppermute | solution.py:415
  211.5 4.7 %collective-permute-done.37 = bf16[4,256,128]{2,1,0:T(8,128)(2,1)S(1)} collective-permute-done((bf16[4,256,128]{2,1,0:T(8,128)(2,1)S(1)}, bf16[4,256,128]{2,1,0:T(8,128)(2,1)S(1)}, u32[]{:S(2)}, u32[]{:S(2)}) %collective-permute-start.37) | collective-permute-done | bytes 262176 | tf_op jit(solution)/shard_map/ppermute | solution.py:415
  220.0 1.9 collective-permute-start.34
  221.8 4.5 %collective-permute-done.23 = bf16[4,256,128]{2,1,0:T(8,128)(2,1)S(1)} collective-permute-done((bf16[4,256,128]{2,1,0:T(8,128)(2,1)S(1)}, bf16[4,256,128]{2,1,0:T(8,128)(2,1)S(1)}, u32[]{:S(2)}, u32[]{:S(2)}) %collective-permute-start.23) | collective-permute-done | bytes 262176 | tf_op jit(solution)/shard_map/ppermute | solution.py:415
  229.1 3.0 %collective-permute-start.41 = (bf16[256,128]{1,0:T(8,128)(2,1)S(1)}, bf16[256,128]{1,0:T(8,128)(2,1)S(1)}, u32[]{:S(2)}, u32[]{:S(2)}) collective-permute-start(bf16[256,128]{1,0:T(8,128)(2,1)S(1)} %get-tuple-element.177), channel_id=1, source_target_pairs={{0,3},{1,0},{2,1},{3,2},{4,7},{5,4},{6,5},{7,6},{8,11},{9,8},{10,9... | collective-permute-start | bytes 196616 | tf_op jit(solution)/shard_map/ppermute | solution.py:411
  233.6 2.9 %collective-permute-start.27 = (bf16[256,128]{1,0:T(8,128)(2,1)S(1)}, bf16[256,128]{1,0:T(8,128)(2,1)S(1)}, u32[]{:S(2)}, u32[]{:S(2)}) collective-permute-start(bf16[256,128]{1,0:T(8,128)(2,1)S(1)} %get-tuple-element.180), channel_id=1, source_target_pairs={{0,3},{1,0},{2,1},{3,2},{4,7},{5,4},{6,5},{7,6},{8,11},{9,8},{10,9... | collective-permute-start | bytes 196616 | tf_op jit(solution)/shard_map/ppermute | solution.py:411
  236.9 1.6 multiply_reduce_fusion.1
  240.3 2.7 concatenate.26
  243.9 4.7 %all-to-all-start.1 = ((f32[32,8,512]{2,1,0:T(8,128)}), f32[32,8,512]{2,1,0:T(8,128)S(1)}, u32[]{:S(2)}, u32[]{:S(2)}) async-start(f32[32,8,512]{2,1,0:T(8,128)} %broadcast_in_dim.159), calls=%async_computation.1 | async-start | bytes 1048576 | tf_op jit(solution)/shard_map/all_to_all | solution.py:674
  250.1 12.9 %all-to-all-done.1 = f32[32,8,512]{2,1,0:T(8,128)S(1)} async-done(((f32[32,8,512]{2,1,0:T(8,128)}), f32[32,8,512]{2,1,0:T(8,128)S(1)}, u32[]{:S(2)}, u32[]{:S(2)}) %all-to-all-start.1) | async-done | bytes 524320 | tf_op jit(solution)/shard_map/all_to_all | solution.py:674
  (254 shorter events, 64.5 us)
Async XLA Ops:
  3.6 18.4 %collective-permute-start.14 = (bf16[256,128]{1,0:T(8,128)(2,1)S(1)}, bf16[256,128]{1,0:T(8,128)(2,1)}, u32[]{:S(2)}, u32[]{:S(2)}) collective-permute-start(bf16[256,128]{1,0:T(8,128)(2,1)S(1)} %pad_maximum_fusion.3), channel_id=1, source_target_pairs={{0,1},{1,2},{2,3},{3,0},{4,5},{5,6},{6,7},{7,4},{8,9},{9,10},{10,1... | collective-permute-start | bytes 196616 | tf_op jit(solution)/shard_map/ppermute | solution.py:411
  6.7 19.1 %collective-permute-start.15 = (bf16[256,128]{1,0:T(8,128)(2,1)S(1)}, bf16[256,128]{1,0:T(8,128)(2,1)}, u32[]{:S(2)}, u32[]{:S(2)}) collective-permute-start(bf16[256,128]{1,0:T(8,128)(2,1)S(1)} %pad_maximum_fusion.3), channel_id=1, source_target_pairs={{0,2},{1,3},{2,0},{3,1},{4,6},{5,7},{6,4},{7,5},{8,10},{9,11},{10,... | collective-permute-start | bytes 196616 | tf_op jit(solution)/shard_map/ppermute | solution.py:411
  9.3 18.0 %collective-permute-start.16 = (bf16[256,128]{1,0:T(8,128)(2,1)S(1)}, bf16[256,128]{1,0:T(8,128)(2,1)}, u32[]{:S(2)}, u32[]{:S(2)}) collective-permute-start(bf16[256,128]{1,0:T(8,128)(2,1)S(1)} %pad_maximum_fusion.3), channel_id=1, source_target_pairs={{0,3},{1,0},{2,1},{3,2},{4,7},{5,4},{6,5},{7,6},{8,11},{9,8},{10,9... | collective-permute-start | bytes 196616 | tf_op jit(solution)/shard_map/ppermute | solution.py:411
  11.5 18.4 %collective-permute-start = (bf16[256,128]{1,0:T(8,128)(2,1)S(1)}, bf16[256,128]{1,0:T(8,128)(2,1)S(1)}, u32[]{:S(2)}, u32[]{:S(2)}) collective-permute-start(bf16[256,128]{1,0:T(8,128)(2,1)S(1)} %bitcast.237), channel_id=1, source_target_pairs={{0,1},{1,2},{2,3},{3,0},{4,5},{5,6},{6,7},{7,4},{8,9},{9,10},{10,1... | collective-permute-start | bytes 196616 | tf_op jit(solution)/shard_map/ppermute | solution.py:411
  12.2 20.6 %collective-permute-start.1 = (bf16[256,128]{1,0:T(8,128)(2,1)S(1)}, bf16[256,128]{1,0:T(8,128)(2,1)S(1)}, u32[]{:S(2)}, u32[]{:S(2)}) collective-permute-start(bf16[256,128]{1,0:T(8,128)(2,1)S(1)} %bitcast.238), channel_id=1, source_target_pairs={{0,2},{1,3},{2,0},{3,1},{4,6},{5,7},{6,4},{7,5},{8,10},{9,11},{10,... | collective-permute-start | bytes 196616 | tf_op jit(solution)/shard_map/ppermute | solution.py:411
  22.0 12.4 %collective-permute-start.2 = (bf16[256,128]{1,0:T(8,128)(2,1)S(1)}, bf16[256,128]{1,0:T(8,128)(2,1)S(1)}, u32[]{:S(2)}, u32[]{:S(2)}) collective-permute-start(bf16[256,128]{1,0:T(8,128)(2,1)S(1)} %bitcast.240), channel_id=1, source_target_pairs={{0,3},{1,0},{2,1},{3,2},{4,7},{5,4},{6,5},{7,6},{8,11},{9,8},{10,9... | collective-permute-start | bytes 196616 | tf_op jit(solution)/shard_map/ppermute | solution.py:411
  25.7 10.6 %collective-permute-start.7 = (bf16[256,128]{1,0:T(8,128)(2,1)}, bf16[256,128]{1,0:T(8,128)(2,1)S(1)}, u32[]{:S(2)}, u32[]{:S(2)}) collective-permute-start(bf16[256,128]{1,0:T(8,128)(2,1)} %pad_maximum_fusion.2), channel_id=1, source_target_pairs={{0,1},{1,2},{2,3},{3,0},{4,5},{5,6},{6,7},{7,4},{8,9},{9,10},{10,1... | collective-permute-start | bytes 196616 | tf_op jit(solution)/shard_map/ppermute | solution.py:411
  27.2 9.6 %collective-permute-start.8 = (bf16[256,128]{1,0:T(8,128)(2,1)}, bf16[256,128]{1,0:T(8,128)(2,1)S(1)}, u32[]{:S(2)}, u32[]{:S(2)}) collective-permute-start(bf16[256,128]{1,0:T(8,128)(2,1)} %pad_maximum_fusion.2), channel_id=1, source_target_pairs={{0,2},{1,3},{2,0},{3,1},{4,6},{5,7},{6,4},{7,5},{8,10},{9,11},{10,... | collective-permute-start | bytes 196616 | tf_op jit(solution)/shard_map/ppermute | solution.py:411
  29.9 8.6 %collective-permute-start.9 = (bf16[256,128]{1,0:T(8,128)(2,1)S(1)}, bf16[256,128]{1,0:T(8,128)(2,1)S(1)}, u32[]{:S(2)}, u32[]{:S(2)}) collective-permute-start(bf16[256,128]{1,0:T(8,128)(2,1)S(1)} %copy-done.44), channel_id=1, source_target_pairs={{0,3},{1,0},{2,1},{3,2},{4,7},{5,4},{6,5},{7,6},{8,11},{9,8},{10,9... | collective-permute-start | bytes 196616 | tf_op jit(solution)/shard_map/ppermute | solution.py:411
  32.9 9.2 %collective-permute-start.17 = (bf16[4,256,128]{2,1,0:T(8,128)(2,1)S(1)}, bf16[4,256,128]{2,1,0:T(8,128)(2,1)S(1)}, u32[]{:S(2)}, u32[]{:S(2)}) collective-permute-start(bf16[4,256,128]{2,1,0:T(8,128)(2,1)S(1)} %bitcast_dynamic-update-slice_fusion.18), channel_id=1, source_target_pairs={{0,8},{4,12},{8,0},{12,4},{16,24},{20,28},{24,16},{28,20},{1,9},{5... | collective-permute-start | bytes 786440 | tf_op jit(solution)/shard_map/ppermute | solution.py:415
  34.5 24.8 %collective-permute-start.18 = (bf16[4,256,128]{2,1,0:T(8,128)(2,1)S(1)}, bf16[4,256,128]{2,1,0:T(8,128)(2,1)S(1)}, u32[]{:S(2)}, u32[]{:S(2)}) collective-permute-start(bf16[4,256,128]{2,1,0:T(8,128)(2,1)S(1)} %bitcast_dynamic-update-slice_fusion.18), channel_id=1, source_target_pairs={{0,16},{4,20},{8,24},{12,28},{16,0},{20,4},{24,8},{28,12},{1,17},{... | collective-permute-start | bytes 786440 | tf_op jit(solution)/shard_map/ppermute | solution.py:415
  36.3 23.1 %collective-permute-start.19 = (bf16[4,256,128]{2,1,0:T(8,128)(2,1)S(1)}, bf16[4,256,128]{2,1,0:T(8,128)(2,1)S(1)}, u32[]{:S(2)}, u32[]{:S(2)}) collective-permute-start(bf16[4,256,128]{2,1,0:T(8,128)(2,1)S(1)} %bitcast_dynamic-update-slice_fusion.18), channel_id=1, source_target_pairs={{0,24},{4,28},{8,16},{12,20},{16,8},{20,12},{24,0},{28,4},{1,25},{... | collective-permute-start | bytes 786440 | tf_op jit(solution)/shard_map/ppermute | solution.py:415
  36.9 38.1 %collective-permute-start.3 = (bf16[1104,128]{1,0:T(8,128)(2,1)S(1)}, bf16[1104,128]{1,0:T(8,128)(2,1)S(1)}, u32[]{:S(2)}, u32[]{:S(2)}) collective-permute-start(bf16[1104,128]{1,0:T(8,128)(2,1)S(1)} %pad_maximum_fusion), channel_id=1, source_target_pairs={{0,8},{4,12},{8,0},{12,4},{16,24},{20,28},{24,16},{28,20},{1,9},{5... | collective-permute-start | bytes 847880 | tf_op jit(solution)/shard_map/ppermute | solution.py:415
  38.5 17.3 %collective-permute-start.10 = (bf16[4,256,128]{2,1,0:T(8,128)(2,1)S(1)}, bf16[4,256,128]{2,1,0:T(8,128)(2,1)S(1)}, u32[]{:S(2)}, u32[]{:S(2)}) collective-permute-start(bf16[4,256,128]{2,1,0:T(8,128)(2,1)S(1)} %bitcast_dynamic-update-slice_fusion.22), channel_id=1, source_target_pairs={{0,8},{4,12},{8,0},{12,4},{16,24},{20,28},{24,16},{28,20},{1,9},{5... | collective-permute-start | bytes 786440 | tf_op jit(solution)/shard_map/ppermute | solution.py:415
  42.1 33.0 %collective-permute-start.4 = (bf16[1104,128]{1,0:T(8,128)(2,1)S(1)}, bf16[1104,128]{1,0:T(8,128)(2,1)S(1)}, u32[]{:S(2)}, u32[]{:S(2)}) collective-permute-start(bf16[1104,128]{1,0:T(8,128)(2,1)S(1)} %pad_maximum_fusion), channel_id=1, source_target_pairs={{0,16},{4,20},{8,24},{12,28},{16,0},{20,4},{24,8},{28,12},{1,17},{... | collective-permute-start | bytes 847880 | tf_op jit(solution)/shard_map/ppermute | solution.py:415
  55.8 19.4 %collective-permute-start.5 = (bf16[1104,128]{1,0:T(8,128)(2,1)S(1)}, bf16[1104,128]{1,0:T(8,128)(2,1)S(1)}, u32[]{:S(2)}, u32[]{:S(2)}) collective-permute-start(bf16[1104,128]{1,0:T(8,128)(2,1)S(1)} %pad_maximum_fusion), channel_id=1, source_target_pairs={{0,24},{4,28},{8,16},{12,20},{16,8},{20,12},{24,0},{28,4},{1,25},{... | collective-permute-start | bytes 847880 | tf_op jit(solution)/shard_map/ppermute | solution.py:415
  59.3 14.5 %collective-permute-start.11 = (bf16[4,256,128]{2,1,0:T(8,128)(2,1)S(1)}, bf16[4,256,128]{2,1,0:T(8,128)(2,1)S(1)}, u32[]{:S(2)}, u32[]{:S(2)}) collective-permute-start(bf16[4,256,128]{2,1,0:T(8,128)(2,1)S(1)} %bitcast_dynamic-update-slice_fusion.22), channel_id=1, source_target_pairs={{0,16},{4,20},{8,24},{12,28},{16,0},{20,4},{24,8},{28,12},{1,17},{... | collective-permute-start | bytes 786440 | tf_op jit(solution)/shard_map/ppermute | solution.py:415
  59.4 14.4 %collective-permute-start.12 = (bf16[4,256,128]{2,1,0:T(8,128)(2,1)S(1)}, bf16[4,256,128]{2,1,0:T(8,128)(2,1)S(1)}, u32[]{:S(2)}, u32[]{:S(2)}) collective-permute-start(bf16[4,256,128]{2,1,0:T(8,128)(2,1)S(1)} %bitcast_dynamic-update-slice_fusion.22), channel_id=1, source_target_pairs={{0,24},{4,28},{8,16},{12,20},{16,8},{20,12},{24,0},{28,4},{1,25},{... | collective-permute-start | bytes 786440 | tf_op jit(solution)/shard_map/ppermute | solution.py:415
  73.7 2.7 collective-permute-start.20
  73.8 4.1 %collective-permute-start.13 = (bf16[4,4,256,128]{3,2,1,0:T(8,128)(2,1)S(1)}, bf16[4,4,256,128]{3,2,1,0:T(8,128)(2,1)S(1)}, u32[]{:S(2)}, u32[]{:S(2)}) collective-permute-start(bf16[4,4,256,128]{3,2,1,0:T(8,128)(2,1)S(1)} %bitcast_dynamic-update-slice_fusion.14), channel_id=1, source_target_pairs={{0,4},{4,0},{8,12},{12,8},{16,20},{20,16},{24,28},{28,24},{1,5},{5... | collective-permute-start | bytes 3145736 | tf_op jit(solution)/shard_map/ppermute | solution.py:415
  75.2 4.3 %collective-permute-start.6 = (bf16[4,1104,128]{2,1,0:T(8,128)(2,1)S(1)}, bf16[4,1104,128]{2,1,0:T(8,128)(2,1)S(1)}, u32[]{:S(2)}, u32[]{:S(2)}) collective-permute-start(bf16[4,1104,128]{2,1,0:T(8,128)(2,1)S(1)} %bitcast_dynamic-update-slice_fusion.6), channel_id=1, source_target_pairs={{0,4},{4,0},{8,12},{12,8},{16,20},{20,16},{24,28},{28,24},{1,5},{5... | collective-permute-start | bytes 3391496 | tf_op jit(solution)/shard_map/ppermute | solution.py:415
  121.4 65.5 %collective-permute-start.28 = (bf16[4,4,256,128]{3,2,1,0:T(8,128)(2,1)}, bf16[4,4,256,128]{3,2,1,0:T(8,128)(2,1)}, u32[]{:S(2)}, u32[]{:S(2)}) collective-permute-start(bf16[4,4,256,128]{3,2,1,0:T(8,128)(2,1)} %dynamic-slice_bitcast_fusion.1), channel_id=1, source_target_pairs={{0,4},{4,0},{8,12},{12,8},{16,20},{20,16},{24,28},{28,24},{1,5},{5... | collective-permute-start | bytes 3145736 | tf_op jit(solution)/shard_map/ppermute | solution.py:415
  136.1 55.7 %collective-permute-start.35 = (bf16[4,4,256,128]{3,2,1,0:T(8,128)(2,1)}, bf16[4,4,256,128]{3,2,1,0:T(8,128)(2,1)}, u32[]{:S(2)}, u32[]{:S(2)}) collective-permute-start(bf16[4,4,256,128]{3,2,1,0:T(8,128)(2,1)} %dynamic-slice_bitcast_fusion), channel_id=1, source_target_pairs={{0,4},{4,0},{8,12},{12,8},{16,20},{20,16},{24,28},{28,24},{1,5},{5... | collective-permute-start | bytes 3145736 | tf_op jit(solution)/shard_map/ppermute | solution.py:415
  163.4 31.7 %collective-permute-start.21 = (bf16[4,4,256,128]{3,2,1,0:T(8,128)(2,1)}, bf16[4,4,256,128]{3,2,1,0:T(8,128)(2,1)}, u32[]{:S(2)}, u32[]{:S(2)}) collective-permute-start(bf16[4,4,256,128]{3,2,1,0:T(8,128)(2,1)} %dynamic-slice_bitcast_fusion.2), channel_id=1, source_target_pairs={{0,4},{4,0},{8,12},{12,8},{16,20},{20,16},{24,28},{28,24},{1,5},{5... | collective-permute-start | bytes 3145736 | tf_op jit(solution)/shard_map/ppermute | solution.py:415
  165.8 9.0 %all-to-all-start = ((bf16[8,5,2,512]{3,2,1,0:T(2,128)(2,1)}), bf16[8,5,2,512]{3,2,1,0:T(2,128)(2,1)S(1)}, u32[]{:S(2)}, u32[]{:S(2)}) async-start(bf16[8,5,2,512]{3,2,1,0:T(2,128)(2,1)} %bitcast.228), calls=%async_computation | async-start | bytes 163840 | tf_op jit(solution)/shard_map/all_to_all | solution.py:628
  188.2 9.6 %collective-permute-start.29 = (bf16[4,256,128]{2,1,0:T(8,128)(2,1)S(1)}, bf16[4,256,128]{2,1,0:T(8,128)(2,1)S(1)}, u32[]{:S(2)}, u32[]{:S(2)}) collective-permute-start(bf16[4,256,128]{2,1,0:T(8,128)(2,1)S(1)} %get-tuple-element.164), channel_id=1, source_target_pairs={{0,8},{4,12},{8,0},{12,4},{16,24},{20,28},{24,16},{28,20},{1,9},{5... | collective-permute-start | bytes 786440 | tf_op jit(solution)/shard_map/ppermute | solution.py:415
  190.1 14.8 %collective-permute-start.30 = (bf16[4,256,128]{2,1,0:T(8,128)(2,1)S(1)}, bf16[4,256,128]{2,1,0:T(8,128)(2,1)S(1)}, u32[]{:S(2)}, u32[]{:S(2)}) collective-permute-start(bf16[4,256,128]{2,1,0:T(8,128)(2,1)S(1)} %get-tuple-element.166), channel_id=1, source_target_pairs={{0,16},{4,20},{8,24},{12,28},{16,0},{20,4},{24,8},{28,12},{1,17},{... | collective-permute-start | bytes 786440 | tf_op jit(solution)/shard_map/ppermute | solution.py:415
  191.6 13.3 %collective-permute-start.31 = (bf16[4,256,128]{2,1,0:T(8,128)(2,1)S(1)}, bf16[4,256,128]{2,1,0:T(8,128)(2,1)S(1)}, u32[]{:S(2)}, u32[]{:S(2)}) collective-permute-start(bf16[4,256,128]{2,1,0:T(8,128)(2,1)S(1)} %get-tuple-element.165), channel_id=1, source_target_pairs={{0,24},{4,28},{8,16},{12,20},{16,8},{20,12},{24,0},{28,4},{1,25},{... | collective-permute-start | bytes 786440 | tf_op jit(solution)/shard_map/ppermute | solution.py:415
  193.1 15.6 %collective-permute-start.36 = (bf16[4,256,128]{2,1,0:T(8,128)(2,1)S(1)}, bf16[4,256,128]{2,1,0:T(8,128)(2,1)S(1)}, u32[]{:S(2)}, u32[]{:S(2)}) collective-permute-start(bf16[4,256,128]{2,1,0:T(8,128)(2,1)S(1)} %get-tuple-element.167), channel_id=1, source_target_pairs={{0,8},{4,12},{8,0},{12,4},{16,24},{20,28},{24,16},{28,20},{1,9},{5... | collective-permute-start | bytes 786440 | tf_op jit(solution)/shard_map/ppermute | solution.py:415
  195.0 21.2 %collective-permute-start.37 = (bf16[4,256,128]{2,1,0:T(8,128)(2,1)S(1)}, bf16[4,256,128]{2,1,0:T(8,128)(2,1)S(1)}, u32[]{:S(2)}, u32[]{:S(2)}) collective-permute-start(bf16[4,256,128]{2,1,0:T(8,128)(2,1)S(1)} %get-tuple-element.169), channel_id=1, source_target_pairs={{0,16},{4,20},{8,24},{12,28},{16,0},{20,4},{24,8},{28,12},{1,17},{... | collective-permute-start | bytes 786440 | tf_op jit(solution)/shard_map/ppermute | solution.py:415
  197.9 18.7 %collective-permute-start.38 = (bf16[4,256,128]{2,1,0:T(8,128)(2,1)S(1)}, bf16[4,256,128]{2,1,0:T(8,128)(2,1)S(1)}, u32[]{:S(2)}, u32[]{:S(2)}) collective-permute-start(bf16[4,256,128]{2,1,0:T(8,128)(2,1)S(1)} %get-tuple-element.168), channel_id=1, source_target_pairs={{0,24},{4,28},{8,16},{12,20},{16,8},{20,12},{24,0},{28,4},{1,25},{... | collective-permute-start | bytes 786440 | tf_op jit(solution)/shard_map/ppermute | solution.py:415
  205.0 15.0 %collective-permute-start.22 = (bf16[4,256,128]{2,1,0:T(8,128)(2,1)S(1)}, bf16[4,256,128]{2,1,0:T(8,128)(2,1)S(1)}, u32[]{:S(2)}, u32[]{:S(2)}) collective-permute-start(bf16[4,256,128]{2,1,0:T(8,128)(2,1)S(1)} %get-tuple-element.170), channel_id=1, source_target_pairs={{0,8},{4,12},{8,0},{12,4},{16,24},{20,28},{24,16},{28,20},{1,9},{5... | collective-permute-start | bytes 786440 | tf_op jit(solution)/shard_map/ppermute | solution.py:415
  205.0 21.4 %collective-permute-start.23 = (bf16[4,256,128]{2,1,0:T(8,128)(2,1)S(1)}, bf16[4,256,128]{2,1,0:T(8,128)(2,1)S(1)}, u32[]{:S(2)}, u32[]{:S(2)}) collective-permute-start(bf16[4,256,128]{2,1,0:T(8,128)(2,1)S(1)} %get-tuple-element.172), channel_id=1, source_target_pairs={{0,16},{4,20},{8,24},{12,28},{16,0},{20,4},{24,8},{28,12},{1,17},{... | collective-permute-start | bytes 786440 | tf_op jit(solution)/shard_map/ppermute | solution.py:415
  208.7 17.9 %collective-permute-start.24 = (bf16[4,256,128]{2,1,0:T(8,128)(2,1)S(1)}, bf16[4,256,128]{2,1,0:T(8,128)(2,1)S(1)}, u32[]{:S(2)}, u32[]{:S(2)}) collective-permute-start(bf16[4,256,128]{2,1,0:T(8,128)(2,1)S(1)} %get-tuple-element.171), channel_id=1, source_target_pairs={{0,24},{4,28},{8,16},{12,20},{16,8},{20,12},{24,0},{28,4},{1,25},{... | collective-permute-start | bytes 786440 | tf_op jit(solution)/shard_map/ppermute | solution.py:415
  216.2 12.9 %collective-permute-start.32 = (bf16[256,128]{1,0:T(8,128)(2,1)S(1)}, bf16[256,128]{1,0:T(8,128)(2,1)S(1)}, u32[]{:S(2)}, u32[]{:S(2)}) collective-permute-start(bf16[256,128]{1,0:T(8,128)(2,1)S(1)} %get-tuple-element.173), channel_id=1, source_target_pairs={{0,1},{1,2},{2,3},{3,0},{4,5},{5,6},{6,7},{7,4},{8,9},{9,10},{10,1... | collective-permute-start | bytes 196616 | tf_op jit(solution)/shard_map/ppermute | solution.py:411
  216.5 15.5 %collective-permute-start.33 = (bf16[256,128]{1,0:T(8,128)(2,1)S(1)}, bf16[256,128]{1,0:T(8,128)(2,1)S(1)}, u32[]{:S(2)}, u32[]{:S(2)}) collective-permute-start(bf16[256,128]{1,0:T(8,128)(2,1)S(1)} %get-tuple-element.175), channel_id=1, source_target_pairs={{0,2},{1,3},{2,0},{3,1},{4,6},{5,7},{6,4},{7,5},{8,10},{9,11},{10,... | collective-permute-start | bytes 196616 | tf_op jit(solution)/shard_map/ppermute | solution.py:411
  220.0 12.1 %collective-permute-start.34 = (bf16[256,128]{1,0:T(8,128)(2,1)S(1)}, bf16[256,128]{1,0:T(8,128)(2,1)S(1)}, u32[]{:S(2)}, u32[]{:S(2)}) collective-permute-start(bf16[256,128]{1,0:T(8,128)(2,1)S(1)} %get-tuple-element.174), channel_id=1, source_target_pairs={{0,3},{1,0},{2,1},{3,2},{4,7},{5,4},{6,5},{7,6},{8,11},{9,8},{10,9... | collective-permute-start | bytes 196616 | tf_op jit(solution)/shard_map/ppermute | solution.py:411
  226.3 7.3 %collective-permute-start.39 = (bf16[256,128]{1,0:T(8,128)(2,1)S(1)}, bf16[256,128]{1,0:T(8,128)(2,1)S(1)}, u32[]{:S(2)}, u32[]{:S(2)}) collective-permute-start(bf16[256,128]{1,0:T(8,128)(2,1)S(1)} %get-tuple-element.176), channel_id=1, source_target_pairs={{0,1},{1,2},{2,3},{3,0},{4,5},{5,6},{6,7},{7,4},{8,9},{9,10},{10,1... | collective-permute-start | bytes 196616 | tf_op jit(solution)/shard_map/ppermute | solution.py:411
  226.6 9.9 %collective-permute-start.40 = (bf16[256,128]{1,0:T(8,128)(2,1)S(1)}, bf16[256,128]{1,0:T(8,128)(2,1)S(1)}, u32[]{:S(2)}, u32[]{:S(2)}) collective-permute-start(bf16[256,128]{1,0:T(8,128)(2,1)S(1)} %get-tuple-element.178), channel_id=1, source_target_pairs={{0,2},{1,3},{2,0},{3,1},{4,6},{5,7},{6,4},{7,5},{8,10},{9,11},{10,... | collective-permute-start | bytes 196616 | tf_op jit(solution)/shard_map/ppermute | solution.py:411
  229.1 7.5 %collective-permute-start.41 = (bf16[256,128]{1,0:T(8,128)(2,1)S(1)}, bf16[256,128]{1,0:T(8,128)(2,1)S(1)}, u32[]{:S(2)}, u32[]{:S(2)}) collective-permute-start(bf16[256,128]{1,0:T(8,128)(2,1)S(1)} %get-tuple-element.177), channel_id=1, source_target_pairs={{0,3},{1,0},{2,1},{3,2},{4,7},{5,4},{6,5},{7,6},{8,11},{9,8},{10,9... | collective-permute-start | bytes 196616 | tf_op jit(solution)/shard_map/ppermute | solution.py:411
  232.0 6.5 %collective-permute-start.25 = (bf16[256,128]{1,0:T(8,128)(2,1)S(1)}, bf16[256,128]{1,0:T(8,128)(2,1)S(1)}, u32[]{:S(2)}, u32[]{:S(2)}) collective-permute-start(bf16[256,128]{1,0:T(8,128)(2,1)S(1)} %get-tuple-element.179), channel_id=1, source_target_pairs={{0,1},{1,2},{2,3},{3,0},{4,5},{5,6},{6,7},{7,4},{8,9},{9,10},{10,1... | collective-permute-start | bytes 196616 | tf_op jit(solution)/shard_map/ppermute | solution.py:411
  232.1 7.1 %collective-permute-start.26 = (bf16[256,128]{1,0:T(8,128)(2,1)S(1)}, bf16[256,128]{1,0:T(8,128)(2,1)S(1)}, u32[]{:S(2)}, u32[]{:S(2)}) collective-permute-start(bf16[256,128]{1,0:T(8,128)(2,1)S(1)} %get-tuple-element.181), channel_id=1, source_target_pairs={{0,2},{1,3},{2,0},{3,1},{4,6},{5,7},{6,4},{7,5},{8,10},{9,11},{10,... | collective-permute-start | bytes 196616 | tf_op jit(solution)/shard_map/ppermute | solution.py:411
  233.6 5.6 %collective-permute-start.27 = (bf16[256,128]{1,0:T(8,128)(2,1)S(1)}, bf16[256,128]{1,0:T(8,128)(2,1)S(1)}, u32[]{:S(2)}, u32[]{:S(2)}) collective-permute-start(bf16[256,128]{1,0:T(8,128)(2,1)S(1)} %get-tuple-element.180), channel_id=1, source_target_pairs={{0,3},{1,0},{2,1},{3,2},{4,7},{5,4},{6,5},{7,6},{8,11},{9,8},{10,9... | collective-permute-start | bytes 196616 | tf_op jit(solution)/shard_map/ppermute | solution.py:411
  238.5 29.4 %copy-start.37 = (f32[64,512]{1,0:T(8,128)}, f32[64,512]{1,0:T(8,128)S(1)}, u32[]{:S(2)}) copy-start(f32[64,512]{1,0:T(8,128)S(1)} %get-tuple-element.160) | copy-start | bytes 393220
  238.5 29.4 %copy-start.38 = (f32[64,512]{1,0:T(8,128)}, f32[64,512]{1,0:T(8,128)S(1)}, u32[]{:S(2)}) copy-start(f32[64,512]{1,0:T(8,128)S(1)} %get-tuple-element.161) | copy-start | bytes 393220
  239.5 29.1 %copy-start.39 = (f32[4,64,128]{2,1,0:T(8,128)}, f32[4,64,128]{2,1,0:T(8,128)S(1)}, u32[]{:S(2)}) copy-start(f32[4,64,128]{2,1,0:T(8,128)S(1)} %get-tuple-element.162) | copy-start | bytes 393220
  239.5 29.1 %copy-start.40 = (f32[4,64,128]{2,1,0:T(8,128)}, f32[4,64,128]{2,1,0:T(8,128)S(1)}, u32[]{:S(2)}) copy-start(f32[4,64,128]{2,1,0:T(8,128)S(1)} %get-tuple-element.163) | copy-start | bytes 393220
  243.9 19.1 %all-to-all-start.1 = ((f32[32,8,512]{2,1,0:T(8,128)}), f32[32,8,512]{2,1,0:T(8,128)S(1)}, u32[]{:S(2)}, u32[]{:S(2)}) async-start(f32[32,8,512]{2,1,0:T(8,128)} %broadcast_in_dim.159), calls=%async_computation.1 | async-start | bytes 1048576 | tf_op jit(solution)/shard_map/all_to_all | solution.py:674
  (45 other events, 370.0 us)

commit v2 on v1

v2 whole, which is shorter than its diff:
```python
import functools

import jax
import jax.numpy as jnp
from jax import lax
from jax.experimental import pallas as pl
from jax.experimental.pallas import tpu as pltpu
from jax.sharding import PartitionSpec as P

HEADS = 8
SPAN = 128
STEP = 5
CHUNKS = 2

masked_value = -1e30
decay_rate = 0.5
matrix_rate = 0.3
vector_rate = 0.5
weight_decay = 0.01
epsilon = 1e-06
gelu_a = 0.7978845608028654
gelu_b = 0.044715

f32 = jnp.float32
b16 = jnp.bfloat16
MIB = 1 << 20
NN = (((1,), (0,)), ((), ()))
NT = (((1,), (1,)), ((), ()))
TN = (((0,), (0,)), ((), ()))


def mm(a, b, dims=NN):
    return lax.dot_general(a, b, dims, preferred_element_type=f32)


def whole():
    return pl.BlockSpec(memory_space=pltpu.VMEM)


def scalars():
    return pl.BlockSpec(memory_space=pltpu.SMEM)


def per_step(*tail):
    zeros = (0,) * len(tail)
    return pl.BlockSpec((1,) + tail, lambda i: (i,) + zeros)


def fixed(*shape):
    zeros = (0,) * len(shape)
    return pl.BlockSpec(shape, lambda i: zeros)


def anywhere():
    return pl.BlockSpec(memory_space=pl.ANY)


def params(mib, steps=1):
    return pltpu.CompilerParams(
        dimension_semantics=("arbitrary",) * steps, vmem_limit_bytes=mib * MIB
    )


def cost(flops, nbytes, trans=0):
    return pl.CostEstimate(flops=int(flops), bytes_accessed=int(nbytes), transcendentals=int(trans))


def norm_parts(values):
    center = values - jnp.mean(values, -1, keepdims=True)
    spread = jnp.mean(center * center, -1, keepdims=True)
    inverse = lax.rsqrt(spread + 1e-05)
    return center * inverse, inverse


def norm_back(gradient, normal, inverse, gain):
    scaled = gradient * gain
    inner = jnp.mean(scaled, -1, keepdims=True)
    cross = jnp.mean(scaled * normal, -1, keepdims=True)
    return inverse * (scaled - inner - normal * cross)


def each_core(core, do):
    @pl.when(core == 0)
    def _():
        do(0, True)
        do(1, False)

    @pl.when(core != 0)
    def _():
        do(0, False)
        do(1, True)


def block(start, size):
    if isinstance(start, int):
        return slice(start, start + size)
    return pl.ds(pl.multiple_of(start, size), size)


def copy_attn(w_ref, own_refs, other_refs, spot, core, dims):
    groups, rows, cols, width = dims

    def do(c, mine):
        for move, buf_ref in enumerate(own_refs if mine else other_refs):
            place = move if spot is None else spot ^ move
            here = block((place * 2 + c) * rows, rows)
            for g in range(groups):
                for m in range(4):
                    at = (g * 4 + m) * rows
                    w_ref[here, m * width + g * cols : m * width + (g + 1) * cols] = buf_ref[
                        at : at + rows, :
                    ]

    each_core(core, do)


def prep_kernel(scal_ref, x_ref, ln_ref, normed_ref, rider_ref, sum_ref):
    i = pl.program_id(0)
    tok, width = x_ref.shape[1:]
    spans = tok // SPAN
    tiles = width // SPAN
    half = sum_ref.shape[0]
    normal, _ = norm_parts(x_ref[0].astype(f32))
    normed = (normal * ln_ref[0:1, :] + ln_ref[1:2, :]).astype(b16)
    normed_ref[0] = normed
    left = scal_ref[2 + i] - scal_ref[0] * tok
    row = lax.broadcasted_iota(jnp.int32, (16, tok), 0)
    col = lax.broadcasted_iota(jnp.int32, (16, tok), 1)
    chosen = jnp.where((col // SPAN == row) & (col < left), 1.0, 0.0)
    amount = jnp.maximum(jnp.sum(chosen, 1, keepdims=True), 1.0)
    total = mm(chosen.astype(b16), normed) / amount

    @pl.when(i == 0)
    def _():
        sum_ref[...] = jnp.zeros_like(sum_ref)

    for s in range(spans):
        for t in range(tiles):
            sum_ref[pl.ds((i * spans + s) * tiles + t, 1), :] = total[
                s : s + 1, t * SPAN : (t + 1) * SPAN
            ]

    @pl.when(i == pl.num_programs(0) - 1)
    def _():
        every = sum_ref[...]
        high = every.astype(b16)
        rider_ref[:half] = high
        rider_ref[half:] = (every - high.astype(f32)).astype(b16)


def pack_kernel(dims, up_ref, down_ref, dep_ref, *out_refs):
    rows, cols, sub, lanes = dims
    for j, out_ref in enumerate(out_refs):
        for h in range(sub):
            c0 = (h * CHUNKS + j) * lanes
            out_ref[h * rows : (h + 1) * rows, :] = up_ref[:, c0 : c0 + lanes].astype(b16)
        out_ref[sub * rows :, :] = down_ref[j * lanes : (j + 1) * lanes, :].T.astype(b16)


def heads_apart(values):
    first = lax.broadcasted_iota(jnp.int32, values.shape, 1) < SPAN // 2
    zero = jnp.zeros_like(values)
    return jnp.concatenate([jnp.where(first, values, zero), jnp.where(first, zero, values)], 0)


def score_masks(scal_ref, i, span, spans, amount):
    length = scal_ref[2 + i]
    mine = scal_ref[0] * spans + span
    key = lax.broadcasted_iota(jnp.int32, (SPAN, 2 * SPAN), 0)
    query = lax.broadcasted_iota(jnp.int32, (SPAN, 2 * SPAN), 1) % SPAN
    local = (key <= query) & (key < length - mine * SPAN)
    index = lax.broadcasted_iota(jnp.int32, (amount, 2 * SPAN), 0)
    summary = (index < mine) & (index * SPAN < length)
    return local, summary


def own_heads(both):
    half = SPAN // 2
    return jnp.concatenate([both[:half, :SPAN], both[half:, SPAN:]], 0)


def gate_kernel(in_ref, dep_ref, out_ref):
    out_ref[...] = in_ref[...]


def forward_kernel(dims, fast, places, scal_ref, normed_ref, x_ref, *refs):
    own_refs, refs = refs[:places], refs[places:]
    other_refs, refs = refs[:places], refs[places:]
    if fast:
        rown_refs, rother_refs = own_refs, other_refs
    else:
        rown_refs, refs = refs[:places], refs[places:]
        rother_refs, refs = refs[:places], refs[places:]
    (ln_ref, dep_ref, q_ref, k_ref, v_ref, ks_ref, vs_ref, nsum_ref, lse_ref, mixed_ref, x2_ref,
     mid_ref, w_ref, token_ref, sums_ref, line_ref) = refs
    i = pl.program_id(0)
    groups, rows, cols, width = dims
    tok = normed_ref.shape[1]
    spans = tok // SPAN
    tiles = width // SPAN
    amount = ks_ref.shape[1]
    factor = (width // HEADS) ** (-0.5)
    half = sums_ref.shape[2]
    base = groups * 4 * rows if fast else 0

    @pl.when(i == 0)
    def _():
        core = scal_ref[0] % 2
        spot = scal_ref[0] // 2 if fast else None
        copy_attn(w_ref, own_refs, other_refs, spot, core, dims)

        def do(c, mine):
            for move, buf_ref in enumerate(rown_refs if mine else rother_refs):
                place = spot ^ move if fast else move
                sums_ref[c, place] = buf_ref[base : base + half, :].astype(f32) + buf_ref[
                    base + half : base + 2 * half, :
                ].astype(f32)

        each_core(core, do)
        token_ref[...] = jnp.zeros_like(token_ref)

    for p in range(places):
        for c in range(2):
            for s in range(spans):
                for t in range(tiles):
                    r = (p * 2 + c) * spans + s
                    line_ref[r : r + 1, t * SPAN : (t + 1) * SPAN] = sums_ref[
                        c, p, pl.ds((i * spans + s) * tiles + t, 1), :
                    ]
    lines = line_ref[...]
    high = lines.astype(b16)
    low = (lines - high.astype(f32)).astype(b16)
    nsum_ref[0] = high
    normed = normed_ref[0]
    q_ref[0] = mm(normed, w_ref[:, :width]).astype(b16)
    k_ref[0] = mm(normed, w_ref[:, width : 2 * width]).astype(b16)
    v_ref[0] = mm(normed, w_ref[:, 2 * width : 3 * width]).astype(b16)
    sums = mm(high, w_ref[:, width : 3 * width]) + mm(low, w_ref[:, width : 3 * width])
    ks_ref[0] = sums[:, :width].astype(b16)
    vs_ref[0] = sums[:, width:].astype(b16)
    for span in range(spans):
        part = slice(span * SPAN, (span + 1) * SPAN)
        local, summary = score_masks(scal_ref, i, span, spans, amount)
        for pair in range(tiles):
            lanes = slice(pair * SPAN, (pair + 1) * SPAN)
            query = heads_apart(q_ref[0, part, lanes] * b16(factor))
            keys = jnp.concatenate([k_ref[0, part, lanes], ks_ref[0, :, lanes]], 0)
            values = jnp.concatenate([v_ref[0, part, lanes], vs_ref[0, :, lanes]], 0)
            scores = mm(keys, query, NT)
            here = jnp.where(local, scores[:SPAN], masked_value)
            there = jnp.where(summary, scores[SPAN:], masked_value)
            top = jnp.maximum(jnp.max(here, 0, keepdims=True), jnp.max(there, 0, keepdims=True))
            here, there = jnp.exp(here - top), jnp.exp(there - top)
            total = jnp.sum(here, 0, keepdims=True) + jnp.sum(there, 0, keepdims=True)
            probs = jnp.concatenate([here.astype(b16), there.astype(b16)], 0)
            lse_ref[0, span, pair : pair + 1, :] = top + jnp.log(total)
            out = mm(values, probs, TN) * (1.0 / total)
            mixed_ref[0, lanes, part] = own_heads(out).astype(b16)
    x2 = x_ref[0].astype(f32) + mm(mixed_ref[0], w_ref[:, 3 * width :], TN)
    x2_ref[0] = x2.astype(b16)
    normal, _ = norm_parts(x2)
    mid_ref[0] = (normal * ln_ref[2:3, :] + ln_ref[3:4, :]).astype(b16)


def mlp_kernel(dims, fast, places, last, scal_ref, mid_ref, g_ref, *refs):
    own_refs, refs = refs[:places], refs[places:]
    other_refs, refs = refs[:places], refs[places:]
    if last:
        (dep_ref, x2_ref, y_in_ref, gm_in_ref,
         y_ref, gm_ref, keep_ref, send_ref, wu_ref, wd_ref, du_ref, dd_ref) = refs
    else:
        (dep_ref, y_ref, gm_ref, keep_ref, send_ref, wu_ref, wd_ref, du_ref, dd_ref) = refs
    groups, rows, cols, sub, lanes = dims
    size = sub * rows + cols
    i = pl.program_id(0)
    core = scal_ref[0] % 2

    def pieces(place, c):
        b = place * 2 + c
        here = block(b * rows, rows)
        there = block(b * lanes, lanes)
        for g in range(groups):
            for h in range(sub):
                at = g * size + h * rows
                yield (
                    slice(at, at + rows),
                    (here, slice((g * sub + h) * lanes, (g * sub + h + 1) * lanes)),
                    True,
                )
            at = g * size + sub * rows
            yield slice(at, at + cols), (slice(g * cols, (g + 1) * cols), there), False

    @pl.when(i == 0)
    def _():
        def do(c, mine):
            for move, buf_ref in enumerate(own_refs if mine else other_refs):
                place = (scal_ref[0] // 2) ^ move if fast else move
                for there, here, is_up in pieces(place, c):
                    (wu_ref if is_up else wd_ref)[here] = buf_ref[there, :]

        each_core(core, do)
        du_ref[...] = jnp.zeros_like(du_ref)
        dd_ref[...] = jnp.zeros_like(dd_ref)

    mid, g = mid_ref[0], g_ref[0]
    up = mm(mid, wu_ref[...])
    grad_act = mm(g, wd_ref[...])
    square = up * up
    half = 0.5 + 0.5 * jnp.tanh(up * (gelu_a + gelu_a * gelu_b * square))
    act = (up * half).astype(b16)
    slope = half + (up * half * (1.0 - half)) * (2.0 * gelu_a + 6.0 * gelu_a * gelu_b * square)
    grad_up = (slope * grad_act).astype(b16)
    y = mm(act, wd_ref[...], NT)
    gm = mm(grad_up, wu_ref[...], NT)
    if last:
        y_ref[0] = (x2_ref[0].astype(f32) + y_in_ref[0].astype(f32) + y).astype(b16)
        gm_ref[0] = (gm_in_ref[0].astype(f32) + gm).astype(b16)
    else:
        y_ref[0] = y.astype(b16)
        gm_ref[0] = gm.astype(b16)
    dd_ref[...] += mm(g, act, TN)
    du_ref[...] += mm(mid, grad_up, TN)

    @pl.when(i == pl.num_programs(0) - 1)
    def _():
        def do(c, mine):
            out_ref = keep_ref if mine else send_ref
            for place in range(places):
                for there, here, is_up in pieces(place, c):
                    out_ref[place, there, :] = (du_ref if is_up else dd_ref)[here].astype(b16)

        each_core(core, do)


def middle_kernel(
    gm_ref, g_ref, x2_ref, mixed_ref, w_ref, ln_ref, gx2_ref, do_ref, dwo_ref, lng_ref
):
    i = pl.program_id(0)
    width = ln_ref.shape[1]

    @pl.when(i == 0)
    def _():
        dwo_ref[...] = jnp.zeros_like(dwo_ref)
        lng_ref[...] = jnp.zeros_like(lng_ref)

    gm = gm_ref[0].astype(f32)
    normal, inverse = norm_parts(x2_ref[0].astype(f32))
    lng_ref[0:1, :] += jnp.sum(gm * normal, 0, keepdims=True)
    lng_ref[1:2, :] += jnp.sum(gm, 0, keepdims=True)
    gx2 = g_ref[0].astype(f32) + norm_back(gm, normal, inverse, ln_ref[2:3, :])
    branch = gx2.astype(b16)
    gx2_ref[0] = branch
    dwo_ref[...] += mm(mixed_ref[0], branch)
    do_ref[0] = mm(branch, w_ref[:, 3 * width :], NT).astype(b16)


def backward_kernel(
    places, scal_ref, do_ref, q_ref, k_ref, v_ref, lse_ref, ks_ref, vs_ref, w_ref, dep_ref,
    dqkv_ref, key_ref, value_ref, h_ref, dqt_ref,
):
    i = pl.program_id(0)
    tok, width = do_ref.shape[1:]
    spans = tok // SPAN
    tiles = width // SPAN
    amount = ks_ref.shape[1]
    factor = (width // HEADS) ** (-0.5)

    @pl.when(i == 0)
    def _():
        h_ref[...] = jnp.zeros_like(h_ref)

    key_parts, value_parts = [], []
    for span in range(spans):
        part = slice(span * SPAN, (span + 1) * SPAN)
        local, summary = score_masks(scal_ref, i, span, spans, amount)
        for pair in range(tiles):
            lanes = slice(pair * SPAN, (pair + 1) * SPAN)
            query = heads_apart(q_ref[0, part, lanes] * b16(factor))
            grad = heads_apart(do_ref[0, part, lanes])
            keys = jnp.concatenate([k_ref[0, part, lanes], ks_ref[0, :, lanes]], 0)
            values = jnp.concatenate([v_ref[0, part, lanes], vs_ref[0, :, lanes]], 0)
            scores = mm(keys, query, NT)
            grads = mm(values, grad, NT)
            total = lse_ref[0, span, pair : pair + 1, :]
            here = jnp.exp(jnp.where(local, scores[:SPAN], masked_value) - total)
            there = jnp.exp(jnp.where(summary, scores[SPAN:], masked_value) - total)
            here_grad, there_grad = here * grads[:SPAN], there * grads[SPAN:]
            dot = jnp.sum(here_grad, 0, keepdims=True) + jnp.sum(there_grad, 0, keepdims=True)
            low = jnp.concatenate([here.astype(b16), there.astype(b16)], 0)
            back = jnp.concatenate(
                [(here_grad - here * dot).astype(b16), (there_grad - there * dot).astype(b16)], 0
            )
            grad_value = mm(low, grad)
            grad_key = mm(back, query)
            dqt_ref[lanes, part] = (own_heads(mm(keys, back, TN)) * factor).astype(b16)
            dqkv_ref[0, part, width + pair * SPAN : width + (pair + 1) * SPAN] = grad_key[
                :SPAN
            ].astype(b16)
            dqkv_ref[0, part, 2 * width + pair * SPAN : 2 * width + (pair + 1) * SPAN] = grad_value[
                :SPAN
            ].astype(b16)
            key_parts.append(grad_key[SPAN:])
            value_parts.append(grad_value[SPAN:])
    dqkv_ref[0, :, :width] = dqt_ref[...].T

    def joined(parts):
        return jnp.concatenate(
            [sum(parts[s * tiles + p] for s in range(spans)) for p in range(tiles)], 1
        ).astype(b16)

    key_part, value_part = joined(key_parts), joined(value_parts)
    key_ref[0], value_ref[0] = key_part, value_part
    extra = mm(key_part, w_ref[:, width : 2 * width], NT) + mm(
        value_part, w_ref[:, 2 * width : 3 * width], NT
    )
    for p in range(places):
        for c in range(2):
            for s in range(spans):
                for t in range(tiles):
                    r = (p * 2 + c) * spans + s
                    h_ref[c, p, pl.ds((i * spans + s) * tiles + t, 1), :] = extra[
                        r : r + 1, t * SPAN : (t + 1) * SPAN
                    ]


def grads_kernel(
    dims, fast, scal_ref, normed_ref, dqkv_ref, nsum_ref, key_ref, value_ref, dwo_ref, h_ref,
    two_ref, dep_ref, *refs
):
    if fast:
        keep_ref, send_ref, nt_ref, dw_ref = refs
        hkeep_ref, hsend_ref = keep_ref, send_ref
    else:
        keep_ref, send_ref, hkeep_ref, hsend_ref, nt_ref, dw_ref = refs
    groups, rows, cols, width = dims
    places, half = h_ref.shape[1:3]
    tiles = width // SPAN
    base = groups * 4 * rows if fast else 0
    used = -(-half // 16) * 16 - 8
    nt_ref[...] = normed_ref[...].T
    dw_ref[:, :width] = mm(nt_ref[...], dqkv_ref[:, :width])
    dw_ref[:, width : 2 * width] = mm(nt_ref[...], dqkv_ref[:, width : 2 * width]) + mm(
        nsum_ref[...], key_ref[...], TN
    )
    dw_ref[:, 2 * width :] = mm(nt_ref[...], dqkv_ref[:, 2 * width :]) + mm(
        nsum_ref[...], value_ref[...], TN
    )
    if fast:
        for p in range(places):
            for c in range(2):
                k, t = divmod(p * 2 + c, tiles)
                piece = two_ref[k : k + 1, t * SPAN : (t + 1) * SPAN]
                high = piece.astype(b16).astype(f32)
                h_ref[c, p, used : used + 1, :] = high
                h_ref[c, p, used + 1 : used + 2, :] = piece - high

    def do(c, mine):
        out_ref, hout_ref = (keep_ref, hkeep_ref) if mine else (send_ref, hsend_ref)
        for p in range(places):
            r0 = (p * 2 + c) * rows
            for g in range(groups):
                for m in range(4):
                    at = (g * 4 + m) * rows
                    from_ref = dwo_ref if m == 3 else dw_ref
                    c0 = g * cols if m == 3 else m * width + g * cols
                    out_ref[p, at : at + rows, :] = from_ref[
                        r0 : r0 + rows, c0 : c0 + cols
                    ].astype(b16)
            hout_ref[p, base : base + half, :] = h_ref[c, p].astype(b16)

    each_core(scal_ref[0] % 2, do)


def project_kernel(dqkv_ref, w_ref, dep_ref, out_ref):
    out_ref[0] = mm(dqkv_ref[0], w_ref[:, : dqkv_ref.shape[2]], NT).astype(out_ref.dtype)


def input_kernel(scal_ref, grad_ref, gx2_ref, x_ref, h_ref, ln_ref, out_ref, lng_ref):
    i = pl.program_id(0)
    tok, width = x_ref.shape[1:]
    spans = tok // SPAN
    tiles = width // SPAN

    @pl.when(i == 0)
    def _():
        lng_ref[...] = jnp.zeros_like(lng_ref)

    left = scal_ref[2 + i] - scal_ref[0] * tok
    place = lax.broadcasted_iota(jnp.int32, (tok, 1), 0)
    extra = []
    for s in range(spans):
        part = slice(s * SPAN, (s + 1) * SPAN)
        amount = jnp.clip(left - s * SPAN, 0, SPAN)
        share = jnp.where(place[part] < left, 1.0, 0.0) / jnp.maximum(amount, 1).astype(f32)
        line = jnp.concatenate(
            [h_ref[pl.ds((i * spans + s) * tiles + t, 1), :] for t in range(tiles)], 1
        )
        extra.append(share * line)
    grad = grad_ref[0].astype(f32) + jnp.concatenate(extra, 0)
    normal, inverse = norm_parts(x_ref[0].astype(f32))
    lng_ref[0:1, :] += jnp.sum(grad * normal, 0, keepdims=True)
    lng_ref[1:2, :] += jnp.sum(grad, 0, keepdims=True)
    out_ref[0] = gx2_ref[0].astype(f32) + norm_back(grad, normal, inverse, ln_ref[0:1, :])


def spread_kernel(count, scal_ref, *refs):
    keeps, gets, outs = refs[:count], refs[count : 2 * count], refs[-4:]
    spot = scal_ref[0] // 2
    at = 0
    for keep_ref, get_ref in zip(keeps, gets):
        size = keep_ref.shape[1]
        for move in range(4):
            there = spot ^ move
            total = keep_ref[there].astype(f32) + get_ref[there].astype(f32)
            outs[move][at : at + size, :] = total.astype(outs[move].dtype)
        at += size


def halves_kernel(scal_ref, *refs):
    spot = scal_ref[0] // 2
    for j, far in enumerate((1, 2)):
        keep_ref, get_ref = refs[j], refs[2 + j]
        stay_ref, out_ref = refs[4 + 2 * j], refs[5 + 2 * j]
        near = 3 - far
        for k, (ref, move) in enumerate(
            ((stay_ref, 0), (stay_ref, near), (out_ref, far), (out_ref, far ^ near))
        ):
            there = spot ^ move
            total = keep_ref[there].astype(f32) + get_ref[there].astype(f32)
            ref[k % 2] = total.astype(ref.dtype)


def turn_kernel(*refs):
    for j in range(2):
        stay_ref, get_ref = refs[2 * j], refs[2 * j + 1]
        own_ref, out_ref = refs[4 + 2 * j], refs[5 + 2 * j]
        own_ref[...] = stay_ref[0] + get_ref[0].astype(f32)
        out_ref[...] = (stay_ref[1] + get_ref[1].astype(f32)).astype(b16)


def collect_kernel(sizes, count, scal_ref, *refs):
    z = scal_ref[1]
    groups = 4
    outs = refs[len(sizes) * count + 1 :]

    def total(terms, start, size):
        rows = pl.ds(start, size)
        value = terms[0][rows, :].astype(f32)
        for ref in terms[1:]:
            value = value + ref[rows, :].astype(f32)
        return value

    at = 0
    for k, size in enumerate(sizes):
        terms = refs[k * count : (k + 1) * count]
        for by in range(groups):
            start = pl.multiple_of(((z + by) % groups) * size, size)
            outs[by][at : at + size, :] = total(terms, start, size).astype(outs[by].dtype)
        at += size
    if len(outs) > groups:
        outs[groups][...] = total(terms, groups * size, outs[groups].shape[0])


def moments(gradient, first, second):
    corr = 1.0 - decay_rate**STEP
    new_first = decay_rate * first + (1.0 - decay_rate) * gradient
    new_second = decay_rate * second + (1.0 - decay_rate) * gradient * gradient
    return (new_first, new_second, new_first / corr / (jnp.sqrt(new_second / corr) + epsilon))


def lane_line(values):
    lane = lax.broadcasted_iota(jnp.int32, (1, SPAN), 1)
    line = jnp.zeros((1, SPAN), f32)
    for at, value in values.items():
        line = line + jnp.where(lane == at, value, 0.0)
    return line


def square_sum(values):
    return jnp.sum(jnp.sum(values * values, 0, keepdims=True), 1, keepdims=True)


def add_up(refs, rows):
    total = refs[0][rows, :].astype(f32)
    for ref in refs[1:]:
        total = total + ref[rows, :].astype(f32)
    return total


def mlp_step_kernel(dims, count, *refs):
    grads = refs[:count]
    (um_ref, uf_ref, us_ref, dm_ref, df_ref, ds_ref,
     u1_ref, u2_ref, ustep_ref, d1_ref, d2_ref, dstep_ref, line_ref) = refs[count:]
    rows, cols, sub, lanes = dims
    size = sub * rows + cols
    sums = [jnp.zeros((1, 1), f32) for _ in range(4)]
    for j in range(CHUNKS):
        for h in range(sub):
            start = j * size + h * rows
            at = (slice(None), slice((h * CHUNKS + j) * lanes, (h * CHUNKS + j + 1) * lanes))
            first, second, way = moments(
                add_up(grads, slice(start, start + rows)), uf_ref[at], us_ref[at]
            )
            step = way + weight_decay * um_ref[at]
            u1_ref[at], u2_ref[at], ustep_ref[at] = first, second, step
            sums[0] += square_sum(um_ref[at])
            sums[2] += square_sum(step)
        start = j * size + sub * rows
        at = (slice(j * lanes, (j + 1) * lanes), slice(None))
        first, second, way = moments(
            add_up(grads, slice(start, start + cols)).T, df_ref[at], ds_ref[at]
        )
        step = way + weight_decay * dm_ref[at]
        d1_ref[at], d2_ref[at], dstep_ref[at] = first, second, step
        sums[1] += square_sum(dm_ref[at])
        sums[3] += square_sum(step)
    line_ref[...] = lane_line({4: sums[0], 5: sums[1], 10: sums[2], 11: sums[3]})


def attn_step_kernel(count, fast, *refs):
    grads = refs[:count]
    (m_ref, f_ref, s_ref, line_ref, one_ref, h_ref,
     m1_ref, m2_ref, step_ref, out_ref, all_ref) = refs[count:]
    rows = m_ref.shape[1]
    tiles = one_ref.shape[1] // SPAN
    values = {}
    for m in range(4):
        first, second, way = moments(
            add_up(grads, slice(m * rows, (m + 1) * rows)), f_ref[m], s_ref[m]
        )
        step = way + weight_decay * m_ref[m]
        m1_ref[m], m2_ref[m], step_ref[m] = first, second, step
        values[m] = square_sum(m_ref[m])
        values[6 + m] = square_sum(step)
    all_ref[...] = jnp.zeros_like(all_ref)
    for k in range(2):
        for t in range(tiles):
            all_ref[k * tiles + t : k * tiles + t + 1, :] = one_ref[
                k : k + 1, t * SPAN : (t + 1) * SPAN
            ]
    at = 2 * tiles
    if fast:
        used = h_ref.shape[0] - 8
        piece = h_ref[used : used + 1, :] + h_ref[used + 1 : used + 2, :]
        high = piece.astype(b16).astype(f32)
        all_ref[at : at + 1, :] = high
        all_ref[at + 1 : at + 2, :] = piece - high
    line = lane_line(values) + line_ref[...]
    for k in range(3):
        piece = line.astype(b16).astype(f32)
        all_ref[at + 2 + k : at + 3 + k, :] = piece
        line = line - piece
    message = all_ref[...].astype(b16)
    for k in range(out_ref.shape[0]):
        out_ref[k] = message


def final_kernel(
    groups, fast, every_ref, two_ref, am_ref, as_ref, um_ref, us_ref, dm_ref, ds_ref, ln_ref, lf_ref, ls_ref,
    an_ref, ac_ref, un_ref, uc_ref, dn_ref, dc_ref, l1_ref, l2_ref, ln_new_ref, norms_ref,
    all_ref, grad_ref,
):
    width = ln_ref.shape[1]
    tiles = width // SPAN
    at = 2 * tiles
    total = None
    for b in range(every_ref.shape[0] // groups):
        part = every_ref[b * groups].astype(f32)
        for k in range(b * groups + 1, (b + 1) * groups):
            part = part + every_ref[k].astype(f32)
        if fast:
            k, t = divmod(b, tiles)
            grad_ref[2 + k : 3 + k, t * SPAN : (t + 1) * SPAN] = (
                part[at : at + 1, :] + part[at + 1 : at + 2, :]
            )
        total = part if total is None else total + part
    all_ref[...] = total
    for k in range(2):
        for t in range(tiles):
            grad_ref[k : k + 1, t * SPAN : (t + 1) * SPAN] = all_ref[
                k * tiles + t : k * tiles + t + 1, :
            ]
    if not fast:
        grad_ref[2:4, :] = two_ref[0:2, :]
    line = all_ref[at + 2 : at + 3, :] + all_ref[at + 3 : at + 4, :] + all_ref[at + 4 : at + 5, :]
    roots = jnp.sqrt(line)
    norms_ref[0:1, :] = roots[:, 0:6]
    norms_ref[1:2, :] = roots[:, 6:12]
    lane = lax.broadcasted_iota(jnp.int32, line.shape, 1)

    def rate(k):
        weight = jnp.sum(jnp.where(lane == k, roots, 0.0), 1, keepdims=True)
        square = jnp.sum(jnp.where(lane == 6 + k, line, 0.0), 1, keepdims=True)
        return matrix_rate * (weight / jnp.sqrt(square + epsilon))

    for m in range(4):
        new = am_ref[m] - rate(m) * as_ref[m]
        an_ref[m] = new
        ac_ref[m] = new.astype(b16)
    new = um_ref[...] - rate(4) * us_ref[...]
    un_ref[...] = new
    uc_ref[...] = new.astype(b16)
    new = dm_ref[...] - rate(5) * ds_ref[...]
    dn_ref[...] = new
    dc_ref[...] = new.astype(b16)
    first, second, way = moments(grad_ref[...], lf_ref[...], ls_ref[...])
    l1_ref[...], l2_ref[...] = first, second
    ln_new_ref[...] = ln_ref[...] - vector_rate * way


def fast_mesh(nb, ng, width):
    return nb == 8 and ng == 4 and width // ng == SPAN


def shift(values, by, ng):
    return lax.ppermute(values, "group", [(j, (j + by) % ng) for j in range(ng)])


def cross(values, bit, nb):
    return lax.ppermute(values, "blk", [(j, j ^ bit) for j in range(nb)])


def put(buffer, piece, at):
    return lax.dynamic_update_slice(buffer, piece[None], (at,) + (0,) * piece.ndim)


def take(buffer, at):
    return lax.dynamic_index_in_dim(buffer, at, 0, keepdims=False)


def gather_group(piece, z, ng):
    out = put(jnp.zeros((ng,) + piece.shape, piece.dtype), piece, z)
    for by in range(1, ng):
        out = put(out, shift(piece, by, ng), (z - by) % ng)
    return out.reshape((-1,) + piece.shape[1:])


def gather_plane(piece, nb):
    return [piece] + [cross(piece, 2 * move, nb) for move in range(1, nb // 2)]


def other_core(pieces, nb):
    return [cross(piece, 1, nb) for piece in pieces]


def body(
    tokens, cotangent, lengths, ln_params, attn_master, attn_first, attn_second,
    up_master, up_first, up_second, down_master, down_first, down_second, ln_first, ln_second,
    *, nb, ng,
):
    seqs, tok, width = tokens.shape
    spans = tok // SPAN
    tiles = width // SPAN
    amount = nb * spans
    rows, cols = attn_master.shape[1:]
    ff_rows = down_master.shape[0]
    sub = nb // ng
    lanes = ff_rows // CHUNKS
    inner = nb * lanes
    places = nb // 2
    size = sub * rows + cols
    attn_rows = ng * 4 * rows
    half = -(-(seqs * spans * tiles + 8) // 16) * 16
    b, z = lax.axis_index("blk").astype(jnp.int32), lax.axis_index("group").astype(jnp.int32)
    core = b % 2
    fast = fast_mesh(nb, ng, width)
    scal = jnp.concatenate([jnp.stack([b, z]), lengths.astype(jnp.int32)])
    shape = jax.ShapeDtypeStruct

    def like(dtype, *tail):
        return shape((seqs,) + tail, dtype)

    def gather_any(piece, over=("blk", "group")):
        every = lax.all_gather(piece, over)
        every = every.reshape((places, 2, -1) + piece.shape[1:])
        every = jnp.swapaxes(every, 0, 1)
        own, other = take(every, core), take(every, 1 - core)
        return [own[p] for p in range(places)], [other[p] for p in range(places)]

    def reduce_any(keep, send, blocks):
        both = jnp.stack([jnp.where(core == 0, keep, send), jnp.where(core == 0, send, keep)])
        both = jnp.swapaxes(both, 0, 1).reshape((nb,) + keep.shape[1:])
        mine = lax.psum_scatter(both, "blk", scatter_dimension=0)
        if not blocks:
            return mine.astype(f32)
        mine = mine.reshape((ng, -1) + mine.shape[1:])
        return lax.psum_scatter(mine, "group", scatter_dimension=0).astype(f32)

    def flat(call, name, outs, scratch, work, *args, scalar=False):
        return pl.pallas_call(
            call,
            in_specs=[scalars()] * scalar + [whole()] * (len(args) - scalar),
            out_specs=[whole()] * len(outs),
            out_shape=outs,
            scratch_shapes=scratch,
            compiler_params=pltpu.CompilerParams(vmem_limit_bytes=16 * MIB),
            cost_estimate=work,
            name=name,
        )(*args)

    attn_piece = attn_master.astype(b16).reshape(4 * rows, cols)
    normed, rider = pl.pallas_call(
        prep_kernel,
        grid=(seqs,),
        in_specs=[scalars(), per_step(tok, width), fixed(4, width)],
        out_specs=[per_step(tok, width), fixed(2 * half, SPAN)],
        out_shape=[like(b16, tok, width), shape((2 * half, SPAN), b16)],
        scratch_shapes=[pltpu.VMEM((half, SPAN), f32)],
        compiler_params=params(16),
        cost_estimate=cost(4e7, 2 * seqs * tok * width * 2),
        name="prep",
    )(scal, tokens, ln_params)

    if fast:
        message = jnp.concatenate([gather_group(attn_piece, z, ng), rider], 0)
        attn_own = gather_plane(message, nb)
        attn_bufs = attn_own + other_core(attn_own, nb)
        pieces = flat(
            functools.partial(pack_kernel, (rows, cols, sub, lanes)), "pack",
            [shape((size, lanes), b16)] * CHUNKS, [], cost(1e6, 1e6),
            up_master, down_master, attn_own[1],
        )
        mlp_z = [gather_group(piece, z, ng) for piece in pieces]
        gates = [mlp_z[0]]
    else:
        up_low = up_master.astype(b16).reshape(rows, sub, CHUNKS, lanes)
        down_low = down_master.astype(b16).T.reshape(cols, CHUNKS, lanes)
        pieces = [
            jnp.concatenate(
                [jnp.swapaxes(up_low[:, :, j], 0, 1).reshape(sub * rows, lanes), down_low[:, j]], 0
            )
            for j in range(CHUNKS)
        ]
        attn_own, attn_other = gather_any(attn_piece)
        ride_own, ride_other = gather_any(rider, "blk")
        attn_bufs = attn_own + attn_other + ride_own + ride_other
        gates = [ln_params]

    dims = (ng, rows, cols, width)
    act_bytes = seqs * tok * width
    q, k, v, ks, vs, nsum, lse, mixed, x2, mid, w_attn, token = pl.pallas_call(
        functools.partial(forward_kernel, dims, fast, places),
        grid=(seqs,),
        in_specs=[scalars(), per_step(tok, width), per_step(tok, width)]
        + [whole()] * len(attn_bufs)
        + [fixed(4, width), whole()],
        out_specs=[
            per_step(tok, width), per_step(tok, width), per_step(tok, width),
            per_step(amount, width), per_step(amount, width), per_step(amount, width),
            per_step(spans, tiles, 2 * SPAN),
            per_step(width, tok), per_step(tok, width), per_step(tok, width),
            whole(), fixed(8, SPAN),
        ],
        out_shape=[
            like(b16, tok, width), like(b16, tok, width), like(b16, tok, width),
            like(b16, amount, width), like(b16, amount, width), like(b16, amount, width),
            like(f32, spans, tiles, 2 * SPAN),
            like(b16, width, tok), like(b16, tok, width), like(b16, tok, width),
            shape((width, 4 * width), b16), shape((8, SPAN), f32),
        ],
        scratch_shapes=[
            pltpu.VMEM((2, places, half, SPAN), f32), pltpu.VMEM((amount, width), f32)
        ],
        compiler_params=params(16),
        cost_estimate=cost(8e9, act_bytes * 18),
        name="forward",
    )(scal, normed, tokens, *attn_bufs, ln_params, gates[0])

    if fast:
        mlp_own = [gather_plane(mlp_z[0], nb)]
        for j in range(1, CHUNKS):
            (gated,) = flat(
                gate_kernel, "gate", [shape(mlp_z[j].shape, b16)], [], cost(1e6, 1e6),
                mlp_z[j], token,
            )
            gates.append(gated)
            mlp_own.append(gather_plane(gated, nb))
        mlp_bufs = [own + other_core(own, nb) for own in mlp_own]
    else:
        mlp_bufs = [sum(gather_any(piece), []) for piece in pieces]
        gates = gates * CHUNKS
    mlp_dims = (ng, rows, cols, sub, lanes)
    mlp_out = shape((places, ng * size, lanes), b16)
    keeps, sends = [], []
    y = gm = None
    for j in range(CHUNKS):
        last = j == CHUNKS - 1
        args = [scal, mid, cotangent, *mlp_bufs[j], gates[min(j + 1, CHUNKS - 1)]]
        in_specs = [scalars(), per_step(tok, width), per_step(tok, width)]
        in_specs += [whole()] * (len(mlp_bufs[j]) + 1)
        if last:
            args += [x2, y, gm]
            in_specs += [per_step(tok, width)] * 3
        y, gm, keep, send = pl.pallas_call(
            functools.partial(mlp_kernel, mlp_dims, fast, places, last),
            grid=(seqs,),
            in_specs=in_specs,
            out_specs=[per_step(tok, width), per_step(tok, width), whole(), whole()],
            out_shape=[like(b16, tok, width), like(b16, tok, width), mlp_out, mlp_out],
            scratch_shapes=[
                pltpu.VMEM((width, inner), b16), pltpu.VMEM((width, inner), b16),
                pltpu.VMEM((width, inner), f32), pltpu.VMEM((width, inner), f32),
            ],
            compiler_params=params(24),
            cost_estimate=cost(9e9, act_bytes * 20),
            name="mlp",
        )(*args)
        keeps.append(keep)
        sends.append(send)
    block_out = y
    if fast:
        gets = [cross(send, 1, nb) for send in sends]

    gx2, grad_mixed, dwo, ln_two = pl.pallas_call(
        middle_kernel,
        grid=(seqs,),
        in_specs=[
            per_step(tok, width), per_step(tok, width), per_step(tok, width),
            per_step(width, tok), whole(), fixed(4, width),
        ],
        out_specs=[
            per_step(tok, width), per_step(tok, width), fixed(width, width), fixed(8, width)
        ],
        out_shape=[
            like(b16, tok, width), like(b16, tok, width), shape((width, width), f32),
            shape((8, width), f32),
        ],
        compiler_params=params(16),
        cost_estimate=cost(3e9, act_bytes * 14),
        name="middle",
    )(gm, cotangent, x2, mixed, w_attn, ln_params)

    block = shape((ng * size, lanes), f32)
    block_low = shape((ng * size, lanes), b16)
    two, two_low = shape((2,) + block.shape, f32), shape((2,) + block.shape, b16)
    if fast:
        stay_a, out_a, stay_b, out_b = flat(
            halves_kernel, "halves", [two, two_low, two, two_low], [], cost(2e6, 16e6),
            scal, *keeps, *gets, scalar=True,
        )
        get_a, get_b = cross(out_a, 2, nb), cross(out_b, 4, nb)
        dep = stay_a
    else:
        dep = ln_two

    dqkv, key_part, value_part, h_part = pl.pallas_call(
        functools.partial(backward_kernel, places),
        grid=(seqs,),
        in_specs=[
            scalars(), per_step(tok, width),
            per_step(tok, width), per_step(tok, width), per_step(tok, width),
            per_step(spans, tiles, 2 * SPAN), per_step(amount, width), per_step(amount, width),
            whole(), anywhere(),
        ],
        out_specs=[
            per_step(tok, 3 * width), per_step(amount, width), per_step(amount, width), whole()
        ],
        out_shape=[
            like(b16, tok, 3 * width), like(b16, amount, width), like(b16, amount, width),
            shape((2, places, half, SPAN), f32),
        ],
        scratch_shapes=[pltpu.VMEM((width, tok), b16)],
        compiler_params=params(16),
        cost_estimate=cost(14e9, act_bytes * 24),
        name="backward",
    )(scal, grad_mixed, q, k, v, lse, ks, vs, w_attn, dep)

    if fast:
        own_a, out_a, own_b, out_b = flat(
            turn_kernel, "turn", [block, block_low] * 2, [], cost(1e6, 10e6),
            stay_a, get_a, stay_b, get_b,
        )
        mlp_parts = [own_a, cross(out_a, 4, nb), own_b, cross(out_b, 2, nb)]
        dep = own_a
    tail = half if fast else 0
    outs = [shape((places, attn_rows + tail, cols), b16)] * 2
    if not fast:
        outs += [shape((places, half, SPAN), b16)] * 2
    parts = flat(
        functools.partial(grads_kernel, dims, fast), "grads", outs,
        [pltpu.VMEM((width, seqs * tok), b16), pltpu.VMEM((width, 3 * width), f32)],
        cost(5e9, 1e7),
        scal, normed.reshape(-1, width), dqkv.reshape(-1, 3 * width), nsum.reshape(-1, width),
        key_part.reshape(-1, width), value_part.reshape(-1, width), dwo, h_part, ln_two, dep,
        scalar=True,
    )

    def collect(terms, sizes, count, tail):
        outs = [shape((sum(sizes), SPAN), f32)] + [shape((sum(sizes), SPAN), b16)] * 3
        if tail:
            outs.append(shape((tail, SPAN), f32))
        return flat(
            functools.partial(collect_kernel, sizes, count), "collect", outs, [], cost(1e6, 4e6),
            scal, *terms, scalar=True,
        )

    if fast:
        attn_low = shape((attn_rows + tail, cols), b16)
        attn_parts = flat(
            functools.partial(spread_kernel, 1), "spread",
            [shape(attn_low.shape, f32)] + [attn_low] * 3, [], cost(1e6, 4e6),
            scal, parts[0], cross(parts[1], 1, nb), scalar=True,
        )
        dep = attn_parts[0]
        attn_parts = [dep] + [cross(attn_parts[m], 2 * m, nb) for m in range(1, 4)]
    else:
        dep = parts[2]

    grad_in = pl.pallas_call(
        project_kernel,
        grid=(seqs,),
        in_specs=[per_step(tok, 3 * width), whole(), anywhere()],
        out_specs=per_step(tok, width),
        out_shape=like(b16, tok, width),
        compiler_params=params(16),
        cost_estimate=cost(3e9, act_bytes * 8),
        name="project",
    )(dqkv, w_attn, dep)

    if fast:
        mlp_sums = collect(mlp_parts + [grad_in], (size,) * CHUNKS, 2, 0)
        mlp_sums = [mlp_sums[0]] + [shift(mlp_sums[by], by, ng) for by in range(1, ng)]
        *attn_sums, own = collect(attn_parts + [grad_in], (4 * rows,), 4, half)
        attn_sums = [attn_sums[0]] + [shift(attn_sums[by], by, ng) for by in range(1, ng)]
    else:
        own = reduce_any(parts[2], parts[3], False)
        attn_sums = [reduce_any(parts[0], parts[1], True)]
        mlp_sums = [
            jnp.concatenate([reduce_any(keep, send, True) for keep, send in zip(keeps, sends)], 0)
        ]
        ln_two = lax.psum(ln_two, ("blk", "group"))

    input_grad, ln_one = pl.pallas_call(
        input_kernel,
        grid=(seqs,),
        in_specs=[
            scalars(), per_step(tok, width), per_step(tok, width), per_step(tok, width),
            whole(), fixed(4, width),
        ],
        out_specs=[per_step(tok, width), fixed(8, width)],
        out_shape=[like(f32, tok, width), shape((8, width), f32)],
        compiler_params=params(16),
        cost_estimate=cost(1e8, act_bytes * 10),
        name="input",
    )(scal, grad_in, gx2, tokens, own, ln_params)

    attn_shape = shape(attn_master.shape, f32)
    up_shape, down_shape = shape(up_master.shape, f32), shape(down_master.shape, f32)
    up_moment1, up_moment2, up_step, down_moment1, down_moment2, down_step, line = flat(
        functools.partial(mlp_step_kernel, (rows, cols, sub, lanes), len(mlp_sums)),
        "mlp_step",
        [up_shape] * 3 + [down_shape] * 3 + [shape((1, SPAN), f32)],
        [],
        cost(1e6, 2e6),
        *mlp_sums, up_master, up_first, up_second, down_master, down_first, down_second,
    )
    lines = -(-(2 * tiles + 5) // 16) * 16
    attn_moment1, attn_moment2, attn_step, message = flat(
        functools.partial(attn_step_kernel, len(attn_sums), fast),
        "attn_step",
        [attn_shape] * 3 + [shape((nb * ng, lines, SPAN), b16)],
        [pltpu.VMEM((lines, SPAN), f32)],
        cost(1e6, 2e6),
        *attn_sums, attn_master, attn_first, attn_second, line, ln_one, own,
    )
    every = lax.all_to_all(message, ("blk", "group"), 0, 0, tiled=True)

    def low(like_this):
        return shape(like_this.shape, b16)

    ln_shape = shape(ln_params.shape, f32)
    (attn_new, attn_copy, up_new, up_copy, down_new, down_copy,
     ln_moment1, ln_moment2, ln_new, norms) = flat(
        functools.partial(final_kernel, ng, fast),
        "final",
        [attn_shape, low(attn_master), up_shape, low(up_master), down_shape, low(down_master)]
        + [ln_shape] * 3 + [shape((2, 6), f32)],
        [pltpu.VMEM((lines, SPAN), f32), pltpu.VMEM((4, width), f32)],
        cost(1e6, 2e6),
        every, ln_two, attn_master, attn_step, up_master, up_step, down_master, down_step,
        ln_params, ln_first, ln_second,
    )
    return (
        block_out, input_grad,
        attn_moment1, attn_moment2, attn_new, attn_copy,
        up_moment1, up_moment2, up_new, up_copy,
        down_moment1, down_moment2, down_new, down_copy,
        ln_moment1, ln_moment2, ln_new, norms,
    )


def solution(mesh):
    seq_spec = P("group", "blk", None)
    attn_spec = P(None, "blk", "group")
    flat_spec = P("blk", "group")
    return jax.shard_map(
        functools.partial(body, nb=mesh.shape["blk"], ng=mesh.shape["group"]),
        mesh=mesh,
        in_specs=(seq_spec, seq_spec, P("group"), P())
        + (attn_spec,) * 3
        + (flat_spec,) * 6
        + (P(), P()),
        out_specs=(seq_spec, seq_spec)
        + (attn_spec,) * 4
        + (flat_spec,) * 8
        + (P(),) * 4,
        check_vma=False,
    )
```

time: 271 us -> 177 us (0.65)
  local copies, waits for them, and re-layouts: 54.4 us -> 2.37 us
  starting transfers between devices: 64.4 us -> 37.7 us
  other arithmetic: 17.8 us -> 1.67 us
  blocking collectives: 0 us -> 11.5 us
  waiting for transfers between devices: 57.8 us -> 49 us
    unnamed x109 -> x32, local copies, waits for them, and re-layouts: 29.5 us -> 2.08 us
    ppermute x18 -> x15, waiting for transfers between devices: 0.73 us -> 20.8 us  [shift(): lax.ppermute(values, 'group', [(j, (j + by) % ng) for j in range(ng)])]
    ppermute x24 -> x31, waiting for transfers between devices: 44.2 us -> 28.2 us  [cross(): return lax.ppermute(values, 'blk', [(j, j ^ bit) for j in range(nb)])]
    all_to_all x2 -> x0, waiting for transfers between devices: 12.9 us -> none  [the longest x1 12.9 us: body(): lax.all_to_all(jnp.broadcast_to(mine[None], (nb * ng,) + mine.shape), ('b...]
    ppermute x18 -> x15, starting transfers between devices: 28.3 us -> 15.8 us  [shift(): lax.ppermute(values, 'group', [(j, (j + by) % ng) for j in range(ng)])]
    all_to_all x0 -> x1, blocking collectives: none -> 11.5 us  [body(): every = lax.all_to_all(message, ('blk', 'group'), 0, 0, tiled=True)]
    convert_element_type x10 -> x0, other arithmetic: 9.89 us -> none  [the longest x3 3.99 us: reduce_all(): total = total + cross(at(spot ^ move).astype(b16), 2 * move, nb).astype(f32)]
    all_to_all x2 -> x0, starting transfers between devices: 8.05 us -> none  [the longest x1 4.69 us: body(): lax.all_to_all(jnp.broadcast_to(mine[None], (nb * ng,) + mine.shape), ('b...]
  transfers between devices with their start and end apart: 44 -> 46, of which waited for: 12 -> 12; matrix products, arithmetic and copies ran while one was open for 11% -> 1% of each run, Pallas kernels for 16% -> 38%
where the time goes in v2:
time: 177 us
  Pallas kernels  73.3 us (41%)
  waiting for transfers between devices  49 us (28%)
  starting transfers between devices  37.7 us (21%)
  blocking collectives  11.5 us (6%)
  local copies, waits for them, and re-layouts  2.37 us (1%)
    ppermute x31, waiting for transfers between devices, cross(): return lax.ppermute(values, 'blk', [(j, j ^ bit) for j in range(nb)])  28.2 us
    pallas_call x2, Pallas kernels, body(): pl.pallas_call(functools.partial(mlp_kernel, mlp_dims, fast, places, last...  24.1 us
    ppermute x31, starting transfers between devices, cross(): return lax.ppermute(values, 'blk', [(j, j ^ bit) for j in range(nb)])  22 us
    ppermute x15, waiting for transfers between devices, shift(): lax.ppermute(values, 'group', [(j, (j + by) % ng) for j in range(ng)])  20.8 us
    ppermute x15, starting transfers between devices, shift(): lax.ppermute(values, 'group', [(j, (j + by) % ng) for j in range(ng)])  15.8 us
    pallas_call x1, Pallas kernels, body(): pl.pallas_call(functools.partial(forward_kernel, dims, fast, places), gri...  13.2 us
    pallas_call x1, Pallas kernels, body(): pl.pallas_call(functools.partial(backward_kernel, places), grid=(seqs,),...  11.8 us
    all_to_all x1, blocking collectives, body(): every = lax.all_to_all(message, ('blk', 'group'), 0, 0, tiled=True)  11.5 us
  transfers between devices with their start and end apart: 46, of which 12 were waited for; matrix products, arithmetic and copies ran while one was open for 1% of the time, Pallas kernels for 38%

profile of v2, /device:TPU:0, one launch (start us, length us, event | category | flops | bytes accessed | tf_op | source)
XLA Modules:
  0.0 176.7 jit_solution(2130148653803653330)
XLA Ops:
  0.7 0.9 convert_element_type.3
  1.6 5.1 %collective-permute-start.2 = (bf16[256,128]{1,0:T(8,128)(2,1)S(1)}, bf16[256,128]{1,0:T(8,128)(2,1)S(1)}, u32[]{:S(2)}, u32[]{:S(2)}) collective-permute-start(bf16[256,128]{1,0:T(8,128)(2,1)S(1)} %bitcast.49), channel_id=1, source_target_pairs={{0,3},{1,0},{2,1},{3,2},{4,7},{5,4},{6,5},{7,6},{8,11},{9,8},{10,9... | collective-permute-start | bytes 196616 | tf_op jit(solution)/shard_map/ppermute | solution.py:716
  6.7 1.0 collective-permute-start
  7.7 0.7 pad_add_fusion.scal_ref
  8.4 1.3 copy-done
  9.7 0.7 copy-done.11
  10.4 2.6 %prep.1 = (bf16[5,256,512]{2,1,0:T(8,128)(2,1)S(1)}, bf16[96,128]{1,0:T(8,128)(2,1)S(1)}) custom-call(s32[7]{0:T(128)S(1)} %pad_add_fusion.scal_ref, bf16[5,256,512]{2,1,0:T(8,128)(2,1)S(1)} %copy-done, f32[4,512]{1,0:T(4,128)S(1)} %copy-done.11), custom_call_target="tpu_custom_call" | custom-call | flops 40000000 | bytes 2621440 | tf_op jit(solution)/shard_map/prep/pallas_call | solution.py:802
  13.2 1.6 collective-permute-start.3
  14.8 1.5 collective-permute-start.5
  16.8 6.2 %collective-permute-done.3.dep_ref.refs_1_ = bf16[1120,128]{1,0:T(8,128)(2,1)S(1)} collective-permute-done((bf16[1120,128]{1,0:T(8,128)(2,1)S(1)}, bf16[1120,128]{1,0:T(8,128)(2,1)S(1)}, u32[]{:S(2)}, u32[]{:S(2)}) %collective-permute-start.3) | collective-permute-done | bytes 286752 | tf_op jit(solution)/shard_map/ppermute | solution.py:720
  23.1 2.9 %collective-permute-start.12 = (bf16[256,128]{1,0:T(8,128)(2,1)S(1)}, bf16[256,128]{1,0:T(8,128)(2,1)S(1)}, u32[]{:S(2)}, u32[]{:S(2)}) collective-permute-start(bf16[256,128]{1,0:T(8,128)(2,1)S(1)} %get-tuple-element.98), channel_id=1, source_target_pairs={{0,3},{1,0},{2,1},{3,2},{4,7},{5,4},{6,5},{7,6},{8,11},{9,8},{10,9... | collective-permute-start | bytes 196616 | tf_op jit(solution)/shard_map/ppermute | solution.py:716
  26.2 6.0 %collective-permute-done.10 = bf16[256,128]{1,0:T(8,128)(2,1)S(1)} collective-permute-done((bf16[256,128]{1,0:T(8,128)(2,1)S(1)}, bf16[256,128]{1,0:T(8,128)(2,1)S(1)}, u32[]{:S(2)}, u32[]{:S(2)}) %collective-permute-start.10) | collective-permute-done | bytes 65568 | tf_op jit(solution)/shard_map/ppermute | solution.py:716
  32.6 5.1 %collective-permute-done.11 = bf16[256,128]{1,0:T(8,128)(2,1)S(1)} collective-permute-done((bf16[256,128]{1,0:T(8,128)(2,1)S(1)}, bf16[256,128]{1,0:T(8,128)(2,1)S(1)}, u32[]{:S(2)}, u32[]{:S(2)}) %collective-permute-start.11) | collective-permute-done | bytes 65568 | tf_op jit(solution)/shard_map/ppermute | solution.py:716
  37.7 1.0 collective-permute-start.15
  38.8 1.0 collective-permute-start.13
  39.8 5.1 %collective-permute-done.13 = bf16[256,128]{1,0:T(8,128)(2,1)S(1)} collective-permute-done((bf16[256,128]{1,0:T(8,128)(2,1)S(1)}, bf16[256,128]{1,0:T(8,128)(2,1)S(1)}, u32[]{:S(2)}, u32[]{:S(2)}) %collective-permute-start.13) | collective-permute-done | bytes 65568 | tf_op jit(solution)/shard_map/ppermute | solution.py:716
  45.5 4.6 %collective-permute-done.14 = bf16[256,128]{1,0:T(8,128)(2,1)S(1)} collective-permute-done((bf16[256,128]{1,0:T(8,128)(2,1)S(1)}, bf16[256,128]{1,0:T(8,128)(2,1)S(1)}, u32[]{:S(2)}, u32[]{:S(2)}) %collective-permute-start.14) | collective-permute-done | bytes 65568 | tf_op jit(solution)/shard_map/ppermute | solution.py:716
  50.7 2.5 %collective-permute-start.25 = (bf16[1024,128]{1,0:T(8,128)(2,1)S(1)}, bf16[1024,128]{1,0:T(8,128)(2,1)S(1)}, u32[]{:S(2)}, u32[]{:S(2)}) collective-permute-start(bf16[1024,128]{1,0:T(8,128)(2,1)S(1)} %bitcast.38), channel_id=1, source_target_pairs={{0,24},{4,28},{8,16},{12,20},{16,8},{20,12},{24,0},{28,4},{1,25},{... | collective-permute-start | bytes 786440 | tf_op jit(solution)/shard_map/ppermute | solution.py:720
  54.2 13.2 %forward.1 = (bf16[5,256,512]{2,1,0:T(8,128)(2,1)S(1)}, bf16[5,256,512]{2,1,0:T(8,128)(2,1)S(1)}, bf16[5,256,512]{2,1,0:T(8,128)(2,1)S(1)}, bf16[5,16,512]{2,1,0...) custom-call(s32[7]{0:T(128)S(1)} %pad_add_fusion.scal_ref, ...), custom_call_target="tpu_custom_call" | custom-call | flops 8000000000 | bytes 11796480 | tf_op jit(solution)/shard_map/forward/pallas_call | solution.py:841
  67.5 2.5 %collective-permute-start.18 = (bf16[1024,128]{1,0:T(8,128)(2,1)S(1)}, bf16[1024,128]{1,0:T(8,128)(2,1)S(1)}, u32[]{:S(2)}, u32[]{:S(2)}) collective-permute-start(bf16[1024,128]{1,0:T(8,128)(2,1)S(1)} %gate.1.refs_8_.refs_0_), channel_id=1, source_target_pairs={{0,24},{4,28},{8,16},{12,20},{16,8},{20,12},{24,0},{28,4},{1,25},{... | collective-permute-start | bytes 786440 | tf_op jit(solution)/shard_map/ppermute | solution.py:720
  71.5 6.2 %collective-permute-done.18.refs_3_ = bf16[1024,128]{1,0:T(8,128)(2,1)S(1)} collective-permute-done((bf16[1024,128]{1,0:T(8,128)(2,1)S(1)}, bf16[1024,128]{1,0:T(8,128)(2,1)S(1)}, u32[]{:S(2)}, u32[]{:S(2)}) %collective-permute-start.18) | collective-permute-done | bytes 262176 | tf_op jit(solution)/shard_map/ppermute | solution.py:720
  77.7 3.7 %collective-permute-done.17.refs_2_ = bf16[1024,128]{1,0:T(8,128)(2,1)S(1)} collective-permute-done((bf16[1024,128]{1,0:T(8,128)(2,1)S(1)}, bf16[1024,128]{1,0:T(8,128)(2,1)S(1)}, u32[]{:S(2)}, u32[]{:S(2)}) %collective-permute-start.17) | collective-permute-done | bytes 262176 | tf_op jit(solution)/shard_map/ppermute | solution.py:720
  82.5 11.6 %mlp.2 = (bf16[5,256,512]{2,1,0:T(8,128)(2,1)S(1)}, bf16[5,256,512]{2,1,0:T(8,128)(2,1)S(1)}, bf16[4,1024,128]{2,1,0:T(8,128)(2,1)S(1)}, bf16[4,1024,128]{2,1,0:T(8,128)(2,1)S(1)}) custom-call(s32[7]{0:T(128)S(1)} %pad_add_fusion.scal_ref, bf16[5,256,512]{2,1,0:T(8,128)(2,1)S(1)} %get-tuple-element.99.mid_ref, bf16[5,256,512]{2,1,0:T(8,128)(2,1)S(1)} %copy-done.15, ...), custom_call_target="tpu_custom_call" | custom-call | flops 8999999488 | bytes 13107200 | tf_op jit(solution)/shard_map/mlp/pallas_call | solution.py:894
  94.3 12.5 %mlp.3 = (bf16[5,256,512]{2,1,0:T(8,128)(2,1)}, bf16[5,256,512]{2,1,0:T(8,128)(2,1)S(1)}, bf16[4,1024,128]{2,1,0:T(8,128)(2,1)S(1)}, bf16[4,1024,128]{2,1,0:T(8,128)(2,1)S(1)}) custom-call(s32[7]{0:T(128)S(1)} %pad_add_fusion.scal_ref, bf16[5,256,512]{2,1,0:T(8,128)(2,1)S(1)} %get-tuple-element.99.mid_ref, bf16[5,256,512]{2,1,0:T(8,128)(2,1)S(1)} %copy-done.15, ...), custom_call_target="tpu_custom_call" | custom-call | flops 8999999488 | bytes 13107200 | tf_op jit(solution)/shard_map/mlp/pallas_call | solution.py:894
  107.2 4.6 %middle.1 = (bf16[5,256,512]{2,1,0:T(8,128)(2,1)S(1)}, bf16[5,256,512]{2,1,0:T(8,128)(2,1)S(1)}, f32[512,512]{1,0:T(8,128)S(1)}, f32[8,512]{1,0:T(8,128)S(1)}) custom-call(bf16[5,256,512]{2,1,0:T(8,128)(2,1)S(1)} %get-tuple-element.106.gm_ref, bf16[5,256,512]{2,1,0:T(8,128)(2,1)S(1)} %copy-done.15, ...), custom_call_target="tpu_custom_call" | custom-call | flops 3000000000 | bytes 9175040 | tf_op jit(solution)/shard_map/middle/pallas_call | solution.py:914
  111.8 1.0 halves.1
  112.9 1.6 collective-permute-start.32
  114.4 0.9 collective-permute-start.33
  115.3 11.8 %backward.1 = (bf16[5,256,1536]{2,1,0:T(8,128)(2,1)S(1)}, bf16[5,16,512]{2,1,0:T(8,128)(2,1)S(1)}, bf16[5,16,512]{2,1,0:T(8,128)(2,1)S(1)}, f32[2,4,48,128]{3,2,1,0:T(8,128)S(1)}) custom-call(s32[7]{0:T(128)S(1)} %pad_add_fusion.scal_ref, bf16[5,256,512]{2,1,0:T(8,128)(2,1)S(1)} %get-tuple-element.109.do_ref, ...), custom_call_target="tpu_custom_call" | custom-call | flops 14000000000 | bytes 15728640 | tf_op jit(solution)/shard_map/backward/pallas_call | solution.py:946
  127.1 0.9 collective-permute-done.33.refs_3_
  128.3 3.3 %grads.1 = (bf16[4,1072,128]{2,1,0:T(8,128)(2,1)S(1)}, bf16[4,1072,128]{2,1,0:T(8,128)(2,1)S(1)}) custom-call(s32[7]{0:T(128)S(1)} %pad_add_fusion.scal_ref, bf16[1280,512]{1,0:T(8,128)(2,1)S(1)} %bitcast.43, bf16[1280,1536]{1,0:T(8,128)(2,1)S(1)} %bitcast.44, bf16[80,512]{1,0:T(8,128)(2,1)S(1)} %bitcast.45, bf16[80,512]{1,0:T(8,128)(2,1)S(1)} %bitcast.46, ...), custom_call_target="tpu_custom_call" | custom-call | flops 5000000000 | bytes 10000000 | tf_op jit(solution)/shard_map/grads/pallas_call | solution.py:790
  131.6 0.9 collective-permute-start.41
  132.5 1.2 collective-permute-start.42
  134.3 0.8 spread.1
  135.1 0.6 collective-permute-start.35
  135.8 1.5 collective-permute-start.36
  137.2 1.4 collective-permute-start.37
  138.7 3.1 %project.1.refs_4_.grad_ref = bf16[5,256,512]{2,1,0:T(8,128)(2,1)S(1)} custom-call(bf16[5,256,1536]{2,1,0:T(8,128)(2,1)S(1)} %get-tuple-element.121.dqkv_ref, bf16[512,2048]{1,0:T(8,128)(2,1)S(1)} %get-tuple-element.108.w_ref, f32[1072,128]{1,0:T(8,128)S(1)} %get-tuple-element.134.dep_ref.refs_0_), custom_call_target="tpu_custom_call" | custom-call | flops 3000000000 | bytes 5242880 | tf_op jit(solution)/shard_map/project/pallas_call | solution.py:1009
  141.8 0.7 collect.3
  142.8 4.8 %collective-permute-done.35.refs_1_ = bf16[1072,128]{1,0:T(8,128)(2,1)S(1)} collective-permute-done((bf16[1072,128]{1,0:T(8,128)(2,1)S(1)}, bf16[1072,128]{1,0:T(8,128)(2,1)S(1)}, u32[]{:S(2)}, u32[]{:S(2)}) %collective-permute-start.35) | collective-permute-done | bytes 274464 | tf_op jit(solution)/shard_map/ppermute | solution.py:720
  147.6 5.6 %collective-permute-done.37.refs_3_ = bf16[1072,128]{1,0:T(8,128)(2,1)S(1)} collective-permute-done((bf16[1072,128]{1,0:T(8,128)(2,1)S(1)}, bf16[1072,128]{1,0:T(8,128)(2,1)S(1)}, u32[]{:S(2)}, u32[]{:S(2)}) %collective-permute-start.37) | collective-permute-done | bytes 274464 | tf_op jit(solution)/shard_map/ppermute | solution.py:720
  153.3 0.7 collect.2
  154.3 3.6 %collective-permute-start.40 = (bf16[256,128]{1,0:T(8,128)(2,1)S(1)}, bf16[256,128]{1,0:T(8,128)(2,1)S(1)}, u32[]{:S(2)}, u32[]{:S(2)}) collective-permute-start(bf16[256,128]{1,0:T(8,128)(2,1)S(1)} %get-tuple-element.144), channel_id=1, source_target_pairs={{0,3},{1,0},{2,1},{3,2},{4,7},{5,4},{6,5},{7,6},{8,11},{9,8},{10,9... | collective-permute-start | bytes 196616 | tf_op jit(solution)/shard_map/ppermute | solution.py:716
  157.9 1.1 mlp_step.1
  159.0 4.3 %input.1 = (f32[5,256,512]{2,1,0:T(8,128)}, f32[8,512]{1,0:T(8,128)S(1)}) custom-call(s32[7]{0:T(128)S(1)} %pad_add_fusion.scal_ref, bf16[5,256,512]{2,1,0:T(8,128)(2,1)S(1)} %project.1.refs_4_.grad_ref, bf16[5,256,512]{2,1,0:T(8,128)(2,1)S(1)} %get-tuple-element.135.gx2_ref, bf16[5,256,512]{2,1,0:T(8,128)(2,1)S(1)} %copy-done.1, ...), custom_call_target="tpu_custom_call" | custom-call | flops 100000000 | bytes 6553600 | tf_op jit(solution)/shard_map/input/pallas_call | solution.py:1033
  163.4 0.8 attn_step.1
  164.2 11.5 %all_to_all.5.every_ref = bf16[32,16,128]{2,1,0:T(8,128)(2,1)S(1)} all-to-all(bf16[32,16,128]{2,1,0:T(8,128)(2,1)S(1)} %get-tuple-element.156), channel_id=1, replica_groups=mesh['blk'=8,'group'=4] {'blk','group'}, dimensions={0} | all-to-all | bytes 262144 | tf_op jit(solution)/shard_map/all_to_all | solution.py:1066
  175.7 0.9 final.1
  (114 shorter events, 8.5 us)
Async XLA Ops:
  1.6 11.6 %collective-permute-start.2 = (bf16[256,128]{1,0:T(8,128)(2,1)S(1)}, bf16[256,128]{1,0:T(8,128)(2,1)S(1)}, u32[]{:S(2)}, u32[]{:S(2)}) collective-permute-start(bf16[256,128]{1,0:T(8,128)(2,1)S(1)} %bitcast.49), channel_id=1, source_target_pairs={{0,3},{1,0},{2,1},{3,2},{4,7},{5,4},{6,5},{7,6},{8,11},{9,8},{10,9... | collective-permute-start | bytes 196616 | tf_op jit(solution)/shard_map/ppermute | solution.py:716
  6.7 6.5 %collective-permute-start.1 = (bf16[256,128]{1,0:T(8,128)(2,1)S(1)}, bf16[256,128]{1,0:T(8,128)(2,1)S(1)}, u32[]{:S(2)}, u32[]{:S(2)}) collective-permute-start(bf16[256,128]{1,0:T(8,128)(2,1)S(1)} %bitcast.50), channel_id=1, source_target_pairs={{0,2},{1,3},{2,0},{3,1},{4,6},{5,7},{6,4},{7,5},{8,10},{9,11},{10,... | collective-permute-start | bytes 196616 | tf_op jit(solution)/shard_map/ppermute | solution.py:716
  6.7 6.4 %collective-permute-start = (bf16[256,128]{1,0:T(8,128)(2,1)S(1)}, bf16[256,128]{1,0:T(8,128)(2,1)S(1)}, u32[]{:S(2)}, u32[]{:S(2)}) collective-permute-start(bf16[256,128]{1,0:T(8,128)(2,1)S(1)} %bitcast.51), channel_id=1, source_target_pairs={{0,1},{1,2},{2,3},{3,0},{4,5},{5,6},{6,7},{7,4},{8,9},{9,10},{10,1... | collective-permute-start | bytes 196616 | tf_op jit(solution)/shard_map/ppermute | solution.py:716
  13.2 41.0 %copy-start.1 = (bf16[5,256,512]{2,1,0:T(8,128)(2,1)S(1)}, bf16[5,256,512]{2,1,0:T(8,128)(2,1)}, u32[]{:S(2)}) copy-start(bf16[5,256,512]{2,1,0:T(8,128)(2,1)} %x_ref.5) | copy-start | bytes 3932164
  13.2 9.8 %collective-permute-start.3 = (bf16[1120,128]{1,0:T(8,128)(2,1)S(1)}, bf16[1120,128]{1,0:T(8,128)(2,1)S(1)}, u32[]{:S(2)}, u32[]{:S(2)}) collective-permute-start(bf16[1120,128]{1,0:T(8,128)(2,1)S(1)} %pad_maximum_fusion.refs_0_), channel_id=1, source_target_pairs={{0,8},{4,12},{8,0},{12,4},{16,24},{20,28},{24,16},{28,20},{1,9},{5... | collective-permute-start | bytes 860168 | tf_op jit(solution)/shard_map/ppermute | solution.py:720
  14.8 35.9 %collective-permute-start.6 = (bf16[1120,128]{1,0:T(8,128)(2,1)S(1)}, bf16[1120,128]{1,0:T(8,128)(2,1)S(1)}, u32[]{:S(2)}, u32[]{:S(2)}) collective-permute-start(bf16[1120,128]{1,0:T(8,128)(2,1)S(1)} %pad_maximum_fusion.refs_0_), channel_id=1, source_target_pairs={{0,4},{4,0},{8,12},{12,8},{16,20},{20,16},{24,28},{28,24},{1,5},{5... | collective-permute-start | bytes 860168 | tf_op jit(solution)/shard_map/ppermute | solution.py:720
  14.8 30.1 %collective-permute-start.5 = (bf16[1120,128]{1,0:T(8,128)(2,1)S(1)}, bf16[1120,128]{1,0:T(8,128)(2,1)S(1)}, u32[]{:S(2)}, u32[]{:S(2)}) collective-permute-start(bf16[1120,128]{1,0:T(8,128)(2,1)S(1)} %pad_maximum_fusion.refs_0_), channel_id=1, source_target_pairs={{0,24},{4,28},{8,16},{12,20},{16,8},{20,12},{24,0},{28,4},{1,25},{... | collective-permute-start | bytes 860168 | tf_op jit(solution)/shard_map/ppermute | solution.py:720
  16.3 28.7 %collective-permute-start.4 = (bf16[1120,128]{1,0:T(8,128)(2,1)S(1)}, bf16[1120,128]{1,0:T(8,128)(2,1)S(1)}, u32[]{:S(2)}, u32[]{:S(2)}) collective-permute-start(bf16[1120,128]{1,0:T(8,128)(2,1)S(1)} %pad_maximum_fusion.refs_0_), channel_id=1, source_target_pairs={{0,16},{4,20},{8,24},{12,28},{16,0},{20,4},{24,8},{28,12},{1,17},{... | collective-permute-start | bytes 860168 | tf_op jit(solution)/shard_map/ppermute | solution.py:720
  23.1 15.6 %collective-permute-start.12 = (bf16[256,128]{1,0:T(8,128)(2,1)S(1)}, bf16[256,128]{1,0:T(8,128)(2,1)S(1)}, u32[]{:S(2)}, u32[]{:S(2)}) collective-permute-start(bf16[256,128]{1,0:T(8,128)(2,1)S(1)} %get-tuple-element.98), channel_id=1, source_target_pairs={{0,3},{1,0},{2,1},{3,2},{4,7},{5,4},{6,5},{7,6},{8,11},{9,8},{10,9... | collective-permute-start | bytes 196616 | tf_op jit(solution)/shard_map/ppermute | solution.py:716
  26.0 6.1 %collective-permute-start.10 = (bf16[256,128]{1,0:T(8,128)(2,1)S(1)}, bf16[256,128]{1,0:T(8,128)(2,1)S(1)}, u32[]{:S(2)}, u32[]{:S(2)}) collective-permute-start(bf16[256,128]{1,0:T(8,128)(2,1)S(1)} %get-tuple-element.98), channel_id=1, source_target_pairs={{0,1},{1,2},{2,3},{3,0},{4,5},{5,6},{6,7},{7,4},{8,9},{9,10},{10,1... | collective-permute-start | bytes 196616 | tf_op jit(solution)/shard_map/ppermute | solution.py:716
  32.2 5.5 %collective-permute-start.11 = (bf16[256,128]{1,0:T(8,128)(2,1)S(1)}, bf16[256,128]{1,0:T(8,128)(2,1)S(1)}, u32[]{:S(2)}, u32[]{:S(2)}) collective-permute-start(bf16[256,128]{1,0:T(8,128)(2,1)S(1)} %get-tuple-element.98), channel_id=1, source_target_pairs={{0,2},{1,3},{2,0},{3,1},{4,6},{5,7},{6,4},{7,5},{8,10},{9,11},{10,... | collective-permute-start | bytes 196616 | tf_op jit(solution)/shard_map/ppermute | solution.py:716
  37.7 12.4 %collective-permute-start.15 = (bf16[256,128]{1,0:T(8,128)(2,1)S(1)}, bf16[256,128]{1,0:T(8,128)(2,1)S(1)}, u32[]{:S(2)}, u32[]{:S(2)}) collective-permute-start(bf16[256,128]{1,0:T(8,128)(2,1)S(1)} %get-tuple-element.100), channel_id=1, source_target_pairs={{0,3},{1,0},{2,1},{3,2},{4,7},{5,4},{6,5},{7,6},{8,11},{9,8},{10,9... | collective-permute-start | bytes 196616 | tf_op jit(solution)/shard_map/ppermute | solution.py:716
  38.8 6.1 %collective-permute-start.13 = (bf16[256,128]{1,0:T(8,128)(2,1)S(1)}, bf16[256,128]{1,0:T(8,128)(2,1)S(1)}, u32[]{:S(2)}, u32[]{:S(2)}) collective-permute-start(bf16[256,128]{1,0:T(8,128)(2,1)S(1)} %get-tuple-element.100), channel_id=1, source_target_pairs={{0,1},{1,2},{2,3},{3,0},{4,5},{5,6},{6,7},{7,4},{8,9},{9,10},{10,1... | collective-permute-start | bytes 196616 | tf_op jit(solution)/shard_map/ppermute | solution.py:716
  44.9 5.2 %collective-permute-start.14 = (bf16[256,128]{1,0:T(8,128)(2,1)S(1)}, bf16[256,128]{1,0:T(8,128)(2,1)S(1)}, u32[]{:S(2)}, u32[]{:S(2)}) collective-permute-start(bf16[256,128]{1,0:T(8,128)(2,1)S(1)} %get-tuple-element.100), channel_id=1, source_target_pairs={{0,2},{1,3},{2,0},{3,1},{4,6},{5,7},{6,4},{7,5},{8,10},{9,11},{10,... | collective-permute-start | bytes 196616 | tf_op jit(solution)/shard_map/ppermute | solution.py:716
  44.9 9.3 %collective-permute-start.7 = (bf16[1120,128]{1,0:T(8,128)(2,1)S(1)}, bf16[1120,128]{1,0:T(8,128)(2,1)S(1)}, u32[]{:S(2)}, u32[]{:S(2)}) collective-permute-start(bf16[1120,128]{1,0:T(8,128)(2,1)S(1)} %collective-permute-done.3.dep_ref.refs_1_), channel_id=1, source_target_pairs={{0,4},{4,0},{8,12},{12,8},{16,20},{20,16},{24,28},{28,24},{1,5},{5... | collective-permute-start | bytes 860168 | tf_op jit(solution)/shard_map/ppermute | solution.py:720
  45.0 8.2 %collective-permute-start.9 = (bf16[1120,128]{1,0:T(8,128)(2,1)S(1)}, bf16[1120,128]{1,0:T(8,128)(2,1)S(1)}, u32[]{:S(2)}, u32[]{:S(2)}) collective-permute-start(bf16[1120,128]{1,0:T(8,128)(2,1)S(1)} %collective-permute-done.5.refs_3_), channel_id=1, source_target_pairs={{0,4},{4,0},{8,12},{12,8},{16,20},{20,16},{24,28},{28,24},{1,5},{5... | collective-permute-start | bytes 860168 | tf_op jit(solution)/shard_map/ppermute | solution.py:720
  50.1 3.6 %collective-permute-start.8 = (bf16[1120,128]{1,0:T(8,128)(2,1)S(1)}, bf16[1120,128]{1,0:T(8,128)(2,1)S(1)}, u32[]{:S(2)}, u32[]{:S(2)}) collective-permute-start(bf16[1120,128]{1,0:T(8,128)(2,1)S(1)} %collective-permute-done.4.refs_2_), channel_id=1, source_target_pairs={{0,4},{4,0},{8,12},{12,8},{16,20},{20,16},{24,28},{28,24},{1,5},{5... | collective-permute-start | bytes 860168 | tf_op jit(solution)/shard_map/ppermute | solution.py:720
  50.1 19.9 %collective-permute-start.26 = (bf16[1024,128]{1,0:T(8,128)(2,1)S(1)}, bf16[1024,128]{1,0:T(8,128)(2,1)S(1)}, u32[]{:S(2)}, u32[]{:S(2)}) collective-permute-start(bf16[1024,128]{1,0:T(8,128)(2,1)S(1)} %bitcast.37), channel_id=1, source_target_pairs={{0,4},{4,0},{8,12},{12,8},{16,20},{20,16},{24,28},{28,24},{1,5},{5... | collective-permute-start | bytes 786440 | tf_op jit(solution)/shard_map/ppermute | solution.py:720
  50.7 19.8 %collective-permute-start.25 = (bf16[1024,128]{1,0:T(8,128)(2,1)S(1)}, bf16[1024,128]{1,0:T(8,128)(2,1)S(1)}, u32[]{:S(2)}, u32[]{:S(2)}) collective-permute-start(bf16[1024,128]{1,0:T(8,128)(2,1)S(1)} %bitcast.38), channel_id=1, source_target_pairs={{0,24},{4,28},{8,16},{12,20},{16,8},{20,12},{24,0},{28,4},{1,25},{... | collective-permute-start | bytes 786440 | tf_op jit(solution)/shard_map/ppermute | solution.py:720
  53.2 17.8 %collective-permute-start.24 = (bf16[1024,128]{1,0:T(8,128)(2,1)S(1)}, bf16[1024,128]{1,0:T(8,128)(2,1)S(1)}, u32[]{:S(2)}, u32[]{:S(2)}) collective-permute-start(bf16[1024,128]{1,0:T(8,128)(2,1)S(1)} %bitcast.39), channel_id=1, source_target_pairs={{0,16},{4,20},{8,24},{12,28},{16,0},{20,4},{24,8},{28,12},{1,17},{... | collective-permute-start | bytes 786440 | tf_op jit(solution)/shard_map/ppermute | solution.py:720
  53.7 17.3 %collective-permute-start.23 = (bf16[1024,128]{1,0:T(8,128)(2,1)S(1)}, bf16[1024,128]{1,0:T(8,128)(2,1)S(1)}, u32[]{:S(2)}, u32[]{:S(2)}) collective-permute-start(bf16[1024,128]{1,0:T(8,128)(2,1)S(1)} %bitcast.40), channel_id=1, source_target_pairs={{0,8},{4,12},{8,0},{12,4},{16,24},{20,28},{24,16},{28,20},{1,9},{5... | collective-permute-start | bytes 786440 | tf_op jit(solution)/shard_map/ppermute | solution.py:720
  54.2 28.2 %copy-start.15 = (bf16[5,256,512]{2,1,0:T(8,128)(2,1)S(1)}, bf16[5,256,512]{2,1,0:T(8,128)(2,1)}, u32[]{:S(2)}) copy-start(bf16[5,256,512]{2,1,0:T(8,128)(2,1)} %g_ref.5) | copy-start | bytes 3932164
  67.5 10.3 %collective-permute-start.18 = (bf16[1024,128]{1,0:T(8,128)(2,1)S(1)}, bf16[1024,128]{1,0:T(8,128)(2,1)S(1)}, u32[]{:S(2)}, u32[]{:S(2)}) collective-permute-start(bf16[1024,128]{1,0:T(8,128)(2,1)S(1)} %gate.1.refs_8_.refs_0_), channel_id=1, source_target_pairs={{0,24},{4,28},{8,16},{12,20},{16,8},{20,12},{24,0},{28,4},{1,25},{... | collective-permute-start | bytes 786440 | tf_op jit(solution)/shard_map/ppermute | solution.py:720
  70.0 11.5 %collective-permute-start.17 = (bf16[1024,128]{1,0:T(8,128)(2,1)S(1)}, bf16[1024,128]{1,0:T(8,128)(2,1)S(1)}, u32[]{:S(2)}, u32[]{:S(2)}) collective-permute-start(bf16[1024,128]{1,0:T(8,128)(2,1)S(1)} %gate.1.refs_8_.refs_0_), channel_id=1, source_target_pairs={{0,16},{4,20},{8,24},{12,28},{16,0},{20,4},{24,8},{28,12},{1,17},{... | collective-permute-start | bytes 786440 | tf_op jit(solution)/shard_map/ppermute | solution.py:720
  70.5 11.0 %collective-permute-start.16 = (bf16[1024,128]{1,0:T(8,128)(2,1)S(1)}, bf16[1024,128]{1,0:T(8,128)(2,1)S(1)}, u32[]{:S(2)}, u32[]{:S(2)}) collective-permute-start(bf16[1024,128]{1,0:T(8,128)(2,1)S(1)} %gate.1.refs_8_.refs_0_), channel_id=1, source_target_pairs={{0,8},{4,12},{8,0},{12,4},{16,24},{20,28},{24,16},{28,20},{1,9},{5... | collective-permute-start | bytes 786440 | tf_op jit(solution)/shard_map/ppermute | solution.py:720
  71.0 10.9 %collective-permute-start.29 = (bf16[1024,128]{1,0:T(8,128)(2,1)S(1)}, bf16[1024,128]{1,0:T(8,128)(2,1)S(1)}, u32[]{:S(2)}, u32[]{:S(2)}) collective-permute-start(bf16[1024,128]{1,0:T(8,128)(2,1)S(1)} %collective-permute-done.25.refs_3_), channel_id=1, source_target_pairs={{0,4},{4,0},{8,12},{12,8},{16,20},{20,16},{24,28},{28,24},{1,5},{5... | collective-permute-start | bytes 786440 | tf_op jit(solution)/shard_map/ppermute | solution.py:720
  71.0 11.0 %collective-permute-start.28 = (bf16[1024,128]{1,0:T(8,128)(2,1)S(1)}, bf16[1024,128]{1,0:T(8,128)(2,1)S(1)}, u32[]{:S(2)}, u32[]{:S(2)}) collective-permute-start(bf16[1024,128]{1,0:T(8,128)(2,1)S(1)} %collective-permute-done.24.refs_2_), channel_id=1, source_target_pairs={{0,4},{4,0},{8,12},{12,8},{16,20},{20,16},{24,28},{28,24},{1,5},{5... | collective-permute-start | bytes 786440 | tf_op jit(solution)/shard_map/ppermute | solution.py:720
  77.7 4.8 %collective-permute-start.27 = (bf16[1024,128]{1,0:T(8,128)(2,1)S(1)}, bf16[1024,128]{1,0:T(8,128)(2,1)S(1)}, u32[]{:S(2)}, u32[]{:S(2)}) collective-permute-start(bf16[1024,128]{1,0:T(8,128)(2,1)S(1)} %collective-permute-done.23.refs_1_), channel_id=1, source_target_pairs={{0,4},{4,0},{8,12},{12,8},{16,20},{20,16},{24,28},{28,24},{1,5},{5... | collective-permute-start | bytes 786440 | tf_op jit(solution)/shard_map/ppermute | solution.py:720
  81.4 12.9 %collective-permute-start.19 = (bf16[1024,128]{1,0:T(8,128)(2,1)S(1)}, bf16[1024,128]{1,0:T(8,128)(2,1)S(1)}, u32[]{:S(2)}, u32[]{:S(2)}) collective-permute-start(bf16[1024,128]{1,0:T(8,128)(2,1)S(1)} %gate.1.refs_8_.refs_0_), channel_id=1, source_target_pairs={{0,4},{4,0},{8,12},{12,8},{16,20},{20,16},{24,28},{28,24},{1,5},{5... | collective-permute-start | bytes 786440 | tf_op jit(solution)/shard_map/ppermute | solution.py:720
  81.5 12.8 %collective-permute-start.22 = (bf16[1024,128]{1,0:T(8,128)(2,1)S(1)}, bf16[1024,128]{1,0:T(8,128)(2,1)S(1)}, u32[]{:S(2)}, u32[]{:S(2)}) collective-permute-start(bf16[1024,128]{1,0:T(8,128)(2,1)S(1)} %collective-permute-done.18.refs_3_), channel_id=1, source_target_pairs={{0,4},{4,0},{8,12},{12,8},{16,20},{20,16},{24,28},{28,24},{1,5},{5... | collective-permute-start | bytes 786440 | tf_op jit(solution)/shard_map/ppermute | solution.py:720
  82.0 12.3 %collective-permute-start.21 = (bf16[1024,128]{1,0:T(8,128)(2,1)S(1)}, bf16[1024,128]{1,0:T(8,128)(2,1)S(1)}, u32[]{:S(2)}, u32[]{:S(2)}) collective-permute-start(bf16[1024,128]{1,0:T(8,128)(2,1)S(1)} %collective-permute-done.17.refs_2_), channel_id=1, source_target_pairs={{0,4},{4,0},{8,12},{12,8},{16,20},{20,16},{24,28},{28,24},{1,5},{5... | collective-permute-start | bytes 786440 | tf_op jit(solution)/shard_map/ppermute | solution.py:720
  82.0 12.3 %collective-permute-start.20 = (bf16[1024,128]{1,0:T(8,128)(2,1)S(1)}, bf16[1024,128]{1,0:T(8,128)(2,1)S(1)}, u32[]{:S(2)}, u32[]{:S(2)}) collective-permute-start(bf16[1024,128]{1,0:T(8,128)(2,1)S(1)} %collective-permute-done.16.refs_1_), channel_id=1, source_target_pairs={{0,4},{4,0},{8,12},{12,8},{16,20},{20,16},{24,28},{28,24},{1,5},{5... | collective-permute-start | bytes 786440 | tf_op jit(solution)/shard_map/ppermute | solution.py:720
  94.1 17.7 %collective-permute-start.30 = (bf16[4,1024,128]{2,1,0:T(8,128)(2,1)S(1)}, bf16[4,1024,128]{2,1,0:T(8,128)(2,1)S(1)}, u32[]{:S(2)}, u32[]{:S(2)}) collective-permute-start(bf16[4,1024,128]{2,1,0:T(8,128)(2,1)S(1)} %get-tuple-element.118), channel_id=1, source_target_pairs={{0,4},{4,0},{8,12},{12,8},{16,20},{20,16},{24,28},{28,24},{1,5},{5... | collective-permute-start | bytes 3145736 | tf_op jit(solution)/shard_map/ppermute | solution.py:720
  106.8 5.0 %collective-permute-start.31 = (bf16[4,1024,128]{2,1,0:T(8,128)(2,1)S(1)}, bf16[4,1024,128]{2,1,0:T(8,128)(2,1)S(1)}, u32[]{:S(2)}, u32[]{:S(2)}) collective-permute-start(bf16[4,1024,128]{2,1,0:T(8,128)(2,1)S(1)} %get-tuple-element.119), channel_id=1, source_target_pairs={{0,4},{4,0},{8,12},{12,8},{16,20},{20,16},{24,28},{28,24},{1,5},{5... | collective-permute-start | bytes 3145736 | tf_op jit(solution)/shard_map/ppermute | solution.py:720
  112.9 14.3 %collective-permute-start.32 = (bf16[2,1024,128]{2,1,0:T(8,128)(2,1)S(1)}, bf16[2,1024,128]{2,1,0:T(8,128)(2,1)S(1)}, u32[]{:S(2)}, u32[]{:S(2)}) collective-permute-start(bf16[2,1024,128]{2,1,0:T(8,128)(2,1)S(1)} %get-tuple-element.128), channel_id=1, source_target_pairs={{0,8},{4,12},{8,0},{12,4},{16,24},{20,28},{24,16},{28,20},{1,9},{5... | collective-permute-start | bytes 1572872 | tf_op jit(solution)/shard_map/ppermute | solution.py:720
  114.4 13.6 %collective-permute-start.33 = (bf16[2,1024,128]{2,1,0:T(8,128)(2,1)S(1)}, bf16[2,1024,128]{2,1,0:T(8,128)(2,1)S(1)}, u32[]{:S(2)}, u32[]{:S(2)}) collective-permute-start(bf16[2,1024,128]{2,1,0:T(8,128)(2,1)S(1)} %get-tuple-element.130), channel_id=1, source_target_pairs={{0,16},{4,20},{8,24},{12,28},{16,0},{20,4},{24,8},{28,12},{1,17},{... | collective-permute-start | bytes 1572872 | tf_op jit(solution)/shard_map/ppermute | solution.py:720
  131.5 2.8 %collective-permute-start.34 = (bf16[4,1072,128]{2,1,0:T(8,128)(2,1)S(1)}, bf16[4,1072,128]{2,1,0:T(8,128)(2,1)S(1)}, u32[]{:S(2)}, u32[]{:S(2)}) collective-permute-start(bf16[4,1072,128]{2,1,0:T(8,128)(2,1)S(1)} %get-tuple-element.133), channel_id=1, source_target_pairs={{0,4},{4,0},{8,12},{12,8},{16,20},{20,16},{24,28},{28,24},{1,5},{5... | collective-permute-start | bytes 3293192 | tf_op jit(solution)/shard_map/ppermute | solution.py:720
  131.6 10.1 %collective-permute-start.41 = (bf16[1024,128]{1,0:T(8,128)(2,1)S(1)}, bf16[1024,128]{1,0:T(8,128)(2,1)S(1)}, u32[]{:S(2)}, u32[]{:S(2)}) collective-permute-start(bf16[1024,128]{1,0:T(8,128)(2,1)S(1)} %get-tuple-element.145), channel_id=1, source_target_pairs={{0,16},{4,20},{8,24},{12,28},{16,0},{20,4},{24,8},{28,12},{1,17},{... | collective-permute-start | bytes 786440 | tf_op jit(solution)/shard_map/ppermute | solution.py:720
  132.5 9.2 %collective-permute-start.42 = (bf16[1024,128]{1,0:T(8,128)(2,1)S(1)}, bf16[1024,128]{1,0:T(8,128)(2,1)S(1)}, u32[]{:S(2)}, u32[]{:S(2)}) collective-permute-start(bf16[1024,128]{1,0:T(8,128)(2,1)S(1)} %get-tuple-element.147), channel_id=1, source_target_pairs={{0,8},{4,12},{8,0},{12,4},{16,24},{20,28},{24,16},{28,20},{1,9},{5... | collective-permute-start | bytes 786440 | tf_op jit(solution)/shard_map/ppermute | solution.py:720
  135.1 12.4 %collective-permute-start.35 = (bf16[1072,128]{1,0:T(8,128)(2,1)S(1)}, bf16[1072,128]{1,0:T(8,128)(2,1)S(1)}, u32[]{:S(2)}, u32[]{:S(2)}) collective-permute-start(bf16[1072,128]{1,0:T(8,128)(2,1)S(1)} %get-tuple-element.136), channel_id=1, source_target_pairs={{0,8},{4,12},{8,0},{12,4},{16,24},{20,28},{24,16},{28,20},{1,9},{5... | collective-permute-start | bytes 823304 | tf_op jit(solution)/shard_map/ppermute | solution.py:720
  135.8 11.9 %collective-permute-start.36 = (bf16[1072,128]{1,0:T(8,128)(2,1)S(1)}, bf16[1072,128]{1,0:T(8,128)(2,1)S(1)}, u32[]{:S(2)}, u32[]{:S(2)}) collective-permute-start(bf16[1072,128]{1,0:T(8,128)(2,1)S(1)} %get-tuple-element.137), channel_id=1, source_target_pairs={{0,16},{4,20},{8,24},{12,28},{16,0},{20,4},{24,8},{28,12},{1,17},{... | collective-permute-start | bytes 823304 | tf_op jit(solution)/shard_map/ppermute | solution.py:720
  137.2 16.0 %collective-permute-start.37 = (bf16[1072,128]{1,0:T(8,128)(2,1)S(1)}, bf16[1072,128]{1,0:T(8,128)(2,1)S(1)}, u32[]{:S(2)}, u32[]{:S(2)}) collective-permute-start(bf16[1072,128]{1,0:T(8,128)(2,1)S(1)} %get-tuple-element.138), channel_id=1, source_target_pairs={{0,24},{4,28},{8,16},{12,20},{16,8},{20,12},{24,0},{28,4},{1,25},{... | collective-permute-start | bytes 823304 | tf_op jit(solution)/shard_map/ppermute | solution.py:720
  142.4 11.8 %collective-permute-start.43 = (bf16[512,128]{1,0:T(8,128)(2,1)S(1)}, bf16[512,128]{1,0:T(8,128)(2,1)S(1)}, u32[]{:S(2)}, u32[]{:S(2)}) collective-permute-start(bf16[512,128]{1,0:T(8,128)(2,1)S(1)} %get-tuple-element.149), channel_id=1, source_target_pairs={{0,1},{1,2},{2,3},{3,0},{4,5},{5,6},{6,7},{7,4},{8,9},{9,10},{10,1... | collective-permute-start | bytes 393224 | tf_op jit(solution)/shard_map/ppermute | solution.py:716
  142.5 15.3 %collective-permute-start.44 = (bf16[512,128]{1,0:T(8,128)(2,1)S(1)}, bf16[512,128]{1,0:T(8,128)(2,1)S(1)}, u32[]{:S(2)}, u32[]{:S(2)}) collective-permute-start(bf16[512,128]{1,0:T(8,128)(2,1)S(1)} %get-tuple-element.150), channel_id=1, source_target_pairs={{0,2},{1,3},{2,0},{3,1},{4,6},{5,7},{6,4},{7,5},{8,10},{9,11},{10,... | collective-permute-start | bytes 393224 | tf_op jit(solution)/shard_map/ppermute | solution.py:716
  147.6 10.3 %collective-permute-start.45 = (bf16[512,128]{1,0:T(8,128)(2,1)S(1)}, bf16[512,128]{1,0:T(8,128)(2,1)S(1)}, u32[]{:S(2)}, u32[]{:S(2)}) collective-permute-start(bf16[512,128]{1,0:T(8,128)(2,1)S(1)} %get-tuple-element.151), channel_id=1, source_target_pairs={{0,3},{1,0},{2,1},{3,2},{4,7},{5,4},{6,5},{7,6},{8,11},{9,8},{10,9... | collective-permute-start | bytes 393224 | tf_op jit(solution)/shard_map/ppermute | solution.py:716
  154.0 9.4 %collective-permute-start.38 = (bf16[256,128]{1,0:T(8,128)(2,1)S(1)}, bf16[256,128]{1,0:T(8,128)(2,1)S(1)}, u32[]{:S(2)}, u32[]{:S(2)}) collective-permute-start(bf16[256,128]{1,0:T(8,128)(2,1)S(1)} %get-tuple-element.142), channel_id=1, source_target_pairs={{0,1},{1,2},{2,3},{3,0},{4,5},{5,6},{6,7},{7,4},{8,9},{9,10},{10,1... | collective-permute-start | bytes 196616 | tf_op jit(solution)/shard_map/ppermute | solution.py:716
  154.0 9.3 %collective-permute-start.39 = (bf16[256,128]{1,0:T(8,128)(2,1)S(1)}, bf16[256,128]{1,0:T(8,128)(2,1)S(1)}, u32[]{:S(2)}, u32[]{:S(2)}) collective-permute-start(bf16[256,128]{1,0:T(8,128)(2,1)S(1)} %get-tuple-element.143), channel_id=1, source_target_pairs={{0,2},{1,3},{2,0},{3,1},{4,6},{5,7},{6,4},{7,5},{8,10},{9,11},{10,... | collective-permute-start | bytes 196616 | tf_op jit(solution)/shard_map/ppermute | solution.py:716
  154.3 9.1 %collective-permute-start.40 = (bf16[256,128]{1,0:T(8,128)(2,1)S(1)}, bf16[256,128]{1,0:T(8,128)(2,1)S(1)}, u32[]{:S(2)}, u32[]{:S(2)}) collective-permute-start(bf16[256,128]{1,0:T(8,128)(2,1)S(1)} %get-tuple-element.144), channel_id=1, source_target_pairs={{0,3},{1,0},{2,1},{3,2},{4,7},{5,4},{6,5},{7,6},{8,11},{9,8},{10,9... | collective-permute-start | bytes 196616 | tf_op jit(solution)/shard_map/ppermute | solution.py:716
  (14 other events, 127.9 us)

commit v3 on v2

--- a/solution.py
+++ b/solution.py
@@ -11,6 +11,8 @@
 SPAN = 128
 STEP = 5
 CHUNKS = 2
+ROW_STEPS = 5
+BATCH = 4
 
 masked_value = -1e30
 decay_rate = 0.5
@@ -105,8 +107,8 @@
             place = move if spot is None else spot ^ move
             here = block((place * 2 + c) * rows, rows)
             for g in range(groups):
-                for m in range(4):
-                    at = (g * 4 + m) * rows
+                for m in range(3):
+                    at = (g * 3 + m) * rows
                     w_ref[here, m * width + g * cols : m * width + (g + 1) * cols] = buf_ref[
                         at : at + rows, :
                     ]
@@ -148,13 +150,17 @@
         rider_ref[half:] = (every - high.astype(f32)).astype(b16)
 
 
-def pack_kernel(dims, up_ref, down_ref, dep_ref, *out_refs):
+def pack_kernel(dims, in_ref, up_ref, down_ref, dep_ref, out_ref):
     rows, cols, sub, lanes = dims
-    for j, out_ref in enumerate(out_refs):
+    out_ref[:rows, :] = in_ref[0].astype(b16)
+    at = rows
+    for j in range(CHUNKS):
         for h in range(sub):
             c0 = (h * CHUNKS + j) * lanes
-            out_ref[h * rows : (h + 1) * rows, :] = up_ref[:, c0 : c0 + lanes].astype(b16)
-        out_ref[sub * rows :, :] = down_ref[j * lanes : (j + 1) * lanes, :].T.astype(b16)
+            out_ref[at : at + rows, :] = up_ref[:, c0 : c0 + lanes].astype(b16)
+            at += rows
+        out_ref[at : at + cols, :] = down_ref[j * lanes : (j + 1) * lanes, :].T.astype(b16)
+        at += cols
 
 
 def heads_apart(values):
@@ -179,11 +185,12 @@
     return jnp.concatenate([both[:half, :SPAN], both[half:, SPAN:]], 0)
 
 
-def gate_kernel(in_ref, dep_ref, out_ref):
-    out_ref[...] = in_ref[...]
-
-
-def forward_kernel(dims, fast, places, scal_ref, normed_ref, x_ref, *refs):
+def gate_kernel(count, *refs):
+    for in_ref, out_ref in zip(refs[:count], refs[-count:]):
+        out_ref[...] = in_ref[...]
+
+
+def forward_kernel(dims, fast, places, scal_ref, normed_ref, *refs):
     own_refs, refs = refs[:places], refs[places:]
     other_refs, refs = refs[:places], refs[places:]
     if fast:
@@ -191,8 +198,8 @@
     else:
         rown_refs, refs = refs[:places], refs[places:]
         rother_refs, refs = refs[:places], refs[places:]
-    (ln_ref, dep_ref, q_ref, k_ref, v_ref, ks_ref, vs_ref, nsum_ref, lse_ref, mixed_ref, x2_ref,
-     mid_ref, w_ref, token_ref, sums_ref, line_ref) = refs
+    (dep_ref, q_ref, k_ref, v_ref, ks_ref, vs_ref, nsum_ref, lse_ref, mixed_ref,
+     w_ref, token_ref, sums_ref, line_ref) = refs
     i = pl.program_id(0)
     groups, rows, cols, width = dims
     tok = normed_ref.shape[1]
@@ -201,7 +208,7 @@
     amount = ks_ref.shape[1]
     factor = (width // HEADS) ** (-0.5)
     half = sums_ref.shape[2]
-    base = groups * 4 * rows if fast else 0
+    base = groups * 3 * rows if fast else 0
 
     @pl.when(i == 0)
     def _():
@@ -241,68 +248,109 @@
     for span in range(spans):
         part = slice(span * SPAN, (span + 1) * SPAN)
         local, summary = score_masks(scal_ref, i, span, spans, amount)
-        for pair in range(tiles):
-            lanes = slice(pair * SPAN, (pair + 1) * SPAN)
+        pairs = [slice(pair * SPAN, (pair + 1) * SPAN) for pair in range(tiles)]
+        scores = []
+        for lanes in pairs:
             query = heads_apart(q_ref[0, part, lanes] * b16(factor))
             keys = jnp.concatenate([k_ref[0, part, lanes], ks_ref[0, :, lanes]], 0)
-            values = jnp.concatenate([v_ref[0, part, lanes], vs_ref[0, :, lanes]], 0)
-            scores = mm(keys, query, NT)
-            here = jnp.where(local, scores[:SPAN], masked_value)
-            there = jnp.where(summary, scores[SPAN:], masked_value)
+            scores.append(mm(keys, query, NT))
+        probs = []
+        for pair in range(tiles):
+            here = jnp.where(local, scores[pair][:SPAN], masked_value)
+            there = jnp.where(summary, scores[pair][SPAN:], masked_value)
             top = jnp.maximum(jnp.max(here, 0, keepdims=True), jnp.max(there, 0, keepdims=True))
             here, there = jnp.exp(here - top), jnp.exp(there - top)
             total = jnp.sum(here, 0, keepdims=True) + jnp.sum(there, 0, keepdims=True)
-            probs = jnp.concatenate([here.astype(b16), there.astype(b16)], 0)
             lse_ref[0, span, pair : pair + 1, :] = top + jnp.log(total)
-            out = mm(values, probs, TN) * (1.0 / total)
-            mixed_ref[0, lanes, part] = own_heads(out).astype(b16)
-    x2 = x_ref[0].astype(f32) + mm(mixed_ref[0], w_ref[:, 3 * width :], TN)
-    x2_ref[0] = x2.astype(b16)
-    normal, _ = norm_parts(x2)
-    mid_ref[0] = (normal * ln_ref[2:3, :] + ln_ref[3:4, :]).astype(b16)
-
-
-def mlp_kernel(dims, fast, places, last, scal_ref, mid_ref, g_ref, *refs):
-    own_refs, refs = refs[:places], refs[places:]
-    other_refs, refs = refs[:places], refs[places:]
+            probs.append(
+                (jnp.concatenate([here.astype(b16), there.astype(b16)], 0), 1.0 / total)
+            )
+        for lanes, (prob, inverse) in zip(pairs, probs):
+            values = jnp.concatenate([v_ref[0, part, lanes], vs_ref[0, :, lanes]], 0)
+            mixed_ref[lanes, part] = own_heads(mm(values, prob, TN) * inverse).astype(b16)
+
+
+def mlp_kernel(dims, near, places, first, last, scal_ref, *refs):
+    if first:
+        mixed_ref, x_ref, ln_ref, *refs = refs
+    else:
+        mid_ref, *refs = refs
+    g_ref, *refs = refs
+    if near:
+        own_refs, refs = refs[:places], refs[places:]
+        other_refs, refs = refs[:places], refs[places:]
+    else:
+        full_ref, *refs = refs
+        if first:
+            out_ref, *refs = refs
+    dep_ref, *refs = refs
     if last:
-        (dep_ref, x2_ref, y_in_ref, gm_in_ref,
-         y_ref, gm_ref, keep_ref, send_ref, wu_ref, wd_ref, du_ref, dd_ref) = refs
-    else:
-        (dep_ref, y_ref, gm_ref, keep_ref, send_ref, wu_ref, wd_ref, du_ref, dd_ref) = refs
+        x2_ref, y_in_ref, gm_in_ref, *refs = refs
+    if first:
+        x2_ref, mid_ref, wo_ref, token_ref, *refs = refs
+    y_ref, gm_ref, keep_ref, send_ref, wu_ref, wd_ref, du_ref, dd_ref = refs
     groups, rows, cols, sub, lanes = dims
     size = sub * rows + cols
+    extra = rows if first and near else 0
     i = pl.program_id(0)
     core = scal_ref[0] % 2
 
-    def pieces(place, c):
+    def pieces(place, c, skip=0):
         b = place * 2 + c
         here = block(b * rows, rows)
         there = block(b * lanes, lanes)
         for g in range(groups):
+            at = g * (size + skip)
+            if skip:
+                yield slice(at, at + rows), (here, slice(g * cols, (g + 1) * cols)), 2
+                at += skip
             for h in range(sub):
-                at = g * size + h * rows
                 yield (
-                    slice(at, at + rows),
+                    slice(at + h * rows, at + (h + 1) * rows),
                     (here, slice((g * sub + h) * lanes, (g * sub + h + 1) * lanes)),
-                    True,
+                    0,
                 )
-            at = g * size + sub * rows
-            yield slice(at, at + cols), (slice(g * cols, (g + 1) * cols), there), False
+            at += sub * rows
+            yield slice(at, at + cols), (slice(g * cols, (g + 1) * cols), there), 1
 
     @pl.when(i == 0)
     def _():
+        def fill(buf, there, here, kind):
+            to_ref = wu_ref if kind == 0 else wd_ref if kind == 1 else wo_ref
+            to_ref[here] = buf[there, :]
+
         def do(c, mine):
             for move, buf_ref in enumerate(own_refs if mine else other_refs):
-                place = (scal_ref[0] // 2) ^ move if fast else move
-                for there, here, is_up in pieces(place, c):
-                    (wu_ref if is_up else wd_ref)[here] = buf_ref[there, :]
-
-        each_core(core, do)
+                for there, here, kind in pieces((scal_ref[0] // 2) ^ move, c, extra):
+                    fill(buf_ref, there, here, kind)
+
+        if near:
+            each_core(core, do)
+        else:
+            for b in range(2 * places):
+                for k, (there, here, kind) in enumerate(pieces(b // 2, b % 2)):
+                    g = k // (sub + 1)
+                    there = slice(there.start - g * size, there.stop - g * size)
+                    fill(full_ref.at[b * groups + g], there, here, kind)
+                if first:
+                    for g in range(groups):
+                        wo_ref[b * rows : (b + 1) * rows, g * cols : (g + 1) * cols] = out_ref[
+                            b * groups + g
+                        ]
         du_ref[...] = jnp.zeros_like(du_ref)
         dd_ref[...] = jnp.zeros_like(dd_ref)
-
-    mid, g = mid_ref[0], g_ref[0]
+        if first:
+            token_ref[...] = jnp.zeros_like(token_ref)
+
+    if first:
+        x2 = x_ref[...].astype(f32) + mm(mixed_ref[...], wo_ref[...], TN)
+        x2_ref[...] = x2.astype(b16)
+        normal, _ = norm_parts(x2)
+        mid = (normal * ln_ref[2:3, :] + ln_ref[3:4, :]).astype(b16)
+        mid_ref[...] = mid
+    else:
+        mid = mid_ref[...]
+    g = g_ref[...]
     up = mm(mid, wu_ref[...])
     grad_act = mm(g, wd_ref[...])
     square = up * up
@@ -313,21 +361,21 @@
     y = mm(act, wd_ref[...], NT)
     gm = mm(grad_up, wu_ref[...], NT)
     if last:
-        y_ref[0] = (x2_ref[0].astype(f32) + y_in_ref[0].astype(f32) + y).astype(b16)
-        gm_ref[0] = (gm_in_ref[0].astype(f32) + gm).astype(b16)
+        y_ref[...] = (x2_ref[...].astype(f32) + y_in_ref[...].astype(f32) + y).astype(b16)
+        gm_ref[...] = (gm_in_ref[...].astype(f32) + gm).astype(b16)
     else:
-        y_ref[0] = y.astype(b16)
-        gm_ref[0] = gm.astype(b16)
+        y_ref[...] = y.astype(b16)
+        gm_ref[...] = gm.astype(b16)
     dd_ref[...] += mm(g, act, TN)
     du_ref[...] += mm(mid, grad_up, TN)
 
     @pl.when(i == pl.num_programs(0) - 1)
     def _():
         def do(c, mine):
-            out_ref = keep_ref if mine else send_ref
+            to_ref = keep_ref if mine else send_ref
             for place in range(places):
-                for there, here, is_up in pieces(place, c):
-                    out_ref[place, there, :] = (du_ref if is_up else dd_ref)[here].astype(b16)
+                for there, here, kind in pieces(place, c):
+                    to_ref[place, there, :] = (dd_ref if kind else du_ref)[here].astype(b16)
 
         each_core(core, do)
 
@@ -336,22 +384,21 @@
     gm_ref, g_ref, x2_ref, mixed_ref, w_ref, ln_ref, gx2_ref, do_ref, dwo_ref, lng_ref
 ):
     i = pl.program_id(0)
-    width = ln_ref.shape[1]
 
     @pl.when(i == 0)
     def _():
         dwo_ref[...] = jnp.zeros_like(dwo_ref)
         lng_ref[...] = jnp.zeros_like(lng_ref)
 
-    gm = gm_ref[0].astype(f32)
-    normal, inverse = norm_parts(x2_ref[0].astype(f32))
+    gm = gm_ref[...].astype(f32)
+    normal, inverse = norm_parts(x2_ref[...].astype(f32))
     lng_ref[0:1, :] += jnp.sum(gm * normal, 0, keepdims=True)
     lng_ref[1:2, :] += jnp.sum(gm, 0, keepdims=True)
-    gx2 = g_ref[0].astype(f32) + norm_back(gm, normal, inverse, ln_ref[2:3, :])
+    gx2 = g_ref[...].astype(f32) + norm_back(gm, normal, inverse, ln_ref[2:3, :])
     branch = gx2.astype(b16)
-    gx2_ref[0] = branch
-    dwo_ref[...] += mm(mixed_ref[0], branch)
-    do_ref[0] = mm(branch, w_ref[:, 3 * width :], NT).astype(b16)
+    gx2_ref[...] = branch
+    dwo_ref[...] += mm(mixed_ref[...], branch)
+    do_ref[...] = mm(branch, w_ref[...], NT).astype(b16)
 
 
 def backward_kernel(
@@ -373,34 +420,45 @@
     for span in range(spans):
         part = slice(span * SPAN, (span + 1) * SPAN)
         local, summary = score_masks(scal_ref, i, span, spans, amount)
-        for pair in range(tiles):
-            lanes = slice(pair * SPAN, (pair + 1) * SPAN)
-            query = heads_apart(q_ref[0, part, lanes] * b16(factor))
-            grad = heads_apart(do_ref[0, part, lanes])
-            keys = jnp.concatenate([k_ref[0, part, lanes], ks_ref[0, :, lanes]], 0)
-            values = jnp.concatenate([v_ref[0, part, lanes], vs_ref[0, :, lanes]], 0)
-            scores = mm(keys, query, NT)
-            grads = mm(values, grad, NT)
-            total = lse_ref[0, span, pair : pair + 1, :]
-            here = jnp.exp(jnp.where(local, scores[:SPAN], masked_value) - total)
-            there = jnp.exp(jnp.where(summary, scores[SPAN:], masked_value) - total)
-            here_grad, there_grad = here * grads[:SPAN], there * grads[SPAN:]
-            dot = jnp.sum(here_grad, 0, keepdims=True) + jnp.sum(there_grad, 0, keepdims=True)
-            low = jnp.concatenate([here.astype(b16), there.astype(b16)], 0)
-            back = jnp.concatenate(
-                [(here_grad - here * dot).astype(b16), (there_grad - there * dot).astype(b16)], 0
-            )
-            grad_value = mm(low, grad)
-            grad_key = mm(back, query)
-            dqt_ref[lanes, part] = (own_heads(mm(keys, back, TN)) * factor).astype(b16)
-            dqkv_ref[0, part, width + pair * SPAN : width + (pair + 1) * SPAN] = grad_key[
-                :SPAN
-            ].astype(b16)
-            dqkv_ref[0, part, 2 * width + pair * SPAN : 2 * width + (pair + 1) * SPAN] = grad_value[
-                :SPAN
-            ].astype(b16)
-            key_parts.append(grad_key[SPAN:])
-            value_parts.append(grad_value[SPAN:])
+        pairs = [slice(pair * SPAN, (pair + 1) * SPAN) for pair in range(tiles)]
+        for two in range(0, tiles, BATCH):
+            batch = pairs[two : two + BATCH]
+            queries = [heads_apart(q_ref[0, part, lanes] * b16(factor)) for lanes in batch]
+            grads = [heads_apart(do_ref[0, part, lanes]) for lanes in batch]
+            keys = [
+                jnp.concatenate([k_ref[0, part, lanes], ks_ref[0, :, lanes]], 0) for lanes in batch
+            ]
+            scores = [mm(key, query, NT) for key, query in zip(keys, queries)]
+            changes = [
+                mm(jnp.concatenate([v_ref[0, part, lanes], vs_ref[0, :, lanes]], 0), grad, NT)
+                for lanes, grad in zip(batch, grads)
+            ]
+            lows, backs = [], []
+            for k, (score, change) in enumerate(zip(scores, changes)):
+                total = lse_ref[0, span, two + k : two + k + 1, :]
+                here = jnp.exp(jnp.where(local, score[:SPAN], masked_value) - total)
+                there = jnp.exp(jnp.where(summary, score[SPAN:], masked_value) - total)
+                here_grad, there_grad = here * change[:SPAN], there * change[SPAN:]
+                dot = jnp.sum(here_grad, 0, keepdims=True) + jnp.sum(there_grad, 0, keepdims=True)
+                lows.append(jnp.concatenate([here.astype(b16), there.astype(b16)], 0))
+                backs.append(
+                    jnp.concatenate(
+                        [
+                            (here_grad - here * dot).astype(b16),
+                            (there_grad - there * dot).astype(b16),
+                        ],
+                        0,
+                    )
+                )
+            for k, lanes in enumerate(batch):
+                grad_value = mm(lows[k], grads[k])
+                grad_key = mm(backs[k], queries[k])
+                dqt_ref[lanes, part] = (own_heads(mm(keys[k], backs[k], TN)) * factor).astype(b16)
+                c0 = width + (two + k) * SPAN
+                dqkv_ref[0, part, c0 : c0 + SPAN] = grad_key[:SPAN].astype(b16)
+                dqkv_ref[0, part, c0 + width : c0 + width + SPAN] = grad_value[:SPAN].astype(b16)
+                key_parts.append(grad_key[SPAN:])
+                value_parts.append(grad_value[SPAN:])
     dqkv_ref[0, :, :width] = dqt_ref[...].T
 
     def joined(parts):
@@ -423,20 +481,8 @@
                     ]
 
 
-def grads_kernel(
-    dims, fast, scal_ref, normed_ref, dqkv_ref, nsum_ref, key_ref, value_ref, dwo_ref, h_ref,
-    two_ref, dep_ref, *refs
-):
-    if fast:
-        keep_ref, send_ref, nt_ref, dw_ref = refs
-        hkeep_ref, hsend_ref = keep_ref, send_ref
-    else:
-        keep_ref, send_ref, hkeep_ref, hsend_ref, nt_ref, dw_ref = refs
-    groups, rows, cols, width = dims
-    places, half = h_ref.shape[1:3]
-    tiles = width // SPAN
-    base = groups * 4 * rows if fast else 0
-    used = -(-half // 16) * 16 - 8
+def grads_kernel(normed_ref, dqkv_ref, nsum_ref, key_ref, value_ref, dw_ref, nt_ref):
+    width = normed_ref.shape[1]
     nt_ref[...] = normed_ref[...].T
     dw_ref[:, :width] = mm(nt_ref[...], dqkv_ref[:, :width])
     dw_ref[:, width : 2 * width] = mm(nt_ref[...], dqkv_ref[:, width : 2 * width]) + mm(
@@ -445,14 +491,19 @@
     dw_ref[:, 2 * width :] = mm(nt_ref[...], dqkv_ref[:, 2 * width :]) + mm(
         nsum_ref[...], value_ref[...], TN
     )
+
+
+def cut_kernel(dims, fast, scal_ref, dw_ref, dwo_ref, h_ref, two_ref, dep_ref, *refs):
     if fast:
-        for p in range(places):
-            for c in range(2):
-                k, t = divmod(p * 2 + c, tiles)
-                piece = two_ref[k : k + 1, t * SPAN : (t + 1) * SPAN]
-                high = piece.astype(b16).astype(f32)
-                h_ref[c, p, used : used + 1, :] = high
-                h_ref[c, p, used + 1 : used + 2, :] = piece - high
+        keep_ref, send_ref = refs
+        hkeep_ref, hsend_ref = keep_ref, send_ref
+    else:
+        keep_ref, send_ref, hkeep_ref, hsend_ref = refs
+    groups, rows, cols, width = dims
+    places, half = h_ref.shape[1:3]
+    tiles = width // SPAN
+    base = groups * 4 * rows if fast else 0
+    used = half - 8
 
     def do(c, mine):
         out_ref, hout_ref = (keep_ref, hkeep_ref) if mine else (send_ref, hsend_ref)
@@ -466,7 +517,15 @@
                     out_ref[p, at : at + rows, :] = from_ref[
                         r0 : r0 + rows, c0 : c0 + cols
                     ].astype(b16)
-            hout_ref[p, base : base + half, :] = h_ref[c, p].astype(b16)
+            ride = h_ref[c, p]
+            if fast:
+                k, t = divmod(p * 2 + c, tiles)
+                piece = two_ref[k : k + 1, t * SPAN : (t + 1) * SPAN]
+                high = piece.astype(b16).astype(f32)
+                row = lax.broadcasted_iota(jnp.int32, ride.shape, 0)
+                ride = jnp.where(row == used, high, ride)
+                ride = jnp.where(row == used + 1, piece - high, ride)
+            hout_ref[p, base : base + half, :] = ride.astype(b16)
 
     each_core(scal_ref[0] % 2, do)
 
@@ -739,6 +798,17 @@
     return [piece] + [cross(piece, 2 * move, nb) for move in range(1, nb // 2)]
 
 
+def gather_cut(piece, cuts, z, ng):
+    came = [(piece, z)] + [(shift(piece, by, ng), (z - by) % ng) for by in range(1, ng)]
+    outs = []
+    for start, stop in cuts:
+        out = jnp.zeros((ng, stop - start, piece.shape[1]), piece.dtype)
+        for part, at in came:
+            out = put(out, part[start:stop], at)
+        outs.append(out.reshape(-1, piece.shape[1]))
+    return outs
+
+
 def other_core(pieces, nb):
     return [cross(piece, 1, nb) for piece in pieces]
 
@@ -798,7 +868,11 @@
             name=name,
         )(*args)
 
-    attn_piece = attn_master.astype(b16).reshape(4 * rows, cols)
+    pack_dims = (rows, cols, sub, lanes)
+
+    attn_piece = attn_master[:3].astype(b16).reshape(3 * rows, cols)
+    if fast:
+        attn_z = gather_group(attn_piece, z, ng)
     normed, rider = pl.pallas_call(
         prep_kernel,
         grid=(seqs,),
@@ -811,92 +885,121 @@
         name="prep",
     )(scal, tokens, ln_params)
 
+    def gate(pieces, *deps):
+        return flat(
+            functools.partial(gate_kernel, len(pieces)), "gate",
+            [shape(piece.shape, b16) for piece in pieces], [], cost(1e6, 1e6), *pieces, *deps,
+        )
+
+    def everywhere(piece):
+        return lax.all_gather(piece, ("blk", "group"))
+
     if fast:
-        message = jnp.concatenate([gather_group(attn_piece, z, ng), rider], 0)
+        message = jnp.concatenate([attn_z, rider], 0)
         attn_own = gather_plane(message, nb)
         attn_bufs = attn_own + other_core(attn_own, nb)
-        pieces = flat(
-            functools.partial(pack_kernel, (rows, cols, sub, lanes)), "pack",
-            [shape((size, lanes), b16)] * CHUNKS, [], cost(1e6, 1e6),
-            up_master, down_master, attn_own[1],
-        )
-        mlp_z = [gather_group(piece, z, ng) for piece in pieces]
-        gates = [mlp_z[0]]
+        pack_out = shape((rows + CHUNKS * size, lanes), b16)
+        piece = pl.pallas_call(
+            functools.partial(pack_kernel, pack_dims),
+            grid=(1,),
+            in_specs=[
+                pl.BlockSpec((1, rows, cols), lambda i: (3, 0, 0)), fixed(*up_master.shape),
+                fixed(*down_master.shape), whole(),
+            ],
+            out_specs=fixed(*pack_out.shape),
+            out_shape=pack_out,
+            cost_estimate=cost(1e6, 1e6),
+            name="pack",
+        )(attn_master, up_master, down_master, attn_bufs[places])
+        mlp_z, late_z = gather_cut(piece, [(0, rows + size), (rows + size, rows + 2 * size)], z, ng)
+        mlp_own = gather_plane(mlp_z, nb)
+        dep = mlp_z
     else:
+        out_piece = attn_master[3].astype(b16)
         up_low = up_master.astype(b16).reshape(rows, sub, CHUNKS, lanes)
         down_low = down_master.astype(b16).T.reshape(cols, CHUNKS, lanes)
-        pieces = [
-            jnp.concatenate(
-                [jnp.swapaxes(up_low[:, :, j], 0, 1).reshape(sub * rows, lanes), down_low[:, j]], 0
-            )
-            for j in range(CHUNKS)
-        ]
         attn_own, attn_other = gather_any(attn_piece)
         ride_own, ride_other = gather_any(rider, "blk")
         attn_bufs = attn_own + attn_other + ride_own + ride_other
-        gates = [ln_params]
+        mlp_bufs = []
+        for j in range(CHUNKS):
+            piece = [jnp.swapaxes(up_low[:, :, j], 0, 1).reshape(sub * rows, lanes), down_low[:, j]]
+            mlp_bufs.append([everywhere(jnp.concatenate(piece, 0))])
+        mlp_bufs[0].append(everywhere(out_piece))
+        dep = ln_params
 
     dims = (ng, rows, cols, width)
     act_bytes = seqs * tok * width
-    q, k, v, ks, vs, nsum, lse, mixed, x2, mid, w_attn, token = pl.pallas_call(
+    q, k, v, ks, vs, nsum, lse, mixed, w_attn, token = pl.pallas_call(
         functools.partial(forward_kernel, dims, fast, places),
         grid=(seqs,),
-        in_specs=[scalars(), per_step(tok, width), per_step(tok, width)]
-        + [whole()] * len(attn_bufs)
-        + [fixed(4, width), whole()],
+        in_specs=[scalars(), per_step(tok, width)] + [whole()] * (len(attn_bufs) + 1),
         out_specs=[
             per_step(tok, width), per_step(tok, width), per_step(tok, width),
             per_step(amount, width), per_step(amount, width), per_step(amount, width),
             per_step(spans, tiles, 2 * SPAN),
-            per_step(width, tok), per_step(tok, width), per_step(tok, width),
+            pl.BlockSpec((width, tok), lambda i: (0, i)),
             whole(), fixed(8, SPAN),
         ],
         out_shape=[
             like(b16, tok, width), like(b16, tok, width), like(b16, tok, width),
             like(b16, amount, width), like(b16, amount, width), like(b16, amount, width),
             like(f32, spans, tiles, 2 * SPAN),
-            like(b16, width, tok), like(b16, tok, width), like(b16, tok, width),
-            shape((width, 4 * width), b16), shape((8, SPAN), f32),
+            shape((width, seqs * tok), b16),
+            shape((width, 3 * width), b16), shape((8, SPAN), f32),
         ],
         scratch_shapes=[
             pltpu.VMEM((2, places, half, SPAN), f32), pltpu.VMEM((amount, width), f32)
         ],
         compiler_params=params(16),
-        cost_estimate=cost(8e9, act_bytes * 18),
+        cost_estimate=cost(8e9, act_bytes * 14),
         name="forward",
-    )(scal, normed, tokens, *attn_bufs, ln_params, gates[0])
+    )(scal, normed, *attn_bufs, dep)
 
     if fast:
-        mlp_own = [gather_plane(mlp_z[0], nb)]
-        for j in range(1, CHUNKS):
-            (gated,) = flat(
-                gate_kernel, "gate", [shape(mlp_z[j].shape, b16)], [], cost(1e6, 1e6),
-                mlp_z[j], token,
-            )
-            gates.append(gated)
-            mlp_own.append(gather_plane(gated, nb))
-        mlp_bufs = [own + other_core(own, nb) for own in mlp_own]
-    else:
-        mlp_bufs = [sum(gather_any(piece), []) for piece in pieces]
-        gates = gates * CHUNKS
+        mlp_own[1:] = gate(mlp_own[1:], token)
+        late_own = gather_plane(gate([late_z], token)[0], nb)
+        mlp_bufs = [mlp_own + other_core(mlp_own, nb)]
+        dep = late_own[0]
     mlp_dims = (ng, rows, cols, sub, lanes)
     mlp_out = shape((places, ng * size, lanes), b16)
+    every_row = seqs * tok
+    tile = every_row // ROW_STEPS
+    flat_tokens, flat_cot = tokens.reshape(-1, width), cotangent.reshape(-1, width)
+    by_rows = pl.BlockSpec((tile, width), lambda i: (i, 0))
+    rows_out = shape((every_row, width), b16)
     keeps, sends = [], []
-    y = gm = None
+    y = gm = x2 = mid = wo = None
     for j in range(CHUNKS):
-        last = j == CHUNKS - 1
-        args = [scal, mid, cotangent, *mlp_bufs[j], gates[min(j + 1, CHUNKS - 1)]]
-        in_specs = [scalars(), per_step(tok, width), per_step(tok, width)]
+        first, last = j == 0, j == CHUNKS - 1
+        if fast and not first:
+            late_own[1:] = gate(late_own[1:], token)
+            mlp_bufs.append(late_own + other_core(late_own, nb))
+        if first:
+            args = [scal, mixed, flat_tokens, ln_params, flat_cot]
+            in_specs = [
+                scalars(), pl.BlockSpec((width, tile), lambda i: (0, i)), by_rows, fixed(4, width),
+                by_rows,
+            ]
+        else:
+            args, in_specs = [scal, mid, flat_cot], [scalars(), by_rows, by_rows]
+        args += [*mlp_bufs[j], dep]
         in_specs += [whole()] * (len(mlp_bufs[j]) + 1)
+        outs = [(by_rows, rows_out), (by_rows, rows_out), (whole(), mlp_out), (whole(), mlp_out)]
+        if first:
+            outs = [
+                (by_rows, rows_out), (by_rows, rows_out), (whole(), shape((width, width), b16)),
+                (fixed(8, SPAN), shape((8, SPAN), f32)),
+            ] + outs
         if last:
             args += [x2, y, gm]
-            in_specs += [per_step(tok, width)] * 3
-        y, gm, keep, send = pl.pallas_call(
-            functools.partial(mlp_kernel, mlp_dims, fast, places, last),
-            grid=(seqs,),
+            in_specs += [by_rows] * 3
+        *more, y, gm, keep, send = pl.pallas_call(
+            functools.partial(mlp_kernel, mlp_dims, fast, places, first, last),
+            grid=(ROW_STEPS,),
             in_specs=in_specs,
-            out_specs=[per_step(tok, width), per_step(tok, width), whole(), whole()],
-            out_shape=[like(b16, tok, width), like(b16, tok, width), mlp_out, mlp_out],
+            out_specs=[spec for spec, _ in outs],
+            out_shape=[out for _, out in outs],
             scratch_shapes=[
                 pltpu.VMEM((width, inner), b16), pltpu.VMEM((width, inner), b16),
                 pltpu.VMEM((width, inner), f32), pltpu.VMEM((width, inner), f32),
@@ -905,30 +1008,29 @@
             cost_estimate=cost(9e9, act_bytes * 20),
             name="mlp",
         )(*args)
+        if first:
+            x2, mid, wo, token = more
         keeps.append(keep)
         sends.append(send)
-    block_out = y
+    block_out = y.reshape(tokens.shape)
     if fast:
         gets = [cross(send, 1, nb) for send in sends]
 
+    by_tok = pl.BlockSpec((tok, width), lambda i: (i, 0))
     gx2, grad_mixed, dwo, ln_two = pl.pallas_call(
         middle_kernel,
         grid=(seqs,),
         in_specs=[
-            per_step(tok, width), per_step(tok, width), per_step(tok, width),
-            per_step(width, tok), whole(), fixed(4, width),
+            by_tok, by_tok, by_tok, pl.BlockSpec((width, tok), lambda i: (0, i)), whole(),
+            fixed(4, width),
         ],
-        out_specs=[
-            per_step(tok, width), per_step(tok, width), fixed(width, width), fixed(8, width)
-        ],
-        out_shape=[
-            like(b16, tok, width), like(b16, tok, width), shape((width, width), f32),
-            shape((8, width), f32),
-        ],
+        out_specs=[by_tok, by_tok, fixed(width, width), fixed(8, width)],
+        out_shape=[rows_out, rows_out, shape((width, width), f32), shape((8, width), f32)],
         compiler_params=params(16),
         cost_estimate=cost(3e9, act_bytes * 14),
         name="middle",
-    )(gm, cotangent, x2, mixed, w_attn, ln_params)
+    )(gm, flat_cot, x2, mixed, wo, ln_params)
+    gx2, grad_mixed = gx2.reshape(tokens.shape), grad_mixed.reshape(tokens.shape)
 
     block = shape((ng * size, lanes), f32)
     block_low = shape((ng * size, lanes), b16)
@@ -976,13 +1078,15 @@
     outs = [shape((places, attn_rows + tail, cols), b16)] * 2
     if not fast:
         outs += [shape((places, half, SPAN), b16)] * 2
+    (dw,) = flat(
+        grads_kernel, "grads", [shape((width, 3 * width), f32)],
+        [pltpu.VMEM((width, seqs * tok), b16)], cost(1e6, 1e5),
+        normed.reshape(-1, width), dqkv.reshape(-1, 3 * width), nsum.reshape(-1, width),
+        key_part.reshape(-1, width), value_part.reshape(-1, width),
+    )
     parts = flat(
-        functools.partial(grads_kernel, dims, fast), "grads", outs,
-        [pltpu.VMEM((width, seqs * tok), b16), pltpu.VMEM((width, 3 * width), f32)],
-        cost(5e9, 1e7),
-        scal, normed.reshape(-1, width), dqkv.reshape(-1, 3 * width), nsum.reshape(-1, width),
-        key_part.reshape(-1, width), value_part.reshape(-1, width), dwo, h_part, ln_two, dep,
-        scalar=True,
+        functools.partial(cut_kernel, dims, fast), "cut", outs, [], cost(1e6, 1e5),
+        scal, dw, dwo, h_part, ln_two, dep, scalar=True,
     )
 
     def collect(terms, sizes, count, tail):

time: 177 us -> 156 us (0.88)
  waiting for transfers between devices: 49 us -> 25.2 us
  starting transfers between devices: 37.7 us -> 41.5 us
  local copies, waits for them, and re-layouts: 2.37 us -> 5.71 us
  Pallas kernels: 73.3 us -> 70.2 us
    ppermute x31, waiting for transfers between devices: 28.2 us -> 16.1 us  [cross(): return lax.ppermute(values, 'blk', [(j, j ^ bit) for j in range(nb)])]
    ppermute x15 -> x12, waiting for transfers between devices: 20.8 us -> 9.06 us  [shift(): lax.ppermute(values, 'group', [(j, (j + by) % ng) for j in range(ng)])]
    pallas_call x3 -> x4, Pallas kernels: 28.7 us -> 33.3 us  [the longest x2 27 us: body(): pl.pallas_call(functools.partial(mlp_kernel, mlp_dims, fast, places, firs...]
    ppermute x15 -> x12, starting transfers between devices: 15.8 us -> 19.9 us  [shift(): lax.ppermute(values, 'group', [(j, (j + by) % ng) for j in range(ng)])]
    pallas_call x1, Pallas kernels: 11.8 us -> 7.91 us  [body(): pl.pallas_call(functools.partial(backward_kernel, places), grid=(seqs,),...]
    pallas_call x1, Pallas kernels: 13.2 us -> 9.46 us  [body(): pl.pallas_call(functools.partial(forward_kernel, dims, fast, places), gri...]
    pallas_call x11 -> x13, Pallas kernels: 9.61 us -> 9.57 us  [flat(): pl.pallas_call(call, in_specs=[scalars()] * scalar + [whole()] * (len(arg...]
  transfers between devices with their start and end apart: 46 -> 43, of which waited for: 12 -> 14; matrix products, arithmetic and copies ran while one was open for 1% -> 2% of each run, Pallas kernels for 38% -> 43%
where the time goes in v3:
time: 156 us
  Pallas kernels  70.2 us (45%)
  starting transfers between devices  41.5 us (27%)
  waiting for transfers between devices  25.2 us (16%)
  blocking collectives  11.4 us (7%)
  local copies, waits for them, and re-layouts  5.71 us (4%)
    pallas_call x2, Pallas kernels, body(): pl.pallas_call(functools.partial(mlp_kernel, mlp_dims, fast, places, firs...  27 us
    ppermute x31, starting transfers between devices, cross(): return lax.ppermute(values, 'blk', [(j, j ^ bit) for j in range(nb)])  21.7 us
    ppermute x12, starting transfers between devices, shift(): lax.ppermute(values, 'group', [(j, (j + by) % ng) for j in range(ng)])  19.9 us
    ppermute x31, waiting for transfers between devices, cross(): return lax.ppermute(values, 'blk', [(j, j ^ bit) for j in range(nb)])  16.1 us
    all_to_all x1, blocking collectives, body(): every = lax.all_to_all(message, ('blk', 'group'), 0, 0, tiled=True)  11.4 us
    pallas_call x13, Pallas kernels, flat(): pl.pallas_call(call, in_specs=[scalars()] * scalar + [whole()] * (len(arg...  9.57 us
    pallas_call x1, Pallas kernels, body(): pl.pallas_call(functools.partial(forward_kernel, dims, fast, places), gri...  9.46 us
    ppermute x12, waiting for transfers between devices, shift(): lax.ppermute(values, 'group', [(j, (j + by) % ng) for j in range(ng)])  9.06 us
  transfers between devices with their start and end apart: 43, of which 14 were waited for; matrix products, arithmetic and copies ran while one was open for 2% of the time, Pallas kernels for 43%

profile of v3, /device:TPU:0, one launch (start us, length us, event | category | flops | bytes accessed | tf_op | source)
XLA Modules:
  0.0 156.0 jit_solution(7249557725264505562)
XLA Ops:
  0.7 0.9 slice.71
  1.6 5.0 %collective-permute-start.2 = (bf16[192,128]{1,0:T(8,128)(2,1)S(1)}, bf16[192,128]{1,0:T(8,128)(2,1)S(1)}, u32[]{:S(2)}, u32[]{:S(2)}) collective-permute-start(bf16[192,128]{1,0:T(8,128)(2,1)S(1)} %bitcast.76), channel_id=1, source_target_pairs={{0,3},{1,0},{2,1},{3,2},{4,7},{5,4},{6,5},{7,6},{8,11},{9,8},{10,9... | collective-permute-start | bytes 147464 | tf_op jit(solution)/shard_map/ppermute | solution.py:775
  6.6 1.0 collective-permute-start
  7.7 0.7 pad_add_fusion.scal_ref
  8.4 1.3 copy-done
  10.4 2.5 %prep.1 = (bf16[5,256,512]{2,1,0:T(8,128)(2,1)S(1)}, bf16[96,128]{1,0:T(8,128)(2,1)S(1)}) custom-call(s32[7]{0:T(128)S(1)} %pad_add_fusion.scal_ref, bf16[5,256,512]{2,1,0:T(8,128)(2,1)S(1)} %copy-done, f32[4,512]{1,0:T(4,128)S(1)} %copy-done.13), custom_call_target="tpu_custom_call" | custom-call | flops 40000000 | bytes 2621440 | tf_op jit(solution)/shard_map/prep/pallas_call | solution.py:876
  13.2 2.5 %collective-permute-start.5 = (bf16[864,128]{1,0:T(8,128)(2,1)S(1)}, bf16[864,128]{1,0:T(8,128)(2,1)S(1)}, u32[]{:S(2)}, u32[]{:S(2)}) collective-permute-start(bf16[864,128]{1,0:T(8,128)(2,1)S(1)} %pad_maximum_fusion.refs_0_), channel_id=1, source_target_pairs={{0,24},{4,28},{8,16},{12,20},{16,8},{20,12},{24,0},{28,4},{1,25},{... | collective-permute-start | bytes 663560 | tf_op jit(solution)/shard_map/ppermute | solution.py:779
  17.4 1.8 %pack.1 = bf16[576,128]{1,0:T(8,128)(2,1)} custom-call(f32[4,64,128]{2,1,0:T(8,128)} %am_ref.1, f32[64,512]{1,0:T(8,128)} %um_ref.1, f32[256,128]{1,0:T(8,128)} %dm_ref.1, bf16[864,128]{1,0:T(8,128)(2,1)} %copy-done.5), custom_call_target="tpu_custom_call" | custom-call | flops 1000000 | bytes 1000000 | tf_op jit(solution)/shard_map/pack/pallas_call | solution.py:902
  19.3 2.8 %collective-permute-start.12 = (bf16[576,128]{1,0:T(8,128)(2,1)}, bf16[576,128]{1,0:T(8,128)(2,1)S(1)}, u32[]{:S(2)}, u32[]{:S(2)}) collective-permute-start(bf16[576,128]{1,0:T(8,128)(2,1)} %pack.1), channel_id=1, source_target_pairs={{0,3},{1,0},{2,1},{3,2},{4,7},{5,4},{6,5},{7,6},{8,11},{9,8},{10,9... | collective-permute-start | bytes 442376 | tf_op jit(solution)/shard_map/ppermute | solution.py:775
  22.1 0.9 fusion.3
  23.1 0.9 fusion.7
  24.0 1.2 collective-permute-start.11
  25.2 1.5 collective-permute-done.4.refs_2_
  27.2 3.7 %collective-permute-done.10 = bf16[576,128]{1,0:T(8,128)(2,1)S(1)} collective-permute-done((bf16[576,128]{1,0:T(8,128)(2,1)}, bf16[576,128]{1,0:T(8,128)(2,1)S(1)}, u32[]{:S(2)}, u32[]{:S(2)}) %collective-permute-start.10) | collective-permute-done | bytes 147488 | tf_op jit(solution)/shard_map/ppermute | solution.py:775
  30.9 5.3 %collective-permute-done.11 = bf16[576,128]{1,0:T(8,128)(2,1)S(1)} collective-permute-done((bf16[576,128]{1,0:T(8,128)(2,1)}, bf16[576,128]{1,0:T(8,128)(2,1)S(1)}, u32[]{:S(2)}, u32[]{:S(2)}) %collective-permute-start.11) | collective-permute-done | bytes 147488 | tf_op jit(solution)/shard_map/ppermute | solution.py:775
  36.4 2.5 %collective-permute-start.15 = (bf16[1280,128]{1,0:T(8,128)(2,1)S(1)}, bf16[1280,128]{1,0:T(8,128)(2,1)S(1)}, u32[]{:S(2)}, u32[]{:S(2)}) collective-permute-start(bf16[1280,128]{1,0:T(8,128)(2,1)S(1)} %bitcast.63), channel_id=1, source_target_pairs={{0,24},{4,28},{8,16},{12,20},{16,8},{20,12},{24,0},{28,4},{1,25},{... | collective-permute-start | bytes 983048 | tf_op jit(solution)/shard_map/ppermute | solution.py:779
  40.0 9.5 %forward.1 = (bf16[5,256,512]{2,1,0:T(8,128)(2,1)S(1)}, bf16[5,256,512]{2,1,0:T(8,128)(2,1)S(1)}, bf16[5,256,512]{2,1,0:T(8,128)(2,1)S(1)}, bf16[5,16,512]{2,1,0...) custom-call(s32[7]{0:T(128)S(1)} %pad_add_fusion.scal_ref, ...), custom_call_target="tpu_custom_call" | custom-call | flops 8000000000 | bytes 9175040 | tf_op jit(solution)/shard_map/forward/pallas_call | solution.py:933
  49.5 4.9 %collective-permute-done.14.refs_1_ = bf16[1280,128]{1,0:T(8,128)(2,1)S(1)} collective-permute-done((bf16[1280,128]{1,0:T(8,128)(2,1)S(1)}, bf16[1280,128]{1,0:T(8,128)(2,1)S(1)}, u32[]{:S(2)}, u32[]{:S(2)}) %collective-permute-start.14) | collective-permute-done | bytes 327712 | tf_op jit(solution)/shard_map/ppermute | solution.py:779
  55.8 1.7 %collective-permute-start.22 = (bf16[1024,128]{1,0:T(8,128)(2,1)S(1)}, bf16[1024,128]{1,0:T(8,128)(2,1)S(1)}, u32[]{:S(2)}, u32[]{:S(2)}) collective-permute-start(bf16[1024,128]{1,0:T(8,128)(2,1)S(1)} %gate.4.refs_12_.refs_2_.refs_10_), channel_id=1, source_target_pairs={{0,24},{4,28},{8,16},{12,20},{16,8},{20,12},{24,0},{28,4},{1,25},{... | collective-permute-start | bytes 786440 | tf_op jit(solution)/shard_map/ppermute | solution.py:779
  57.5 1.2 collective-permute-start.21
  59.3 14.3 %mlp.2 = (bf16[1280,512]{1,0:T(8,128)(2,1)S(1)}, bf16[1280,512]{1,0:T(8,128)(2,1)S(1)}, bf16[512,512]{1,0:T(8,128)(2,1)S(1)}, f32[8,128]{1,0:T(8,128)S(1)}, bf16...) custom-call(s32[7]{0:T(128)S(1)} %pad_add_fusion.scal_ref, ...), custom_call_target="tpu_custom_call" | custom-call | flops 8999999488 | bytes 13107200 | tf_op jit(solution)/shard_map/mlp/pallas_call | solution.py:997
  76.0 12.7 %mlp.3 = (bf16[1280,512]{1,0:T(8,128)(2,1)}, bf16[1280,512]{1,0:T(8,128)(2,1)S(1)}, bf16[4,1024,128]{2,1,0:T(8,128)(2,1)S(1)}, bf16[4,1024,128]{2,1,0:T(8,128)(2,1)S(1)}) custom-call(s32[7]{0:T(128)S(1)} %pad_add_fusion.scal_ref, bf16[1280,512]{1,0:T(8,128)(2,1)S(1)} %get-tuple-element.109.refs_0_, bf16[1280,512]{1,0:T(8,128)(2,1)S(1)} %bitcast.72, ...), custom_call_target="tpu_custom_call" | custom-call | flops 8999999488 | bytes 13107200 | tf_op jit(solution)/shard_map/mlp/pallas_call | solution.py:997
  88.9 4.5 %middle.1 = (bf16[1280,512]{1,0:T(8,128)(2,1)S(1)}, bf16[1280,512]{1,0:T(8,128)(2,1)S(1)}, f32[512,512]{1,0:T(8,128)S(1)}, f32[8,512]{1,0:T(8,128)S(1)}) custom-call(bf16[1280,512]{1,0:T(8,128)(2,1)S(1)} %get-tuple-element.118.gm_ref, bf16[1280,512]{1,0:T(8,128)(2,1)S(1)} %bitcast.73, bf16[1280,512]{1,0:T(8,128)(2,1)S(1)} %get-tuple-element.114.refs_11_.x2_ref, ...), custom_call_target="tpu_custom_call" | custom-call | flops 3000000000 | bytes 9175040 | tf_op jit(solution)/shard_map/middle/pallas_call | solution.py:1020
  93.4 1.0 halves.1
  94.4 1.6 %collective-permute-start.29 = (bf16[2,1024,128]{2,1,0:T(8,128)(2,1)S(1)}, bf16[2,1024,128]{2,1,0:T(8,128)(2,1)S(1)}, u32[]{:S(2)}, u32[]{:S(2)}) collective-permute-start(bf16[2,1024,128]{2,1,0:T(8,128)(2,1)S(1)} %get-tuple-element.140), channel_id=1, source_target_pairs={{0,8},{4,12},{8,0},{12,4},{16,24},{20,28},{24,16},{28,20},{1,9},{5... | collective-permute-start | bytes 1572872 | tf_op jit(solution)/shard_map/ppermute | solution.py:779
  96.0 0.8 collective-permute-start.30
  96.8 7.9 %backward.1 = (bf16[5,256,1536]{2,1,0:T(8,128)(2,1)S(1)}, bf16[5,16,512]{2,1,0:T(8,128)(2,1)S(1)}, bf16[5,16,512]{2,1,0:T(8,128)(2,1)S(1)}, f32[2,4,48,128]{3,2,1,0:T(8,128)S(1)}) custom-call(s32[7]{0:T(128)S(1)} %pad_add_fusion.scal_ref, bf16[5,256,512]{2,1,0:T(8,128)(2,1)S(1)} %bitcast.74, bf16[5,256,512]{2,1,0:T(8,128)(2,1)S(1)} %get-tuple-element.121.q_ref, ...), custom_call_target="tpu_custom_call" | custom-call | flops 14000000000 | bytes 15728640 | tf_op jit(solution)/shard_map/backward/pallas_call | solution.py:1048
  104.7 2.5 %grads.1.dw_ref = f32[512,1536]{1,0:T(8,128)S(1)} custom-call(bf16[1280,512]{1,0:T(8,128)(2,1)S(1)} %bitcast.60, bf16[1280,1536]{1,0:T(8,128)(2,1)S(1)} %bitcast.58, bf16[80,512]{1,0:T(8,128)(2,1)S(1)} %bitcast.68, bf16[80,512]{1,0:T(8,128)(2,1)S(1)} %bitcast.69, bf16[80,512]{1,0:T(8,128)(2,1)S(1)} %bitcast.70), custom_call_target="tpu_custom_call" | custom-call | flops 1000000 | bytes 100000 | tf_op jit(solution)/shard_map/grads/pallas_call | solution.py:860
  107.3 1.4 collective-permute-done.29.refs_1_
  108.7 1.2 collective-permute-done.30.refs_3_
  110.1 0.8 cut.1
  111.0 0.9 collective-permute-start.38
  111.8 1.1 collective-permute-start.39
  113.0 0.7 collective-permute-done.31.refs_1_
  113.7 0.8 spread.1
  115.1 1.4 collective-permute-start.33
  116.5 1.6 collective-permute-start.34
  118.0 3.0 %project.1.refs_4_.grad_ref = bf16[5,256,512]{2,1,0:T(8,128)(2,1)S(1)} custom-call(bf16[5,256,1536]{2,1,0:T(8,128)(2,1)S(1)} %get-tuple-element.133.dqkv_ref, bf16[512,1536]{1,0:T(8,128)(2,1)S(1)} %get-tuple-element.127.w_ref, f32[1072,128]{1,0:T(8,128)S(1)} %get-tuple-element.146.dep_ref.refs_0_), custom_call_target="tpu_custom_call" | custom-call | flops 3000000000 | bytes 5242880 | tf_op jit(solution)/shard_map/project/pallas_call | solution.py:1113
  121.8 3.2 %collective-permute-start.41 = (bf16[512,128]{1,0:T(8,128)(2,1)S(1)}, bf16[512,128]{1,0:T(8,128)(2,1)S(1)}, u32[]{:S(2)}, u32[]{:S(2)}) collective-permute-start(bf16[512,128]{1,0:T(8,128)(2,1)S(1)} %get-tuple-element.162), channel_id=1, source_target_pairs={{0,2},{1,3},{2,0},{3,1},{4,6},{5,7},{6,4},{7,5},{8,10},{9,11},{10,... | collective-permute-start | bytes 393224 | tf_op jit(solution)/shard_map/ppermute | solution.py:775
  125.0 1.9 %collective-permute-done.32.refs_1_ = bf16[1072,128]{1,0:T(8,128)(2,1)S(1)} collective-permute-done((bf16[1072,128]{1,0:T(8,128)(2,1)S(1)}, bf16[1072,128]{1,0:T(8,128)(2,1)S(1)}, u32[]{:S(2)}, u32[]{:S(2)}) %collective-permute-start.32) | collective-permute-done | bytes 274464 | tf_op jit(solution)/shard_map/ppermute | solution.py:779
  126.9 2.7 %collective-permute-start.42 = (bf16[512,128]{1,0:T(8,128)(2,1)S(1)}, bf16[512,128]{1,0:T(8,128)(2,1)S(1)}, u32[]{:S(2)}, u32[]{:S(2)}) collective-permute-start(bf16[512,128]{1,0:T(8,128)(2,1)S(1)} %get-tuple-element.163), channel_id=1, source_target_pairs={{0,3},{1,0},{2,1},{3,2},{4,7},{5,4},{6,5},{7,6},{8,11},{9,8},{10,9... | collective-permute-start | bytes 393224 | tf_op jit(solution)/shard_map/ppermute | solution.py:775
  129.6 3.0 %collective-permute-done.34.refs_3_ = bf16[1072,128]{1,0:T(8,128)(2,1)S(1)} collective-permute-done((bf16[1072,128]{1,0:T(8,128)(2,1)S(1)}, bf16[1072,128]{1,0:T(8,128)(2,1)S(1)}, u32[]{:S(2)}, u32[]{:S(2)}) %collective-permute-start.34) | collective-permute-done | bytes 274464 | tf_op jit(solution)/shard_map/ppermute | solution.py:779
  133.4 3.2 %collective-permute-start.36 = (bf16[256,128]{1,0:T(8,128)(2,1)S(1)}, bf16[256,128]{1,0:T(8,128)(2,1)S(1)}, u32[]{:S(2)}, u32[]{:S(2)}) collective-permute-start(bf16[256,128]{1,0:T(8,128)(2,1)S(1)} %get-tuple-element.155), channel_id=1, source_target_pairs={{0,2},{1,3},{2,0},{3,1},{4,6},{5,7},{6,4},{7,5},{8,10},{9,11},{10,... | collective-permute-start | bytes 196616 | tf_op jit(solution)/shard_map/ppermute | solution.py:775
  137.3 1.1 mlp_step.1
  138.4 4.4 %input.1 = (f32[5,256,512]{2,1,0:T(8,128)}, f32[8,512]{1,0:T(8,128)S(1)}) custom-call(s32[7]{0:T(128)S(1)} %pad_add_fusion.scal_ref, bf16[5,256,512]{2,1,0:T(8,128)(2,1)S(1)} %project.1.refs_4_.grad_ref, bf16[5,256,512]{2,1,0:T(8,128)(2,1)S(1)} %bitcast.59, bf16[5,256,512]{2,1,0:T(8,128)(2,1)S(1)} %copy-done.1, ...), custom_call_target="tpu_custom_call" | custom-call | flops 100000000 | bytes 6553600 | tf_op jit(solution)/shard_map/input/pallas_call | solution.py:1137
  142.8 0.8 attn_step.1
  143.6 11.4 %all_to_all.5.every_ref = bf16[32,16,128]{2,1,0:T(8,128)(2,1)S(1)} all-to-all(bf16[32,16,128]{2,1,0:T(8,128)(2,1)S(1)} %get-tuple-element.168), channel_id=1, replica_groups=mesh['blk'=8,'group'=4] {'blk','group'}, dimensions={0} | all-to-all | bytes 262144 | tf_op jit(solution)/shard_map/all_to_all | solution.py:1170
  155.0 0.9 final.1
  (115 shorter events, 11.9 us)
Async XLA Ops:
  1.6 11.5 %collective-permute-start.2 = (bf16[192,128]{1,0:T(8,128)(2,1)S(1)}, bf16[192,128]{1,0:T(8,128)(2,1)S(1)}, u32[]{:S(2)}, u32[]{:S(2)}) collective-permute-start(bf16[192,128]{1,0:T(8,128)(2,1)S(1)} %bitcast.76), channel_id=1, source_target_pairs={{0,3},{1,0},{2,1},{3,2},{4,7},{5,4},{6,5},{7,6},{8,11},{9,8},{10,9... | collective-permute-start | bytes 147464 | tf_op jit(solution)/shard_map/ppermute | solution.py:775
  6.6 6.4 %collective-permute-start.1 = (bf16[192,128]{1,0:T(8,128)(2,1)S(1)}, bf16[192,128]{1,0:T(8,128)(2,1)S(1)}, u32[]{:S(2)}, u32[]{:S(2)}) collective-permute-start(bf16[192,128]{1,0:T(8,128)(2,1)S(1)} %bitcast.77), channel_id=1, source_target_pairs={{0,2},{1,3},{2,0},{3,1},{4,6},{5,7},{6,4},{7,5},{8,10},{9,11},{10,... | collective-permute-start | bytes 147464 | tf_op jit(solution)/shard_map/ppermute | solution.py:775
  6.6 6.4 %collective-permute-start = (bf16[192,128]{1,0:T(8,128)(2,1)S(1)}, bf16[192,128]{1,0:T(8,128)(2,1)S(1)}, u32[]{:S(2)}, u32[]{:S(2)}) collective-permute-start(bf16[192,128]{1,0:T(8,128)(2,1)S(1)} %bitcast.78), channel_id=1, source_target_pairs={{0,1},{1,2},{2,3},{3,0},{4,5},{5,6},{6,7},{7,4},{8,9},{9,10},{10,1... | collective-permute-start | bytes 147464 | tf_op jit(solution)/shard_map/ppermute | solution.py:775
  13.1 3.6 %collective-permute-start.6 = (bf16[864,128]{1,0:T(8,128)(2,1)S(1)}, bf16[864,128]{1,0:T(8,128)(2,1)S(1)}, u32[]{:S(2)}, u32[]{:S(2)}) collective-permute-start(bf16[864,128]{1,0:T(8,128)(2,1)S(1)} %pad_maximum_fusion.refs_0_), channel_id=1, source_target_pairs={{0,4},{4,0},{8,12},{12,8},{16,20},{20,16},{24,28},{28,24},{1,5},{5... | collective-permute-start | bytes 663560 | tf_op jit(solution)/shard_map/ppermute | solution.py:779
  13.2 10.8 %collective-permute-start.5 = (bf16[864,128]{1,0:T(8,128)(2,1)S(1)}, bf16[864,128]{1,0:T(8,128)(2,1)S(1)}, u32[]{:S(2)}, u32[]{:S(2)}) collective-permute-start(bf16[864,128]{1,0:T(8,128)(2,1)S(1)} %pad_maximum_fusion.refs_0_), channel_id=1, source_target_pairs={{0,24},{4,28},{8,16},{12,20},{16,8},{20,12},{24,0},{28,4},{1,25},{... | collective-permute-start | bytes 663560 | tf_op jit(solution)/shard_map/ppermute | solution.py:779
  15.7 11.0 %collective-permute-start.4 = (bf16[864,128]{1,0:T(8,128)(2,1)S(1)}, bf16[864,128]{1,0:T(8,128)(2,1)S(1)}, u32[]{:S(2)}, u32[]{:S(2)}) collective-permute-start(bf16[864,128]{1,0:T(8,128)(2,1)S(1)} %pad_maximum_fusion.refs_0_), channel_id=1, source_target_pairs={{0,16},{4,20},{8,24},{12,28},{16,0},{20,4},{24,8},{28,12},{1,17},{... | collective-permute-start | bytes 663560 | tf_op jit(solution)/shard_map/ppermute | solution.py:779
  16.2 10.6 %collective-permute-start.3 = (bf16[864,128]{1,0:T(8,128)(2,1)S(1)}, bf16[864,128]{1,0:T(8,128)(2,1)S(1)}, u32[]{:S(2)}, u32[]{:S(2)}) collective-permute-start(bf16[864,128]{1,0:T(8,128)(2,1)S(1)} %pad_maximum_fusion.refs_0_), channel_id=1, source_target_pairs={{0,8},{4,12},{8,0},{12,4},{16,24},{20,28},{24,16},{28,20},{1,9},{5... | collective-permute-start | bytes 663560 | tf_op jit(solution)/shard_map/ppermute | solution.py:779
  19.3 20.7 %copy-start.6 = (bf16[864,128]{1,0:T(8,128)(2,1)S(1)}, bf16[864,128]{1,0:T(8,128)(2,1)}, u32[]{:S(2)}) copy-start(bf16[864,128]{1,0:T(8,128)(2,1)} %copy-done.5) | copy-start | bytes 663556
  19.3 17.0 %collective-permute-start.12 = (bf16[576,128]{1,0:T(8,128)(2,1)}, bf16[576,128]{1,0:T(8,128)(2,1)S(1)}, u32[]{:S(2)}, u32[]{:S(2)}) collective-permute-start(bf16[576,128]{1,0:T(8,128)(2,1)} %pack.1), channel_id=1, source_target_pairs={{0,3},{1,0},{2,1},{3,2},{4,7},{5,4},{6,5},{7,6},{8,11},{9,8},{10,9... | collective-permute-start | bytes 442376 | tf_op jit(solution)/shard_map/ppermute | solution.py:775
  22.1 8.8 %collective-permute-start.10 = (bf16[576,128]{1,0:T(8,128)(2,1)}, bf16[576,128]{1,0:T(8,128)(2,1)S(1)}, u32[]{:S(2)}, u32[]{:S(2)}) collective-permute-start(bf16[576,128]{1,0:T(8,128)(2,1)} %pack.1), channel_id=1, source_target_pairs={{0,1},{1,2},{2,3},{3,0},{4,5},{5,6},{6,7},{7,4},{8,9},{9,10},{10,1... | collective-permute-start | bytes 442376 | tf_op jit(solution)/shard_map/ppermute | solution.py:775
  24.0 12.3 %collective-permute-start.11 = (bf16[576,128]{1,0:T(8,128)(2,1)}, bf16[576,128]{1,0:T(8,128)(2,1)S(1)}, u32[]{:S(2)}, u32[]{:S(2)}) collective-permute-start(bf16[576,128]{1,0:T(8,128)(2,1)} %pack.1), channel_id=1, source_target_pairs={{0,2},{1,3},{2,0},{3,1},{4,6},{5,7},{6,4},{7,5},{8,10},{9,11},{10,... | collective-permute-start | bytes 442376 | tf_op jit(solution)/shard_map/ppermute | solution.py:775
  26.7 12.2 %collective-permute-start.9 = (bf16[864,128]{1,0:T(8,128)(2,1)S(1)}, bf16[864,128]{1,0:T(8,128)(2,1)S(1)}, u32[]{:S(2)}, u32[]{:S(2)}) collective-permute-start(bf16[864,128]{1,0:T(8,128)(2,1)S(1)} %collective-permute-done.5.refs_3_), channel_id=1, source_target_pairs={{0,4},{4,0},{8,12},{12,8},{16,20},{20,16},{24,28},{28,24},{1,5},{5... | collective-permute-start | bytes 663560 | tf_op jit(solution)/shard_map/ppermute | solution.py:779
  26.8 12.7 %collective-permute-start.8 = (bf16[864,128]{1,0:T(8,128)(2,1)S(1)}, bf16[864,128]{1,0:T(8,128)(2,1)S(1)}, u32[]{:S(2)}, u32[]{:S(2)}) collective-permute-start(bf16[864,128]{1,0:T(8,128)(2,1)S(1)} %collective-permute-done.4.refs_2_), channel_id=1, source_target_pairs={{0,4},{4,0},{8,12},{12,8},{16,20},{20,16},{24,28},{28,24},{1,5},{5... | collective-permute-start | bytes 663560 | tf_op jit(solution)/shard_map/ppermute | solution.py:779
  30.9 9.1 %collective-permute-start.7 = (bf16[864,128]{1,0:T(8,128)(2,1)S(1)}, bf16[864,128]{1,0:T(8,128)(2,1)S(1)}, u32[]{:S(2)}, u32[]{:S(2)}) collective-permute-start(bf16[864,128]{1,0:T(8,128)(2,1)S(1)} %collective-permute-done.3.refs_1_), channel_id=1, source_target_pairs={{0,4},{4,0},{8,12},{12,8},{16,20},{20,16},{24,28},{28,24},{1,5},{5... | collective-permute-start | bytes 663560 | tf_op jit(solution)/shard_map/ppermute | solution.py:779
  36.3 19.5 %collective-permute-start.16 = (bf16[1280,128]{1,0:T(8,128)(2,1)S(1)}, bf16[1280,128]{1,0:T(8,128)(2,1)S(1)}, u32[]{:S(2)}, u32[]{:S(2)}) collective-permute-start(bf16[1280,128]{1,0:T(8,128)(2,1)S(1)} %bitcast.62), channel_id=1, source_target_pairs={{0,4},{4,0},{8,12},{12,8},{16,20},{20,16},{24,28},{28,24},{1,5},{5... | collective-permute-start | bytes 983048 | tf_op jit(solution)/shard_map/ppermute | solution.py:779
  36.4 13.1 %collective-permute-start.15 = (bf16[1280,128]{1,0:T(8,128)(2,1)S(1)}, bf16[1280,128]{1,0:T(8,128)(2,1)S(1)}, u32[]{:S(2)}, u32[]{:S(2)}) collective-permute-start(bf16[1280,128]{1,0:T(8,128)(2,1)S(1)} %bitcast.63), channel_id=1, source_target_pairs={{0,24},{4,28},{8,16},{12,20},{16,8},{20,12},{24,0},{28,4},{1,25},{... | collective-permute-start | bytes 983048 | tf_op jit(solution)/shard_map/ppermute | solution.py:779
  38.9 15.5 %collective-permute-start.14 = (bf16[1280,128]{1,0:T(8,128)(2,1)S(1)}, bf16[1280,128]{1,0:T(8,128)(2,1)S(1)}, u32[]{:S(2)}, u32[]{:S(2)}) collective-permute-start(bf16[1280,128]{1,0:T(8,128)(2,1)S(1)} %bitcast.64), channel_id=1, source_target_pairs={{0,16},{4,20},{8,24},{12,28},{16,0},{20,4},{24,8},{28,12},{1,17},{... | collective-permute-start | bytes 983048 | tf_op jit(solution)/shard_map/ppermute | solution.py:779
  39.5 15.0 %collective-permute-start.13 = (bf16[1280,128]{1,0:T(8,128)(2,1)S(1)}, bf16[1280,128]{1,0:T(8,128)(2,1)S(1)}, u32[]{:S(2)}, u32[]{:S(2)}) collective-permute-start(bf16[1280,128]{1,0:T(8,128)(2,1)S(1)} %bitcast.65), channel_id=1, source_target_pairs={{0,8},{4,12},{8,0},{12,4},{16,24},{20,28},{24,16},{28,20},{1,9},{5... | collective-permute-start | bytes 983048 | tf_op jit(solution)/shard_map/ppermute | solution.py:779
  40.0 19.3 %copy-start.17 = (bf16[5,256,512]{2,1,0:T(8,128)(2,1)S(1)}, bf16[5,256,512]{2,1,0:T(8,128)(2,1)}, u32[]{:S(2)}) copy-start(bf16[5,256,512]{2,1,0:T(8,128)(2,1)} %param.16) | copy-start | bytes 3932164
  54.6 3.0 %collective-permute-start.17 = (bf16[1280,128]{1,0:T(8,128)(2,1)S(1)}, bf16[1280,128]{1,0:T(8,128)(2,1)S(1)}, u32[]{:S(2)}, u32[]{:S(2)}) collective-permute-start(bf16[1280,128]{1,0:T(8,128)(2,1)S(1)} %get-tuple-element.106.refs_5_), channel_id=1, source_target_pairs={{0,4},{4,0},{8,12},{12,8},{16,20},{20,16},{24,28},{28,24},{1,5},{5... | collective-permute-start | bytes 983048 | tf_op jit(solution)/shard_map/ppermute | solution.py:779
  54.7 4.1 %collective-permute-start.18 = (bf16[1280,128]{1,0:T(8,128)(2,1)S(1)}, bf16[1280,128]{1,0:T(8,128)(2,1)S(1)}, u32[]{:S(2)}, u32[]{:S(2)}) collective-permute-start(bf16[1280,128]{1,0:T(8,128)(2,1)S(1)} %get-tuple-element.107.refs_6_), channel_id=1, source_target_pairs={{0,4},{4,0},{8,12},{12,8},{16,20},{20,16},{24,28},{28,24},{1,5},{5... | collective-permute-start | bytes 983048 | tf_op jit(solution)/shard_map/ppermute | solution.py:779
  55.2 4.1 %collective-permute-start.19 = (bf16[1280,128]{1,0:T(8,128)(2,1)S(1)}, bf16[1280,128]{1,0:T(8,128)(2,1)S(1)}, u32[]{:S(2)}, u32[]{:S(2)}) collective-permute-start(bf16[1280,128]{1,0:T(8,128)(2,1)S(1)} %get-tuple-element.108.refs_7_), channel_id=1, source_target_pairs={{0,4},{4,0},{8,12},{12,8},{16,20},{20,16},{24,28},{28,24},{1,5},{5... | collective-permute-start | bytes 983048 | tf_op jit(solution)/shard_map/ppermute | solution.py:779
  55.3 19.5 %collective-permute-start.23 = (bf16[1024,128]{1,0:T(8,128)(2,1)S(1)}, bf16[1024,128]{1,0:T(8,128)(2,1)S(1)}, u32[]{:S(2)}, u32[]{:S(2)}) collective-permute-start(bf16[1024,128]{1,0:T(8,128)(2,1)S(1)} %gate.4.refs_12_.refs_2_.refs_10_), channel_id=1, source_target_pairs={{0,4},{4,0},{8,12},{12,8},{16,20},{20,16},{24,28},{28,24},{1,5},{5... | collective-permute-start | bytes 786440 | tf_op jit(solution)/shard_map/ppermute | solution.py:779
  55.8 17.8 %collective-permute-start.22 = (bf16[1024,128]{1,0:T(8,128)(2,1)S(1)}, bf16[1024,128]{1,0:T(8,128)(2,1)S(1)}, u32[]{:S(2)}, u32[]{:S(2)}) collective-permute-start(bf16[1024,128]{1,0:T(8,128)(2,1)S(1)} %gate.4.refs_12_.refs_2_.refs_10_), channel_id=1, source_target_pairs={{0,24},{4,28},{8,16},{12,20},{16,8},{20,12},{24,0},{28,4},{1,25},{... | collective-permute-start | bytes 786440 | tf_op jit(solution)/shard_map/ppermute | solution.py:779
  57.5 16.1 %collective-permute-start.21 = (bf16[1024,128]{1,0:T(8,128)(2,1)S(1)}, bf16[1024,128]{1,0:T(8,128)(2,1)S(1)}, u32[]{:S(2)}, u32[]{:S(2)}) collective-permute-start(bf16[1024,128]{1,0:T(8,128)(2,1)S(1)} %gate.4.refs_12_.refs_2_.refs_10_), channel_id=1, source_target_pairs={{0,16},{4,20},{8,24},{12,28},{16,0},{20,4},{24,8},{28,12},{1,17},{... | collective-permute-start | bytes 786440 | tf_op jit(solution)/shard_map/ppermute | solution.py:779
  58.8 14.8 %collective-permute-start.20 = (bf16[1024,128]{1,0:T(8,128)(2,1)S(1)}, bf16[1024,128]{1,0:T(8,128)(2,1)S(1)}, u32[]{:S(2)}, u32[]{:S(2)}) collective-permute-start(bf16[1024,128]{1,0:T(8,128)(2,1)S(1)} %gate.4.refs_12_.refs_2_.refs_10_), channel_id=1, source_target_pairs={{0,8},{4,12},{8,0},{12,4},{16,24},{20,28},{24,16},{28,20},{1,9},{5... | collective-permute-start | bytes 786440 | tf_op jit(solution)/shard_map/ppermute | solution.py:779
  73.7 1.6 %collective-permute-start.24 = (bf16[1024,128]{1,0:T(8,128)(2,1)S(1)}, bf16[1024,128]{1,0:T(8,128)(2,1)S(1)}, u32[]{:S(2)}, u32[]{:S(2)}) collective-permute-start(bf16[1024,128]{1,0:T(8,128)(2,1)S(1)} %get-tuple-element.111.refs_3_), channel_id=1, source_target_pairs={{0,4},{4,0},{8,12},{12,8},{16,20},{20,16},{24,28},{28,24},{1,5},{5... | collective-permute-start | bytes 786440 | tf_op jit(solution)/shard_map/ppermute | solution.py:779
  73.8 1.9 %collective-permute-start.25 = (bf16[1024,128]{1,0:T(8,128)(2,1)S(1)}, bf16[1024,128]{1,0:T(8,128)(2,1)S(1)}, u32[]{:S(2)}, u32[]{:S(2)}) collective-permute-start(bf16[1024,128]{1,0:T(8,128)(2,1)S(1)} %get-tuple-element.112.refs_4_), channel_id=1, source_target_pairs={{0,4},{4,0},{8,12},{12,8},{16,20},{20,16},{24,28},{28,24},{1,5},{5... | collective-permute-start | bytes 786440 | tf_op jit(solution)/shard_map/ppermute | solution.py:779
  74.3 1.8 %collective-permute-start.26 = (bf16[1024,128]{1,0:T(8,128)(2,1)S(1)}, bf16[1024,128]{1,0:T(8,128)(2,1)S(1)}, u32[]{:S(2)}, u32[]{:S(2)}) collective-permute-start(bf16[1024,128]{1,0:T(8,128)(2,1)S(1)} %get-tuple-element.113.refs_5_), channel_id=1, source_target_pairs={{0,4},{4,0},{8,12},{12,8},{16,20},{20,16},{24,28},{28,24},{1,5},{5... | collective-permute-start | bytes 786440 | tf_op jit(solution)/shard_map/ppermute | solution.py:779
  74.3 19.1 %collective-permute-start.27 = (bf16[4,1024,128]{2,1,0:T(8,128)(2,1)S(1)}, bf16[4,1024,128]{2,1,0:T(8,128)(2,1)S(1)}, u32[]{:S(2)}, u32[]{:S(2)}) collective-permute-start(bf16[4,1024,128]{2,1,0:T(8,128)(2,1)S(1)} %get-tuple-element.130), channel_id=1, source_target_pairs={{0,4},{4,0},{8,12},{12,8},{16,20},{20,16},{24,28},{28,24},{1,5},{5... | collective-permute-start | bytes 3145736 | tf_op jit(solution)/shard_map/ppermute | solution.py:779
  88.7 4.7 %collective-permute-start.28 = (bf16[4,1024,128]{2,1,0:T(8,128)(2,1)S(1)}, bf16[4,1024,128]{2,1,0:T(8,128)(2,1)S(1)}, u32[]{:S(2)}, u32[]{:S(2)}) collective-permute-start(bf16[4,1024,128]{2,1,0:T(8,128)(2,1)S(1)} %get-tuple-element.131), channel_id=1, source_target_pairs={{0,4},{4,0},{8,12},{12,8},{16,20},{20,16},{24,28},{28,24},{1,5},{5... | collective-permute-start | bytes 3145736 | tf_op jit(solution)/shard_map/ppermute | solution.py:779
  94.4 14.3 %collective-permute-start.29 = (bf16[2,1024,128]{2,1,0:T(8,128)(2,1)S(1)}, bf16[2,1024,128]{2,1,0:T(8,128)(2,1)S(1)}, u32[]{:S(2)}, u32[]{:S(2)}) collective-permute-start(bf16[2,1024,128]{2,1,0:T(8,128)(2,1)S(1)} %get-tuple-element.140), channel_id=1, source_target_pairs={{0,8},{4,12},{8,0},{12,4},{16,24},{20,28},{24,16},{28,20},{1,9},{5... | collective-permute-start | bytes 1572872 | tf_op jit(solution)/shard_map/ppermute | solution.py:779
  96.0 13.9 %collective-permute-start.30 = (bf16[2,1024,128]{2,1,0:T(8,128)(2,1)S(1)}, bf16[2,1024,128]{2,1,0:T(8,128)(2,1)S(1)}, u32[]{:S(2)}, u32[]{:S(2)}) collective-permute-start(bf16[2,1024,128]{2,1,0:T(8,128)(2,1)S(1)} %get-tuple-element.142), channel_id=1, source_target_pairs={{0,16},{4,20},{8,24},{12,28},{16,0},{20,4},{24,8},{28,12},{1,17},{... | collective-permute-start | bytes 1572872 | tf_op jit(solution)/shard_map/ppermute | solution.py:779
  110.9 2.8 %collective-permute-start.31 = (bf16[4,1072,128]{2,1,0:T(8,128)(2,1)S(1)}, bf16[4,1072,128]{2,1,0:T(8,128)(2,1)S(1)}, u32[]{:S(2)}, u32[]{:S(2)}) collective-permute-start(bf16[4,1072,128]{2,1,0:T(8,128)(2,1)S(1)} %get-tuple-element.145), channel_id=1, source_target_pairs={{0,4},{4,0},{8,12},{12,8},{16,20},{20,16},{24,28},{28,24},{1,5},{5... | collective-permute-start | bytes 3293192 | tf_op jit(solution)/shard_map/ppermute | solution.py:779
  111.0 10.1 %collective-permute-start.38 = (bf16[1024,128]{1,0:T(8,128)(2,1)S(1)}, bf16[1024,128]{1,0:T(8,128)(2,1)S(1)}, u32[]{:S(2)}, u32[]{:S(2)}) collective-permute-start(bf16[1024,128]{1,0:T(8,128)(2,1)S(1)} %get-tuple-element.157), channel_id=1, source_target_pairs={{0,16},{4,20},{8,24},{12,28},{16,0},{20,4},{24,8},{28,12},{1,17},{... | collective-permute-start | bytes 786440 | tf_op jit(solution)/shard_map/ppermute | solution.py:779
  111.8 9.3 %collective-permute-start.39 = (bf16[1024,128]{1,0:T(8,128)(2,1)S(1)}, bf16[1024,128]{1,0:T(8,128)(2,1)S(1)}, u32[]{:S(2)}, u32[]{:S(2)}) collective-permute-start(bf16[1024,128]{1,0:T(8,128)(2,1)S(1)} %get-tuple-element.159), channel_id=1, source_target_pairs={{0,8},{4,12},{8,0},{12,4},{16,24},{20,28},{24,16},{28,20},{1,9},{5... | collective-permute-start | bytes 786440 | tf_op jit(solution)/shard_map/ppermute | solution.py:779
  114.5 12.4 %collective-permute-start.32 = (bf16[1072,128]{1,0:T(8,128)(2,1)S(1)}, bf16[1072,128]{1,0:T(8,128)(2,1)S(1)}, u32[]{:S(2)}, u32[]{:S(2)}) collective-permute-start(bf16[1072,128]{1,0:T(8,128)(2,1)S(1)} %get-tuple-element.148), channel_id=1, source_target_pairs={{0,8},{4,12},{8,0},{12,4},{16,24},{20,28},{24,16},{28,20},{1,9},{5... | collective-permute-start | bytes 823304 | tf_op jit(solution)/shard_map/ppermute | solution.py:779
  115.1 14.6 %collective-permute-start.33 = (bf16[1072,128]{1,0:T(8,128)(2,1)S(1)}, bf16[1072,128]{1,0:T(8,128)(2,1)S(1)}, u32[]{:S(2)}, u32[]{:S(2)}) collective-permute-start(bf16[1072,128]{1,0:T(8,128)(2,1)S(1)} %get-tuple-element.149), channel_id=1, source_target_pairs={{0,16},{4,20},{8,24},{12,28},{16,0},{20,4},{24,8},{28,12},{1,17},{... | collective-permute-start | bytes 823304 | tf_op jit(solution)/shard_map/ppermute | solution.py:779
  116.5 16.1 %collective-permute-start.34 = (bf16[1072,128]{1,0:T(8,128)(2,1)S(1)}, bf16[1072,128]{1,0:T(8,128)(2,1)S(1)}, u32[]{:S(2)}, u32[]{:S(2)}) collective-permute-start(bf16[1072,128]{1,0:T(8,128)(2,1)S(1)} %get-tuple-element.150), channel_id=1, source_target_pairs={{0,24},{4,28},{8,16},{12,20},{16,8},{20,12},{24,0},{28,4},{1,25},{... | collective-permute-start | bytes 823304 | tf_op jit(solution)/shard_map/ppermute | solution.py:779
  121.8 14.8 %collective-permute-start.40 = (bf16[512,128]{1,0:T(8,128)(2,1)S(1)}, bf16[512,128]{1,0:T(8,128)(2,1)S(1)}, u32[]{:S(2)}, u32[]{:S(2)}) collective-permute-start(bf16[512,128]{1,0:T(8,128)(2,1)S(1)} %get-tuple-element.161), channel_id=1, source_target_pairs={{0,1},{1,2},{2,3},{3,0},{4,5},{5,6},{6,7},{7,4},{8,9},{9,10},{10,1... | collective-permute-start | bytes 393224 | tf_op jit(solution)/shard_map/ppermute | solution.py:775
  121.8 15.4 %collective-permute-start.41 = (bf16[512,128]{1,0:T(8,128)(2,1)S(1)}, bf16[512,128]{1,0:T(8,128)(2,1)S(1)}, u32[]{:S(2)}, u32[]{:S(2)}) collective-permute-start(bf16[512,128]{1,0:T(8,128)(2,1)S(1)} %get-tuple-element.162), channel_id=1, source_target_pairs={{0,2},{1,3},{2,0},{3,1},{4,6},{5,7},{6,4},{7,5},{8,10},{9,11},{10,... | collective-permute-start | bytes 393224 | tf_op jit(solution)/shard_map/ppermute | solution.py:775
  126.9 10.4 %copy-start.11 = (f32[256,128]{1,0:T(8,128)S(1)}, f32[256,128]{1,0:T(8,128)}, u32[]{:S(2)}) copy-start(f32[256,128]{1,0:T(8,128)} %refs_8_.1) | copy-start | bytes 393220
  126.9 10.3 %collective-permute-start.42 = (bf16[512,128]{1,0:T(8,128)(2,1)S(1)}, bf16[512,128]{1,0:T(8,128)(2,1)S(1)}, u32[]{:S(2)}, u32[]{:S(2)}) collective-permute-start(bf16[512,128]{1,0:T(8,128)(2,1)S(1)} %get-tuple-element.163), channel_id=1, source_target_pairs={{0,3},{1,0},{2,1},{3,2},{4,7},{5,4},{6,5},{7,6},{8,11},{9,8},{10,9... | collective-permute-start | bytes 393224 | tf_op jit(solution)/shard_map/ppermute | solution.py:775
  133.3 9.4 %collective-permute-start.35 = (bf16[256,128]{1,0:T(8,128)(2,1)S(1)}, bf16[256,128]{1,0:T(8,128)(2,1)S(1)}, u32[]{:S(2)}, u32[]{:S(2)}) collective-permute-start(bf16[256,128]{1,0:T(8,128)(2,1)S(1)} %get-tuple-element.154), channel_id=1, source_target_pairs={{0,1},{1,2},{2,3},{3,0},{4,5},{5,6},{6,7},{7,4},{8,9},{9,10},{10,1... | collective-permute-start | bytes 196616 | tf_op jit(solution)/shard_map/ppermute | solution.py:775
  133.4 9.4 %collective-permute-start.36 = (bf16[256,128]{1,0:T(8,128)(2,1)S(1)}, bf16[256,128]{1,0:T(8,128)(2,1)S(1)}, u32[]{:S(2)}, u32[]{:S(2)}) collective-permute-start(bf16[256,128]{1,0:T(8,128)(2,1)S(1)} %get-tuple-element.155), channel_id=1, source_target_pairs={{0,2},{1,3},{2,0},{3,1},{4,6},{5,7},{6,4},{7,5},{8,10},{9,11},{10,... | collective-permute-start | bytes 196616 | tf_op jit(solution)/shard_map/ppermute | solution.py:775
  136.6 6.2 %collective-permute-start.37 = (bf16[256,128]{1,0:T(8,128)(2,1)S(1)}, bf16[256,128]{1,0:T(8,128)(2,1)S(1)}, u32[]{:S(2)}, u32[]{:S(2)}) collective-permute-start(bf16[256,128]{1,0:T(8,128)(2,1)S(1)} %get-tuple-element.156), channel_id=1, source_target_pairs={{0,3},{1,0},{2,1},{3,2},{4,7},{5,4},{6,5},{7,6},{8,11},{9,8},{10,9... | collective-permute-start | bytes 196616 | tf_op jit(solution)/shard_map/ppermute | solution.py:775
  138.4 16.7 %copy-start.15 = (f32[4,512]{1,0:T(4,128)S(1)}, f32[4,512]{1,0:T(4,128)}, u32[]{:S(2)}) copy-start(f32[4,512]{1,0:T(4,128)} %lf_ref.1) | copy-start | bytes 24580
  138.4 16.6 %copy-start.16 = (f32[4,512]{1,0:T(4,128)S(1)}, f32[4,512]{1,0:T(4,128)}, u32[]{:S(2)}) copy-start(f32[4,512]{1,0:T(4,128)} %ls_ref.1) | copy-start | bytes 24580
  (13 other events, 87.3 us)

commit v4 on v3

--- a/solution.py
+++ b/solution.py
@@ -64,7 +64,7 @@
 
 
 def cost(flops, nbytes, trans=0):
-    return pl.CostEstimate(flops=int(flops), bytes_accessed=int(nbytes), transcendentals=int(trans))
+    return pl.CostEstimate(flops=int(flops * 0.03), bytes_accessed=int(nbytes * 0.03), transcendentals=int(trans))
 
 
 def norm_parts(values):
@@ -799,7 +799,10 @@
 
 
 def gather_cut(piece, cuts, z, ng):
-    came = [(piece, z)] + [(shift(piece, by, ng), (z - by) % ng) for by in range(1, ng)]
+    near, far = shift(piece, 1, ng), shift(piece, ng - 1, ng)
+    came = [
+        (piece, z), (near, (z - 1) % ng), (far, (z + 1) % ng), (shift(near, 1, ng), (z - 2) % ng)
+    ]
     outs = []
     for start, stop in cuts:
         out = jnp.zeros((ng, stop - start, piece.shape[1]), piece.dtype)
@@ -910,7 +913,7 @@
             out_shape=pack_out,
             cost_estimate=cost(1e6, 1e6),
             name="pack",
-        )(attn_master, up_master, down_master, attn_bufs[places])
+        )(attn_master, up_master, down_master, attn_piece)
         mlp_z, late_z = gather_cut(piece, [(0, rows + size), (rows + size, rows + 2 * size)], z, ng)
         mlp_own = gather_plane(mlp_z, nb)
         dep = mlp_z

time: 156 us -> 147 us (0.942)
  waiting for transfers between devices: 25.2 us -> 14.9 us
  starting transfers between devices: 41.5 us -> 44.8 us
  local copies, waits for them, and re-layouts: 5.71 us -> 3.91 us
    ppermute x12, waiting for transfers between devices: 9.06 us -> 1.87 us  [shift(): lax.ppermute(values, 'group', [(j, (j + by) % ng) for j in range(ng)])]
    ppermute x31, waiting for transfers between devices: 16.1 us -> 13.1 us  [cross(): return lax.ppermute(values, 'blk', [(j, j ^ bit) for j in range(nb)])]
    unnamed x36 -> x32, local copies, waits for them, and re-layouts: 2.77 us -> 0.07 us
    ppermute x12, starting transfers between devices: 19.9 us -> 22.6 us  [shift(): lax.ppermute(values, 'group', [(j, (j + by) % ng) for j in range(ng)])]
  transfers between devices with their start and end apart: 43 -> 43, of which waited for: 14 -> 14; matrix products, arithmetic and copies ran while one was open for 2% -> 2% of each run, Pallas kernels for 43% -> 45%
where the time goes in v4:
time: 147 us
  Pallas kernels  70.3 us (48%)
  starting transfers between devices  44.8 us (30%)
  waiting for transfers between devices  14.9 us (10%)
  blocking collectives  11.3 us (8%)
  local copies, waits for them, and re-layouts  3.91 us (3%)
    pallas_call x2, Pallas kernels, body(): pl.pallas_call(functools.partial(mlp_kernel, mlp_dims, fast, places, firs...  27 us
    ppermute x12, starting transfers between devices, shift(): lax.ppermute(values, 'group', [(j, (j + by) % ng) for j in range(ng)])  22.6 us
    ppermute x31, starting transfers between devices, cross(): return lax.ppermute(values, 'blk', [(j, j ^ bit) for j in range(nb)])  22.2 us
    ppermute x31, waiting for transfers between devices, cross(): return lax.ppermute(values, 'blk', [(j, j ^ bit) for j in range(nb)])  13.1 us
    all_to_all x1, blocking collectives, body(): every = lax.all_to_all(message, ('blk', 'group'), 0, 0, tiled=True)  11.3 us
    pallas_call x13, Pallas kernels, flat(): pl.pallas_call(call, in_specs=[scalars()] * scalar + [whole()] * (len(arg...  9.7 us
    pallas_call x1, Pallas kernels, body(): pl.pallas_call(functools.partial(forward_kernel, dims, fast, places), gri...  9.26 us
    pallas_call x1, Pallas kernels, body(): pl.pallas_call(functools.partial(backward_kernel, places), grid=(seqs,),...  8.16 us
  transfers between devices with their start and end apart: 43, of which 14 were waited for; matrix products, arithmetic and copies ran while one was open for 2% of the time, Pallas kernels for 45%

profile of v4, /device:TPU:0, one launch (start us, length us, event | category | flops | bytes accessed | tf_op | source)
XLA Modules:
  0.0 146.5 jit_solution(14559025398800559899)
XLA Ops:
  0.7 1.0 slice.71
  1.7 5.1 %collective-permute-start.2 = (bf16[192,128]{1,0:T(8,128)(2,1)S(1)}, bf16[192,128]{1,0:T(8,128)(2,1)S(1)}, u32[]{:S(2)}, u32[]{:S(2)}) collective-permute-start(bf16[192,128]{1,0:T(8,128)(2,1)S(1)} %bitcast.76), channel_id=1, source_target_pairs={{0,3},{1,0},{2,1},{3,2},{4,7},{5,4},{6,5},{7,6},{8,11},{9,8},{10,9... | collective-permute-start | bytes 147464 | tf_op jit(solution)/shard_map/ppermute | solution.py:775
  6.8 1.0 collective-permute-start
  7.8 1.8 %pack.1 = bf16[576,128]{1,0:T(8,128)(2,1)} custom-call(f32[4,64,128]{2,1,0:T(8,128)} %am_ref.1, f32[64,512]{1,0:T(8,128)} %um_ref.1, f32[256,128]{1,0:T(8,128)} %dm_ref.1, bf16[192,128]{1,0:T(8,128)(2,1)} %bitcast.79), custom_call_target="tpu_custom_call" | custom-call | flops 30000 | bytes 30000 | tf_op jit(solution)/shard_map/pack/pallas_call | solution.py:905
  9.6 2.8 %collective-permute-start.11 = (bf16[576,128]{1,0:T(8,128)(2,1)}, bf16[576,128]{1,0:T(8,128)(2,1)S(1)}, u32[]{:S(2)}, u32[]{:S(2)}) collective-permute-start(bf16[576,128]{1,0:T(8,128)(2,1)} %pack.1), channel_id=1, source_target_pairs={{0,3},{1,0},{2,1},{3,2},{4,7},{5,4},{6,5},{7,6},{8,11},{9,8},{10,9... | collective-permute-start | bytes 442376 | tf_op jit(solution)/shard_map/ppermute | solution.py:775
  12.4 0.9 fusion.3
  13.4 0.8 bitcast_dynamic-update-slice_fusion.3
  14.3 2.6 %prep.1 = (bf16[5,256,512]{2,1,0:T(8,128)(2,1)S(1)}, bf16[96,128]{1,0:T(8,128)(2,1)S(1)}) custom-call(s32[7]{0:T(128)S(1)} %pad_add_fusion.scal_ref, bf16[5,256,512]{2,1,0:T(8,128)(2,1)S(1)} %copy-done.1, f32[4,512]{1,0:T(4,128)S(1)} %copy-done.5), custom_call_target="tpu_custom_call" | custom-call | flops 1200000 | bytes 78643 | tf_op jit(solution)/shard_map/prep/pallas_call | solution.py:879
  17.1 2.5 %collective-permute-start.5 = (bf16[864,128]{1,0:T(8,128)(2,1)S(1)}, bf16[864,128]{1,0:T(8,128)(2,1)S(1)}, u32[]{:S(2)}, u32[]{:S(2)}) collective-permute-start(bf16[864,128]{1,0:T(8,128)(2,1)S(1)} %pad_maximum_fusion.refs_0_), channel_id=1, source_target_pairs={{0,24},{4,28},{8,16},{12,20},{16,8},{20,12},{24,0},{28,4},{1,25},{... | collective-permute-start | bytes 663560 | tf_op jit(solution)/shard_map/ppermute | solution.py:779
  20.1 1.0 collective-permute-start.3
  21.1 1.3 collective-permute-start.12
  22.4 3.9 %collective-permute-done.5.refs_3_ = bf16[864,128]{1,0:T(8,128)(2,1)S(1)} collective-permute-done((bf16[864,128]{1,0:T(8,128)(2,1)S(1)}, bf16[864,128]{1,0:T(8,128)(2,1)S(1)}, u32[]{:S(2)}, u32[]{:S(2)}) %collective-permute-start.5) | collective-permute-done | bytes 221216 | tf_op jit(solution)/shard_map/ppermute | solution.py:779
  26.3 1.8 %collective-permute-done.12 = bf16[576,128]{1,0:T(8,128)(2,1)S(1)} collective-permute-done((bf16[576,128]{1,0:T(8,128)(2,1)S(1)}, bf16[576,128]{1,0:T(8,128)(2,1)S(1)}, u32[]{:S(2)}, u32[]{:S(2)}) %collective-permute-start.12) | collective-permute-done | bytes 147488 | tf_op jit(solution)/shard_map/ppermute | solution.py:775
  28.2 2.5 %collective-permute-start.15 = (bf16[1280,128]{1,0:T(8,128)(2,1)S(1)}, bf16[1280,128]{1,0:T(8,128)(2,1)S(1)}, u32[]{:S(2)}, u32[]{:S(2)}) collective-permute-start(bf16[1280,128]{1,0:T(8,128)(2,1)S(1)} %bitcast.63), channel_id=1, source_target_pairs={{0,24},{4,28},{8,16},{12,20},{16,8},{20,12},{24,0},{28,4},{1,25},{... | collective-permute-start | bytes 983048 | tf_op jit(solution)/shard_map/ppermute | solution.py:779
  31.2 0.8 collective-permute-start.13
  32.1 0.9 fusion.7
  33.6 0.9 collective-permute-done.8.refs_6_
  34.8 9.3 %forward.1 = (bf16[5,256,512]{2,1,0:T(8,128)(2,1)S(1)}, bf16[5,256,512]{2,1,0:T(8,128)(2,1)S(1)}, bf16[5,256,512]{2,1,0:T(8,128)(2,1)S(1)}, bf16[5,16,512]{2,1,0...) custom-call(s32[7]{0:T(128)S(1)} %pad_add_fusion.scal_ref, ...), custom_call_target="tpu_custom_call" | custom-call | flops 240000000 | bytes 275251 | tf_op jit(solution)/shard_map/forward/pallas_call | solution.py:936
  45.6 1.8 %collective-permute-start.22 = (bf16[1024,128]{1,0:T(8,128)(2,1)S(1)}, bf16[1024,128]{1,0:T(8,128)(2,1)S(1)}, u32[]{:S(2)}, u32[]{:S(2)}) collective-permute-start(bf16[1024,128]{1,0:T(8,128)(2,1)S(1)} %gate.4.refs_12_.refs_2_.refs_10_), channel_id=1, source_target_pairs={{0,24},{4,28},{8,16},{12,20},{16,8},{20,12},{24,0},{28,4},{1,25},{... | collective-permute-start | bytes 786440 | tf_op jit(solution)/shard_map/ppermute | solution.py:779
  47.4 1.4 collective-permute-start.21
  49.2 14.3 %mlp.2 = (bf16[1280,512]{1,0:T(8,128)(2,1)S(1)}, bf16[1280,512]{1,0:T(8,128)(2,1)S(1)}, bf16[512,512]{1,0:T(8,128)(2,1)S(1)}, f32[8,128]{1,0:T(8,128)S(1)}, bf16...) custom-call(s32[7]{0:T(128)S(1)} %pad_add_fusion.scal_ref, ...), custom_call_target="tpu_custom_call" | custom-call | flops 270000000 | bytes 393216 | tf_op jit(solution)/shard_map/mlp/pallas_call | solution.py:1000
  66.0 12.7 %mlp.3 = (bf16[1280,512]{1,0:T(8,128)(2,1)}, bf16[1280,512]{1,0:T(8,128)(2,1)S(1)}, bf16[4,1024,128]{2,1,0:T(8,128)(2,1)S(1)}, bf16[4,1024,128]{2,1,0:T(8,128)(2,1)S(1)}) custom-call(s32[7]{0:T(128)S(1)} %pad_add_fusion.scal_ref, bf16[1280,512]{1,0:T(8,128)(2,1)S(1)} %get-tuple-element.109.refs_0_, bf16[1280,512]{1,0:T(8,128)(2,1)S(1)} %bitcast.59, ...), custom_call_target="tpu_custom_call" | custom-call | flops 270000000 | bytes 393216 | tf_op jit(solution)/shard_map/mlp/pallas_call | solution.py:1000
  79.1 2.3 %collective-permute-done.28.refs_3_ = bf16[4,1024,128]{2,1,0:T(8,128)(2,1)S(1)} collective-permute-done((bf16[4,1024,128]{2,1,0:T(8,128)(2,1)S(1)}, bf16[4,1024,128]{2,1,0:T(8,128)(2,1)S(1)}, u32[]{:S(2)}, u32[]{:S(2)}) %collective-permute-start.28) | collective-permute-done | bytes 1048608 | tf_op jit(solution)/shard_map/ppermute | solution.py:779
  81.4 1.0 halves.1
  82.4 1.7 %collective-permute-start.29 = (bf16[2,1024,128]{2,1,0:T(8,128)(2,1)S(1)}, bf16[2,1024,128]{2,1,0:T(8,128)(2,1)S(1)}, u32[]{:S(2)}, u32[]{:S(2)}) collective-permute-start(bf16[2,1024,128]{2,1,0:T(8,128)(2,1)S(1)} %get-tuple-element.140), channel_id=1, source_target_pairs={{0,8},{4,12},{8,0},{12,4},{16,24},{20,28},{24,16},{28,20},{1,9},{5... | collective-permute-start | bytes 1572872 | tf_op jit(solution)/shard_map/ppermute | solution.py:779
  84.8 4.5 %middle.1 = (bf16[1280,512]{1,0:T(8,128)(2,1)S(1)}, bf16[1280,512]{1,0:T(8,128)(2,1)S(1)}, f32[512,512]{1,0:T(8,128)S(1)}, f32[8,512]{1,0:T(8,128)S(1)}) custom-call(bf16[1280,512]{1,0:T(8,128)(2,1)S(1)} %get-tuple-element.118.gm_ref, bf16[1280,512]{1,0:T(8,128)(2,1)S(1)} %bitcast.60, bf16[1280,512]{1,0:T(8,128)(2,1)S(1)} %get-tuple-element.114.refs_11_.x2_ref, ...), custom_call_target="tpu_custom_call" | custom-call | flops 90000000 | bytes 275251 | tf_op jit(solution)/shard_map/middle/pallas_call | solution.py:1023
  89.3 8.2 %backward.1 = (bf16[5,256,1536]{2,1,0:T(8,128)(2,1)S(1)}, bf16[5,16,512]{2,1,0:T(8,128)(2,1)S(1)}, bf16[5,16,512]{2,1,0:T(8,128)(2,1)S(1)}, f32[2,4,48,128]{3,2,1,0:T(8,128)S(1)}) custom-call(s32[7]{0:T(128)S(1)} %pad_add_fusion.scal_ref, bf16[5,256,512]{2,1,0:T(8,128)(2,1)S(1)} %bitcast.69, bf16[5,256,512]{2,1,0:T(8,128)(2,1)S(1)} %get-tuple-element.121.q_ref, ...), custom_call_target="tpu_custom_call" | custom-call | flops 420000000 | bytes 471859 | tf_op jit(solution)/shard_map/backward/pallas_call | solution.py:1051
  97.4 2.5 %grads.1.dw_ref = f32[512,1536]{1,0:T(8,128)S(1)} custom-call(bf16[1280,512]{1,0:T(8,128)(2,1)S(1)} %bitcast.62, bf16[1280,1536]{1,0:T(8,128)(2,1)S(1)} %bitcast.57, bf16[80,512]{1,0:T(8,128)(2,1)S(1)} %bitcast.72, bf16[80,512]{1,0:T(8,128)(2,1)S(1)} %bitcast.73, bf16[80,512]{1,0:T(8,128)(2,1)S(1)} %bitcast.74), custom_call_target="tpu_custom_call" | custom-call | flops 30000 | bytes 3000 | tf_op jit(solution)/shard_map/grads/pallas_call | solution.py:863
  100.2 0.9 cut.1
  101.1 1.5 %collective-permute-start.38 = (bf16[1024,128]{1,0:T(8,128)(2,1)S(1)}, bf16[1024,128]{1,0:T(8,128)(2,1)S(1)}, u32[]{:S(2)}, u32[]{:S(2)}) collective-permute-start(bf16[1024,128]{1,0:T(8,128)(2,1)S(1)} %get-tuple-element.157), channel_id=1, source_target_pairs={{0,16},{4,20},{8,24},{12,28},{16,0},{20,4},{24,8},{28,12},{1,17},{... | collective-permute-start | bytes 786440 | tf_op jit(solution)/shard_map/ppermute | solution.py:779
  103.0 0.9 collective-permute-done.31.refs_1_
  103.8 0.8 spread.1
  104.6 1.3 collective-permute-start.32
  106.5 1.7 %collective-permute-start.34 = (bf16[1072,128]{1,0:T(8,128)(2,1)S(1)}, bf16[1072,128]{1,0:T(8,128)(2,1)S(1)}, u32[]{:S(2)}, u32[]{:S(2)}) collective-permute-start(bf16[1072,128]{1,0:T(8,128)(2,1)S(1)} %get-tuple-element.150), channel_id=1, source_target_pairs={{0,24},{4,28},{8,16},{12,20},{16,8},{20,12},{24,0},{28,4},{1,25},{... | collective-permute-start | bytes 823304 | tf_op jit(solution)/shard_map/ppermute | solution.py:779
  108.2 3.0 %project.1.refs_4_.grad_ref = bf16[5,256,512]{2,1,0:T(8,128)(2,1)S(1)} custom-call(bf16[5,256,1536]{2,1,0:T(8,128)(2,1)S(1)} %get-tuple-element.133.dqkv_ref, bf16[512,1536]{1,0:T(8,128)(2,1)S(1)} %get-tuple-element.127.w_ref, f32[1072,128]{1,0:T(8,128)S(1)} %get-tuple-element.146.dep_ref.refs_0_), custom_call_target="tpu_custom_call" | custom-call | flops 90000000 | bytes 157286 | tf_op jit(solution)/shard_map/project/pallas_call | solution.py:1116
  112.4 1.6 %collective-permute-start.40 = (bf16[512,128]{1,0:T(8,128)(2,1)S(1)}, bf16[512,128]{1,0:T(8,128)(2,1)S(1)}, u32[]{:S(2)}, u32[]{:S(2)}) collective-permute-start(bf16[512,128]{1,0:T(8,128)(2,1)S(1)} %get-tuple-element.161), channel_id=1, source_target_pairs={{0,1},{1,2},{2,3},{3,0},{4,5},{5,6},{6,7},{7,4},{8,9},{9,10},{10,1... | collective-permute-start | bytes 393224 | tf_op jit(solution)/shard_map/ppermute | solution.py:775
  114.0 2.7 %collective-permute-start.41 = (bf16[512,128]{1,0:T(8,128)(2,1)S(1)}, bf16[512,128]{1,0:T(8,128)(2,1)S(1)}, u32[]{:S(2)}, u32[]{:S(2)}) collective-permute-start(bf16[512,128]{1,0:T(8,128)(2,1)S(1)} %get-tuple-element.162), channel_id=1, source_target_pairs={{0,2},{1,3},{2,0},{3,1},{4,6},{5,7},{6,4},{7,5},{8,10},{9,11},{10,... | collective-permute-start | bytes 393224 | tf_op jit(solution)/shard_map/ppermute | solution.py:775
  116.7 1.0 collective-permute-done.32.refs_1_
  117.7 3.7 %collective-permute-start.42 = (bf16[512,128]{1,0:T(8,128)(2,1)S(1)}, bf16[512,128]{1,0:T(8,128)(2,1)S(1)}, u32[]{:S(2)}, u32[]{:S(2)}) collective-permute-start(bf16[512,128]{1,0:T(8,128)(2,1)S(1)} %get-tuple-element.163), channel_id=1, source_target_pairs={{0,3},{1,0},{2,1},{3,2},{4,7},{5,4},{6,5},{7,6},{8,11},{9,8},{10,9... | collective-permute-start | bytes 393224 | tf_op jit(solution)/shard_map/ppermute | solution.py:775
  121.4 1.4 collective-permute-done.34.refs_3_
  122.8 0.7 collect.2
  123.5 1.7 %collective-permute-start.35 = (bf16[256,128]{1,0:T(8,128)(2,1)S(1)}, bf16[256,128]{1,0:T(8,128)(2,1)S(1)}, u32[]{:S(2)}, u32[]{:S(2)}) collective-permute-start(bf16[256,128]{1,0:T(8,128)(2,1)S(1)} %get-tuple-element.154), channel_id=1, source_target_pairs={{0,1},{1,2},{2,3},{3,0},{4,5},{5,6},{6,7},{7,4},{8,9},{9,10},{10,1... | collective-permute-start | bytes 196616 | tf_op jit(solution)/shard_map/ppermute | solution.py:775
  125.1 2.7 %collective-permute-start.36 = (bf16[256,128]{1,0:T(8,128)(2,1)S(1)}, bf16[256,128]{1,0:T(8,128)(2,1)S(1)}, u32[]{:S(2)}, u32[]{:S(2)}) collective-permute-start(bf16[256,128]{1,0:T(8,128)(2,1)S(1)} %get-tuple-element.155), channel_id=1, source_target_pairs={{0,2},{1,3},{2,0},{3,1},{4,6},{5,7},{6,4},{7,5},{8,10},{9,11},{10,... | collective-permute-start | bytes 196616 | tf_op jit(solution)/shard_map/ppermute | solution.py:775
  127.9 1.1 mlp_step.1
  129.1 4.4 %input.1 = (f32[5,256,512]{2,1,0:T(8,128)}, f32[8,512]{1,0:T(8,128)S(1)}) custom-call(s32[7]{0:T(128)S(1)} %pad_add_fusion.scal_ref, bf16[5,256,512]{2,1,0:T(8,128)(2,1)S(1)} %project.1.refs_4_.grad_ref, bf16[5,256,512]{2,1,0:T(8,128)(2,1)S(1)} %bitcast.70, bf16[5,256,512]{2,1,0:T(8,128)(2,1)S(1)} %copy-done.1, ...), custom_call_target="tpu_custom_call" | custom-call | flops 3000000 | bytes 196608 | tf_op jit(solution)/shard_map/input/pallas_call | solution.py:1140
  133.4 0.8 attn_step.1
  134.3 11.3 %all_to_all.5.every_ref = bf16[32,16,128]{2,1,0:T(8,128)(2,1)S(1)} all-to-all(bf16[32,16,128]{2,1,0:T(8,128)(2,1)S(1)} %get-tuple-element.168), channel_id=1, replica_groups=mesh['blk'=8,'group'=4] {'blk','group'}, dimensions={0} | all-to-all | bytes 262144 | tf_op jit(solution)/shard_map/all_to_all | solution.py:1173
  145.6 0.9 final.1
  (111 shorter events, 10.1 us)
Async XLA Ops:
  0.7 13.6 %copy-start.15 = (s32[5]{0:T(128)S(1)}, s32[5]{0:T(128)}, u32[]{:S(2)}) copy-start(s32[5]{0:T(128)} %param.17) | copy-start | bytes 64
  0.7 13.6 %copy-start.5 = (f32[4,512]{1,0:T(4,128)S(1)}, f32[4,512]{1,0:T(4,128)}, u32[]{:S(2)}) copy-start(f32[4,512]{1,0:T(4,128)} %ln_ref.7) | copy-start | bytes 24580
  0.7 13.6 %copy-start.1 = (bf16[5,256,512]{2,1,0:T(8,128)(2,1)S(1)}, bf16[5,256,512]{2,1,0:T(8,128)(2,1)}, u32[]{:S(2)}) copy-start(bf16[5,256,512]{2,1,0:T(8,128)(2,1)} %x_ref.3) | copy-start | bytes 3932164
  1.7 15.3 %collective-permute-start.2 = (bf16[192,128]{1,0:T(8,128)(2,1)S(1)}, bf16[192,128]{1,0:T(8,128)(2,1)S(1)}, u32[]{:S(2)}, u32[]{:S(2)}) collective-permute-start(bf16[192,128]{1,0:T(8,128)(2,1)S(1)} %bitcast.76), channel_id=1, source_target_pairs={{0,3},{1,0},{2,1},{3,2},{4,7},{5,4},{6,5},{7,6},{8,11},{9,8},{10,9... | collective-permute-start | bytes 147464 | tf_op jit(solution)/shard_map/ppermute | solution.py:775
  6.8 10.1 %collective-permute-start.1 = (bf16[192,128]{1,0:T(8,128)(2,1)S(1)}, bf16[192,128]{1,0:T(8,128)(2,1)S(1)}, u32[]{:S(2)}, u32[]{:S(2)}) collective-permute-start(bf16[192,128]{1,0:T(8,128)(2,1)S(1)} %bitcast.77), channel_id=1, source_target_pairs={{0,2},{1,3},{2,0},{3,1},{4,6},{5,7},{6,4},{7,5},{8,10},{9,11},{10,... | collective-permute-start | bytes 147464 | tf_op jit(solution)/shard_map/ppermute | solution.py:775
  6.8 10.1 %collective-permute-start = (bf16[192,128]{1,0:T(8,128)(2,1)S(1)}, bf16[192,128]{1,0:T(8,128)(2,1)S(1)}, u32[]{:S(2)}, u32[]{:S(2)}) collective-permute-start(bf16[192,128]{1,0:T(8,128)(2,1)S(1)} %bitcast.78), channel_id=1, source_target_pairs={{0,1},{1,2},{2,3},{3,0},{4,5},{5,6},{6,7},{7,4},{8,9},{9,10},{10,1... | collective-permute-start | bytes 147464 | tf_op jit(solution)/shard_map/ppermute | solution.py:775
  9.6 11.5 %collective-permute-start.11 = (bf16[576,128]{1,0:T(8,128)(2,1)}, bf16[576,128]{1,0:T(8,128)(2,1)S(1)}, u32[]{:S(2)}, u32[]{:S(2)}) collective-permute-start(bf16[576,128]{1,0:T(8,128)(2,1)} %pack.1), channel_id=1, source_target_pairs={{0,3},{1,0},{2,1},{3,2},{4,7},{5,4},{6,5},{7,6},{8,11},{9,8},{10,9... | collective-permute-start | bytes 442376 | tf_op jit(solution)/shard_map/ppermute | solution.py:775
  12.4 7.7 %collective-permute-start.10 = (bf16[576,128]{1,0:T(8,128)(2,1)}, bf16[576,128]{1,0:T(8,128)(2,1)S(1)}, u32[]{:S(2)}, u32[]{:S(2)}) collective-permute-start(bf16[576,128]{1,0:T(8,128)(2,1)} %pack.1), channel_id=1, source_target_pairs={{0,1},{1,2},{2,3},{3,0},{4,5},{5,6},{6,7},{7,4},{8,9},{9,10},{10,1... | collective-permute-start | bytes 442376 | tf_op jit(solution)/shard_map/ppermute | solution.py:775
  17.0 13.7 %collective-permute-start.6 = (bf16[864,128]{1,0:T(8,128)(2,1)S(1)}, bf16[864,128]{1,0:T(8,128)(2,1)S(1)}, u32[]{:S(2)}, u32[]{:S(2)}) collective-permute-start(bf16[864,128]{1,0:T(8,128)(2,1)S(1)} %pad_maximum_fusion.refs_0_), channel_id=1, source_target_pairs={{0,4},{4,0},{8,12},{12,8},{16,20},{20,16},{24,28},{28,24},{1,5},{5... | collective-permute-start | bytes 663560 | tf_op jit(solution)/shard_map/ppermute | solution.py:779
  17.1 9.2 %collective-permute-start.5 = (bf16[864,128]{1,0:T(8,128)(2,1)S(1)}, bf16[864,128]{1,0:T(8,128)(2,1)S(1)}, u32[]{:S(2)}, u32[]{:S(2)}) collective-permute-start(bf16[864,128]{1,0:T(8,128)(2,1)S(1)} %pad_maximum_fusion.refs_0_), channel_id=1, source_target_pairs={{0,24},{4,28},{8,16},{12,20},{16,8},{20,12},{24,0},{28,4},{1,25},{... | collective-permute-start | bytes 663560 | tf_op jit(solution)/shard_map/ppermute | solution.py:779
  19.6 11.6 %collective-permute-start.4 = (bf16[864,128]{1,0:T(8,128)(2,1)S(1)}, bf16[864,128]{1,0:T(8,128)(2,1)S(1)}, u32[]{:S(2)}, u32[]{:S(2)}) collective-permute-start(bf16[864,128]{1,0:T(8,128)(2,1)S(1)} %pad_maximum_fusion.refs_0_), channel_id=1, source_target_pairs={{0,16},{4,20},{8,24},{12,28},{16,0},{20,4},{24,8},{28,12},{1,17},{... | collective-permute-start | bytes 663560 | tf_op jit(solution)/shard_map/ppermute | solution.py:779
  20.1 12.9 %collective-permute-start.3 = (bf16[864,128]{1,0:T(8,128)(2,1)S(1)}, bf16[864,128]{1,0:T(8,128)(2,1)S(1)}, u32[]{:S(2)}, u32[]{:S(2)}) collective-permute-start(bf16[864,128]{1,0:T(8,128)(2,1)S(1)} %pad_maximum_fusion.refs_0_), channel_id=1, source_target_pairs={{0,8},{4,12},{8,0},{12,4},{16,24},{20,28},{24,16},{28,20},{1,9},{5... | collective-permute-start | bytes 663560 | tf_op jit(solution)/shard_map/ppermute | solution.py:779
  21.1 7.1 %collective-permute-start.12 = (bf16[576,128]{1,0:T(8,128)(2,1)S(1)}, bf16[576,128]{1,0:T(8,128)(2,1)S(1)}, u32[]{:S(2)}, u32[]{:S(2)}) collective-permute-start(bf16[576,128]{1,0:T(8,128)(2,1)S(1)} %collective-permute-done.10), channel_id=1, source_target_pairs={{0,1},{1,2},{2,3},{3,0},{4,5},{5,6},{6,7},{7,4},{8,9},{9,10},{10,1... | collective-permute-start | bytes 442376 | tf_op jit(solution)/shard_map/ppermute | solution.py:775
  26.3 6.7 %collective-permute-start.9 = (bf16[864,128]{1,0:T(8,128)(2,1)S(1)}, bf16[864,128]{1,0:T(8,128)(2,1)S(1)}, u32[]{:S(2)}, u32[]{:S(2)}) collective-permute-start(bf16[864,128]{1,0:T(8,128)(2,1)S(1)} %collective-permute-done.5.refs_3_), channel_id=1, source_target_pairs={{0,4},{4,0},{8,12},{12,8},{16,20},{20,16},{24,28},{28,24},{1,5},{5... | collective-permute-start | bytes 663560 | tf_op jit(solution)/shard_map/ppermute | solution.py:779
  28.2 15.9 %collective-permute-start.15 = (bf16[1280,128]{1,0:T(8,128)(2,1)S(1)}, bf16[1280,128]{1,0:T(8,128)(2,1)S(1)}, u32[]{:S(2)}, u32[]{:S(2)}) collective-permute-start(bf16[1280,128]{1,0:T(8,128)(2,1)S(1)} %bitcast.63), channel_id=1, source_target_pairs={{0,24},{4,28},{8,16},{12,20},{16,8},{20,12},{24,0},{28,4},{1,25},{... | collective-permute-start | bytes 983048 | tf_op jit(solution)/shard_map/ppermute | solution.py:779
  30.7 14.0 %collective-permute-start.14 = (bf16[1280,128]{1,0:T(8,128)(2,1)S(1)}, bf16[1280,128]{1,0:T(8,128)(2,1)S(1)}, u32[]{:S(2)}, u32[]{:S(2)}) collective-permute-start(bf16[1280,128]{1,0:T(8,128)(2,1)S(1)} %bitcast.64), channel_id=1, source_target_pairs={{0,16},{4,20},{8,24},{12,28},{16,0},{20,4},{24,8},{28,12},{1,17},{... | collective-permute-start | bytes 983048 | tf_op jit(solution)/shard_map/ppermute | solution.py:779
  31.2 13.5 %collective-permute-start.13 = (bf16[1280,128]{1,0:T(8,128)(2,1)S(1)}, bf16[1280,128]{1,0:T(8,128)(2,1)S(1)}, u32[]{:S(2)}, u32[]{:S(2)}) collective-permute-start(bf16[1280,128]{1,0:T(8,128)(2,1)S(1)} %bitcast.65), channel_id=1, source_target_pairs={{0,8},{4,12},{8,0},{12,4},{16,24},{20,28},{24,16},{28,20},{1,9},{5... | collective-permute-start | bytes 983048 | tf_op jit(solution)/shard_map/ppermute | solution.py:779
  33.0 1.5 %collective-permute-start.8 = (bf16[864,128]{1,0:T(8,128)(2,1)S(1)}, bf16[864,128]{1,0:T(8,128)(2,1)S(1)}, u32[]{:S(2)}, u32[]{:S(2)}) collective-permute-start(bf16[864,128]{1,0:T(8,128)(2,1)S(1)} %collective-permute-done.4.refs_2_), channel_id=1, source_target_pairs={{0,4},{4,0},{8,12},{12,8},{16,20},{20,16},{24,28},{28,24},{1,5},{5... | collective-permute-start | bytes 663560 | tf_op jit(solution)/shard_map/ppermute | solution.py:779
  33.1 1.8 %collective-permute-start.7 = (bf16[864,128]{1,0:T(8,128)(2,1)S(1)}, bf16[864,128]{1,0:T(8,128)(2,1)S(1)}, u32[]{:S(2)}, u32[]{:S(2)}) collective-permute-start(bf16[864,128]{1,0:T(8,128)(2,1)S(1)} %collective-permute-done.3.refs_1_), channel_id=1, source_target_pairs={{0,4},{4,0},{8,12},{12,8},{16,20},{20,16},{24,28},{28,24},{1,5},{5... | collective-permute-start | bytes 663560 | tf_op jit(solution)/shard_map/ppermute | solution.py:779
  34.5 12.8 %collective-permute-start.16 = (bf16[1280,128]{1,0:T(8,128)(2,1)S(1)}, bf16[1280,128]{1,0:T(8,128)(2,1)S(1)}, u32[]{:S(2)}, u32[]{:S(2)}) collective-permute-start(bf16[1280,128]{1,0:T(8,128)(2,1)S(1)} %bitcast.66), channel_id=1, source_target_pairs={{0,4},{4,0},{8,12},{12,8},{16,20},{20,16},{24,28},{28,24},{1,5},{5... | collective-permute-start | bytes 983048 | tf_op jit(solution)/shard_map/ppermute | solution.py:779
  44.8 3.9 %collective-permute-start.17 = (bf16[1280,128]{1,0:T(8,128)(2,1)S(1)}, bf16[1280,128]{1,0:T(8,128)(2,1)S(1)}, u32[]{:S(2)}, u32[]{:S(2)}) collective-permute-start(bf16[1280,128]{1,0:T(8,128)(2,1)S(1)} %get-tuple-element.106.refs_5_), channel_id=1, source_target_pairs={{0,4},{4,0},{8,12},{12,8},{16,20},{20,16},{24,28},{28,24},{1,5},{5... | collective-permute-start | bytes 983048 | tf_op jit(solution)/shard_map/ppermute | solution.py:779
  44.9 4.2 %collective-permute-start.18 = (bf16[1280,128]{1,0:T(8,128)(2,1)S(1)}, bf16[1280,128]{1,0:T(8,128)(2,1)S(1)}, u32[]{:S(2)}, u32[]{:S(2)}) collective-permute-start(bf16[1280,128]{1,0:T(8,128)(2,1)S(1)} %get-tuple-element.107.refs_6_), channel_id=1, source_target_pairs={{0,4},{4,0},{8,12},{12,8},{16,20},{20,16},{24,28},{28,24},{1,5},{5... | collective-permute-start | bytes 983048 | tf_op jit(solution)/shard_map/ppermute | solution.py:779
  45.5 3.7 %collective-permute-start.19 = (bf16[1280,128]{1,0:T(8,128)(2,1)S(1)}, bf16[1280,128]{1,0:T(8,128)(2,1)S(1)}, u32[]{:S(2)}, u32[]{:S(2)}) collective-permute-start(bf16[1280,128]{1,0:T(8,128)(2,1)S(1)} %get-tuple-element.108.refs_7_), channel_id=1, source_target_pairs={{0,4},{4,0},{8,12},{12,8},{16,20},{20,16},{24,28},{28,24},{1,5},{5... | collective-permute-start | bytes 983048 | tf_op jit(solution)/shard_map/ppermute | solution.py:779
  45.6 17.9 %collective-permute-start.22 = (bf16[1024,128]{1,0:T(8,128)(2,1)S(1)}, bf16[1024,128]{1,0:T(8,128)(2,1)S(1)}, u32[]{:S(2)}, u32[]{:S(2)}) collective-permute-start(bf16[1024,128]{1,0:T(8,128)(2,1)S(1)} %gate.4.refs_12_.refs_2_.refs_10_), channel_id=1, source_target_pairs={{0,24},{4,28},{8,16},{12,20},{16,8},{20,12},{24,0},{28,4},{1,25},{... | collective-permute-start | bytes 786440 | tf_op jit(solution)/shard_map/ppermute | solution.py:779
  47.4 16.1 %collective-permute-start.21 = (bf16[1024,128]{1,0:T(8,128)(2,1)S(1)}, bf16[1024,128]{1,0:T(8,128)(2,1)S(1)}, u32[]{:S(2)}, u32[]{:S(2)}) collective-permute-start(bf16[1024,128]{1,0:T(8,128)(2,1)S(1)} %gate.4.refs_12_.refs_2_.refs_10_), channel_id=1, source_target_pairs={{0,16},{4,20},{8,24},{12,28},{16,0},{20,4},{24,8},{28,12},{1,17},{... | collective-permute-start | bytes 786440 | tf_op jit(solution)/shard_map/ppermute | solution.py:779
  48.8 14.7 %collective-permute-start.20 = (bf16[1024,128]{1,0:T(8,128)(2,1)S(1)}, bf16[1024,128]{1,0:T(8,128)(2,1)S(1)}, u32[]{:S(2)}, u32[]{:S(2)}) collective-permute-start(bf16[1024,128]{1,0:T(8,128)(2,1)S(1)} %gate.4.refs_12_.refs_2_.refs_10_), channel_id=1, source_target_pairs={{0,8},{4,12},{8,0},{12,4},{16,24},{20,28},{24,16},{28,20},{1,9},{5... | collective-permute-start | bytes 786440 | tf_op jit(solution)/shard_map/ppermute | solution.py:779
  49.2 15.5 %collective-permute-start.23 = (bf16[1024,128]{1,0:T(8,128)(2,1)S(1)}, bf16[1024,128]{1,0:T(8,128)(2,1)S(1)}, u32[]{:S(2)}, u32[]{:S(2)}) collective-permute-start(bf16[1024,128]{1,0:T(8,128)(2,1)S(1)} %gate.4.refs_12_.refs_2_.refs_10_), channel_id=1, source_target_pairs={{0,4},{4,0},{8,12},{12,8},{16,20},{20,16},{24,28},{28,24},{1,5},{5... | collective-permute-start | bytes 786440 | tf_op jit(solution)/shard_map/ppermute | solution.py:779
  63.6 1.7 %collective-permute-start.24 = (bf16[1024,128]{1,0:T(8,128)(2,1)S(1)}, bf16[1024,128]{1,0:T(8,128)(2,1)S(1)}, u32[]{:S(2)}, u32[]{:S(2)}) collective-permute-start(bf16[1024,128]{1,0:T(8,128)(2,1)S(1)} %get-tuple-element.111.refs_3_), channel_id=1, source_target_pairs={{0,4},{4,0},{8,12},{12,8},{16,20},{20,16},{24,28},{28,24},{1,5},{5... | collective-permute-start | bytes 786440 | tf_op jit(solution)/shard_map/ppermute | solution.py:779
  64.1 1.5 %collective-permute-start.25 = (bf16[1024,128]{1,0:T(8,128)(2,1)S(1)}, bf16[1024,128]{1,0:T(8,128)(2,1)S(1)}, u32[]{:S(2)}, u32[]{:S(2)}) collective-permute-start(bf16[1024,128]{1,0:T(8,128)(2,1)S(1)} %get-tuple-element.112.refs_4_), channel_id=1, source_target_pairs={{0,4},{4,0},{8,12},{12,8},{16,20},{20,16},{24,28},{28,24},{1,5},{5... | collective-permute-start | bytes 786440 | tf_op jit(solution)/shard_map/ppermute | solution.py:779
  64.2 1.8 %collective-permute-start.26 = (bf16[1024,128]{1,0:T(8,128)(2,1)S(1)}, bf16[1024,128]{1,0:T(8,128)(2,1)S(1)}, u32[]{:S(2)}, u32[]{:S(2)}) collective-permute-start(bf16[1024,128]{1,0:T(8,128)(2,1)S(1)} %get-tuple-element.113.refs_5_), channel_id=1, source_target_pairs={{0,4},{4,0},{8,12},{12,8},{16,20},{20,16},{24,28},{28,24},{1,5},{5... | collective-permute-start | bytes 786440 | tf_op jit(solution)/shard_map/ppermute | solution.py:779
  64.6 14.5 %collective-permute-start.27 = (bf16[4,1024,128]{2,1,0:T(8,128)(2,1)S(1)}, bf16[4,1024,128]{2,1,0:T(8,128)(2,1)S(1)}, u32[]{:S(2)}, u32[]{:S(2)}) collective-permute-start(bf16[4,1024,128]{2,1,0:T(8,128)(2,1)S(1)} %get-tuple-element.130), channel_id=1, source_target_pairs={{0,4},{4,0},{8,12},{12,8},{16,20},{20,16},{24,28},{28,24},{1,5},{5... | collective-permute-start | bytes 3145736 | tf_op jit(solution)/shard_map/ppermute | solution.py:779
  78.7 2.7 %collective-permute-start.28 = (bf16[4,1024,128]{2,1,0:T(8,128)(2,1)S(1)}, bf16[4,1024,128]{2,1,0:T(8,128)(2,1)S(1)}, u32[]{:S(2)}, u32[]{:S(2)}) collective-permute-start(bf16[4,1024,128]{2,1,0:T(8,128)(2,1)S(1)} %get-tuple-element.131), channel_id=1, source_target_pairs={{0,4},{4,0},{8,12},{12,8},{16,20},{20,16},{24,28},{28,24},{1,5},{5... | collective-permute-start | bytes 3145736 | tf_op jit(solution)/shard_map/ppermute | solution.py:779
  82.4 17.5 %collective-permute-start.29 = (bf16[2,1024,128]{2,1,0:T(8,128)(2,1)S(1)}, bf16[2,1024,128]{2,1,0:T(8,128)(2,1)S(1)}, u32[]{:S(2)}, u32[]{:S(2)}) collective-permute-start(bf16[2,1024,128]{2,1,0:T(8,128)(2,1)S(1)} %get-tuple-element.140), channel_id=1, source_target_pairs={{0,8},{4,12},{8,0},{12,4},{16,24},{20,28},{24,16},{28,20},{1,9},{5... | collective-permute-start | bytes 1572872 | tf_op jit(solution)/shard_map/ppermute | solution.py:779
  84.2 15.8 %collective-permute-start.30 = (bf16[2,1024,128]{2,1,0:T(8,128)(2,1)S(1)}, bf16[2,1024,128]{2,1,0:T(8,128)(2,1)S(1)}, u32[]{:S(2)}, u32[]{:S(2)}) collective-permute-start(bf16[2,1024,128]{2,1,0:T(8,128)(2,1)S(1)} %get-tuple-element.142), channel_id=1, source_target_pairs={{0,16},{4,20},{8,24},{12,28},{16,0},{20,4},{24,8},{28,12},{1,17},{... | collective-permute-start | bytes 1572872 | tf_op jit(solution)/shard_map/ppermute | solution.py:779
  101.0 2.8 %collective-permute-start.31 = (bf16[4,1072,128]{2,1,0:T(8,128)(2,1)S(1)}, bf16[4,1072,128]{2,1,0:T(8,128)(2,1)S(1)}, u32[]{:S(2)}, u32[]{:S(2)}) collective-permute-start(bf16[4,1072,128]{2,1,0:T(8,128)(2,1)S(1)} %get-tuple-element.145), channel_id=1, source_target_pairs={{0,4},{4,0},{8,12},{12,8},{16,20},{20,16},{24,28},{28,24},{1,5},{5... | collective-permute-start | bytes 3293192 | tf_op jit(solution)/shard_map/ppermute | solution.py:779
  101.1 10.1 %collective-permute-start.38 = (bf16[1024,128]{1,0:T(8,128)(2,1)S(1)}, bf16[1024,128]{1,0:T(8,128)(2,1)S(1)}, u32[]{:S(2)}, u32[]{:S(2)}) collective-permute-start(bf16[1024,128]{1,0:T(8,128)(2,1)S(1)} %get-tuple-element.157), channel_id=1, source_target_pairs={{0,16},{4,20},{8,24},{12,28},{16,0},{20,4},{24,8},{28,12},{1,17},{... | collective-permute-start | bytes 786440 | tf_op jit(solution)/shard_map/ppermute | solution.py:779
  102.6 9.2 %collective-permute-start.39 = (bf16[1024,128]{1,0:T(8,128)(2,1)S(1)}, bf16[1024,128]{1,0:T(8,128)(2,1)S(1)}, u32[]{:S(2)}, u32[]{:S(2)}) collective-permute-start(bf16[1024,128]{1,0:T(8,128)(2,1)S(1)} %get-tuple-element.159), channel_id=1, source_target_pairs={{0,8},{4,12},{8,0},{12,4},{16,24},{20,28},{24,16},{28,20},{1,9},{5... | collective-permute-start | bytes 786440 | tf_op jit(solution)/shard_map/ppermute | solution.py:779
  104.6 13.0 %collective-permute-start.32 = (bf16[1072,128]{1,0:T(8,128)(2,1)S(1)}, bf16[1072,128]{1,0:T(8,128)(2,1)S(1)}, u32[]{:S(2)}, u32[]{:S(2)}) collective-permute-start(bf16[1072,128]{1,0:T(8,128)(2,1)S(1)} %get-tuple-element.148), channel_id=1, source_target_pairs={{0,8},{4,12},{8,0},{12,4},{16,24},{20,28},{24,16},{28,20},{1,9},{5... | collective-permute-start | bytes 823304 | tf_op jit(solution)/shard_map/ppermute | solution.py:779
  105.9 15.5 %collective-permute-start.33 = (bf16[1072,128]{1,0:T(8,128)(2,1)S(1)}, bf16[1072,128]{1,0:T(8,128)(2,1)S(1)}, u32[]{:S(2)}, u32[]{:S(2)}) collective-permute-start(bf16[1072,128]{1,0:T(8,128)(2,1)S(1)} %get-tuple-element.149), channel_id=1, source_target_pairs={{0,16},{4,20},{8,24},{12,28},{16,0},{20,4},{24,8},{28,12},{1,17},{... | collective-permute-start | bytes 823304 | tf_op jit(solution)/shard_map/ppermute | solution.py:779
  106.5 16.3 %collective-permute-start.34 = (bf16[1072,128]{1,0:T(8,128)(2,1)S(1)}, bf16[1072,128]{1,0:T(8,128)(2,1)S(1)}, u32[]{:S(2)}, u32[]{:S(2)}) collective-permute-start(bf16[1072,128]{1,0:T(8,128)(2,1)S(1)} %get-tuple-element.150), channel_id=1, source_target_pairs={{0,24},{4,28},{8,16},{12,20},{16,8},{20,12},{24,0},{28,4},{1,25},{... | collective-permute-start | bytes 823304 | tf_op jit(solution)/shard_map/ppermute | solution.py:779
  112.4 15.4 %collective-permute-start.40 = (bf16[512,128]{1,0:T(8,128)(2,1)S(1)}, bf16[512,128]{1,0:T(8,128)(2,1)S(1)}, u32[]{:S(2)}, u32[]{:S(2)}) collective-permute-start(bf16[512,128]{1,0:T(8,128)(2,1)S(1)} %get-tuple-element.161), channel_id=1, source_target_pairs={{0,1},{1,2},{2,3},{3,0},{4,5},{5,6},{6,7},{7,4},{8,9},{9,10},{10,1... | collective-permute-start | bytes 393224 | tf_op jit(solution)/shard_map/ppermute | solution.py:775
  114.0 13.8 %collective-permute-start.41 = (bf16[512,128]{1,0:T(8,128)(2,1)S(1)}, bf16[512,128]{1,0:T(8,128)(2,1)S(1)}, u32[]{:S(2)}, u32[]{:S(2)}) collective-permute-start(bf16[512,128]{1,0:T(8,128)(2,1)S(1)} %get-tuple-element.162), channel_id=1, source_target_pairs={{0,2},{1,3},{2,0},{3,1},{4,6},{5,7},{6,4},{7,5},{8,10},{9,11},{10,... | collective-permute-start | bytes 393224 | tf_op jit(solution)/shard_map/ppermute | solution.py:775
  117.7 10.2 %collective-permute-start.42 = (bf16[512,128]{1,0:T(8,128)(2,1)S(1)}, bf16[512,128]{1,0:T(8,128)(2,1)S(1)}, u32[]{:S(2)}, u32[]{:S(2)}) collective-permute-start(bf16[512,128]{1,0:T(8,128)(2,1)S(1)} %get-tuple-element.163), channel_id=1, source_target_pairs={{0,3},{1,0},{2,1},{3,2},{4,7},{5,4},{6,5},{7,6},{8,11},{9,8},{10,9... | collective-permute-start | bytes 393224 | tf_op jit(solution)/shard_map/ppermute | solution.py:775
  123.5 9.9 %collective-permute-start.35 = (bf16[256,128]{1,0:T(8,128)(2,1)S(1)}, bf16[256,128]{1,0:T(8,128)(2,1)S(1)}, u32[]{:S(2)}, u32[]{:S(2)}) collective-permute-start(bf16[256,128]{1,0:T(8,128)(2,1)S(1)} %get-tuple-element.154), channel_id=1, source_target_pairs={{0,1},{1,2},{2,3},{3,0},{4,5},{5,6},{6,7},{7,4},{8,9},{9,10},{10,1... | collective-permute-start | bytes 196616 | tf_op jit(solution)/shard_map/ppermute | solution.py:775
  125.1 8.3 %collective-permute-start.36 = (bf16[256,128]{1,0:T(8,128)(2,1)S(1)}, bf16[256,128]{1,0:T(8,128)(2,1)S(1)}, u32[]{:S(2)}, u32[]{:S(2)}) collective-permute-start(bf16[256,128]{1,0:T(8,128)(2,1)S(1)} %get-tuple-element.155), channel_id=1, source_target_pairs={{0,2},{1,3},{2,0},{3,1},{4,6},{5,7},{6,4},{7,5},{8,10},{9,11},{10,... | collective-permute-start | bytes 196616 | tf_op jit(solution)/shard_map/ppermute | solution.py:775
  127.8 5.6 %collective-permute-start.37 = (bf16[256,128]{1,0:T(8,128)(2,1)S(1)}, bf16[256,128]{1,0:T(8,128)(2,1)S(1)}, u32[]{:S(2)}, u32[]{:S(2)}) collective-permute-start(bf16[256,128]{1,0:T(8,128)(2,1)S(1)} %get-tuple-element.156), channel_id=1, source_target_pairs={{0,3},{1,0},{2,1},{3,2},{4,7},{5,4},{6,5},{7,6},{8,11},{9,8},{10,9... | collective-permute-start | bytes 196616 | tf_op jit(solution)/shard_map/ppermute | solution.py:775
  129.0 16.6 %copy-start.12 = (f32[4,512]{1,0:T(4,128)S(1)}, f32[4,512]{1,0:T(4,128)}, u32[]{:S(2)}) copy-start(f32[4,512]{1,0:T(4,128)} %lf_ref.1) | copy-start | bytes 24580
  129.0 16.6 %copy-start.13 = (f32[4,512]{1,0:T(4,128)S(1)}, f32[4,512]{1,0:T(4,128)}, u32[]{:S(2)}) copy-start(f32[4,512]{1,0:T(4,128)} %ls_ref.1) | copy-start | bytes 24580
  (11 other events, 85.9 us)

commit v5 on v4

--- a/solution.py
+++ b/solution.py
@@ -245,29 +245,32 @@
     sums = mm(high, w_ref[:, width : 3 * width]) + mm(low, w_ref[:, width : 3 * width])
     ks_ref[0] = sums[:, :width].astype(b16)
     vs_ref[0] = sums[:, width:].astype(b16)
-    for span in range(spans):
-        part = slice(span * SPAN, (span + 1) * SPAN)
-        local, summary = score_masks(scal_ref, i, span, spans, amount)
-        pairs = [slice(pair * SPAN, (pair + 1) * SPAN) for pair in range(tiles)]
-        scores = []
-        for lanes in pairs:
-            query = heads_apart(q_ref[0, part, lanes] * b16(factor))
-            keys = jnp.concatenate([k_ref[0, part, lanes], ks_ref[0, :, lanes]], 0)
-            scores.append(mm(keys, query, NT))
-        probs = []
-        for pair in range(tiles):
-            here = jnp.where(local, scores[pair][:SPAN], masked_value)
-            there = jnp.where(summary, scores[pair][SPAN:], masked_value)
-            top = jnp.maximum(jnp.max(here, 0, keepdims=True), jnp.max(there, 0, keepdims=True))
-            here, there = jnp.exp(here - top), jnp.exp(there - top)
-            total = jnp.sum(here, 0, keepdims=True) + jnp.sum(there, 0, keepdims=True)
-            lse_ref[0, span, pair : pair + 1, :] = top + jnp.log(total)
-            probs.append(
-                (jnp.concatenate([here.astype(b16), there.astype(b16)], 0), 1.0 / total)
-            )
-        for lanes, (prob, inverse) in zip(pairs, probs):
-            values = jnp.concatenate([v_ref[0, part, lanes], vs_ref[0, :, lanes]], 0)
-            mixed_ref[lanes, part] = own_heads(mm(values, prob, TN) * inverse).astype(b16)
+    units = [(span, pair) for span in range(spans) for pair in range(tiles)]
+    masks = [score_masks(scal_ref, i, span, spans, amount) for span in range(spans)]
+
+    def places(span, pair):
+        return slice(span * SPAN, (span + 1) * SPAN), slice(pair * SPAN, (pair + 1) * SPAN)
+
+    scores = []
+    for unit in units:
+        part, lanes = places(*unit)
+        query = heads_apart(q_ref[0, part, lanes] * b16(factor))
+        keys = jnp.concatenate([k_ref[0, part, lanes], ks_ref[0, :, lanes]], 0)
+        scores.append(mm(keys, query, NT))
+    probs = []
+    for (span, pair), score in zip(units, scores):
+        local, summary = masks[span]
+        here = jnp.where(local, score[:SPAN], masked_value)
+        there = jnp.where(summary, score[SPAN:], masked_value)
+        top = jnp.maximum(jnp.max(here, 0, keepdims=True), jnp.max(there, 0, keepdims=True))
+        here, there = jnp.exp(here - top), jnp.exp(there - top)
+        total = jnp.sum(here, 0, keepdims=True) + jnp.sum(there, 0, keepdims=True)
+        lse_ref[0, span, pair : pair + 1, :] = top + jnp.log(total)
+        probs.append((jnp.concatenate([here.astype(b16), there.astype(b16)], 0), 1.0 / total))
+    for unit, (prob, inverse) in zip(units, probs):
+        part, lanes = places(*unit)
+        values = jnp.concatenate([v_ref[0, part, lanes], vs_ref[0, :, lanes]], 0)
+        mixed_ref[lanes, part] = own_heads(mm(values, prob, TN) * inverse).astype(b16)
 
 
 def mlp_kernel(dims, near, places, first, last, scal_ref, *refs):
@@ -381,23 +384,19 @@
 
 
 def middle_kernel(
-    gm_ref, g_ref, x2_ref, mixed_ref, w_ref, ln_ref, gx2_ref, do_ref, dwo_ref, lng_ref
+    second, gm_ref, g_ref, x2_ref, mixed_ref, w_ref, ln_ref, *refs
 ):
-    i = pl.program_id(0)
-
-    @pl.when(i == 0)
-    def _():
-        dwo_ref[...] = jnp.zeros_like(dwo_ref)
-        lng_ref[...] = jnp.zeros_like(lng_ref)
-
+    gx2_ref, do_ref, dwo_ref, lng_ref = refs[-4:]
     gm = gm_ref[...].astype(f32)
     normal, inverse = norm_parts(x2_ref[...].astype(f32))
+    lng_ref[...] = refs[3][...] if second else jnp.zeros_like(lng_ref)
     lng_ref[0:1, :] += jnp.sum(gm * normal, 0, keepdims=True)
     lng_ref[1:2, :] += jnp.sum(gm, 0, keepdims=True)
     gx2 = g_ref[...].astype(f32) + norm_back(gm, normal, inverse, ln_ref[2:3, :])
     branch = gx2.astype(b16)
     gx2_ref[...] = branch
-    dwo_ref[...] += mm(mixed_ref[...], branch)
+    grad = mm(mixed_ref[...], branch)
+    dwo_ref[...] = grad + refs[2][...] if second else grad
     do_ref[...] = mm(branch, w_ref[...], NT).astype(b16)
 
 
@@ -579,7 +578,7 @@
     spot = scal_ref[0] // 2
     for j, far in enumerate((1, 2)):
         keep_ref, get_ref = refs[j], refs[2 + j]
-        stay_ref, out_ref = refs[4 + 2 * j], refs[5 + 2 * j]
+        stay_ref, out_ref = refs[-4 + 2 * j], refs[-3 + 2 * j]
         near = 3 - far
         for k, (ref, move) in enumerate(
             ((stay_ref, 0), (stay_ref, near), (out_ref, far), (out_ref, far ^ near))
@@ -1019,21 +1018,25 @@
     if fast:
         gets = [cross(send, 1, nb) for send in sends]
 
-    by_tok = pl.BlockSpec((tok, width), lambda i: (i, 0))
-    gx2, grad_mixed, dwo, ln_two = pl.pallas_call(
-        middle_kernel,
-        grid=(seqs,),
-        in_specs=[
-            by_tok, by_tok, by_tok, pl.BlockSpec((width, tok), lambda i: (0, i)), whole(),
-            fixed(4, width),
-        ],
-        out_specs=[by_tok, by_tok, fixed(width, width), fixed(8, width)],
-        out_shape=[rows_out, rows_out, shape((width, width), f32), shape((8, width), f32)],
-        compiler_params=params(16),
-        cost_estimate=cost(3e9, act_bytes * 14),
-        name="middle",
-    )(gm, flat_cot, x2, mixed, wo, ln_params)
-    gx2, grad_mixed = gx2.reshape(tokens.shape), grad_mixed.reshape(tokens.shape)
+    def middle(k, *more):
+        rows_k = pl.BlockSpec((every_row // 2, width), lambda i: (k, 0))
+        return pl.pallas_call(
+            functools.partial(middle_kernel, bool(more)),
+            grid=(1,),
+            in_specs=[
+                rows_k, rows_k, rows_k, pl.BlockSpec((width, every_row // 2), lambda i: (0, k)),
+                whole(), fixed(4, width),
+            ]
+            + [anywhere(), anywhere(), fixed(width, width), fixed(8, width), anywhere()][: len(more)],
+            out_specs=[rows_k, rows_k, fixed(width, width), fixed(8, width)],
+            out_shape=[rows_out, rows_out, shape((width, width), f32), shape((8, width), f32)],
+            input_output_aliases={6: 0, 7: 1} if more else {},
+            compiler_params=params(24),
+            cost_estimate=cost(3e9, act_bytes * 14),
+            name="middle",
+        )(gm, flat_cot, x2, mixed, wo, ln_params, *more)
+
+    halfway = middle(0)
 
     block = shape((ng * size, lanes), f32)
     block_low = shape((ng * size, lanes), b16)
@@ -1041,12 +1044,14 @@
     if fast:
         stay_a, out_a, stay_b, out_b = flat(
             halves_kernel, "halves", [two, two_low, two, two_low], [], cost(2e6, 16e6),
-            scal, *keeps, *gets, scalar=True,
+            scal, *keeps, *gets, halfway[3], scalar=True,
         )
         get_a, get_b = cross(out_a, 2, nb), cross(out_b, 4, nb)
         dep = stay_a
     else:
-        dep = ln_two
+        dep = ln_params
+    gx2, grad_mixed, dwo, ln_two = middle(1, *halfway, dep)
+    gx2, grad_mixed = gx2.reshape(tokens.shape), grad_mixed.reshape(tokens.shape)
 
     dqkv, key_part, value_part, h_part = pl.pallas_call(
         functools.partial(backward_kernel, places),

time: 147 us -> 145 us (0.986)
  Pallas kernels: 70.3 us -> 68.4 us
    pallas_call x1 -> x2, Pallas kernels: 4.5 us -> 3.55 us  [middle(): pl.pallas_call(functools.partial(middle_kernel, bool(more)), grid=(1,), i...]
where the time goes in v5:
time: 145 us
  Pallas kernels  68.4 us (47%)
  starting transfers between devices  44.8 us (31%)
  waiting for transfers between devices  14.7 us (10%)
  blocking collectives  11.4 us (8%)
  local copies, waits for them, and re-layouts  3.91 us (3%)
    pallas_call x2, Pallas kernels, body(): pl.pallas_call(functools.partial(mlp_kernel, mlp_dims, fast, places, firs...  27 us
    ppermute x12, starting transfers between devices, shift(): lax.ppermute(values, 'group', [(j, (j + by) % ng) for j in range(ng)])  22.5 us
    ppermute x31, starting transfers between devices, cross(): return lax.ppermute(values, 'blk', [(j, j ^ bit) for j in range(nb)])  22.2 us
    ppermute x31, waiting for transfers between devices, cross(): return lax.ppermute(values, 'blk', [(j, j ^ bit) for j in range(nb)])  12.9 us
    all_to_all x1, blocking collectives, body(): every = lax.all_to_all(message, ('blk', 'group'), 0, 0, tiled=True)  11.4 us
    pallas_call x13, Pallas kernels, flat(): pl.pallas_call(call, in_specs=[scalars()] * scalar + [whole()] * (len(arg...  9.64 us
    pallas_call x1, Pallas kernels, body(): pl.pallas_call(functools.partial(forward_kernel, dims, fast, places), gri...  8.56 us
    pallas_call x1, Pallas kernels, body(): pl.pallas_call(functools.partial(backward_kernel, places), grid=(seqs,),...  7.94 us
  transfers between devices with their start and end apart: 43, of which 14 were waited for; matrix products, arithmetic and copies ran while one was open for 2% of the time, Pallas kernels for 45%

profile of v5, /device:TPU:0, one launch (start us, length us, event | category | flops | bytes accessed | tf_op | source)
XLA Modules:
  0.0 144.5 jit_solution(4152109440654795216)
XLA Ops:
  0.7 1.0 slice.71
  1.7 5.1 %collective-permute-start.2 = (bf16[192,128]{1,0:T(8,128)(2,1)S(1)}, bf16[192,128]{1,0:T(8,128)(2,1)S(1)}, u32[]{:S(2)}, u32[]{:S(2)}) collective-permute-start(bf16[192,128]{1,0:T(8,128)(2,1)S(1)} %bitcast.77), channel_id=1, source_target_pairs={{0,3},{1,0},{2,1},{3,2},{4,7},{5,4},{6,5},{7,6},{8,11},{9,8},{10,9... | collective-permute-start | bytes 147464 | tf_op jit(solution)/shard_map/ppermute | solution.py:774
  6.8 1.0 collective-permute-start
  7.8 1.8 %pack.1 = bf16[576,128]{1,0:T(8,128)(2,1)} custom-call(f32[4,64,128]{2,1,0:T(8,128)} %am_ref.1, f32[64,512]{1,0:T(8,128)} %um_ref.1, f32[256,128]{1,0:T(8,128)} %dm_ref.1, bf16[192,128]{1,0:T(8,128)(2,1)} %bitcast.80), custom_call_target="tpu_custom_call" | custom-call | flops 30000 | bytes 30000 | tf_op jit(solution)/shard_map/pack/pallas_call | solution.py:904
  9.6 2.8 %collective-permute-start.11 = (bf16[576,128]{1,0:T(8,128)(2,1)}, bf16[576,128]{1,0:T(8,128)(2,1)S(1)}, u32[]{:S(2)}, u32[]{:S(2)}) collective-permute-start(bf16[576,128]{1,0:T(8,128)(2,1)} %pack.1), channel_id=1, source_target_pairs={{0,3},{1,0},{2,1},{3,2},{4,7},{5,4},{6,5},{7,6},{8,11},{9,8},{10,9... | collective-permute-start | bytes 442376 | tf_op jit(solution)/shard_map/ppermute | solution.py:774
  12.4 0.9 fusion.3
  13.4 0.8 bitcast_dynamic-update-slice_fusion.3
  14.3 2.6 %prep.1 = (bf16[5,256,512]{2,1,0:T(8,128)(2,1)S(1)}, bf16[96,128]{1,0:T(8,128)(2,1)S(1)}) custom-call(s32[7]{0:T(128)S(1)} %pad_add_fusion.scal_ref, bf16[5,256,512]{2,1,0:T(8,128)(2,1)S(1)} %copy-done.1, f32[4,512]{1,0:T(4,128)S(1)} %copy-done.5), custom_call_target="tpu_custom_call" | custom-call | flops 1200000 | bytes 78643 | tf_op jit(solution)/shard_map/prep/pallas_call | solution.py:878
  17.1 2.5 %collective-permute-start.5 = (bf16[864,128]{1,0:T(8,128)(2,1)S(1)}, bf16[864,128]{1,0:T(8,128)(2,1)S(1)}, u32[]{:S(2)}, u32[]{:S(2)}) collective-permute-start(bf16[864,128]{1,0:T(8,128)(2,1)S(1)} %pad_maximum_fusion.refs_0_), channel_id=1, source_target_pairs={{0,24},{4,28},{8,16},{12,20},{16,8},{20,12},{24,0},{28,4},{1,25},{... | collective-permute-start | bytes 663560 | tf_op jit(solution)/shard_map/ppermute | solution.py:778
  20.1 1.0 collective-permute-start.3
  21.1 1.3 collective-permute-start.12
  22.4 3.9 %collective-permute-done.5.refs_3_ = bf16[864,128]{1,0:T(8,128)(2,1)S(1)} collective-permute-done((bf16[864,128]{1,0:T(8,128)(2,1)S(1)}, bf16[864,128]{1,0:T(8,128)(2,1)S(1)}, u32[]{:S(2)}, u32[]{:S(2)}) %collective-permute-start.5) | collective-permute-done | bytes 221216 | tf_op jit(solution)/shard_map/ppermute | solution.py:778
  26.3 1.8 %collective-permute-done.12 = bf16[576,128]{1,0:T(8,128)(2,1)S(1)} collective-permute-done((bf16[576,128]{1,0:T(8,128)(2,1)S(1)}, bf16[576,128]{1,0:T(8,128)(2,1)S(1)}, u32[]{:S(2)}, u32[]{:S(2)}) %collective-permute-start.12) | collective-permute-done | bytes 147488 | tf_op jit(solution)/shard_map/ppermute | solution.py:774
  28.2 2.5 %collective-permute-start.15 = (bf16[1280,128]{1,0:T(8,128)(2,1)S(1)}, bf16[1280,128]{1,0:T(8,128)(2,1)S(1)}, u32[]{:S(2)}, u32[]{:S(2)}) collective-permute-start(bf16[1280,128]{1,0:T(8,128)(2,1)S(1)} %bitcast.66), channel_id=1, source_target_pairs={{0,24},{4,28},{8,16},{12,20},{16,8},{20,12},{24,0},{28,4},{1,25},{... | collective-permute-start | bytes 983048 | tf_op jit(solution)/shard_map/ppermute | solution.py:778
  31.2 0.8 collective-permute-start.13
  32.1 0.9 fusion.7
  33.6 0.9 collective-permute-done.8.refs_6_
  34.8 8.6 %forward.1 = (bf16[5,256,512]{2,1,0:T(8,128)(2,1)S(1)}, bf16[5,256,512]{2,1,0:T(8,128)(2,1)S(1)}, bf16[5,256,512]{2,1,0:T(8,128)(2,1)S(1)}, bf16[5,16,512]{2,1,0...) custom-call(s32[7]{0:T(128)S(1)} %pad_add_fusion.scal_ref, ...), custom_call_target="tpu_custom_call" | custom-call | flops 240000000 | bytes 275251 | tf_op jit(solution)/shard_map/forward/pallas_call | solution.py:935
  43.4 1.2 collective-permute-done.14.refs_1_
  45.6 1.8 %collective-permute-start.22 = (bf16[1024,128]{1,0:T(8,128)(2,1)S(1)}, bf16[1024,128]{1,0:T(8,128)(2,1)S(1)}, u32[]{:S(2)}, u32[]{:S(2)}) collective-permute-start(bf16[1024,128]{1,0:T(8,128)(2,1)S(1)} %gate.4.refs_12_.refs_2_.refs_10_), channel_id=1, source_target_pairs={{0,24},{4,28},{8,16},{12,20},{16,8},{20,12},{24,0},{28,4},{1,25},{... | collective-permute-start | bytes 786440 | tf_op jit(solution)/shard_map/ppermute | solution.py:778
  47.4 1.4 collective-permute-start.21
  49.2 14.3 %mlp.2 = (bf16[1280,512]{1,0:T(8,128)(2,1)S(1)}, bf16[1280,512]{1,0:T(8,128)(2,1)S(1)}, bf16[512,512]{1,0:T(8,128)(2,1)S(1)}, f32[8,128]{1,0:T(8,128)S(1)}, bf16...) custom-call(s32[7]{0:T(128)S(1)} %pad_add_fusion.scal_ref, ...), custom_call_target="tpu_custom_call" | custom-call | flops 270000000 | bytes 393216 | tf_op jit(solution)/shard_map/mlp/pallas_call | solution.py:999
  66.1 12.7 %mlp.3 = (bf16[1280,512]{1,0:T(8,128)(2,1)}, bf16[1280,512]{1,0:T(8,128)(2,1)S(1)}, bf16[4,1024,128]{2,1,0:T(8,128)(2,1)S(1)}, bf16[4,1024,128]{2,1,0:T(8,128)(2,1)S(1)}) custom-call(s32[7]{0:T(128)S(1)} %pad_add_fusion.scal_ref, bf16[1280,512]{1,0:T(8,128)(2,1)S(1)} %get-tuple-element.113.refs_0_, bf16[1280,512]{1,0:T(8,128)(2,1)S(1)} %bitcast.58, ...), custom_call_target="tpu_custom_call" | custom-call | flops 270000000 | bytes 393216 | tf_op jit(solution)/shard_map/mlp/pallas_call | solution.py:999
  79.1 1.8 %middle.2 = (bf16[1280,512]{1,0:T(8,128)(2,1)S(1)}, bf16[1280,512]{1,0:T(8,128)(2,1)S(1)}, f32[512,512]{1,0:T(8,128)S(1)}, f32[8,512]{1,0:T(8,128)S(1)}) custom-call(bf16[1280,512]{1,0:T(8,128)(2,1)S(1)} %get-tuple-element.122.gm_ref, bf16[1280,512]{1,0:T(8,128)(2,1)S(1)} %bitcast.59, bf16[1280,512]{1,0:T(8,128)(2,1)S(1)} %get-tuple-element.118.refs_11_.x2_ref, ...), custom_call_target="tpu_custom_call" | custom-call | flops 90000000 | bytes 275251 | tf_op jit(solution)/shard_map/middle/pallas_call | solution.py:1023
  81.4 1.0 halves.1
  82.4 1.7 %collective-permute-start.29 = (bf16[2,1024,128]{2,1,0:T(8,128)(2,1)S(1)}, bf16[2,1024,128]{2,1,0:T(8,128)(2,1)S(1)}, u32[]{:S(2)}, u32[]{:S(2)}) collective-permute-start(bf16[2,1024,128]{2,1,0:T(8,128)(2,1)S(1)} %get-tuple-element.148), channel_id=1, source_target_pairs={{0,8},{4,12},{8,0},{12,4},{16,24},{20,28},{24,16},{28,20},{1,9},{5... | collective-permute-start | bytes 1572872 | tf_op jit(solution)/shard_map/ppermute | solution.py:778
  84.8 1.8 %middle.3 = (bf16[1280,512]{1,0:T(8,128)(2,1)S(1)}, bf16[1280,512]{1,0:T(8,128)(2,1)S(1)}, f32[512,512]{1,0:T(8,128)S(1)}, f32[8,512]{1,0:T(8,128)S(1)}) custom-call(bf16[1280,512]{1,0:T(8,128)(2,1)S(1)} %get-tuple-element.122.gm_ref, bf16[1280,512]{1,0:T(8,128)(2,1)S(1)} %bitcast.60, ...), custom_call_target="tpu_custom_call", output_to_operand_aliasing={{0}: (6, {}), {1}: (7, {})} | custom-call | flops 90000000 | bytes 275251 | tf_op jit(solution)/shard_map/middle/pallas_call | solution.py:1023
  86.6 7.9 %backward.1 = (bf16[5,256,1536]{2,1,0:T(8,128)(2,1)S(1)}, bf16[5,16,512]{2,1,0:T(8,128)(2,1)S(1)}, bf16[5,16,512]{2,1,0:T(8,128)(2,1)S(1)}, f32[2,4,48,128]{3,2,1,0:T(8,128)S(1)}) custom-call(s32[7]{0:T(128)S(1)} %pad_add_fusion.scal_ref, bf16[5,256,512]{2,1,0:T(8,128)(2,1)S(1)} %bitcast.63, bf16[5,256,512]{2,1,0:T(8,128)(2,1)S(1)} %get-tuple-element.134.q_ref, ...), custom_call_target="tpu_custom_call" | custom-call | flops 420000000 | bytes 471859 | tf_op jit(solution)/shard_map/backward/pallas_call | solution.py:1056
  94.5 2.5 %grads.1.dw_ref = f32[512,1536]{1,0:T(8,128)S(1)} custom-call(bf16[1280,512]{1,0:T(8,128)(2,1)S(1)} %bitcast.65, bf16[1280,1536]{1,0:T(8,128)(2,1)S(1)} %bitcast.61, bf16[80,512]{1,0:T(8,128)(2,1)S(1)} %bitcast.73, bf16[80,512]{1,0:T(8,128)(2,1)S(1)} %bitcast.74, bf16[80,512]{1,0:T(8,128)(2,1)S(1)} %bitcast.75), custom_call_target="tpu_custom_call" | custom-call | flops 30000 | bytes 3000 | tf_op jit(solution)/shard_map/grads/pallas_call | solution.py:862
  97.0 1.0 collective-permute-done.30.refs_3_
  98.2 0.9 cut.1
  99.9 1.2 collective-permute-start.39
  101.0 0.8 collective-permute-done.31.refs_1_
  101.9 0.8 spread.1
  103.1 1.4 collective-permute-start.33
  104.6 1.7 %collective-permute-start.34 = (bf16[1072,128]{1,0:T(8,128)(2,1)S(1)}, bf16[1072,128]{1,0:T(8,128)(2,1)S(1)}, u32[]{:S(2)}, u32[]{:S(2)}) collective-permute-start(bf16[1072,128]{1,0:T(8,128)(2,1)S(1)} %get-tuple-element.158), channel_id=1, source_target_pairs={{0,24},{4,28},{8,16},{12,20},{16,8},{20,12},{24,0},{28,4},{1,25},{... | collective-permute-start | bytes 823304 | tf_op jit(solution)/shard_map/ppermute | solution.py:778
  106.2 3.0 %project.1.refs_4_.grad_ref = bf16[5,256,512]{2,1,0:T(8,128)(2,1)S(1)} custom-call(bf16[5,256,1536]{2,1,0:T(8,128)(2,1)S(1)} %get-tuple-element.141.dqkv_ref, bf16[512,1536]{1,0:T(8,128)(2,1)S(1)} %get-tuple-element.140.w_ref, f32[1072,128]{1,0:T(8,128)S(1)} %get-tuple-element.154.dep_ref.refs_0_), custom_call_target="tpu_custom_call" | custom-call | flops 90000000 | bytes 157286 | tf_op jit(solution)/shard_map/project/pallas_call | solution.py:1121
  110.0 1.6 %collective-permute-start.40 = (bf16[512,128]{1,0:T(8,128)(2,1)S(1)}, bf16[512,128]{1,0:T(8,128)(2,1)S(1)}, u32[]{:S(2)}, u32[]{:S(2)}) collective-permute-start(bf16[512,128]{1,0:T(8,128)(2,1)S(1)} %get-tuple-element.169), channel_id=1, source_target_pairs={{0,1},{1,2},{2,3},{3,0},{4,5},{5,6},{6,7},{7,4},{8,9},{9,10},{10,1... | collective-permute-start | bytes 393224 | tf_op jit(solution)/shard_map/ppermute | solution.py:774
  111.6 2.7 %collective-permute-start.41 = (bf16[512,128]{1,0:T(8,128)(2,1)S(1)}, bf16[512,128]{1,0:T(8,128)(2,1)S(1)}, u32[]{:S(2)}, u32[]{:S(2)}) collective-permute-start(bf16[512,128]{1,0:T(8,128)(2,1)S(1)} %get-tuple-element.170), channel_id=1, source_target_pairs={{0,2},{1,3},{2,0},{3,1},{4,6},{5,7},{6,4},{7,5},{8,10},{9,11},{10,... | collective-permute-start | bytes 393224 | tf_op jit(solution)/shard_map/ppermute | solution.py:774
  114.9 3.8 %collective-permute-start.42 = (bf16[512,128]{1,0:T(8,128)(2,1)S(1)}, bf16[512,128]{1,0:T(8,128)(2,1)S(1)}, u32[]{:S(2)}, u32[]{:S(2)}) collective-permute-start(bf16[512,128]{1,0:T(8,128)(2,1)S(1)} %get-tuple-element.171), channel_id=1, source_target_pairs={{0,3},{1,0},{2,1},{3,2},{4,7},{5,4},{6,5},{7,6},{8,11},{9,8},{10,9... | collective-permute-start | bytes 393224 | tf_op jit(solution)/shard_map/ppermute | solution.py:774
  118.7 2.1 %collective-permute-done.34.refs_3_ = bf16[1072,128]{1,0:T(8,128)(2,1)S(1)} collective-permute-done((bf16[1072,128]{1,0:T(8,128)(2,1)S(1)}, bf16[1072,128]{1,0:T(8,128)(2,1)S(1)}, u32[]{:S(2)}, u32[]{:S(2)}) %collective-permute-start.34) | collective-permute-done | bytes 274464 | tf_op jit(solution)/shard_map/ppermute | solution.py:778
  121.5 1.6 %collective-permute-start.35 = (bf16[256,128]{1,0:T(8,128)(2,1)S(1)}, bf16[256,128]{1,0:T(8,128)(2,1)S(1)}, u32[]{:S(2)}, u32[]{:S(2)}) collective-permute-start(bf16[256,128]{1,0:T(8,128)(2,1)S(1)} %get-tuple-element.162), channel_id=1, source_target_pairs={{0,1},{1,2},{2,3},{3,0},{4,5},{5,6},{6,7},{7,4},{8,9},{9,10},{10,1... | collective-permute-start | bytes 196616 | tf_op jit(solution)/shard_map/ppermute | solution.py:774
  123.1 2.7 %collective-permute-start.36 = (bf16[256,128]{1,0:T(8,128)(2,1)S(1)}, bf16[256,128]{1,0:T(8,128)(2,1)S(1)}, u32[]{:S(2)}, u32[]{:S(2)}) collective-permute-start(bf16[256,128]{1,0:T(8,128)(2,1)S(1)} %get-tuple-element.163), channel_id=1, source_target_pairs={{0,2},{1,3},{2,0},{3,1},{4,6},{5,7},{6,4},{7,5},{8,10},{9,11},{10,... | collective-permute-start | bytes 196616 | tf_op jit(solution)/shard_map/ppermute | solution.py:774
  125.9 1.1 mlp_step.1
  127.0 4.4 %input.1 = (f32[5,256,512]{2,1,0:T(8,128)}, f32[8,512]{1,0:T(8,128)S(1)}) custom-call(s32[7]{0:T(128)S(1)} %pad_add_fusion.scal_ref, bf16[5,256,512]{2,1,0:T(8,128)(2,1)S(1)} %project.1.refs_4_.grad_ref, bf16[5,256,512]{2,1,0:T(8,128)(2,1)S(1)} %bitcast.64, bf16[5,256,512]{2,1,0:T(8,128)(2,1)S(1)} %copy-done.1, ...), custom_call_target="tpu_custom_call" | custom-call | flops 3000000 | bytes 196608 | tf_op jit(solution)/shard_map/input/pallas_call | solution.py:1145
  131.4 0.8 attn_step.1
  132.2 11.4 %all_to_all.5.every_ref = bf16[32,16,128]{2,1,0:T(8,128)(2,1)S(1)} all-to-all(bf16[32,16,128]{2,1,0:T(8,128)(2,1)S(1)} %get-tuple-element.176), channel_id=1, replica_groups=mesh['blk'=8,'group'=4] {'blk','group'}, dimensions={0} | all-to-all | bytes 262144 | tf_op jit(solution)/shard_map/all_to_all | solution.py:1178
  143.6 0.9 final.1
  (112 shorter events, 11.1 us)
Async XLA Ops:
  0.7 13.6 %copy-start.15 = (s32[5]{0:T(128)S(1)}, s32[5]{0:T(128)}, u32[]{:S(2)}) copy-start(s32[5]{0:T(128)} %param.17) | copy-start | bytes 64
  0.7 13.6 %copy-start.5 = (f32[4,512]{1,0:T(4,128)S(1)}, f32[4,512]{1,0:T(4,128)}, u32[]{:S(2)}) copy-start(f32[4,512]{1,0:T(4,128)} %ln_ref.9) | copy-start | bytes 24580
  0.7 13.6 %copy-start.1 = (bf16[5,256,512]{2,1,0:T(8,128)(2,1)S(1)}, bf16[5,256,512]{2,1,0:T(8,128)(2,1)}, u32[]{:S(2)}) copy-start(bf16[5,256,512]{2,1,0:T(8,128)(2,1)} %x_ref.3) | copy-start | bytes 3932164
  1.7 15.3 %collective-permute-start.2 = (bf16[192,128]{1,0:T(8,128)(2,1)S(1)}, bf16[192,128]{1,0:T(8,128)(2,1)S(1)}, u32[]{:S(2)}, u32[]{:S(2)}) collective-permute-start(bf16[192,128]{1,0:T(8,128)(2,1)S(1)} %bitcast.77), channel_id=1, source_target_pairs={{0,3},{1,0},{2,1},{3,2},{4,7},{5,4},{6,5},{7,6},{8,11},{9,8},{10,9... | collective-permute-start | bytes 147464 | tf_op jit(solution)/shard_map/ppermute | solution.py:774
  6.8 10.1 %collective-permute-start.1 = (bf16[192,128]{1,0:T(8,128)(2,1)S(1)}, bf16[192,128]{1,0:T(8,128)(2,1)S(1)}, u32[]{:S(2)}, u32[]{:S(2)}) collective-permute-start(bf16[192,128]{1,0:T(8,128)(2,1)S(1)} %bitcast.78), channel_id=1, source_target_pairs={{0,2},{1,3},{2,0},{3,1},{4,6},{5,7},{6,4},{7,5},{8,10},{9,11},{10,... | collective-permute-start | bytes 147464 | tf_op jit(solution)/shard_map/ppermute | solution.py:774
  6.8 10.1 %collective-permute-start = (bf16[192,128]{1,0:T(8,128)(2,1)S(1)}, bf16[192,128]{1,0:T(8,128)(2,1)S(1)}, u32[]{:S(2)}, u32[]{:S(2)}) collective-permute-start(bf16[192,128]{1,0:T(8,128)(2,1)S(1)} %bitcast.79), channel_id=1, source_target_pairs={{0,1},{1,2},{2,3},{3,0},{4,5},{5,6},{6,7},{7,4},{8,9},{9,10},{10,1... | collective-permute-start | bytes 147464 | tf_op jit(solution)/shard_map/ppermute | solution.py:774
  9.6 11.5 %collective-permute-start.11 = (bf16[576,128]{1,0:T(8,128)(2,1)}, bf16[576,128]{1,0:T(8,128)(2,1)S(1)}, u32[]{:S(2)}, u32[]{:S(2)}) collective-permute-start(bf16[576,128]{1,0:T(8,128)(2,1)} %pack.1), channel_id=1, source_target_pairs={{0,3},{1,0},{2,1},{3,2},{4,7},{5,4},{6,5},{7,6},{8,11},{9,8},{10,9... | collective-permute-start | bytes 442376 | tf_op jit(solution)/shard_map/ppermute | solution.py:774
  12.4 7.7 %collective-permute-start.10 = (bf16[576,128]{1,0:T(8,128)(2,1)}, bf16[576,128]{1,0:T(8,128)(2,1)S(1)}, u32[]{:S(2)}, u32[]{:S(2)}) collective-permute-start(bf16[576,128]{1,0:T(8,128)(2,1)} %pack.1), channel_id=1, source_target_pairs={{0,1},{1,2},{2,3},{3,0},{4,5},{5,6},{6,7},{7,4},{8,9},{9,10},{10,1... | collective-permute-start | bytes 442376 | tf_op jit(solution)/shard_map/ppermute | solution.py:774
  17.0 13.7 %collective-permute-start.6 = (bf16[864,128]{1,0:T(8,128)(2,1)S(1)}, bf16[864,128]{1,0:T(8,128)(2,1)S(1)}, u32[]{:S(2)}, u32[]{:S(2)}) collective-permute-start(bf16[864,128]{1,0:T(8,128)(2,1)S(1)} %pad_maximum_fusion.refs_0_), channel_id=1, source_target_pairs={{0,4},{4,0},{8,12},{12,8},{16,20},{20,16},{24,28},{28,24},{1,5},{5... | collective-permute-start | bytes 663560 | tf_op jit(solution)/shard_map/ppermute | solution.py:778
  17.1 9.2 %collective-permute-start.5 = (bf16[864,128]{1,0:T(8,128)(2,1)S(1)}, bf16[864,128]{1,0:T(8,128)(2,1)S(1)}, u32[]{:S(2)}, u32[]{:S(2)}) collective-permute-start(bf16[864,128]{1,0:T(8,128)(2,1)S(1)} %pad_maximum_fusion.refs_0_), channel_id=1, source_target_pairs={{0,24},{4,28},{8,16},{12,20},{16,8},{20,12},{24,0},{28,4},{1,25},{... | collective-permute-start | bytes 663560 | tf_op jit(solution)/shard_map/ppermute | solution.py:778
  19.6 11.6 %collective-permute-start.4 = (bf16[864,128]{1,0:T(8,128)(2,1)S(1)}, bf16[864,128]{1,0:T(8,128)(2,1)S(1)}, u32[]{:S(2)}, u32[]{:S(2)}) collective-permute-start(bf16[864,128]{1,0:T(8,128)(2,1)S(1)} %pad_maximum_fusion.refs_0_), channel_id=1, source_target_pairs={{0,16},{4,20},{8,24},{12,28},{16,0},{20,4},{24,8},{28,12},{1,17},{... | collective-permute-start | bytes 663560 | tf_op jit(solution)/shard_map/ppermute | solution.py:778
  20.1 12.9 %collective-permute-start.3 = (bf16[864,128]{1,0:T(8,128)(2,1)S(1)}, bf16[864,128]{1,0:T(8,128)(2,1)S(1)}, u32[]{:S(2)}, u32[]{:S(2)}) collective-permute-start(bf16[864,128]{1,0:T(8,128)(2,1)S(1)} %pad_maximum_fusion.refs_0_), channel_id=1, source_target_pairs={{0,8},{4,12},{8,0},{12,4},{16,24},{20,28},{24,16},{28,20},{1,9},{5... | collective-permute-start | bytes 663560 | tf_op jit(solution)/shard_map/ppermute | solution.py:778
  21.1 7.1 %collective-permute-start.12 = (bf16[576,128]{1,0:T(8,128)(2,1)S(1)}, bf16[576,128]{1,0:T(8,128)(2,1)S(1)}, u32[]{:S(2)}, u32[]{:S(2)}) collective-permute-start(bf16[576,128]{1,0:T(8,128)(2,1)S(1)} %collective-permute-done.10), channel_id=1, source_target_pairs={{0,1},{1,2},{2,3},{3,0},{4,5},{5,6},{6,7},{7,4},{8,9},{9,10},{10,1... | collective-permute-start | bytes 442376 | tf_op jit(solution)/shard_map/ppermute | solution.py:774
  26.3 6.7 %collective-permute-start.9 = (bf16[864,128]{1,0:T(8,128)(2,1)S(1)}, bf16[864,128]{1,0:T(8,128)(2,1)S(1)}, u32[]{:S(2)}, u32[]{:S(2)}) collective-permute-start(bf16[864,128]{1,0:T(8,128)(2,1)S(1)} %collective-permute-done.5.refs_3_), channel_id=1, source_target_pairs={{0,4},{4,0},{8,12},{12,8},{16,20},{20,16},{24,28},{28,24},{1,5},{5... | collective-permute-start | bytes 663560 | tf_op jit(solution)/shard_map/ppermute | solution.py:778
  28.2 15.2 %collective-permute-start.15 = (bf16[1280,128]{1,0:T(8,128)(2,1)S(1)}, bf16[1280,128]{1,0:T(8,128)(2,1)S(1)}, u32[]{:S(2)}, u32[]{:S(2)}) collective-permute-start(bf16[1280,128]{1,0:T(8,128)(2,1)S(1)} %bitcast.66), channel_id=1, source_target_pairs={{0,24},{4,28},{8,16},{12,20},{16,8},{20,12},{24,0},{28,4},{1,25},{... | collective-permute-start | bytes 983048 | tf_op jit(solution)/shard_map/ppermute | solution.py:778
  30.7 14.0 %collective-permute-start.14 = (bf16[1280,128]{1,0:T(8,128)(2,1)S(1)}, bf16[1280,128]{1,0:T(8,128)(2,1)S(1)}, u32[]{:S(2)}, u32[]{:S(2)}) collective-permute-start(bf16[1280,128]{1,0:T(8,128)(2,1)S(1)} %bitcast.67), channel_id=1, source_target_pairs={{0,16},{4,20},{8,24},{12,28},{16,0},{20,4},{24,8},{28,12},{1,17},{... | collective-permute-start | bytes 983048 | tf_op jit(solution)/shard_map/ppermute | solution.py:778
  31.2 13.5 %collective-permute-start.13 = (bf16[1280,128]{1,0:T(8,128)(2,1)S(1)}, bf16[1280,128]{1,0:T(8,128)(2,1)S(1)}, u32[]{:S(2)}, u32[]{:S(2)}) collective-permute-start(bf16[1280,128]{1,0:T(8,128)(2,1)S(1)} %bitcast.68), channel_id=1, source_target_pairs={{0,8},{4,12},{8,0},{12,4},{16,24},{20,28},{24,16},{28,20},{1,9},{5... | collective-permute-start | bytes 983048 | tf_op jit(solution)/shard_map/ppermute | solution.py:778
  33.0 1.5 %collective-permute-start.8 = (bf16[864,128]{1,0:T(8,128)(2,1)S(1)}, bf16[864,128]{1,0:T(8,128)(2,1)S(1)}, u32[]{:S(2)}, u32[]{:S(2)}) collective-permute-start(bf16[864,128]{1,0:T(8,128)(2,1)S(1)} %collective-permute-done.4.refs_2_), channel_id=1, source_target_pairs={{0,4},{4,0},{8,12},{12,8},{16,20},{20,16},{24,28},{28,24},{1,5},{5... | collective-permute-start | bytes 663560 | tf_op jit(solution)/shard_map/ppermute | solution.py:778
  33.1 1.8 %collective-permute-start.7 = (bf16[864,128]{1,0:T(8,128)(2,1)S(1)}, bf16[864,128]{1,0:T(8,128)(2,1)S(1)}, u32[]{:S(2)}, u32[]{:S(2)}) collective-permute-start(bf16[864,128]{1,0:T(8,128)(2,1)S(1)} %collective-permute-done.3.refs_1_), channel_id=1, source_target_pairs={{0,4},{4,0},{8,12},{12,8},{16,20},{20,16},{24,28},{28,24},{1,5},{5... | collective-permute-start | bytes 663560 | tf_op jit(solution)/shard_map/ppermute | solution.py:778
  34.5 12.8 %collective-permute-start.16 = (bf16[1280,128]{1,0:T(8,128)(2,1)S(1)}, bf16[1280,128]{1,0:T(8,128)(2,1)S(1)}, u32[]{:S(2)}, u32[]{:S(2)}) collective-permute-start(bf16[1280,128]{1,0:T(8,128)(2,1)S(1)} %bitcast.69), channel_id=1, source_target_pairs={{0,4},{4,0},{8,12},{12,8},{16,20},{20,16},{24,28},{28,24},{1,5},{5... | collective-permute-start | bytes 983048 | tf_op jit(solution)/shard_map/ppermute | solution.py:778
  44.8 3.9 %collective-permute-start.17 = (bf16[1280,128]{1,0:T(8,128)(2,1)S(1)}, bf16[1280,128]{1,0:T(8,128)(2,1)S(1)}, u32[]{:S(2)}, u32[]{:S(2)}) collective-permute-start(bf16[1280,128]{1,0:T(8,128)(2,1)S(1)} %get-tuple-element.110.refs_5_), channel_id=1, source_target_pairs={{0,4},{4,0},{8,12},{12,8},{16,20},{20,16},{24,28},{28,24},{1,5},{5... | collective-permute-start | bytes 983048 | tf_op jit(solution)/shard_map/ppermute | solution.py:778
  44.9 4.2 %collective-permute-start.18 = (bf16[1280,128]{1,0:T(8,128)(2,1)S(1)}, bf16[1280,128]{1,0:T(8,128)(2,1)S(1)}, u32[]{:S(2)}, u32[]{:S(2)}) collective-permute-start(bf16[1280,128]{1,0:T(8,128)(2,1)S(1)} %get-tuple-element.111.refs_6_), channel_id=1, source_target_pairs={{0,4},{4,0},{8,12},{12,8},{16,20},{20,16},{24,28},{28,24},{1,5},{5... | collective-permute-start | bytes 983048 | tf_op jit(solution)/shard_map/ppermute | solution.py:778
  45.5 3.7 %collective-permute-start.19 = (bf16[1280,128]{1,0:T(8,128)(2,1)S(1)}, bf16[1280,128]{1,0:T(8,128)(2,1)S(1)}, u32[]{:S(2)}, u32[]{:S(2)}) collective-permute-start(bf16[1280,128]{1,0:T(8,128)(2,1)S(1)} %get-tuple-element.112.refs_7_), channel_id=1, source_target_pairs={{0,4},{4,0},{8,12},{12,8},{16,20},{20,16},{24,28},{28,24},{1,5},{5... | collective-permute-start | bytes 983048 | tf_op jit(solution)/shard_map/ppermute | solution.py:778
  45.6 17.9 %collective-permute-start.22 = (bf16[1024,128]{1,0:T(8,128)(2,1)S(1)}, bf16[1024,128]{1,0:T(8,128)(2,1)S(1)}, u32[]{:S(2)}, u32[]{:S(2)}) collective-permute-start(bf16[1024,128]{1,0:T(8,128)(2,1)S(1)} %gate.4.refs_12_.refs_2_.refs_10_), channel_id=1, source_target_pairs={{0,24},{4,28},{8,16},{12,20},{16,8},{20,12},{24,0},{28,4},{1,25},{... | collective-permute-start | bytes 786440 | tf_op jit(solution)/shard_map/ppermute | solution.py:778
  47.4 16.2 %collective-permute-start.21 = (bf16[1024,128]{1,0:T(8,128)(2,1)S(1)}, bf16[1024,128]{1,0:T(8,128)(2,1)S(1)}, u32[]{:S(2)}, u32[]{:S(2)}) collective-permute-start(bf16[1024,128]{1,0:T(8,128)(2,1)S(1)} %gate.4.refs_12_.refs_2_.refs_10_), channel_id=1, source_target_pairs={{0,16},{4,20},{8,24},{12,28},{16,0},{20,4},{24,8},{28,12},{1,17},{... | collective-permute-start | bytes 786440 | tf_op jit(solution)/shard_map/ppermute | solution.py:778
  48.8 14.8 %collective-permute-start.20 = (bf16[1024,128]{1,0:T(8,128)(2,1)S(1)}, bf16[1024,128]{1,0:T(8,128)(2,1)S(1)}, u32[]{:S(2)}, u32[]{:S(2)}) collective-permute-start(bf16[1024,128]{1,0:T(8,128)(2,1)S(1)} %gate.4.refs_12_.refs_2_.refs_10_), channel_id=1, source_target_pairs={{0,8},{4,12},{8,0},{12,4},{16,24},{20,28},{24,16},{28,20},{1,9},{5... | collective-permute-start | bytes 786440 | tf_op jit(solution)/shard_map/ppermute | solution.py:778
  49.2 15.6 %collective-permute-start.23 = (bf16[1024,128]{1,0:T(8,128)(2,1)S(1)}, bf16[1024,128]{1,0:T(8,128)(2,1)S(1)}, u32[]{:S(2)}, u32[]{:S(2)}) collective-permute-start(bf16[1024,128]{1,0:T(8,128)(2,1)S(1)} %gate.4.refs_12_.refs_2_.refs_10_), channel_id=1, source_target_pairs={{0,4},{4,0},{8,12},{12,8},{16,20},{20,16},{24,28},{28,24},{1,5},{5... | collective-permute-start | bytes 786440 | tf_op jit(solution)/shard_map/ppermute | solution.py:778
  63.6 1.7 %collective-permute-start.24 = (bf16[1024,128]{1,0:T(8,128)(2,1)S(1)}, bf16[1024,128]{1,0:T(8,128)(2,1)S(1)}, u32[]{:S(2)}, u32[]{:S(2)}) collective-permute-start(bf16[1024,128]{1,0:T(8,128)(2,1)S(1)} %get-tuple-element.115.refs_3_), channel_id=1, source_target_pairs={{0,4},{4,0},{8,12},{12,8},{16,20},{20,16},{24,28},{28,24},{1,5},{5... | collective-permute-start | bytes 786440 | tf_op jit(solution)/shard_map/ppermute | solution.py:778
  64.2 1.5 %collective-permute-start.25 = (bf16[1024,128]{1,0:T(8,128)(2,1)S(1)}, bf16[1024,128]{1,0:T(8,128)(2,1)S(1)}, u32[]{:S(2)}, u32[]{:S(2)}) collective-permute-start(bf16[1024,128]{1,0:T(8,128)(2,1)S(1)} %get-tuple-element.116.refs_4_), channel_id=1, source_target_pairs={{0,4},{4,0},{8,12},{12,8},{16,20},{20,16},{24,28},{28,24},{1,5},{5... | collective-permute-start | bytes 786440 | tf_op jit(solution)/shard_map/ppermute | solution.py:778
  64.2 1.8 %collective-permute-start.26 = (bf16[1024,128]{1,0:T(8,128)(2,1)S(1)}, bf16[1024,128]{1,0:T(8,128)(2,1)S(1)}, u32[]{:S(2)}, u32[]{:S(2)}) collective-permute-start(bf16[1024,128]{1,0:T(8,128)(2,1)S(1)} %get-tuple-element.117.refs_5_), channel_id=1, source_target_pairs={{0,4},{4,0},{8,12},{12,8},{16,20},{20,16},{24,28},{28,24},{1,5},{5... | collective-permute-start | bytes 786440 | tf_op jit(solution)/shard_map/ppermute | solution.py:778
  64.7 16.3 %collective-permute-start.27 = (bf16[4,1024,128]{2,1,0:T(8,128)(2,1)S(1)}, bf16[4,1024,128]{2,1,0:T(8,128)(2,1)S(1)}, u32[]{:S(2)}, u32[]{:S(2)}) collective-permute-start(bf16[4,1024,128]{2,1,0:T(8,128)(2,1)S(1)} %get-tuple-element.130), channel_id=1, source_target_pairs={{0,4},{4,0},{8,12},{12,8},{16,20},{20,16},{24,28},{28,24},{1,5},{5... | collective-permute-start | bytes 3145736 | tf_op jit(solution)/shard_map/ppermute | solution.py:778
  78.8 2.7 %collective-permute-start.28 = (bf16[4,1024,128]{2,1,0:T(8,128)(2,1)S(1)}, bf16[4,1024,128]{2,1,0:T(8,128)(2,1)S(1)}, u32[]{:S(2)}, u32[]{:S(2)}) collective-permute-start(bf16[4,1024,128]{2,1,0:T(8,128)(2,1)S(1)} %get-tuple-element.131), channel_id=1, source_target_pairs={{0,4},{4,0},{8,12},{12,8},{16,20},{20,16},{24,28},{28,24},{1,5},{5... | collective-permute-start | bytes 3145736 | tf_op jit(solution)/shard_map/ppermute | solution.py:778
  82.4 14.6 %collective-permute-start.29 = (bf16[2,1024,128]{2,1,0:T(8,128)(2,1)S(1)}, bf16[2,1024,128]{2,1,0:T(8,128)(2,1)S(1)}, u32[]{:S(2)}, u32[]{:S(2)}) collective-permute-start(bf16[2,1024,128]{2,1,0:T(8,128)(2,1)S(1)} %get-tuple-element.148), channel_id=1, source_target_pairs={{0,8},{4,12},{8,0},{12,4},{16,24},{20,28},{24,16},{28,20},{1,9},{5... | collective-permute-start | bytes 1572872 | tf_op jit(solution)/shard_map/ppermute | solution.py:778
  84.2 13.9 %collective-permute-start.30 = (bf16[2,1024,128]{2,1,0:T(8,128)(2,1)S(1)}, bf16[2,1024,128]{2,1,0:T(8,128)(2,1)S(1)}, u32[]{:S(2)}, u32[]{:S(2)}) collective-permute-start(bf16[2,1024,128]{2,1,0:T(8,128)(2,1)S(1)} %get-tuple-element.150), channel_id=1, source_target_pairs={{0,16},{4,20},{8,24},{12,28},{16,0},{20,4},{24,8},{28,12},{1,17},{... | collective-permute-start | bytes 1572872 | tf_op jit(solution)/shard_map/ppermute | solution.py:778
  99.1 2.8 %collective-permute-start.31 = (bf16[4,1072,128]{2,1,0:T(8,128)(2,1)S(1)}, bf16[4,1072,128]{2,1,0:T(8,128)(2,1)S(1)}, u32[]{:S(2)}, u32[]{:S(2)}) collective-permute-start(bf16[4,1072,128]{2,1,0:T(8,128)(2,1)S(1)} %get-tuple-element.153), channel_id=1, source_target_pairs={{0,4},{4,0},{8,12},{12,8},{16,20},{20,16},{24,28},{28,24},{1,5},{5... | collective-permute-start | bytes 3293192 | tf_op jit(solution)/shard_map/ppermute | solution.py:778
  99.2 10.1 %collective-permute-start.38 = (bf16[1024,128]{1,0:T(8,128)(2,1)S(1)}, bf16[1024,128]{1,0:T(8,128)(2,1)S(1)}, u32[]{:S(2)}, u32[]{:S(2)}) collective-permute-start(bf16[1024,128]{1,0:T(8,128)(2,1)S(1)} %get-tuple-element.165), channel_id=1, source_target_pairs={{0,16},{4,20},{8,24},{12,28},{16,0},{20,4},{24,8},{28,12},{1,17},{... | collective-permute-start | bytes 786440 | tf_op jit(solution)/shard_map/ppermute | solution.py:778
  99.9 9.5 %collective-permute-start.39 = (bf16[1024,128]{1,0:T(8,128)(2,1)S(1)}, bf16[1024,128]{1,0:T(8,128)(2,1)S(1)}, u32[]{:S(2)}, u32[]{:S(2)}) collective-permute-start(bf16[1024,128]{1,0:T(8,128)(2,1)S(1)} %get-tuple-element.167), channel_id=1, source_target_pairs={{0,8},{4,12},{8,0},{12,4},{16,24},{20,28},{24,16},{28,20},{1,9},{5... | collective-permute-start | bytes 786440 | tf_op jit(solution)/shard_map/ppermute | solution.py:778
  102.7 12.2 %collective-permute-start.32 = (bf16[1072,128]{1,0:T(8,128)(2,1)S(1)}, bf16[1072,128]{1,0:T(8,128)(2,1)S(1)}, u32[]{:S(2)}, u32[]{:S(2)}) collective-permute-start(bf16[1072,128]{1,0:T(8,128)(2,1)S(1)} %get-tuple-element.156), channel_id=1, source_target_pairs={{0,8},{4,12},{8,0},{12,4},{16,24},{20,28},{24,16},{28,20},{1,9},{5... | collective-permute-start | bytes 823304 | tf_op jit(solution)/shard_map/ppermute | solution.py:778
  103.1 15.6 %collective-permute-start.33 = (bf16[1072,128]{1,0:T(8,128)(2,1)S(1)}, bf16[1072,128]{1,0:T(8,128)(2,1)S(1)}, u32[]{:S(2)}, u32[]{:S(2)}) collective-permute-start(bf16[1072,128]{1,0:T(8,128)(2,1)S(1)} %get-tuple-element.157), channel_id=1, source_target_pairs={{0,16},{4,20},{8,24},{12,28},{16,0},{20,4},{24,8},{28,12},{1,17},{... | collective-permute-start | bytes 823304 | tf_op jit(solution)/shard_map/ppermute | solution.py:778
  104.6 16.3 %collective-permute-start.34 = (bf16[1072,128]{1,0:T(8,128)(2,1)S(1)}, bf16[1072,128]{1,0:T(8,128)(2,1)S(1)}, u32[]{:S(2)}, u32[]{:S(2)}) collective-permute-start(bf16[1072,128]{1,0:T(8,128)(2,1)S(1)} %get-tuple-element.158), channel_id=1, source_target_pairs={{0,24},{4,28},{8,16},{12,20},{16,8},{20,12},{24,0},{28,4},{1,25},{... | collective-permute-start | bytes 823304 | tf_op jit(solution)/shard_map/ppermute | solution.py:778
  110.0 15.8 %collective-permute-start.40 = (bf16[512,128]{1,0:T(8,128)(2,1)S(1)}, bf16[512,128]{1,0:T(8,128)(2,1)S(1)}, u32[]{:S(2)}, u32[]{:S(2)}) collective-permute-start(bf16[512,128]{1,0:T(8,128)(2,1)S(1)} %get-tuple-element.169), channel_id=1, source_target_pairs={{0,1},{1,2},{2,3},{3,0},{4,5},{5,6},{6,7},{7,4},{8,9},{9,10},{10,1... | collective-permute-start | bytes 393224 | tf_op jit(solution)/shard_map/ppermute | solution.py:774
  111.6 14.2 %collective-permute-start.41 = (bf16[512,128]{1,0:T(8,128)(2,1)S(1)}, bf16[512,128]{1,0:T(8,128)(2,1)S(1)}, u32[]{:S(2)}, u32[]{:S(2)}) collective-permute-start(bf16[512,128]{1,0:T(8,128)(2,1)S(1)} %get-tuple-element.170), channel_id=1, source_target_pairs={{0,2},{1,3},{2,0},{3,1},{4,6},{5,7},{6,4},{7,5},{8,10},{9,11},{10,... | collective-permute-start | bytes 393224 | tf_op jit(solution)/shard_map/ppermute | solution.py:774
  114.9 10.9 %collective-permute-start.42 = (bf16[512,128]{1,0:T(8,128)(2,1)S(1)}, bf16[512,128]{1,0:T(8,128)(2,1)S(1)}, u32[]{:S(2)}, u32[]{:S(2)}) collective-permute-start(bf16[512,128]{1,0:T(8,128)(2,1)S(1)} %get-tuple-element.171), channel_id=1, source_target_pairs={{0,3},{1,0},{2,1},{3,2},{4,7},{5,4},{6,5},{7,6},{8,11},{9,8},{10,9... | collective-permute-start | bytes 393224 | tf_op jit(solution)/shard_map/ppermute | solution.py:774
  121.5 9.8 %collective-permute-start.35 = (bf16[256,128]{1,0:T(8,128)(2,1)S(1)}, bf16[256,128]{1,0:T(8,128)(2,1)S(1)}, u32[]{:S(2)}, u32[]{:S(2)}) collective-permute-start(bf16[256,128]{1,0:T(8,128)(2,1)S(1)} %get-tuple-element.162), channel_id=1, source_target_pairs={{0,1},{1,2},{2,3},{3,0},{4,5},{5,6},{6,7},{7,4},{8,9},{9,10},{10,1... | collective-permute-start | bytes 196616 | tf_op jit(solution)/shard_map/ppermute | solution.py:774
  123.1 8.2 %collective-permute-start.36 = (bf16[256,128]{1,0:T(8,128)(2,1)S(1)}, bf16[256,128]{1,0:T(8,128)(2,1)S(1)}, u32[]{:S(2)}, u32[]{:S(2)}) collective-permute-start(bf16[256,128]{1,0:T(8,128)(2,1)S(1)} %get-tuple-element.163), channel_id=1, source_target_pairs={{0,2},{1,3},{2,0},{3,1},{4,6},{5,7},{6,4},{7,5},{8,10},{9,11},{10,... | collective-permute-start | bytes 196616 | tf_op jit(solution)/shard_map/ppermute | solution.py:774
  125.8 5.6 %collective-permute-start.37 = (bf16[256,128]{1,0:T(8,128)(2,1)S(1)}, bf16[256,128]{1,0:T(8,128)(2,1)S(1)}, u32[]{:S(2)}, u32[]{:S(2)}) collective-permute-start(bf16[256,128]{1,0:T(8,128)(2,1)S(1)} %get-tuple-element.164), channel_id=1, source_target_pairs={{0,3},{1,0},{2,1},{3,2},{4,7},{5,4},{6,5},{7,6},{8,11},{9,8},{10,9... | collective-permute-start | bytes 196616 | tf_op jit(solution)/shard_map/ppermute | solution.py:774
  127.0 16.6 %copy-start.12 = (f32[4,512]{1,0:T(4,128)S(1)}, f32[4,512]{1,0:T(4,128)}, u32[]{:S(2)}) copy-start(f32[4,512]{1,0:T(4,128)} %lf_ref.1) | copy-start | bytes 24580
  127.0 16.6 %copy-start.13 = (f32[4,512]{1,0:T(4,128)S(1)}, f32[4,512]{1,0:T(4,128)}, u32[]{:S(2)}) copy-start(f32[4,512]{1,0:T(4,128)} %ls_ref.1) | copy-start | bytes 24580
  (11 other events, 90.7 us)

commit v6 on v5

--- a/solution.py
+++ b/solution.py
@@ -97,6 +97,19 @@
     if isinstance(start, int):
         return slice(start, start + size)
     return pl.ds(pl.multiple_of(start, size), size)
+
+
+def over_seqs(step, moving, unrolled, *refs):
+    count = next(ref.shape[0] for ref, moves in zip(refs, moving) if moves)
+
+    def one(i):
+        step(i, *(ref.at[pl.ds(i, 1)] if moves else ref for ref, moves in zip(refs, moving)))
+
+    if unrolled:
+        for i in range(count):
+            one(i)
+    else:
+        pl.loop(0, count)(one)
 
 
 def copy_attn(w_ref, own_refs, other_refs, spot, core, dims):
@@ -116,8 +129,7 @@
     each_core(core, do)
 
 
-def prep_kernel(scal_ref, x_ref, ln_ref, normed_ref, rider_ref, sum_ref):
-    i = pl.program_id(0)
+def prep_kernel(seqs, i, scal_ref, x_ref, ln_ref, normed_ref, rider_ref, sum_ref):
     tok, width = x_ref.shape[1:]
     spans = tok // SPAN
     tiles = width // SPAN
@@ -132,18 +144,16 @@
     amount = jnp.maximum(jnp.sum(chosen, 1, keepdims=True), 1.0)
     total = mm(chosen.astype(b16), normed) / amount
 
-    @pl.when(i == 0)
-    def _():
+    if i == 0:
         sum_ref[...] = jnp.zeros_like(sum_ref)
 
     for s in range(spans):
         for t in range(tiles):
-            sum_ref[pl.ds((i * spans + s) * tiles + t, 1), :] = total[
+            sum_ref[(i * spans + s) * tiles + t : (i * spans + s) * tiles + t + 1, :] = total[
                 s : s + 1, t * SPAN : (t + 1) * SPAN
             ]
 
-    @pl.when(i == pl.num_programs(0) - 1)
-    def _():
+    if i == seqs - 1:
         every = sum_ref[...]
         high = every.astype(b16)
         rider_ref[:half] = high
@@ -875,17 +885,14 @@
     attn_piece = attn_master[:3].astype(b16).reshape(3 * rows, cols)
     if fast:
         attn_z = gather_group(attn_piece, z, ng)
-    normed, rider = pl.pallas_call(
-        prep_kernel,
-        grid=(seqs,),
-        in_specs=[scalars(), per_step(tok, width), fixed(4, width)],
-        out_specs=[per_step(tok, width), fixed(2 * half, SPAN)],
-        out_shape=[like(b16, tok, width), shape((2 * half, SPAN), b16)],
-        scratch_shapes=[pltpu.VMEM((half, SPAN), f32)],
-        compiler_params=params(16),
-        cost_estimate=cost(4e7, 2 * seqs * tok * width * 2),
-        name="prep",
-    )(scal, tokens, ln_params)
+    normed, rider = flat(
+        functools.partial(
+            over_seqs, functools.partial(prep_kernel, seqs), (False, True, False, True, False, False), True
+        ),
+        "prep", [like(b16, tok, width), shape((2 * half, SPAN), b16)],
+        [pltpu.VMEM((half, SPAN), f32)], cost(4e7, 2 * seqs * tok * width * 2),
+        scal, tokens, ln_params, scalar=True,
+    )
 
     def gate(pieces, *deps):
         return flat(

time: 145 us -> 144 us (level)
    pallas_call x1 -> x0, Pallas kernels: 2.56 us -> none  [body(): pl.pallas_call(prep_kernel, grid=(seqs,), in_specs=[scalars(), per_step(t...]
    ppermute x31, waiting for transfers between devices: 12.9 us -> 10.4 us  [cross(): return lax.ppermute(values, 'blk', [(j, j ^ bit) for j in range(nb)])]
    pallas_call x13 -> x14, Pallas kernels: 9.64 us -> 11.3 us  [flat(): pl.pallas_call(call, in_specs=[scalars()] * scalar + [whole()] * (len(arg...]
    ppermute x12, waiting for transfers between devices: 1.87 us -> 3.37 us  [shift(): lax.ppermute(values, 'group', [(j, (j + by) % ng) for j in range(ng)])]
  transfers between devices with their start and end apart: 43 -> 43, of which waited for: 14 -> 15; matrix products, arithmetic and copies ran while one was open for 2% -> 2% of each run, Pallas kernels for 45% -> 44%
where the time goes in v6:
time: 144 us
  Pallas kernels  67.5 us (47%)
  starting transfers between devices  45.8 us (32%)
  waiting for transfers between devices  13.8 us (10%)
  blocking collectives  11.3 us (8%)
  local copies, waits for them, and re-layouts  3.91 us (3%)
    pallas_call x2, Pallas kernels, body(): pl.pallas_call(functools.partial(mlp_kernel, mlp_dims, fast, places, firs...  27 us
    ppermute x12, starting transfers between devices, shift(): lax.ppermute(values, 'group', [(j, (j + by) % ng) for j in range(ng)])  23.3 us
    ppermute x31, starting transfers between devices, cross(): return lax.ppermute(values, 'blk', [(j, j ^ bit) for j in range(nb)])  22.5 us
    all_to_all x1, blocking collectives, body(): every = lax.all_to_all(message, ('blk', 'group'), 0, 0, tiled=True)  11.3 us
    pallas_call x14, Pallas kernels, flat(): pl.pallas_call(call, in_specs=[scalars()] * scalar + [whole()] * (len(arg...  11.3 us
    ppermute x31, waiting for transfers between devices, cross(): return lax.ppermute(values, 'blk', [(j, j ^ bit) for j in range(nb)])  10.4 us
    pallas_call x1, Pallas kernels, body(): pl.pallas_call(functools.partial(forward_kernel, dims, fast, places), gri...  8.56 us
    pallas_call x1, Pallas kernels, body(): pl.pallas_call(functools.partial(backward_kernel, places), grid=(seqs,),...  7.94 us
  transfers between devices with their start and end apart: 43, of which 15 were waited for; matrix products, arithmetic and copies ran while one was open for 2% of the time, Pallas kernels for 44%

profile of v6, /device:TPU:0, one launch (start us, length us, event | category | flops | bytes accessed | tf_op | source)
XLA Modules:
  0.0 143.6 jit_solution(3396252767591413750)
XLA Ops:
  0.7 1.0 slice.71
  1.7 5.1 %collective-permute-start.2 = (bf16[192,128]{1,0:T(8,128)(2,1)S(1)}, bf16[192,128]{1,0:T(8,128)(2,1)S(1)}, u32[]{:S(2)}, u32[]{:S(2)}) collective-permute-start(bf16[192,128]{1,0:T(8,128)(2,1)S(1)} %bitcast.77), channel_id=1, source_target_pairs={{0,3},{1,0},{2,1},{3,2},{4,7},{5,4},{6,5},{7,6},{8,11},{9,8},{10,9... | collective-permute-start | bytes 147464 | tf_op jit(solution)/shard_map/ppermute | solution.py:784
  6.8 1.0 collective-permute-start
  7.8 1.8 %pack.1 = bf16[576,128]{1,0:T(8,128)(2,1)} custom-call(f32[4,64,128]{2,1,0:T(8,128)} %am_ref.1, f32[64,512]{1,0:T(8,128)} %um_ref.1, f32[256,128]{1,0:T(8,128)} %dm_ref.1, bf16[192,128]{1,0:T(8,128)(2,1)} %bitcast.80), custom_call_target="tpu_custom_call" | custom-call | flops 30000 | bytes 30000 | tf_op jit(solution)/shard_map/pack/pallas_call | solution.py:911
  9.6 2.8 %collective-permute-start.11 = (bf16[576,128]{1,0:T(8,128)(2,1)}, bf16[576,128]{1,0:T(8,128)(2,1)S(1)}, u32[]{:S(2)}, u32[]{:S(2)}) collective-permute-start(bf16[576,128]{1,0:T(8,128)(2,1)} %pack.1), channel_id=1, source_target_pairs={{0,3},{1,0},{2,1},{3,2},{4,7},{5,4},{6,5},{7,6},{8,11},{9,8},{10,9... | collective-permute-start | bytes 442376 | tf_op jit(solution)/shard_map/ppermute | solution.py:784
  12.4 0.9 fusion.3
  13.4 0.8 bitcast_dynamic-update-slice_fusion.3
  14.3 1.6 %prep.1 = (bf16[5,256,512]{2,1,0:T(8,128)(2,1)S(1)}, bf16[96,128]{1,0:T(8,128)(2,1)S(1)}) custom-call(s32[7]{0:T(128)S(1)} %pad_add_fusion.refs_0_.scal_ref, bf16[5,256,512]{2,1,0:T(8,128)(2,1)S(1)} %copy-done.1, f32[4,512]{1,0:T(4,128)S(1)} %copy-done.5), custom_call_target="tpu_custom_call" | custom-call | flops 1200000 | bytes 78643 | tf_op jit(solution)/shard_map/prep/pallas_call | solution.py:872
  16.1 2.5 %collective-permute-start.5 = (bf16[864,128]{1,0:T(8,128)(2,1)S(1)}, bf16[864,128]{1,0:T(8,128)(2,1)S(1)}, u32[]{:S(2)}, u32[]{:S(2)}) collective-permute-start(bf16[864,128]{1,0:T(8,128)(2,1)S(1)} %pad_maximum_fusion.refs_0_), channel_id=1, source_target_pairs={{0,24},{4,28},{8,16},{12,20},{16,8},{20,12},{24,0},{28,4},{1,25},{... | collective-permute-start | bytes 663560 | tf_op jit(solution)/shard_map/ppermute | solution.py:788
  19.6 1.5 %collective-permute-start.3 = (bf16[864,128]{1,0:T(8,128)(2,1)S(1)}, bf16[864,128]{1,0:T(8,128)(2,1)S(1)}, u32[]{:S(2)}, u32[]{:S(2)}) collective-permute-start(bf16[864,128]{1,0:T(8,128)(2,1)S(1)} %pad_maximum_fusion.refs_0_), channel_id=1, source_target_pairs={{0,8},{4,12},{8,0},{12,4},{16,24},{20,28},{24,16},{28,20},{1,9},{5... | collective-permute-start | bytes 663560 | tf_op jit(solution)/shard_map/ppermute | solution.py:788
  21.1 1.5 %collective-permute-start.12 = (bf16[576,128]{1,0:T(8,128)(2,1)S(1)}, bf16[576,128]{1,0:T(8,128)(2,1)S(1)}, u32[]{:S(2)}, u32[]{:S(2)}) collective-permute-start(bf16[576,128]{1,0:T(8,128)(2,1)S(1)} %collective-permute-done.10), channel_id=1, source_target_pairs={{0,1},{1,2},{2,3},{3,0},{4,5},{5,6},{6,7},{7,4},{8,9},{9,10},{10,1... | collective-permute-start | bytes 442376 | tf_op jit(solution)/shard_map/ppermute | solution.py:784
  22.6 2.8 %collective-permute-done.5.refs_3_ = bf16[864,128]{1,0:T(8,128)(2,1)S(1)} collective-permute-done((bf16[864,128]{1,0:T(8,128)(2,1)S(1)}, bf16[864,128]{1,0:T(8,128)(2,1)S(1)}, u32[]{:S(2)}, u32[]{:S(2)}) %collective-permute-start.5) | collective-permute-done | bytes 221216 | tf_op jit(solution)/shard_map/ppermute | solution.py:788
  25.4 2.9 %collective-permute-done.12 = bf16[576,128]{1,0:T(8,128)(2,1)S(1)} collective-permute-done((bf16[576,128]{1,0:T(8,128)(2,1)S(1)}, bf16[576,128]{1,0:T(8,128)(2,1)S(1)}, u32[]{:S(2)}, u32[]{:S(2)}) %collective-permute-start.12) | collective-permute-done | bytes 147488 | tf_op jit(solution)/shard_map/ppermute | solution.py:784
  28.3 1.6 %collective-permute-start.15 = (bf16[1280,128]{1,0:T(8,128)(2,1)S(1)}, bf16[1280,128]{1,0:T(8,128)(2,1)S(1)}, u32[]{:S(2)}, u32[]{:S(2)}) collective-permute-start(bf16[1280,128]{1,0:T(8,128)(2,1)S(1)} %bitcast.66), channel_id=1, source_target_pairs={{0,24},{4,28},{8,16},{12,20},{16,8},{20,12},{24,0},{28,4},{1,25},{... | collective-permute-start | bytes 983048 | tf_op jit(solution)/shard_map/ppermute | solution.py:788
  30.4 1.4 collective-permute-start.13
  31.9 0.9 fusion.7
  33.4 0.9 collective-permute-done.8.refs_6_
  34.6 8.6 %forward.1 = (bf16[5,256,512]{2,1,0:T(8,128)(2,1)S(1)}, bf16[5,256,512]{2,1,0:T(8,128)(2,1)S(1)}, bf16[5,256,512]{2,1,0:T(8,128)(2,1)S(1)}, bf16[5,16,512]{2,1,0...) custom-call(s32[7]{0:T(128)S(1)} %pad_add_fusion.refs_0_.scal_ref, ...), custom_call_target="tpu_custom_call" | custom-call | flops 240000000 | bytes 275251 | tf_op jit(solution)/shard_map/forward/pallas_call | solution.py:942
  44.7 1.7 %collective-permute-start.22 = (bf16[1024,128]{1,0:T(8,128)(2,1)S(1)}, bf16[1024,128]{1,0:T(8,128)(2,1)S(1)}, u32[]{:S(2)}, u32[]{:S(2)}) collective-permute-start(bf16[1024,128]{1,0:T(8,128)(2,1)S(1)} %gate.4.refs_12_.refs_2_.refs_10_), channel_id=1, source_target_pairs={{0,24},{4,28},{8,16},{12,20},{16,8},{20,12},{24,0},{28,4},{1,25},{... | collective-permute-start | bytes 786440 | tf_op jit(solution)/shard_map/ppermute | solution.py:788
  46.3 1.3 collective-permute-start.21
  48.2 14.3 %mlp.2 = (bf16[1280,512]{1,0:T(8,128)(2,1)S(1)}, bf16[1280,512]{1,0:T(8,128)(2,1)S(1)}, bf16[512,512]{1,0:T(8,128)(2,1)S(1)}, f32[8,128]{1,0:T(8,128)S(1)}, bf16...) custom-call(s32[7]{0:T(128)S(1)} %pad_add_fusion.refs_0_.scal_ref, ...), custom_call_target="tpu_custom_call" | custom-call | flops 270000000 | bytes 393216 | tf_op jit(solution)/shard_map/mlp/pallas_call | solution.py:1006
  65.1 12.7 %mlp.3 = (bf16[1280,512]{1,0:T(8,128)(2,1)}, bf16[1280,512]{1,0:T(8,128)(2,1)S(1)}, bf16[4,1024,128]{2,1,0:T(8,128)(2,1)S(1)}, bf16[4,1024,128]{2,1,0:T(8,128)(2,1)S(1)}) custom-call(s32[7]{0:T(128)S(1)} %pad_add_fusion.refs_0_.scal_ref, bf16[1280,512]{1,0:T(8,128)(2,1)S(1)} %get-tuple-element.113.refs_0_, bf16[1280,512]{1,0:T(8,128)(2,1)S(1)} %bitcast.58, ...), custom_call_target="tpu_custom_call" | custom-call | flops 270000000 | bytes 393216 | tf_op jit(solution)/shard_map/mlp/pallas_call | solution.py:1006
  78.2 1.8 %middle.2 = (bf16[1280,512]{1,0:T(8,128)(2,1)S(1)}, bf16[1280,512]{1,0:T(8,128)(2,1)S(1)}, f32[512,512]{1,0:T(8,128)S(1)}, f32[8,512]{1,0:T(8,128)S(1)}) custom-call(bf16[1280,512]{1,0:T(8,128)(2,1)S(1)} %get-tuple-element.122.gm_ref, bf16[1280,512]{1,0:T(8,128)(2,1)S(1)} %bitcast.59, bf16[1280,512]{1,0:T(8,128)(2,1)S(1)} %get-tuple-element.118.refs_11_.x2_ref, ...), custom_call_target="tpu_custom_call" | custom-call | flops 90000000 | bytes 275251 | tf_op jit(solution)/shard_map/middle/pallas_call | solution.py:1030
  80.5 1.0 halves.1
  81.5 1.6 %collective-permute-start.29 = (bf16[2,1024,128]{2,1,0:T(8,128)(2,1)S(1)}, bf16[2,1024,128]{2,1,0:T(8,128)(2,1)S(1)}, u32[]{:S(2)}, u32[]{:S(2)}) collective-permute-start(bf16[2,1024,128]{2,1,0:T(8,128)(2,1)S(1)} %get-tuple-element.148), channel_id=1, source_target_pairs={{0,8},{4,12},{8,0},{12,4},{16,24},{20,28},{24,16},{28,20},{1,9},{5... | collective-permute-start | bytes 1572872 | tf_op jit(solution)/shard_map/ppermute | solution.py:788
  83.0 0.7 collective-permute-start.30
  83.7 1.8 %middle.3 = (bf16[1280,512]{1,0:T(8,128)(2,1)S(1)}, bf16[1280,512]{1,0:T(8,128)(2,1)S(1)}, f32[512,512]{1,0:T(8,128)S(1)}, f32[8,512]{1,0:T(8,128)S(1)}) custom-call(bf16[1280,512]{1,0:T(8,128)(2,1)S(1)} %get-tuple-element.122.gm_ref, bf16[1280,512]{1,0:T(8,128)(2,1)S(1)} %bitcast.60, ...), custom_call_target="tpu_custom_call", output_to_operand_aliasing={{0}: (6, {}), {1}: (7, {})} | custom-call | flops 90000000 | bytes 275251 | tf_op jit(solution)/shard_map/middle/pallas_call | solution.py:1030
  85.5 7.9 %backward.1 = (bf16[5,256,1536]{2,1,0:T(8,128)(2,1)S(1)}, bf16[5,16,512]{2,1,0:T(8,128)(2,1)S(1)}, bf16[5,16,512]{2,1,0:T(8,128)(2,1)S(1)}, f32[2,4,48,128]{3,2,1,0:T(8,128)S(1)}) custom-call(s32[7]{0:T(128)S(1)} %pad_add_fusion.refs_0_.scal_ref, bf16[5,256,512]{2,1,0:T(8,128)(2,1)S(1)} %bitcast.63, bf16[5,256,512]{2,1,0:T(8,128)(2,1)S(1)} %get-tuple-element.134.q_ref, ...), custom_call_target="tpu_custom_call" | custom-call | flops 420000000 | bytes 471859 | tf_op jit(solution)/shard_map/backward/pallas_call | solution.py:1063
  93.5 2.5 %grads.1.dw_ref = f32[512,1536]{1,0:T(8,128)S(1)} custom-call(bf16[1280,512]{1,0:T(8,128)(2,1)S(1)} %bitcast.65, bf16[1280,1536]{1,0:T(8,128)(2,1)S(1)} %bitcast.61, bf16[80,512]{1,0:T(8,128)(2,1)S(1)} %bitcast.73, bf16[80,512]{1,0:T(8,128)(2,1)S(1)} %bitcast.74, bf16[80,512]{1,0:T(8,128)(2,1)S(1)} %bitcast.75), custom_call_target="tpu_custom_call" | custom-call | flops 30000 | bytes 3000 | tf_op jit(solution)/shard_map/grads/pallas_call | solution.py:872
  96.0 0.9 collective-permute-done.30.refs_3_
  97.1 0.9 cut.1
  98.0 0.8 collective-permute-start.38
  98.8 1.3 collective-permute-start.39
  100.7 0.8 spread.1
  102.2 1.4 collective-permute-start.33
  103.6 1.5 %collective-permute-start.34 = (bf16[1072,128]{1,0:T(8,128)(2,1)S(1)}, bf16[1072,128]{1,0:T(8,128)(2,1)S(1)}, u32[]{:S(2)}, u32[]{:S(2)}) collective-permute-start(bf16[1072,128]{1,0:T(8,128)(2,1)S(1)} %get-tuple-element.158), channel_id=1, source_target_pairs={{0,24},{4,28},{8,16},{12,20},{16,8},{20,12},{24,0},{28,4},{1,25},{... | collective-permute-start | bytes 823304 | tf_op jit(solution)/shard_map/ppermute | solution.py:788
  105.1 3.0 %project.1.refs_4_.grad_ref = bf16[5,256,512]{2,1,0:T(8,128)(2,1)S(1)} custom-call(bf16[5,256,1536]{2,1,0:T(8,128)(2,1)S(1)} %get-tuple-element.141.dqkv_ref, bf16[512,1536]{1,0:T(8,128)(2,1)S(1)} %get-tuple-element.140.w_ref, f32[1072,128]{1,0:T(8,128)S(1)} %get-tuple-element.154.dep_ref.refs_0_), custom_call_target="tpu_custom_call" | custom-call | flops 90000000 | bytes 157286 | tf_op jit(solution)/shard_map/project/pallas_call | solution.py:1128
  108.8 1.8 %collective-permute-start.40 = (bf16[512,128]{1,0:T(8,128)(2,1)S(1)}, bf16[512,128]{1,0:T(8,128)(2,1)S(1)}, u32[]{:S(2)}, u32[]{:S(2)}) collective-permute-start(bf16[512,128]{1,0:T(8,128)(2,1)S(1)} %get-tuple-element.169), channel_id=1, source_target_pairs={{0,1},{1,2},{2,3},{3,0},{4,5},{5,6},{6,7},{7,4},{8,9},{9,10},{10,1... | collective-permute-start | bytes 393224 | tf_op jit(solution)/shard_map/ppermute | solution.py:784
  110.6 2.7 %collective-permute-start.41 = (bf16[512,128]{1,0:T(8,128)(2,1)S(1)}, bf16[512,128]{1,0:T(8,128)(2,1)S(1)}, u32[]{:S(2)}, u32[]{:S(2)}) collective-permute-start(bf16[512,128]{1,0:T(8,128)(2,1)S(1)} %get-tuple-element.170), channel_id=1, source_target_pairs={{0,2},{1,3},{2,0},{3,1},{4,6},{5,7},{6,4},{7,5},{8,10},{9,11},{10,... | collective-permute-start | bytes 393224 | tf_op jit(solution)/shard_map/ppermute | solution.py:784
  113.9 3.9 %collective-permute-start.42 = (bf16[512,128]{1,0:T(8,128)(2,1)S(1)}, bf16[512,128]{1,0:T(8,128)(2,1)S(1)}, u32[]{:S(2)}, u32[]{:S(2)}) collective-permute-start(bf16[512,128]{1,0:T(8,128)(2,1)S(1)} %get-tuple-element.171), channel_id=1, source_target_pairs={{0,3},{1,0},{2,1},{3,2},{4,7},{5,4},{6,5},{7,6},{8,11},{9,8},{10,9... | collective-permute-start | bytes 393224 | tf_op jit(solution)/shard_map/ppermute | solution.py:784
  117.8 1.9 %collective-permute-done.34.refs_3_ = bf16[1072,128]{1,0:T(8,128)(2,1)S(1)} collective-permute-done((bf16[1072,128]{1,0:T(8,128)(2,1)S(1)}, bf16[1072,128]{1,0:T(8,128)(2,1)S(1)}, u32[]{:S(2)}, u32[]{:S(2)}) %collective-permute-start.34) | collective-permute-done | bytes 274464 | tf_op jit(solution)/shard_map/ppermute | solution.py:788
  120.4 1.8 %collective-permute-start.35 = (bf16[256,128]{1,0:T(8,128)(2,1)S(1)}, bf16[256,128]{1,0:T(8,128)(2,1)S(1)}, u32[]{:S(2)}, u32[]{:S(2)}) collective-permute-start(bf16[256,128]{1,0:T(8,128)(2,1)S(1)} %get-tuple-element.162), channel_id=1, source_target_pairs={{0,1},{1,2},{2,3},{3,0},{4,5},{5,6},{6,7},{7,4},{8,9},{9,10},{10,1... | collective-permute-start | bytes 196616 | tf_op jit(solution)/shard_map/ppermute | solution.py:784
  122.1 2.7 %collective-permute-start.36 = (bf16[256,128]{1,0:T(8,128)(2,1)S(1)}, bf16[256,128]{1,0:T(8,128)(2,1)S(1)}, u32[]{:S(2)}, u32[]{:S(2)}) collective-permute-start(bf16[256,128]{1,0:T(8,128)(2,1)S(1)} %get-tuple-element.163), channel_id=1, source_target_pairs={{0,2},{1,3},{2,0},{3,1},{4,6},{5,7},{6,4},{7,5},{8,10},{9,11},{10,... | collective-permute-start | bytes 196616 | tf_op jit(solution)/shard_map/ppermute | solution.py:784
  124.9 1.1 mlp_step.1
  126.1 4.4 %input.1 = (f32[5,256,512]{2,1,0:T(8,128)}, f32[8,512]{1,0:T(8,128)S(1)}) custom-call(s32[7]{0:T(128)S(1)} %pad_add_fusion.refs_0_.scal_ref, bf16[5,256,512]{2,1,0:T(8,128)(2,1)S(1)} %project.1.refs_4_.grad_ref, bf16[5,256,512]{2,1,0:T(8,128)(2,1)S(1)} %bitcast.64, bf16[5,256,512]{2,1,0:T(8,128)(2,1)S(1)} %copy-done.1, ...), custom_call_target="tpu_custom_call" | custom-call | flops 3000000 | bytes 196608 | tf_op jit(solution)/shard_map/input/pallas_call | solution.py:1152
  130.5 0.8 attn_step.1
  131.3 11.3 %all_to_all.5.every_ref = bf16[32,16,128]{2,1,0:T(8,128)(2,1)S(1)} all-to-all(bf16[32,16,128]{2,1,0:T(8,128)(2,1)S(1)} %get-tuple-element.176), channel_id=1, replica_groups=mesh['blk'=8,'group'=4] {'blk','group'}, dimensions={0} | all-to-all | bytes 262144 | tf_op jit(solution)/shard_map/all_to_all | solution.py:1185
  142.6 0.9 final.1
  (112 shorter events, 11.5 us)
Async XLA Ops:
  0.7 13.6 %copy-start.15 = (s32[5]{0:T(128)S(1)}, s32[5]{0:T(128)}, u32[]{:S(2)}) copy-start(s32[5]{0:T(128)} %param.17) | copy-start | bytes 64
  0.7 13.6 %copy-start.5 = (f32[4,512]{1,0:T(4,128)S(1)}, f32[4,512]{1,0:T(4,128)}, u32[]{:S(2)}) copy-start(f32[4,512]{1,0:T(4,128)} %ln_ref.7) | copy-start | bytes 24580
  0.7 13.6 %copy-start.1 = (bf16[5,256,512]{2,1,0:T(8,128)(2,1)S(1)}, bf16[5,256,512]{2,1,0:T(8,128)(2,1)}, u32[]{:S(2)}) copy-start(bf16[5,256,512]{2,1,0:T(8,128)(2,1)} %x_ref.1) | copy-start | bytes 3932164
  1.7 14.3 %collective-permute-start.2 = (bf16[192,128]{1,0:T(8,128)(2,1)S(1)}, bf16[192,128]{1,0:T(8,128)(2,1)S(1)}, u32[]{:S(2)}, u32[]{:S(2)}) collective-permute-start(bf16[192,128]{1,0:T(8,128)(2,1)S(1)} %bitcast.77), channel_id=1, source_target_pairs={{0,3},{1,0},{2,1},{3,2},{4,7},{5,4},{6,5},{7,6},{8,11},{9,8},{10,9... | collective-permute-start | bytes 147464 | tf_op jit(solution)/shard_map/ppermute | solution.py:784
  6.8 9.2 %collective-permute-start.1 = (bf16[192,128]{1,0:T(8,128)(2,1)S(1)}, bf16[192,128]{1,0:T(8,128)(2,1)S(1)}, u32[]{:S(2)}, u32[]{:S(2)}) collective-permute-start(bf16[192,128]{1,0:T(8,128)(2,1)S(1)} %bitcast.78), channel_id=1, source_target_pairs={{0,2},{1,3},{2,0},{3,1},{4,6},{5,7},{6,4},{7,5},{8,10},{9,11},{10,... | collective-permute-start | bytes 147464 | tf_op jit(solution)/shard_map/ppermute | solution.py:784
  6.8 9.1 %collective-permute-start = (bf16[192,128]{1,0:T(8,128)(2,1)S(1)}, bf16[192,128]{1,0:T(8,128)(2,1)S(1)}, u32[]{:S(2)}, u32[]{:S(2)}) collective-permute-start(bf16[192,128]{1,0:T(8,128)(2,1)S(1)} %bitcast.79), channel_id=1, source_target_pairs={{0,1},{1,2},{2,3},{3,0},{4,5},{5,6},{6,7},{7,4},{8,9},{9,10},{10,1... | collective-permute-start | bytes 147464 | tf_op jit(solution)/shard_map/ppermute | solution.py:784
  9.6 11.5 %collective-permute-start.11 = (bf16[576,128]{1,0:T(8,128)(2,1)}, bf16[576,128]{1,0:T(8,128)(2,1)S(1)}, u32[]{:S(2)}, u32[]{:S(2)}) collective-permute-start(bf16[576,128]{1,0:T(8,128)(2,1)} %pack.1), channel_id=1, source_target_pairs={{0,3},{1,0},{2,1},{3,2},{4,7},{5,4},{6,5},{7,6},{8,11},{9,8},{10,9... | collective-permute-start | bytes 442376 | tf_op jit(solution)/shard_map/ppermute | solution.py:784
  12.4 7.2 %collective-permute-start.10 = (bf16[576,128]{1,0:T(8,128)(2,1)}, bf16[576,128]{1,0:T(8,128)(2,1)S(1)}, u32[]{:S(2)}, u32[]{:S(2)}) collective-permute-start(bf16[576,128]{1,0:T(8,128)(2,1)} %pack.1), channel_id=1, source_target_pairs={{0,1},{1,2},{2,3},{3,0},{4,5},{5,6},{6,7},{7,4},{8,9},{9,10},{10,1... | collective-permute-start | bytes 442376 | tf_op jit(solution)/shard_map/ppermute | solution.py:784
  16.1 13.9 %collective-permute-start.6 = (bf16[864,128]{1,0:T(8,128)(2,1)S(1)}, bf16[864,128]{1,0:T(8,128)(2,1)S(1)}, u32[]{:S(2)}, u32[]{:S(2)}) collective-permute-start(bf16[864,128]{1,0:T(8,128)(2,1)S(1)} %pad_maximum_fusion.refs_0_), channel_id=1, source_target_pairs={{0,4},{4,0},{8,12},{12,8},{16,20},{20,16},{24,28},{28,24},{1,5},{5... | collective-permute-start | bytes 663560 | tf_op jit(solution)/shard_map/ppermute | solution.py:788
  16.1 9.2 %collective-permute-start.5 = (bf16[864,128]{1,0:T(8,128)(2,1)S(1)}, bf16[864,128]{1,0:T(8,128)(2,1)S(1)}, u32[]{:S(2)}, u32[]{:S(2)}) collective-permute-start(bf16[864,128]{1,0:T(8,128)(2,1)S(1)} %pad_maximum_fusion.refs_0_), channel_id=1, source_target_pairs={{0,24},{4,28},{8,16},{12,20},{16,8},{20,12},{24,0},{28,4},{1,25},{... | collective-permute-start | bytes 663560 | tf_op jit(solution)/shard_map/ppermute | solution.py:788
  18.7 11.8 %collective-permute-start.4 = (bf16[864,128]{1,0:T(8,128)(2,1)S(1)}, bf16[864,128]{1,0:T(8,128)(2,1)S(1)}, u32[]{:S(2)}, u32[]{:S(2)}) collective-permute-start(bf16[864,128]{1,0:T(8,128)(2,1)S(1)} %pad_maximum_fusion.refs_0_), channel_id=1, source_target_pairs={{0,16},{4,20},{8,24},{12,28},{16,0},{20,4},{24,8},{28,12},{1,17},{... | collective-permute-start | bytes 663560 | tf_op jit(solution)/shard_map/ppermute | solution.py:788
  19.6 13.2 %collective-permute-start.3 = (bf16[864,128]{1,0:T(8,128)(2,1)S(1)}, bf16[864,128]{1,0:T(8,128)(2,1)S(1)}, u32[]{:S(2)}, u32[]{:S(2)}) collective-permute-start(bf16[864,128]{1,0:T(8,128)(2,1)S(1)} %pad_maximum_fusion.refs_0_), channel_id=1, source_target_pairs={{0,8},{4,12},{8,0},{12,4},{16,24},{20,28},{24,16},{28,20},{1,9},{5... | collective-permute-start | bytes 663560 | tf_op jit(solution)/shard_map/ppermute | solution.py:788
  21.1 7.2 %collective-permute-start.12 = (bf16[576,128]{1,0:T(8,128)(2,1)S(1)}, bf16[576,128]{1,0:T(8,128)(2,1)S(1)}, u32[]{:S(2)}, u32[]{:S(2)}) collective-permute-start(bf16[576,128]{1,0:T(8,128)(2,1)S(1)} %collective-permute-done.10), channel_id=1, source_target_pairs={{0,1},{1,2},{2,3},{3,0},{4,5},{5,6},{6,7},{7,4},{8,9},{9,10},{10,1... | collective-permute-start | bytes 442376 | tf_op jit(solution)/shard_map/ppermute | solution.py:784
  25.4 7.5 %collective-permute-start.9 = (bf16[864,128]{1,0:T(8,128)(2,1)S(1)}, bf16[864,128]{1,0:T(8,128)(2,1)S(1)}, u32[]{:S(2)}, u32[]{:S(2)}) collective-permute-start(bf16[864,128]{1,0:T(8,128)(2,1)S(1)} %collective-permute-done.5.refs_3_), channel_id=1, source_target_pairs={{0,4},{4,0},{8,12},{12,8},{16,20},{20,16},{24,28},{28,24},{1,5},{5... | collective-permute-start | bytes 663560 | tf_op jit(solution)/shard_map/ppermute | solution.py:788
  28.3 14.9 %collective-permute-start.15 = (bf16[1280,128]{1,0:T(8,128)(2,1)S(1)}, bf16[1280,128]{1,0:T(8,128)(2,1)S(1)}, u32[]{:S(2)}, u32[]{:S(2)}) collective-permute-start(bf16[1280,128]{1,0:T(8,128)(2,1)S(1)} %bitcast.66), channel_id=1, source_target_pairs={{0,24},{4,28},{8,16},{12,20},{16,8},{20,12},{24,0},{28,4},{1,25},{... | collective-permute-start | bytes 983048 | tf_op jit(solution)/shard_map/ppermute | solution.py:788
  29.9 13.8 %collective-permute-start.14 = (bf16[1280,128]{1,0:T(8,128)(2,1)S(1)}, bf16[1280,128]{1,0:T(8,128)(2,1)S(1)}, u32[]{:S(2)}, u32[]{:S(2)}) collective-permute-start(bf16[1280,128]{1,0:T(8,128)(2,1)S(1)} %bitcast.67), channel_id=1, source_target_pairs={{0,16},{4,20},{8,24},{12,28},{16,0},{20,4},{24,8},{28,12},{1,17},{... | collective-permute-start | bytes 983048 | tf_op jit(solution)/shard_map/ppermute | solution.py:788
  30.4 13.4 %collective-permute-start.13 = (bf16[1280,128]{1,0:T(8,128)(2,1)S(1)}, bf16[1280,128]{1,0:T(8,128)(2,1)S(1)}, u32[]{:S(2)}, u32[]{:S(2)}) collective-permute-start(bf16[1280,128]{1,0:T(8,128)(2,1)S(1)} %bitcast.68), channel_id=1, source_target_pairs={{0,8},{4,12},{8,0},{12,4},{16,24},{20,28},{24,16},{28,20},{1,9},{5... | collective-permute-start | bytes 983048 | tf_op jit(solution)/shard_map/ppermute | solution.py:788
  32.8 1.5 %collective-permute-start.8 = (bf16[864,128]{1,0:T(8,128)(2,1)S(1)}, bf16[864,128]{1,0:T(8,128)(2,1)S(1)}, u32[]{:S(2)}, u32[]{:S(2)}) collective-permute-start(bf16[864,128]{1,0:T(8,128)(2,1)S(1)} %collective-permute-done.4.refs_2_), channel_id=1, source_target_pairs={{0,4},{4,0},{8,12},{12,8},{16,20},{20,16},{24,28},{28,24},{1,5},{5... | collective-permute-start | bytes 663560 | tf_op jit(solution)/shard_map/ppermute | solution.py:788
  32.9 1.8 %collective-permute-start.7 = (bf16[864,128]{1,0:T(8,128)(2,1)S(1)}, bf16[864,128]{1,0:T(8,128)(2,1)S(1)}, u32[]{:S(2)}, u32[]{:S(2)}) collective-permute-start(bf16[864,128]{1,0:T(8,128)(2,1)S(1)} %collective-permute-done.3.refs_1_), channel_id=1, source_target_pairs={{0,4},{4,0},{8,12},{12,8},{16,20},{20,16},{24,28},{28,24},{1,5},{5... | collective-permute-start | bytes 663560 | tf_op jit(solution)/shard_map/ppermute | solution.py:788
  34.3 12.0 %collective-permute-start.16 = (bf16[1280,128]{1,0:T(8,128)(2,1)S(1)}, bf16[1280,128]{1,0:T(8,128)(2,1)S(1)}, u32[]{:S(2)}, u32[]{:S(2)}) collective-permute-start(bf16[1280,128]{1,0:T(8,128)(2,1)S(1)} %bitcast.69), channel_id=1, source_target_pairs={{0,4},{4,0},{8,12},{12,8},{16,20},{20,16},{24,28},{28,24},{1,5},{5... | collective-permute-start | bytes 983048 | tf_op jit(solution)/shard_map/ppermute | solution.py:788
  43.9 3.8 %collective-permute-start.17 = (bf16[1280,128]{1,0:T(8,128)(2,1)S(1)}, bf16[1280,128]{1,0:T(8,128)(2,1)S(1)}, u32[]{:S(2)}, u32[]{:S(2)}) collective-permute-start(bf16[1280,128]{1,0:T(8,128)(2,1)S(1)} %get-tuple-element.110.refs_5_), channel_id=1, source_target_pairs={{0,4},{4,0},{8,12},{12,8},{16,20},{20,16},{24,28},{28,24},{1,5},{5... | collective-permute-start | bytes 983048 | tf_op jit(solution)/shard_map/ppermute | solution.py:788
  44.0 4.2 %collective-permute-start.18 = (bf16[1280,128]{1,0:T(8,128)(2,1)S(1)}, bf16[1280,128]{1,0:T(8,128)(2,1)S(1)}, u32[]{:S(2)}, u32[]{:S(2)}) collective-permute-start(bf16[1280,128]{1,0:T(8,128)(2,1)S(1)} %get-tuple-element.111.refs_6_), channel_id=1, source_target_pairs={{0,4},{4,0},{8,12},{12,8},{16,20},{20,16},{24,28},{28,24},{1,5},{5... | collective-permute-start | bytes 983048 | tf_op jit(solution)/shard_map/ppermute | solution.py:788
  44.5 3.7 %collective-permute-start.19 = (bf16[1280,128]{1,0:T(8,128)(2,1)S(1)}, bf16[1280,128]{1,0:T(8,128)(2,1)S(1)}, u32[]{:S(2)}, u32[]{:S(2)}) collective-permute-start(bf16[1280,128]{1,0:T(8,128)(2,1)S(1)} %get-tuple-element.112.refs_7_), channel_id=1, source_target_pairs={{0,4},{4,0},{8,12},{12,8},{16,20},{20,16},{24,28},{28,24},{1,5},{5... | collective-permute-start | bytes 983048 | tf_op jit(solution)/shard_map/ppermute | solution.py:788
  44.7 17.9 %collective-permute-start.22 = (bf16[1024,128]{1,0:T(8,128)(2,1)S(1)}, bf16[1024,128]{1,0:T(8,128)(2,1)S(1)}, u32[]{:S(2)}, u32[]{:S(2)}) collective-permute-start(bf16[1024,128]{1,0:T(8,128)(2,1)S(1)} %gate.4.refs_12_.refs_2_.refs_10_), channel_id=1, source_target_pairs={{0,24},{4,28},{8,16},{12,20},{16,8},{20,12},{24,0},{28,4},{1,25},{... | collective-permute-start | bytes 786440 | tf_op jit(solution)/shard_map/ppermute | solution.py:788
  46.3 16.2 %collective-permute-start.21 = (bf16[1024,128]{1,0:T(8,128)(2,1)S(1)}, bf16[1024,128]{1,0:T(8,128)(2,1)S(1)}, u32[]{:S(2)}, u32[]{:S(2)}) collective-permute-start(bf16[1024,128]{1,0:T(8,128)(2,1)S(1)} %gate.4.refs_12_.refs_2_.refs_10_), channel_id=1, source_target_pairs={{0,16},{4,20},{8,24},{12,28},{16,0},{20,4},{24,8},{28,12},{1,17},{... | collective-permute-start | bytes 786440 | tf_op jit(solution)/shard_map/ppermute | solution.py:788
  47.7 14.9 %collective-permute-start.20 = (bf16[1024,128]{1,0:T(8,128)(2,1)S(1)}, bf16[1024,128]{1,0:T(8,128)(2,1)S(1)}, u32[]{:S(2)}, u32[]{:S(2)}) collective-permute-start(bf16[1024,128]{1,0:T(8,128)(2,1)S(1)} %gate.4.refs_12_.refs_2_.refs_10_), channel_id=1, source_target_pairs={{0,8},{4,12},{8,0},{12,4},{16,24},{20,28},{24,16},{28,20},{1,9},{5... | collective-permute-start | bytes 786440 | tf_op jit(solution)/shard_map/ppermute | solution.py:788
  48.2 15.6 %collective-permute-start.23 = (bf16[1024,128]{1,0:T(8,128)(2,1)S(1)}, bf16[1024,128]{1,0:T(8,128)(2,1)S(1)}, u32[]{:S(2)}, u32[]{:S(2)}) collective-permute-start(bf16[1024,128]{1,0:T(8,128)(2,1)S(1)} %gate.4.refs_12_.refs_2_.refs_10_), channel_id=1, source_target_pairs={{0,4},{4,0},{8,12},{12,8},{16,20},{20,16},{24,28},{28,24},{1,5},{5... | collective-permute-start | bytes 786440 | tf_op jit(solution)/shard_map/ppermute | solution.py:788
  62.7 1.7 %collective-permute-start.24 = (bf16[1024,128]{1,0:T(8,128)(2,1)S(1)}, bf16[1024,128]{1,0:T(8,128)(2,1)S(1)}, u32[]{:S(2)}, u32[]{:S(2)}) collective-permute-start(bf16[1024,128]{1,0:T(8,128)(2,1)S(1)} %get-tuple-element.115.refs_3_), channel_id=1, source_target_pairs={{0,4},{4,0},{8,12},{12,8},{16,20},{20,16},{24,28},{28,24},{1,5},{5... | collective-permute-start | bytes 786440 | tf_op jit(solution)/shard_map/ppermute | solution.py:788
  63.2 1.5 %collective-permute-start.25 = (bf16[1024,128]{1,0:T(8,128)(2,1)S(1)}, bf16[1024,128]{1,0:T(8,128)(2,1)S(1)}, u32[]{:S(2)}, u32[]{:S(2)}) collective-permute-start(bf16[1024,128]{1,0:T(8,128)(2,1)S(1)} %get-tuple-element.116.refs_4_), channel_id=1, source_target_pairs={{0,4},{4,0},{8,12},{12,8},{16,20},{20,16},{24,28},{28,24},{1,5},{5... | collective-permute-start | bytes 786440 | tf_op jit(solution)/shard_map/ppermute | solution.py:788
  63.3 1.8 %collective-permute-start.26 = (bf16[1024,128]{1,0:T(8,128)(2,1)S(1)}, bf16[1024,128]{1,0:T(8,128)(2,1)S(1)}, u32[]{:S(2)}, u32[]{:S(2)}) collective-permute-start(bf16[1024,128]{1,0:T(8,128)(2,1)S(1)} %get-tuple-element.117.refs_5_), channel_id=1, source_target_pairs={{0,4},{4,0},{8,12},{12,8},{16,20},{20,16},{24,28},{28,24},{1,5},{5... | collective-permute-start | bytes 786440 | tf_op jit(solution)/shard_map/ppermute | solution.py:788
  63.7 16.3 %collective-permute-start.27 = (bf16[4,1024,128]{2,1,0:T(8,128)(2,1)S(1)}, bf16[4,1024,128]{2,1,0:T(8,128)(2,1)S(1)}, u32[]{:S(2)}, u32[]{:S(2)}) collective-permute-start(bf16[4,1024,128]{2,1,0:T(8,128)(2,1)S(1)} %get-tuple-element.130), channel_id=1, source_target_pairs={{0,4},{4,0},{8,12},{12,8},{16,20},{20,16},{24,28},{28,24},{1,5},{5... | collective-permute-start | bytes 3145736 | tf_op jit(solution)/shard_map/ppermute | solution.py:788
  77.8 2.7 %collective-permute-start.28 = (bf16[4,1024,128]{2,1,0:T(8,128)(2,1)S(1)}, bf16[4,1024,128]{2,1,0:T(8,128)(2,1)S(1)}, u32[]{:S(2)}, u32[]{:S(2)}) collective-permute-start(bf16[4,1024,128]{2,1,0:T(8,128)(2,1)S(1)} %get-tuple-element.131), channel_id=1, source_target_pairs={{0,4},{4,0},{8,12},{12,8},{16,20},{20,16},{24,28},{28,24},{1,5},{5... | collective-permute-start | bytes 3145736 | tf_op jit(solution)/shard_map/ppermute | solution.py:788
  81.5 14.5 %collective-permute-start.29 = (bf16[2,1024,128]{2,1,0:T(8,128)(2,1)S(1)}, bf16[2,1024,128]{2,1,0:T(8,128)(2,1)S(1)}, u32[]{:S(2)}, u32[]{:S(2)}) collective-permute-start(bf16[2,1024,128]{2,1,0:T(8,128)(2,1)S(1)} %get-tuple-element.148), channel_id=1, source_target_pairs={{0,8},{4,12},{8,0},{12,4},{16,24},{20,28},{24,16},{28,20},{1,9},{5... | collective-permute-start | bytes 1572872 | tf_op jit(solution)/shard_map/ppermute | solution.py:788
  83.0 13.9 %collective-permute-start.30 = (bf16[2,1024,128]{2,1,0:T(8,128)(2,1)S(1)}, bf16[2,1024,128]{2,1,0:T(8,128)(2,1)S(1)}, u32[]{:S(2)}, u32[]{:S(2)}) collective-permute-start(bf16[2,1024,128]{2,1,0:T(8,128)(2,1)S(1)} %get-tuple-element.150), channel_id=1, source_target_pairs={{0,16},{4,20},{8,24},{12,28},{16,0},{20,4},{24,8},{28,12},{1,17},{... | collective-permute-start | bytes 1572872 | tf_op jit(solution)/shard_map/ppermute | solution.py:788
  97.9 2.8 %collective-permute-start.31 = (bf16[4,1072,128]{2,1,0:T(8,128)(2,1)S(1)}, bf16[4,1072,128]{2,1,0:T(8,128)(2,1)S(1)}, u32[]{:S(2)}, u32[]{:S(2)}) collective-permute-start(bf16[4,1072,128]{2,1,0:T(8,128)(2,1)S(1)} %get-tuple-element.153), channel_id=1, source_target_pairs={{0,4},{4,0},{8,12},{12,8},{16,20},{20,16},{24,28},{28,24},{1,5},{5... | collective-permute-start | bytes 3293192 | tf_op jit(solution)/shard_map/ppermute | solution.py:788
  98.0 10.1 %collective-permute-start.38 = (bf16[1024,128]{1,0:T(8,128)(2,1)S(1)}, bf16[1024,128]{1,0:T(8,128)(2,1)S(1)}, u32[]{:S(2)}, u32[]{:S(2)}) collective-permute-start(bf16[1024,128]{1,0:T(8,128)(2,1)S(1)} %get-tuple-element.165), channel_id=1, source_target_pairs={{0,16},{4,20},{8,24},{12,28},{16,0},{20,4},{24,8},{28,12},{1,17},{... | collective-permute-start | bytes 786440 | tf_op jit(solution)/shard_map/ppermute | solution.py:788
  98.8 9.4 %collective-permute-start.39 = (bf16[1024,128]{1,0:T(8,128)(2,1)S(1)}, bf16[1024,128]{1,0:T(8,128)(2,1)S(1)}, u32[]{:S(2)}, u32[]{:S(2)}) collective-permute-start(bf16[1024,128]{1,0:T(8,128)(2,1)S(1)} %get-tuple-element.167), channel_id=1, source_target_pairs={{0,8},{4,12},{8,0},{12,4},{16,24},{20,28},{24,16},{28,20},{1,9},{5... | collective-permute-start | bytes 786440 | tf_op jit(solution)/shard_map/ppermute | solution.py:788
  101.5 12.3 %collective-permute-start.32 = (bf16[1072,128]{1,0:T(8,128)(2,1)S(1)}, bf16[1072,128]{1,0:T(8,128)(2,1)S(1)}, u32[]{:S(2)}, u32[]{:S(2)}) collective-permute-start(bf16[1072,128]{1,0:T(8,128)(2,1)S(1)} %get-tuple-element.156), channel_id=1, source_target_pairs={{0,8},{4,12},{8,0},{12,4},{16,24},{20,28},{24,16},{28,20},{1,9},{5... | collective-permute-start | bytes 823304 | tf_op jit(solution)/shard_map/ppermute | solution.py:788
  102.2 15.6 %collective-permute-start.33 = (bf16[1072,128]{1,0:T(8,128)(2,1)S(1)}, bf16[1072,128]{1,0:T(8,128)(2,1)S(1)}, u32[]{:S(2)}, u32[]{:S(2)}) collective-permute-start(bf16[1072,128]{1,0:T(8,128)(2,1)S(1)} %get-tuple-element.157), channel_id=1, source_target_pairs={{0,16},{4,20},{8,24},{12,28},{16,0},{20,4},{24,8},{28,12},{1,17},{... | collective-permute-start | bytes 823304 | tf_op jit(solution)/shard_map/ppermute | solution.py:788
  103.6 16.1 %collective-permute-start.34 = (bf16[1072,128]{1,0:T(8,128)(2,1)S(1)}, bf16[1072,128]{1,0:T(8,128)(2,1)S(1)}, u32[]{:S(2)}, u32[]{:S(2)}) collective-permute-start(bf16[1072,128]{1,0:T(8,128)(2,1)S(1)} %get-tuple-element.158), channel_id=1, source_target_pairs={{0,24},{4,28},{8,16},{12,20},{16,8},{20,12},{24,0},{28,4},{1,25},{... | collective-permute-start | bytes 823304 | tf_op jit(solution)/shard_map/ppermute | solution.py:788
  108.8 16.0 %collective-permute-start.40 = (bf16[512,128]{1,0:T(8,128)(2,1)S(1)}, bf16[512,128]{1,0:T(8,128)(2,1)S(1)}, u32[]{:S(2)}, u32[]{:S(2)}) collective-permute-start(bf16[512,128]{1,0:T(8,128)(2,1)S(1)} %get-tuple-element.169), channel_id=1, source_target_pairs={{0,1},{1,2},{2,3},{3,0},{4,5},{5,6},{6,7},{7,4},{8,9},{9,10},{10,1... | collective-permute-start | bytes 393224 | tf_op jit(solution)/shard_map/ppermute | solution.py:784
  110.6 14.3 %collective-permute-start.41 = (bf16[512,128]{1,0:T(8,128)(2,1)S(1)}, bf16[512,128]{1,0:T(8,128)(2,1)S(1)}, u32[]{:S(2)}, u32[]{:S(2)}) collective-permute-start(bf16[512,128]{1,0:T(8,128)(2,1)S(1)} %get-tuple-element.170), channel_id=1, source_target_pairs={{0,2},{1,3},{2,0},{3,1},{4,6},{5,7},{6,4},{7,5},{8,10},{9,11},{10,... | collective-permute-start | bytes 393224 | tf_op jit(solution)/shard_map/ppermute | solution.py:784
  113.9 11.0 %collective-permute-start.42 = (bf16[512,128]{1,0:T(8,128)(2,1)S(1)}, bf16[512,128]{1,0:T(8,128)(2,1)S(1)}, u32[]{:S(2)}, u32[]{:S(2)}) collective-permute-start(bf16[512,128]{1,0:T(8,128)(2,1)S(1)} %get-tuple-element.171), channel_id=1, source_target_pairs={{0,3},{1,0},{2,1},{3,2},{4,7},{5,4},{6,5},{7,6},{8,11},{9,8},{10,9... | collective-permute-start | bytes 393224 | tf_op jit(solution)/shard_map/ppermute | solution.py:784
  120.4 10.1 %collective-permute-start.35 = (bf16[256,128]{1,0:T(8,128)(2,1)S(1)}, bf16[256,128]{1,0:T(8,128)(2,1)S(1)}, u32[]{:S(2)}, u32[]{:S(2)}) collective-permute-start(bf16[256,128]{1,0:T(8,128)(2,1)S(1)} %get-tuple-element.162), channel_id=1, source_target_pairs={{0,1},{1,2},{2,3},{3,0},{4,5},{5,6},{6,7},{7,4},{8,9},{9,10},{10,1... | collective-permute-start | bytes 196616 | tf_op jit(solution)/shard_map/ppermute | solution.py:784
  122.1 8.3 %collective-permute-start.36 = (bf16[256,128]{1,0:T(8,128)(2,1)S(1)}, bf16[256,128]{1,0:T(8,128)(2,1)S(1)}, u32[]{:S(2)}, u32[]{:S(2)}) collective-permute-start(bf16[256,128]{1,0:T(8,128)(2,1)S(1)} %get-tuple-element.163), channel_id=1, source_target_pairs={{0,2},{1,3},{2,0},{3,1},{4,6},{5,7},{6,4},{7,5},{8,10},{9,11},{10,... | collective-permute-start | bytes 196616 | tf_op jit(solution)/shard_map/ppermute | solution.py:784
  124.9 5.6 %collective-permute-start.37 = (bf16[256,128]{1,0:T(8,128)(2,1)S(1)}, bf16[256,128]{1,0:T(8,128)(2,1)S(1)}, u32[]{:S(2)}, u32[]{:S(2)}) collective-permute-start(bf16[256,128]{1,0:T(8,128)(2,1)S(1)} %get-tuple-element.164), channel_id=1, source_target_pairs={{0,3},{1,0},{2,1},{3,2},{4,7},{5,4},{6,5},{7,6},{8,11},{9,8},{10,9... | collective-permute-start | bytes 196616 | tf_op jit(solution)/shard_map/ppermute | solution.py:784
  126.0 16.6 %copy-start.12 = (f32[4,512]{1,0:T(4,128)S(1)}, f32[4,512]{1,0:T(4,128)}, u32[]{:S(2)}) copy-start(f32[4,512]{1,0:T(4,128)} %lf_ref.1) | copy-start | bytes 24580
  126.1 16.6 %copy-start.13 = (f32[4,512]{1,0:T(4,128)S(1)}, f32[4,512]{1,0:T(4,128)}, u32[]{:S(2)}) copy-start(f32[4,512]{1,0:T(4,128)} %ls_ref.1) | copy-start | bytes 24580
  (11 other events, 90.8 us)
